TPU v7x, 32 devices: a whole 2x2x4 slice. The times are simulated.
32 devices in a mesh: energy: 8 (over y, x, core), slab: 4 (over z).
Axes of the slice: x: 2, y: 2, z: 4, core: 2. Of those that a mesh axis runs over, the one named last changes fastest.
Arguments:
- g_lesser: bfloat16 [8, 4, 320, 640], P('energy', 'slab'), may hold values from -6 to 6
- g_retarded: bfloat16 [8, 4, 320, 640], P('energy', 'slab'), may hold values from -0.25 to 0.25
- screened: bfloat16 [8, 4, 320, 640], P(None, 'slab', 'energy'), may hold values from -2 to 2
- coupling: bfloat16 [4, 320, 320], P('slab'), may hold values from -1.5 to 1.5, as said below
Outputs:
- correction: bfloat16 [8, 4, 320, 640], P('energy', 'slab')
Inputs may be any that keep to these rules, and one draw needn't show every extreme that they name: `coupling`: coupling_s is the diagonal entries between 0.75 and 1 plus independent small entries.
All inputs are finite; a program needn't handle non-finite values.
Results may differ from a plain program's by a relative error of at most 0.02.
Values may be sent and summed in bfloat16 or wider, within the bound.
No kernel may reach another device: no remote copies, remote signals or barrier semaphores. Data moves between devices by JAX's collectives and lax.ppermute only.
A program may use at most 64 MiB of HBM per device.

v0:
```python
import math

import jax
import jax.numpy as jnp
from jax import lax
from jax.sharding import PartitionSpec as P


def passed_along(array, axis, by):
    devices = lax.axis_size(axis)
    pairs = [(i, i + by) for i in range(devices) if 0 <= i + by < devices]
    return lax.ppermute(array, axis, pairs)


def spectral(owned, inter):
    count = owned.shape[0]
    half = owned.shape[-1] // 2
    rows = owned.shape[2]
    length = 2 * count
    freq = jnp.arange(length, dtype=jnp.int32)[:, None]
    point = jnp.arange(count, dtype=jnp.int32)[None, :]
    phase = (freq * point % length).astype(jnp.float32) * (2.0 * math.pi / length)
    fwd_re = jnp.cos(phase)
    fwd_im = -jnp.sin(phase)
    inv_re = jnp.cos(phase).T / length
    inv_im = jnp.sin(phase).T / length
    exact = lax.Precision.HIGHEST

    def forward(block):
        values = block.astype(jnp.float32)
        part_re = values[..., :half].reshape(count, -1)
        part_im = values[..., half:].reshape(count, -1)
        out_re = jnp.dot(fwd_re, part_re, precision=exact) - jnp.dot(
            fwd_im, part_im, precision=exact
        )
        out_im = jnp.dot(fwd_re, part_im, precision=exact) + jnp.dot(
            fwd_im, part_re, precision=exact
        )
        return (out_re, out_im)

    lesser_re, lesser_im = forward(owned)
    inter_re, inter_im = forward(inter)
    prod_re = lesser_re * inter_re - lesser_im * inter_im
    prod_im = lesser_re * inter_im + lesser_im * inter_re
    conv_re = jnp.dot(inv_re, prod_re, precision=exact) - jnp.dot(inv_im, prod_im, precision=exact)
    conv_im = jnp.dot(inv_re, prod_im, precision=exact) + jnp.dot(inv_im, prod_re, precision=exact)
    shape = (count, owned.shape[1], rows, half)
    return jnp.concatenate([-conv_im.reshape(shape), conv_re.reshape(shape)], axis=-1).astype(
        jnp.bfloat16
    )


def transport(link, state):
    count = state.shape[0]
    half = state.shape[-1] // 2
    left = jnp.einsum("ab,nbc->nac", link, state, preferred_element_type=jnp.float32).astype(
        jnp.bfloat16
    )
    parts = left.reshape(count, half, 2, half)
    moved = jnp.einsum("nakb,cb->nakc", parts, link, preferred_element_type=jnp.float32)
    return moved.reshape(count, half, 2 * half)


def sandwich(green, state):
    half = green.shape[-1] // 2
    green_re = green[..., :half]
    green_im = green[..., half:]
    state_re = state[..., :half]
    state_im = state[..., half:]
    right_mat = jnp.concatenate(
        [jnp.concatenate([state_re, state_im], -1), jnp.concatenate([-state_im, state_re], -1)], 1
    )
    left = jnp.einsum("nab,nbc->nac", green, right_mat, preferred_element_type=jnp.float32).astype(
        jnp.bfloat16
    )
    tr_re = jnp.swapaxes(green_re, 1, 2)
    tr_im = jnp.swapaxes(green_im, 1, 2)
    adjoint = jnp.concatenate(
        [jnp.concatenate([tr_re, -tr_im], -1), jnp.concatenate([tr_im, tr_re], -1)], 1
    )
    return jnp.einsum("nab,nbc->nac", left, adjoint, preferred_element_type=jnp.float32).astype(
        jnp.bfloat16
    )


def local(g_lesser, g_retarded, screened, coupling):
    owned = lax.all_to_all(g_lesser, "energy", split_axis=2, concat_axis=0, tiled=True)
    sigma_rows = spectral(owned, screened)
    sigma = lax.all_to_all(sigma_rows, "energy", split_axis=0, concat_axis=2, tiled=True)[:, 0]
    link = coupling[0]
    green = g_retarded[:, 0]
    base = sigma.astype(jnp.float32)

    def relay_step(turn, state):
        before = passed_along(state.astype(jnp.bfloat16), "slab", 1)
        return base + transport(link, before)

    state = lax.fori_loop(0, lax.axis_size("slab") - 1, relay_step, base)
    return sandwich(green, state.astype(jnp.bfloat16))[:, None]


def solution(mesh):
    placed = (
        P("energy", "slab", None, None),
        P("energy", "slab", None, None),
        P(None, "slab", "energy", None),
        P("slab", None, None),
    )
    return jax.shard_map(
        local,
        mesh=mesh,
        in_specs=placed,
        out_specs=P("energy", "slab", None, None),
        check_vma=False,
    )
```

profile of v0, /device:TPU:26, one launch (start us, length us, event | category | flops | bytes accessed | tf_op | source)
XLA Modules:
  0.0 86.0 jit_solution(8874216670199014097)
XLA Ops:
  0.0 1.6 %copy.28 = bf16[1,1,320,640]{3,1,0,2:T(2,128)(2,1)S(1)} copy(bf16[1,1,320,640]{3,2,1,0:T(8,128)(2,1)} %param.6) | data formatting | bytes 819200 | tf_op args[0]
  2.2 3.1 %reduce = bf16[320,640]{1,0:T(8,128)(2,1)S(1)} reduce(bf16[320,1,1,640]{3,2,1,0:T(2,128)(2,1)S(1)} %bitcast.80, bf16[]{:T(256)} %broadcast.78), dimensions={1,2}, to_apply=%bitcast.68.reduce_sub_computation | reduce | bytes 819202
  5.3 0.9 reshape.134
  6.1 4.3 %all-to-all-start = ((bf16[8,2,12800]{2,1,0:T(2,128)(2,1)}), bf16[8,2,12800]{2,1,0:T(2,128)(2,1)S(1)}, u32[]{:S(2)}, u32[]{:S(2)}) async-start(bf16[8,2,12800]{2,1,0:T(2,128)(2,1)} %reshape.134), calls=%async_computation | async-start | bytes 819200 | tf_op jit(solution)/shard_map/all_to_all | solution.py:87
  11.4 0.5 convolution_add_fusion.1
  12.5 0.5 convolution_subtract_fusion
  13.0 4.4 %all-to-all-done = bf16[8,2,12800]{2,1,0:T(2,128)(2,1)S(1)} async-done(((bf16[8,2,12800]{2,1,0:T(2,128)(2,1)}), bf16[8,2,12800]{2,1,0:T(2,128)(2,1)S(1)}, u32[]{:S(2)}, u32[]{:S(2)}) %all-to-all-start) | async-done | bytes 409632 | tf_op jit(solution)/shard_map/all_to_all | solution.py:87
  19.9 0.7 multiply_add_fusion
  20.6 0.5 fusion.51
  21.2 0.5 fusion.50
  21.7 0.6 fusion.6
  22.5 0.5 fusion.7
  23.2 0.9 %pad_maximum_fusion = bf16[8,1,40,640]{3,2,1,0:T(8,128)(2,1)} fusion(bf16[8,1,40,320]{3,2,1,0:T(8,128)(2,1)S(1)} %bitcast.87, bf16[8,1,40,320]{3,2,1,0:T(8,128)(2,1)S(1)} %bitcast.86), kind=kLoop, calls=%fused_computation.33 | loop fusion | flops 819200 | bytes 819200 | tf_op jit(solution)/shard_map/concatenate | solution.py:48
  24.1 4.8 %all-to-all-start.1 = ((bf16[8,1,40,640]{3,2,1,0:T(8,128)(2,1)}), bf16[8,1,40,640]{3,2,1,0:T(8,128)(2,1)S(1)}, u32[]{:S(2)}, u32[]{:S(2)}) async-start(bf16[8,1,40,640]{3,2,1,0:T(8,128)(2,1)} %pad_maximum_fusion), calls=%async_computation.1 | async-start | bytes 819200 | tf_op jit(solution)/shard_map/all_to_all | solution.py:89
  29.1 6.9 %all-to-all-done.1 = bf16[8,1,40,640]{3,2,1,0:T(8,128)(2,1)S(1)} async-done(((bf16[8,1,40,640]{3,2,1,0:T(8,128)(2,1)}), bf16[8,1,40,640]{3,2,1,0:T(8,128)(2,1)S(1)}, u32[]{:S(2)}, u32[]{:S(2)}) %all-to-all-start.1) | async-done | bytes 409632 | tf_op jit(solution)/shard_map/all_to_all | solution.py:89
  36.3 0.9 %copy-done = bf16[1,320,320]{2,1,0:T(8,128)(2,1)S(1)} copy-done((bf16[1,320,320]{2,1,0:T(8,128)(2,1)S(1)}, bf16[1,320,320]{2,1,0:T(8,128)(2,1)}, u32[]{:S(2)}) %copy-start) | copy-done | bytes 204824
  37.2 46.9 %while.10 = (s32[]{:T(128)}, bf16[1,320,640]{1,2,0:T(8,128)(2,1)S(1)}, bf16[320,320]{1,0:T(8,128)(2,1)S(1)}, f32[1,320,640]{1,2,0:T(8,128)S(1)}, s32[]{:T(128)}) while((s32[]{:T(128)}, bf16[1,320,640]{1,2,0:T(8,128)(2,1)S(1)}, bf16[320,320]{1,0:T(8,128)(2,1)S(1)}, f32[1,320,640]{1,2,0:T(8,128)S(1)}, s32[]{:T(128)}) %tuple.30), condition=%wide.region_1.2_spmd, body=%wide.region_0.1_spmd.sunk | while | flops 262758400 | bytes 6963301 | solution.py:98
  37.2 1.3 %collective-permute-start = (bf16[1,320,640]{1,2,0:T(8,128)(2,1)S(1)}, bf16[1,320,640]{1,2,0:T(8,128)(2,1)S(1)}, u32[]{:S(2)}, u32[]{:S(2)}) collective-permute-start(bf16[1,320,640]{1,2,0:T(8,128)(2,1)S(1)} %get-tuple-element.90), channel_id=1, source_target_pairs={{0,1},{1,2},{2,3},{4,5},{5,6},{6,7},{8,9},{9,10},{10,11},{12,13},{... | collective-permute-start | bytes 1228808 | tf_op jit(solution)/shard_map/while/body/eval_jaxpr/ppermute | solution.py:12
  38.5 13.8 %collective-permute-done = bf16[1,320,640]{1,2,0:T(8,128)(2,1)S(1)} collective-permute-done((bf16[1,320,640]{1,2,0:T(8,128)(2,1)S(1)}, bf16[1,320,640]{1,2,0:T(8,128)(2,1)S(1)}, u32[]{:S(2)}, u32[]{:S(2)}) %collective-permute-start) | collective-permute-done | bytes 409632 | tf_op jit(solution)/shard_map/while/body/eval_jaxpr/ppermute | solution.py:12
  53.7 1.3 %collective-permute-start = (bf16[1,320,640]{1,2,0:T(8,128)(2,1)S(1)}, bf16[1,320,640]{1,2,0:T(8,128)(2,1)S(1)}, u32[]{:S(2)}, u32[]{:S(2)}) collective-permute-start(bf16[1,320,640]{1,2,0:T(8,128)(2,1)S(1)} %get-tuple-element.90), channel_id=1, source_target_pairs={{0,1},{1,2},{2,3},{4,5},{5,6},{6,7},{8,9},{9,10},{10,11},{12,13},{... | collective-permute-start | bytes 1228808 | tf_op jit(solution)/shard_map/while/body/eval_jaxpr/ppermute | solution.py:12
  55.0 12.9 %collective-permute-done = bf16[1,320,640]{1,2,0:T(8,128)(2,1)S(1)} collective-permute-done((bf16[1,320,640]{1,2,0:T(8,128)(2,1)S(1)}, bf16[1,320,640]{1,2,0:T(8,128)(2,1)S(1)}, u32[]{:S(2)}, u32[]{:S(2)}) %collective-permute-start) | collective-permute-done | bytes 409632 | tf_op jit(solution)/shard_map/while/body/eval_jaxpr/ppermute | solution.py:12
  69.4 1.3 %collective-permute-start = (bf16[1,320,640]{1,2,0:T(8,128)(2,1)S(1)}, bf16[1,320,640]{1,2,0:T(8,128)(2,1)S(1)}, u32[]{:S(2)}, u32[]{:S(2)}) collective-permute-start(bf16[1,320,640]{1,2,0:T(8,128)(2,1)S(1)} %get-tuple-element.90), channel_id=1, source_target_pairs={{0,1},{1,2},{2,3},{4,5},{5,6},{6,7},{8,9},{9,10},{10,11},{12,13},{... | collective-permute-start | bytes 1228808 | tf_op jit(solution)/shard_map/while/body/eval_jaxpr/ppermute | solution.py:12
  70.7 12.0 %collective-permute-done = bf16[1,320,640]{1,2,0:T(8,128)(2,1)S(1)} collective-permute-done((bf16[1,320,640]{1,2,0:T(8,128)(2,1)S(1)}, bf16[1,320,640]{1,2,0:T(8,128)(2,1)S(1)}, u32[]{:S(2)}, u32[]{:S(2)}) %collective-permute-start) | collective-permute-done | bytes 409632 | tf_op jit(solution)/shard_map/while/body/eval_jaxpr/ppermute | solution.py:12
  84.2 1.7 %fusion.8 = bf16[1,1,320,640]{3,2,1,0:T(8,128)(2,1)} fusion(bf16[1,320,320]{1,2,0:T(8,128)(2,1)S(1)} %get-tuple-element.51, bf16[1,320,320]{1,2,0:T(8,128)(2,1)S(1)} %get-tuple-element.50, bf16[1,320,640]{1,2,0:T(8,128)(2,1)S(1)} %get-tuple-element.27, bf16[1,320,320]{1,2,0:T(8,128)(2,1)S(1)} %get-tuple-element.53, ...), kind=kOutput, calls=%fused_computation.18 | convolution fusion | flops 530432000 | bytes 2252800 | tf_op jit(solution)/shard_map/nab,nbc->nac/dot_general | solution.py:81
  (37 shorter events, 9.5 us)
Async XLA Ops:
  5.3 5.1 %copy-start.2 = (bf16[8,1,40,640]{3,2,1,0:T(8,128)(2,1)S(1)}, bf16[8,1,40,640]{3,2,1,0:T(8,128)(2,1)}, u32[]{:S(2)}) copy-start(bf16[8,1,40,640]{3,2,1,0:T(8,128)(2,1)} %param.8) | copy-start | bytes 1228804
  6.1 11.3 %all-to-all-start = ((bf16[8,2,12800]{2,1,0:T(2,128)(2,1)}), bf16[8,2,12800]{2,1,0:T(2,128)(2,1)S(1)}, u32[]{:S(2)}, u32[]{:S(2)}) async-start(bf16[8,2,12800]{2,1,0:T(2,128)(2,1)} %reshape.134), calls=%async_computation | async-start | bytes 819200 | tf_op jit(solution)/shard_map/all_to_all | solution.py:87
  23.0 5.9 %copy-start.1 = (bf16[1,1,320,640]{3,2,1,0:T(8,128)(2,1)S(1)}, bf16[1,1,320,640]{3,2,1,0:T(8,128)(2,1)}, u32[]{:S(2)}) copy-start(bf16[1,1,320,640]{3,2,1,0:T(8,128)(2,1)} %param.7) | copy-start | bytes 1228804
  24.1 11.9 %all-to-all-start.1 = ((bf16[8,1,40,640]{3,2,1,0:T(8,128)(2,1)}), bf16[8,1,40,640]{3,2,1,0:T(8,128)(2,1)S(1)}, u32[]{:S(2)}, u32[]{:S(2)}) async-start(bf16[8,1,40,640]{3,2,1,0:T(8,128)(2,1)} %pad_maximum_fusion), calls=%async_computation.1 | async-start | bytes 819200 | tf_op jit(solution)/shard_map/all_to_all | solution.py:89
  36.3 0.9 %copy-start = (bf16[1,320,320]{2,1,0:T(8,128)(2,1)S(1)}, bf16[1,320,320]{2,1,0:T(8,128)(2,1)}, u32[]{:S(2)}) copy-start(bf16[1,320,320]{2,1,0:T(8,128)(2,1)} %param.9) | copy-start | bytes 614404
  37.2 15.1 %collective-permute-start = (bf16[1,320,640]{1,2,0:T(8,128)(2,1)S(1)}, bf16[1,320,640]{1,2,0:T(8,128)(2,1)S(1)}, u32[]{:S(2)}, u32[]{:S(2)}) collective-permute-start(bf16[1,320,640]{1,2,0:T(8,128)(2,1)S(1)} %get-tuple-element.90), channel_id=1, source_target_pairs={{0,1},{1,2},{2,3},{4,5},{5,6},{6,7},{8,9},{9,10},{10,11},{12,13},{... | collective-permute-start | bytes 1228808 | tf_op jit(solution)/shard_map/while/body/eval_jaxpr/ppermute | solution.py:12
  53.7 14.2 %collective-permute-start = (bf16[1,320,640]{1,2,0:T(8,128)(2,1)S(1)}, bf16[1,320,640]{1,2,0:T(8,128)(2,1)S(1)}, u32[]{:S(2)}, u32[]{:S(2)}) collective-permute-start(bf16[1,320,640]{1,2,0:T(8,128)(2,1)S(1)} %get-tuple-element.90), channel_id=1, source_target_pairs={{0,1},{1,2},{2,3},{4,5},{5,6},{6,7},{8,9},{9,10},{10,11},{12,13},{... | collective-permute-start | bytes 1228808 | tf_op jit(solution)/shard_map/while/body/eval_jaxpr/ppermute | solution.py:12
  69.4 13.3 %collective-permute-start = (bf16[1,320,640]{1,2,0:T(8,128)(2,1)S(1)}, bf16[1,320,640]{1,2,0:T(8,128)(2,1)S(1)}, u32[]{:S(2)}, u32[]{:S(2)}) collective-permute-start(bf16[1,320,640]{1,2,0:T(8,128)(2,1)S(1)} %get-tuple-element.90), channel_id=1, source_target_pairs={{0,1},{1,2},{2,3},{4,5},{5,6},{6,7},{8,9},{9,10},{10,11},{12,13},{... | collective-permute-start | bytes 1228808 | tf_op jit(solution)/shard_map/while/body/eval_jaxpr/ppermute | solution.py:12
where the time goes:
time: 86.4 us; the launch traced here: 86 us
  waiting for transfers between devices  50.1 us (58%)
  starting transfers between devices  12.9 us (15%)
  matrix products  10.8 us (12%)
  local copies, waits for them, and re-layouts  7.18 us (8%)
  other arithmetic  4.51 us (5%)
    ppermute x3, waiting for transfers between devices, passed_along(): return lax.ppermute(array, axis, pairs)  38.8 us
    all_to_all x1, waiting for transfers between devices, local(): lax.all_to_all(sigma_rows, 'energy', split_axis=0, concat_axis=2, tiled=T...  6.93 us
    all_to_all x1, starting transfers between devices, local(): lax.all_to_all(sigma_rows, 'energy', split_axis=0, concat_axis=2, tiled=T...  4.83 us
    all_to_all x1, waiting for transfers between devices, local(): lax.all_to_all(g_lesser, 'energy', split_axis=2, concat_axis=0, tiled=True)  4.43 us
    unnamed x11, local copies, waits for them, and re-layouts  4.27 us
    all_to_all x1, starting transfers between devices, local(): lax.all_to_all(g_lesser, 'energy', split_axis=2, concat_axis=0, tiled=True)  4.25 us
    ppermute x3, starting transfers between devices, passed_along(): return lax.ppermute(array, axis, pairs)  3.86 us
    unnamed x2, other arithmetic  3.17 us
  transfers between devices with their start and end apart: 5, of which 5 were waited for; matrix products, arithmetic and copies ran while one was open for 3% of the time, Pallas kernels for 0%

commit v1 on v0

v1 whole, which is shorter than its diff:
```python
import functools

import jax
import jax.numpy as jnp
from jax import lax
from jax.experimental import pallas as pl
from jax.experimental.pallas import tpu as pltpu
from jax.sharding import PartitionSpec as P

ENERGY = "energy"
SLAB = "slab"
WHOLE = pl.BlockSpec(memory_space=pltpu.VMEM)
SCALAR = pl.BlockSpec(memory_space=pltpu.SMEM)


def in_vmem(*arrays):
    return [pltpu.with_memory_space_constraint(x, pltpu.VMEM) for x in arrays]


def swap_with(array, mask):
    devices = lax.axis_size(ENERGY)
    return lax.ppermute(array, ENERGY, [(i, i ^ mask) for i in range(devices)])


def conv_kernel(chips, place_ref, inter_ref, *refs):
    pieces = refs[: 2 * chips]
    re_ref, im_ref, a_ref, b_ref, w_ref, v_ref, sum_ref = refs[2 * chips :]
    chip, side = place_ref[0], place_ref[1]
    rows, width = inter_ref.shape[1:]
    half = width // 2
    left = lax.broadcasted_iota(jnp.int32, (rows, width), 1) < half

    def swapped(x):
        return jnp.concatenate([x[:, half:], x[:, :half]], axis=1)

    @pl.when(side == 0)
    def _():
        a_ref[0] = jnp.zeros((rows, width), jnp.float32)
        b_ref[0] = jnp.zeros((rows, width), jnp.float32)

    for other in range(2):
        for j in range(chips):
            x = pieces[other * chips + j][...].astype(jnp.float32)
            y = swapped(x)
            slot = 2 * (chip ^ j) + (side ^ other) + 1 - side
            a_ref[slot] = jnp.where(left, x, y)
            b_ref[slot] = jnp.where(left, y, x)
    for m in range(2 * chips):
        x = inter_ref[m].astype(jnp.float32)
        y = swapped(x)
        w_ref[m] = x
        v_ref[m] = jnp.where(left, -y, y)

    step = 8 if rows % 8 == 0 else rows
    lanes = 128 if width % 128 == 0 else width

    def tile(t, carry):
        here = pl.ds(pl.multiple_of(t * step, step), step)
        for c in range(0, width, lanes):
            at = pl.ds(c, lanes)
            for j in range(chips):
                total = None
                for m in range(2 * j + 2):
                    s = 2 * j + 1 - m
                    term = a_ref[s, here, at] * v_ref[m, here, at] - b_ref[s, here, at] * w_ref[m, here, at]
                    total = term if total is None else total + term
                sum_ref[j, here, at] = total
        return carry

    lax.fori_loop(0, rows // step, tile, 0)
    for j in range(chips):
        out = sum_ref[j].astype(jnp.bfloat16)
        re_ref[chip ^ j] = out[:, :half]
        im_ref[chip ^ j] = out[:, half:]


def convolve(chips, place, inter, pieces):
    count, rows, width = inter.shape
    part = pltpu.VMEM((chips, rows, width // 2), jnp.bfloat16)
    block = lambda n: pltpu.VMEM((n, rows, width), jnp.float32)
    return pl.pallas_call(
        functools.partial(conv_kernel, chips),
        out_shape=[part, part],
        in_specs=[SCALAR] + [WHOLE] * (1 + 2 * chips),
        out_specs=[WHOLE, WHOLE],
        scratch_shapes=[block(count + 1), block(count + 1), block(count), block(count), block(chips)],
        compiler_params=pltpu.CompilerParams(vmem_limit_bytes=24 << 20),
        cost_estimate=pl.CostEstimate(flops=count * count * rows * width * 4, bytes_accessed=0, transcendentals=0),
    )(place, *in_vmem(inter, *pieces))


def gather_kernel(place_ref, first_ref, *refs):
    chip = place_ref[0]
    out_ref = refs[-1]
    out_ref[chip] = first_ref[0]
    for j, ref in enumerate(refs[:-1]):
        out_ref[chip ^ (j + 1)] = ref[...]


def gathered(place, own, pieces):
    chips, rows, half = own.shape
    out = pl.pallas_call(
        gather_kernel,
        out_shape=pltpu.VMEM((chips, rows, half), jnp.bfloat16),
        in_specs=[SCALAR] + [WHOLE] * chips,
        out_specs=WHOLE,
    )(place, *in_vmem(own, *pieces))
    return out.reshape(chips * rows, half)


def moved(link, state):
    left = jnp.dot(link, state, preferred_element_type=jnp.float32).astype(jnp.bfloat16)
    return lax.dot_general(left, link, (((1,), (1,)), ((), ())), preferred_element_type=jnp.float32)


def sandwich(green, state_re, state_im):
    half = green.shape[-1] // 2
    green_re, green_im = green[:, :half], green[:, half:]

    def dot(a, b):
        return jnp.dot(a, b, preferred_element_type=jnp.float32)

    def dot_t(a, b):
        return lax.dot_general(a, b, (((1,), (1,)), ((), ())), preferred_element_type=jnp.float32)

    left_re = (dot(green_re, state_re) - dot(green_im, state_im)).astype(jnp.bfloat16)
    left_im = (dot(green_re, state_im) + dot(green_im, state_re)).astype(jnp.bfloat16)
    out_re = dot_t(left_re, green_re) + dot_t(left_im, green_im)
    out_im = dot_t(left_im, green_re) - dot_t(left_re, green_im)
    return jnp.concatenate([out_re, out_im], axis=-1).astype(jnp.bfloat16)


def local(g_lesser, g_retarded, screened, coupling):
    devices = lax.axis_size(ENERGY)
    slabs = lax.axis_size(SLAB)
    chips = devices // 2
    me = lax.axis_index(ENERGY)
    slab = lax.axis_index(SLAB)
    chip, side = me // 2, me % 2
    place = jnp.stack([chip, side]).astype(jnp.int32)

    lesser = g_lesser[0, 0]
    size, width = lesser.shape
    rows = size // chips
    inter = screened[:, 0]
    inter_other = swap_with(inter, 1)
    first = jnp.where(side == 0, inter, inter_other)
    second = jnp.where(side == 0, inter_other, inter)
    inter_rows = jnp.concatenate([first, second], axis=1)

    mine = [lax.dynamic_slice(lesser, (rows * (chip ^ j), 0), (rows, width)) for j in range(chips)]
    pieces = [mine[0]] + [swap_with(mine[j], 2 * j) for j in range(1, chips)]
    pieces = pieces + [swap_with(x, 1) for x in pieces]
    re_rows, im_rows = convolve(chips, place, inter_rows, pieces)

    re_parts = [swap_with(re_rows[j], 2 * j) for j in range(1, chips)]
    im_parts = [swap_with(im_rows[j], 2 * j) for j in range(1, chips)]
    sigma_re = gathered(place, re_rows, re_parts)
    sigma_im = gathered(place, im_rows, im_parts)

    link = coupling[0]
    payload = sigma_re
    state_re = sigma_re
    for p in range(1, slabs + 1):
        pairs = [(s, s + 1) for s in (p - 1, p - 2) if 0 <= s and s + 1 < slabs]
        came = lax.ppermute(payload, SLAB, pairs)
        base = jnp.where(slab >= p, sigma_re, sigma_im)
        payload = (base.astype(jnp.float32) + moved(link, came)).astype(jnp.bfloat16)
        state_re = jnp.where(slab == p, payload, state_re)
        state_im = payload if p == 1 else jnp.where(slab + 1 == p, payload, state_im)
    return sandwich(g_retarded[0, 0], state_re, state_im)[None, None]


def solution(mesh):
    placed = (
        P(ENERGY, SLAB, None, None),
        P(ENERGY, SLAB, None, None),
        P(None, SLAB, ENERGY, None),
        P(SLAB, None, None),
    )
    return jax.shard_map(
        local,
        mesh=mesh,
        in_specs=placed,
        out_specs=P(ENERGY, SLAB, None, None),
        check_vma=False,
    )
```

time: 86.4 us -> 58.9 us (0.68)
  the two profiles are of different devices: /device:TPU:26 before, /device:TPU:16 now
where the time goes in v1:
time: 58.9 us; the launch traced here: 57.7 us
  waiting for transfers between devices  28.6 us (49%)
  starting transfers between devices  16.5 us (28%)
  matrix products  6.12 us (10%)
  Pallas kernels  3.44 us (6%)
  local copies, waits for them, and re-layouts  1.43 us (2%)
  other arithmetic  1.27 us (2%)
    ppermute x4, waiting for transfers between devices, local(): came = lax.ppermute(payload, SLAB, pairs)  20.1 us
    ppermute x14, starting transfers between devices, swap_with(): return lax.ppermute(array, ENERGY, [(i, i ^ mask) for i in range(devices)])  10.7 us
    ppermute x14, waiting for transfers between devices, swap_with(): return lax.ppermute(array, ENERGY, [(i, i ^ mask) for i in range(devices)])  8.54 us
    ppermute x4, starting transfers between devices, local(): came = lax.ppermute(payload, SLAB, pairs)  5.82 us
    dot_general x4, matrix products, moved(): lax.dot_general(left, link, (((1,), (1,)), ((), ())), preferred_element_t...  2.84 us
    pallas_call x1, Pallas kernels, convolve(): pl.pallas_call(functools.partial(conv_kernel, chips), out_shape=[part, pa...  2.06 us
    dot_general x4, matrix products, dot(): return jnp.dot(a, b, preferred_element_type=jnp.float32)  1.64 us
    dot_general x4, matrix products, dot_t(): lax.dot_general(a, b, (((1,), (1,)), ((), ())), preferred_element_type=jn...  1.64 us
  transfers between devices with their start and end apart: 18, of which 12 were waited for; matrix products, arithmetic and copies ran while one was open for 3% of the time, Pallas kernels for 2%

profile of v1, /device:TPU:16, one launch (start us, length us, event | category | flops | bytes accessed | tf_op | source)
XLA Modules:
  0.0 57.7 jit_solution(10552026960265845628)
XLA Ops:
  0.1 1.2 %dynamic-slice_bitcast_fusion = (bf16[80,640]{1,0:T(8,128)(2,1)S(1)}, bf16[80,640]{1,0:T(8,128)(2,1)S(1)}, bf16[80,640]{1,0:T(8,128)(2,1)S(1)}, bf16[80,640]{1,0:T(8,128)(2,1)S(1)}) fusion(bf16[1,1,320,640]{3,2,1,0:T(8,128)(2,1)} %param.4, s32[]{:T(128)S(6)} %select_n.113, s32[]{:T(128)S(6)} %select_n.111, s32[]{:T(128)S(6)} %select_n.110, s32[]{:T(128)S(6)} %select_n.112), kind=kLoop, calls=%fused_computation.48 | loop fusion | bytes 819216 | tf_op jit(solution)/shard_map/dynamic_slice | solution.py:151
  1.2 1.6 %collective-permute-start.1 = (bf16[80,640]{1,0:T(8,128)(2,1)S(1)}, bf16[80,640]{1,0:T(8,128)(2,1)S(1)}, u32[]{:S(2)}, u32[]{:S(2)}) collective-permute-start(bf16[80,640]{1,0:T(8,128)(2,1)S(1)} %get-tuple-element.18), channel_id=1, source_target_pairs={{0,8},{4,12},{8,0},{12,4},{16,24},{20,28},{24,16},{28,20},{1,9},{5... | collective-permute-start | bytes 307208 | tf_op jit(solution)/shard_map/ppermute | solution.py:22
  2.8 1.5 %collective-permute-start.2 = (bf16[80,640]{1,0:T(8,128)(2,1)S(1)}, bf16[80,640]{1,0:T(8,128)(2,1)S(1)}, u32[]{:S(2)}, u32[]{:S(2)}) collective-permute-start(bf16[80,640]{1,0:T(8,128)(2,1)S(1)} %get-tuple-element.20), channel_id=1, source_target_pairs={{0,16},{4,20},{8,24},{12,28},{16,0},{20,4},{24,8},{28,12},{1,17},{... | collective-permute-start | bytes 307208 | tf_op jit(solution)/shard_map/ppermute | solution.py:22
  4.9 1.6 %collective-permute-done.1.refs_1_ = bf16[80,640]{1,0:T(8,128)(2,1)S(1)} collective-permute-done((bf16[80,640]{1,0:T(8,128)(2,1)S(1)}, bf16[80,640]{1,0:T(8,128)(2,1)S(1)}, u32[]{:S(2)}, u32[]{:S(2)}) %collective-permute-start.1) | collective-permute-done | bytes 102432 | tf_op jit(solution)/shard_map/ppermute | solution.py:22
  6.5 2.4 %collective-permute-done.2.refs_2_ = bf16[80,640]{1,0:T(8,128)(2,1)S(1)} collective-permute-done((bf16[80,640]{1,0:T(8,128)(2,1)S(1)}, bf16[80,640]{1,0:T(8,128)(2,1)S(1)}, u32[]{:S(2)}, u32[]{:S(2)}) %collective-permute-start.2) | collective-permute-done | bytes 102432 | tf_op jit(solution)/shard_map/ppermute | solution.py:22
  8.9 1.0 %collective-permute-done.3.refs_3_ = bf16[80,640]{1,0:T(8,128)(2,1)S(1)} collective-permute-done((bf16[80,640]{1,0:T(8,128)(2,1)S(1)}, bf16[80,640]{1,0:T(8,128)(2,1)S(1)}, u32[]{:S(2)}, u32[]{:S(2)}) %collective-permute-start.3) | collective-permute-done | bytes 102432 | tf_op jit(solution)/shard_map/ppermute | solution.py:22
  10.2 1.0 %collective-permute-done.7.refs_7_ = bf16[80,640]{1,0:T(8,128)(2,1)S(1)} collective-permute-done((bf16[80,640]{1,0:T(8,128)(2,1)S(1)}, bf16[80,640]{1,0:T(8,128)(2,1)S(1)}, u32[]{:S(2)}, u32[]{:S(2)}) %collective-permute-start.7) | collective-permute-done | bytes 102432 | tf_op jit(solution)/shard_map/ppermute | solution.py:22
  11.2 2.1 %shard_map.46 = (bf16[4,80,320]{2,1,0:T(8,128)(2,1)S(1)}, bf16[4,80,320]{2,1,0:T(8,128)(2,1)S(1)}) custom-call(s32[2]{0:T(128)S(1)} %pad_add_fusion.place_ref, bf16[8,80,640]{2,1,0:T(8,128)(2,1)S(1)} %pad_maximum_fusion.inter_ref, bf16[80,640]{1,0:T(8,128)(2,1)S(1)} %get-tuple-element.19.refs_0_, bf16[80,640]{1,0:T(8,128)(2,1)S(1)} %collective-permute-done.1.refs_1_, ...), custom_call_target="tpu_custom_call" | custom-call | flops 13107200 | tf_op jit(solution)/shard_map/pallas_call | solution.py:81
  13.3 1.7 %collective-permute-start.10 = (bf16[80,320]{1,0:T(8,128)(2,1)S(1)}, bf16[80,320]{1,0:T(8,128)(2,1)S(1)}, u32[]{:S(2)}, u32[]{:S(2)}) collective-permute-start(bf16[80,320]{1,0:T(8,128)(2,1)S(1)} %get-tuple-element.21), channel_id=1, source_target_pairs={{0,24},{4,28},{8,16},{12,20},{16,8},{20,12},{24,0},{28,4},{1,25},{... | collective-permute-start | bytes 153608 | tf_op jit(solution)/shard_map/ppermute | solution.py:22
  15.0 1.5 %collective-permute-start.8 = (bf16[80,320]{1,0:T(8,128)(2,1)S(1)}, bf16[80,320]{1,0:T(8,128)(2,1)S(1)}, u32[]{:S(2)}, u32[]{:S(2)}) collective-permute-start(bf16[80,320]{1,0:T(8,128)(2,1)S(1)} %get-tuple-element.23), channel_id=1, source_target_pairs={{0,8},{4,12},{8,0},{12,4},{16,24},{20,28},{24,16},{28,20},{1,9},{5... | collective-permute-start | bytes 153608 | tf_op jit(solution)/shard_map/ppermute | solution.py:22
  16.9 1.3 %collective-permute-start.11 = (bf16[80,320]{1,0:T(8,128)(2,1)S(1)}, bf16[80,320]{1,0:T(8,128)(2,1)S(1)}, u32[]{:S(2)}, u32[]{:S(2)}) collective-permute-start(bf16[80,320]{1,0:T(8,128)(2,1)S(1)} %get-tuple-element.26), channel_id=1, source_target_pairs={{0,8},{4,12},{8,0},{12,4},{16,24},{20,28},{24,16},{28,20},{1,9},{5... | collective-permute-start | bytes 153608 | tf_op jit(solution)/shard_map/ppermute | solution.py:22
  18.1 1.0 %collective-permute-start.12 = (bf16[80,320]{1,0:T(8,128)(2,1)S(1)}, bf16[80,320]{1,0:T(8,128)(2,1)S(1)}, u32[]{:S(2)}, u32[]{:S(2)}) collective-permute-start(bf16[80,320]{1,0:T(8,128)(2,1)S(1)} %get-tuple-element.25), channel_id=1, source_target_pairs={{0,16},{4,20},{8,24},{12,28},{16,0},{20,4},{24,8},{28,12},{1,17},{... | collective-permute-start | bytes 153608 | tf_op jit(solution)/shard_map/ppermute | solution.py:22
  19.1 1.3 %collective-permute-start.13 = (bf16[80,320]{1,0:T(8,128)(2,1)S(1)}, bf16[80,320]{1,0:T(8,128)(2,1)S(1)}, u32[]{:S(2)}, u32[]{:S(2)}) collective-permute-start(bf16[80,320]{1,0:T(8,128)(2,1)S(1)} %get-tuple-element.24), channel_id=1, source_target_pairs={{0,24},{4,28},{8,16},{12,20},{16,8},{20,12},{24,0},{28,4},{1,25},{... | collective-permute-start | bytes 153608 | tf_op jit(solution)/shard_map/ppermute | solution.py:22
  21.1 0.7 %shard_map.47 = bf16[4,80,320]{2,1,0:T(8,128)(2,1)S(1)} custom-call(s32[2]{0:T(128)} %copy-done.1, bf16[4,80,320]{2,1,0:T(8,128)(2,1)S(1)} %get-tuple-element.7.first_ref, bf16[80,320]{1,0:T(8,128)(2,1)S(1)} %collective-permute-done.8.refs_0_, bf16[80,320]{1,0:T(8,128)(2,1)S(1)} %collective-permute-done.9.refs_1_, ...), custom_call_target="tpu_custom_call" | custom-call | tf_op jit(solution)/shard_map/pallas_call | solution.py:102
  22.9 1.3 %collective-permute-done.13.refs_2_ = bf16[80,320]{1,0:T(8,128)(2,1)S(1)} collective-permute-done((bf16[80,320]{1,0:T(8,128)(2,1)S(1)}, bf16[80,320]{1,0:T(8,128)(2,1)S(1)}, u32[]{:S(2)}, u32[]{:S(2)}) %collective-permute-start.13) | collective-permute-done | bytes 51232 | tf_op jit(solution)/shard_map/ppermute | solution.py:22
  24.2 0.7 %shard_map.48 = bf16[4,80,320]{2,1,0:T(8,128)(2,1)S(1)} custom-call(s32[2]{0:T(128)} %copy-done.1, bf16[4,80,320]{2,1,0:T(8,128)(2,1)S(1)} %get-tuple-element.8.first_ref, bf16[80,320]{1,0:T(8,128)(2,1)S(1)} %collective-permute-done.11.refs_0_, bf16[80,320]{1,0:T(8,128)(2,1)S(1)} %collective-permute-done.12.refs_1_, ...), custom_call_target="tpu_custom_call" | custom-call | tf_op jit(solution)/shard_map/pallas_call | solution.py:102
  25.8 1.3 %collective-permute-start.15 = (bf16[320,320]{1,0:T(8,128)(2,1)S(1)}, bf16[320,320]{1,0:T(8,128)(2,1)S(1)}, u32[]{:S(2)}, u32[]{:S(2)}) collective-permute-start(bf16[320,320]{1,0:T(8,128)(2,1)S(1)} %add_convert_fusion.3), channel_id=1, source_target_pairs={{1,2},{0,1},{5,6},{4,5},{9,10},{8,9},{13,14},{12,13},{17,18},{16,1... | collective-permute-start | bytes 614408 | tf_op jit(solution)/shard_map/ppermute | solution.py:166
  27.1 10.3 %collective-permute-done.15 = bf16[320,320]{1,0:T(8,128)(2,1)S(1)} collective-permute-done((bf16[320,320]{1,0:T(8,128)(2,1)S(1)}, bf16[320,320]{1,0:T(8,128)(2,1)S(1)}, u32[]{:S(2)}, u32[]{:S(2)}) %collective-permute-start.15) | collective-permute-done | bytes 204832 | tf_op jit(solution)/shard_map/ppermute | solution.py:166
  38.1 1.9 %collective-permute-start.16 = (bf16[320,320]{1,0:T(8,128)(2,1)S(1)}, bf16[320,320]{1,0:T(8,128)(2,1)S(1)}, u32[]{:S(2)}, u32[]{:S(2)}) collective-permute-start(bf16[320,320]{1,0:T(8,128)(2,1)S(1)} %add_convert_fusion.2), channel_id=1, source_target_pairs={{2,3},{1,2},{6,7},{5,6},{10,11},{9,10},{14,15},{13,14},{18,19},{17... | collective-permute-start | bytes 614408 | tf_op jit(solution)/shard_map/ppermute | solution.py:166
  40.0 6.2 %collective-permute-done.16 = bf16[320,320]{1,0:T(8,128)(2,1)S(1)} collective-permute-done((bf16[320,320]{1,0:T(8,128)(2,1)S(1)}, bf16[320,320]{1,0:T(8,128)(2,1)S(1)}, u32[]{:S(2)}, u32[]{:S(2)}) %collective-permute-start.16) | collective-permute-done | bytes 204832 | tf_op jit(solution)/shard_map/ppermute | solution.py:166
  46.9 1.9 %collective-permute-start.17 = (bf16[320,320]{1,0:T(8,128)(2,1)S(1)}, bf16[320,320]{1,0:T(8,128)(2,1)S(1)}, u32[]{:S(2)}, u32[]{:S(2)}) collective-permute-start(bf16[320,320]{1,0:T(8,128)(2,1)S(1)} %add_convert_fusion.1), channel_id=1, source_target_pairs={{2,3},{6,7},{10,11},{14,15},{18,19},{22,23},{26,27},{30,31}} | collective-permute-start | bytes 614408 | tf_op jit(solution)/shard_map/ppermute | solution.py:166
  48.8 3.7 %collective-permute-done.17 = bf16[320,320]{1,0:T(8,128)(2,1)S(1)} collective-permute-done((bf16[320,320]{1,0:T(8,128)(2,1)S(1)}, bf16[320,320]{1,0:T(8,128)(2,1)S(1)}, u32[]{:S(2)}, u32[]{:S(2)}) %collective-permute-start.17) | collective-permute-done | bytes 204832 | tf_op jit(solution)/shard_map/ppermute | solution.py:166
  52.5 0.8 %select_select_fusion.1 = (bf16[320,320]{1,0:T(8,128)(2,1)S(1)}, bf16[320,320]{1,0:T(8,128)(2,1)S(1)}) fusion(bf16[320,320]{1,0:T(8,128)(2,1)S(1)} %add_convert_fusion.1, bf16[320,320]{1,0:T(8,128)(2,1)S(1)} %add_convert_fusion.2, bf16[320,320]{1,0:T(8,128)(2,1)S(1)} %add_convert_fusion.3, pred[]{:T(512)S(6)} %eq.31, pred[]{:T(512)S(6)} %eq.30, ...), kind=kOutput, calls=%fused_computation.35 | convolution fusion | flops 132198400 | bytes 1843207 | tf_op jit(solution)/shard_map/dot_general | solution.py:113
  56.8 0.9 %pad_maximum_fusion.1 = bf16[1,1,320,640]{3,2,1,0:T(8,128)(2,1)} fusion(bf16[1,1,320,320]{3,2,1,0:T(8,128)(2,1)S(1)} %fusion.4, bf16[1,1,320,320]{3,2,1,0:T(8,128)(2,1)S(1)} %fusion.5), kind=kLoop, calls=%fused_computation.23 | loop fusion | flops 819200 | bytes 819200 | tf_op jit(solution)/shard_map/concatenate | solution.py:130
  (43 shorter events, 8.8 us)
Async XLA Ops:
  0.0 25.1 %copy-start = (bf16[1,320,320]{2,1,0:T(8,128)(2,1)S(1)}, bf16[1,320,320]{2,1,0:T(8,128)(2,1)}, u32[]{:S(2)}) copy-start(bf16[1,320,320]{2,1,0:T(8,128)(2,1)} %param.7) | copy-start | bytes 614404
  0.0 9.9 %copy-start.3 = (bf16[8,1,40,640]{3,2,1,0:T(8,128)(2,1)S(1)}, bf16[8,1,40,640]{3,2,1,0:T(8,128)(2,1)}, u32[]{:S(2)}) copy-start(bf16[8,1,40,640]{3,2,1,0:T(8,128)(2,1)} %param.6) | copy-start | bytes 1228804
  0.0 9.9 %collective-permute-start = (bf16[8,40,640]{2,1,0:T(8,128)(2,1)}, bf16[8,40,640]{2,1,0:T(8,128)(2,1)S(1)}, u32[]{:S(2)}, u32[]{:S(2)}) collective-permute-start(bf16[8,40,640]{2,1,0:T(8,128)(2,1)} %bitcast.95), channel_id=1, source_target_pairs={{0,4},{4,0},{8,12},{12,8},{16,20},{20,16},{24,28},{28,24},{1,5},{5... | collective-permute-start | bytes 1228808 | tf_op jit(solution)/shard_map/ppermute | solution.py:22
  1.2 5.2 %collective-permute-start.1 = (bf16[80,640]{1,0:T(8,128)(2,1)S(1)}, bf16[80,640]{1,0:T(8,128)(2,1)S(1)}, u32[]{:S(2)}, u32[]{:S(2)}) collective-permute-start(bf16[80,640]{1,0:T(8,128)(2,1)S(1)} %get-tuple-element.18), channel_id=1, source_target_pairs={{0,8},{4,12},{8,0},{12,4},{16,24},{20,28},{24,16},{28,20},{1,9},{5... | collective-permute-start | bytes 307208 | tf_op jit(solution)/shard_map/ppermute | solution.py:22
  2.8 6.1 %collective-permute-start.2 = (bf16[80,640]{1,0:T(8,128)(2,1)S(1)}, bf16[80,640]{1,0:T(8,128)(2,1)S(1)}, u32[]{:S(2)}, u32[]{:S(2)}) collective-permute-start(bf16[80,640]{1,0:T(8,128)(2,1)S(1)} %get-tuple-element.20), channel_id=1, source_target_pairs={{0,16},{4,20},{8,24},{12,28},{16,0},{20,4},{24,8},{28,12},{1,17},{... | collective-permute-start | bytes 307208 | tf_op jit(solution)/shard_map/ppermute | solution.py:22
  4.3 5.6 %collective-permute-start.3 = (bf16[80,640]{1,0:T(8,128)(2,1)S(1)}, bf16[80,640]{1,0:T(8,128)(2,1)S(1)}, u32[]{:S(2)}, u32[]{:S(2)}) collective-permute-start(bf16[80,640]{1,0:T(8,128)(2,1)S(1)} %get-tuple-element.17), channel_id=1, source_target_pairs={{0,24},{4,28},{8,16},{12,20},{16,8},{20,12},{24,0},{28,4},{1,25},{... | collective-permute-start | bytes 307208 | tf_op jit(solution)/shard_map/ppermute | solution.py:22
  4.8 5.3 %collective-permute-start.4 = (bf16[80,640]{1,0:T(8,128)(2,1)S(1)}, bf16[80,640]{1,0:T(8,128)(2,1)S(1)}, u32[]{:S(2)}, u32[]{:S(2)}) collective-permute-start(bf16[80,640]{1,0:T(8,128)(2,1)S(1)} %get-tuple-element.19.refs_0_), channel_id=1, source_target_pairs={{0,4},{4,0},{8,12},{12,8},{16,20},{20,16},{24,28},{28,24},{1,5},{5... | collective-permute-start | bytes 307208 | tf_op jit(solution)/shard_map/ppermute | solution.py:22
  4.9 6.3 %copy-start.1 = (s32[2]{0:T(128)}, s32[2]{0:T(128)S(1)}, u32[]{:S(2)}) copy-start(s32[2]{0:T(128)S(1)} %pad_add_fusion.place_ref) | copy-start | bytes 28
  6.5 3.6 %collective-permute-start.5 = (bf16[80,640]{1,0:T(8,128)(2,1)S(1)}, bf16[80,640]{1,0:T(8,128)(2,1)S(1)}, u32[]{:S(2)}, u32[]{:S(2)}) collective-permute-start(bf16[80,640]{1,0:T(8,128)(2,1)S(1)} %collective-permute-done.1.refs_1_), channel_id=1, source_target_pairs={{0,4},{4,0},{8,12},{12,8},{16,20},{20,16},{24,28},{28,24},{1,5},{5... | collective-permute-start | bytes 307208 | tf_op jit(solution)/shard_map/ppermute | solution.py:22
  8.9 1.3 %collective-permute-start.6 = (bf16[80,640]{1,0:T(8,128)(2,1)S(1)}, bf16[80,640]{1,0:T(8,128)(2,1)S(1)}, u32[]{:S(2)}, u32[]{:S(2)}) collective-permute-start(bf16[80,640]{1,0:T(8,128)(2,1)S(1)} %collective-permute-done.2.refs_2_), channel_id=1, source_target_pairs={{0,4},{4,0},{8,12},{12,8},{16,20},{20,16},{24,28},{28,24},{1,5},{5... | collective-permute-start | bytes 307208 | tf_op jit(solution)/shard_map/ppermute | solution.py:22
  9.9 1.3 %collective-permute-start.7 = (bf16[80,640]{1,0:T(8,128)(2,1)S(1)}, bf16[80,640]{1,0:T(8,128)(2,1)S(1)}, u32[]{:S(2)}, u32[]{:S(2)}) collective-permute-start(bf16[80,640]{1,0:T(8,128)(2,1)S(1)} %collective-permute-done.3.refs_3_), channel_id=1, source_target_pairs={{0,4},{4,0},{8,12},{12,8},{16,20},{20,16},{24,28},{28,24},{1,5},{5... | collective-permute-start | bytes 307208 | tf_op jit(solution)/shard_map/ppermute | solution.py:22
  13.3 5.8 %collective-permute-start.10 = (bf16[80,320]{1,0:T(8,128)(2,1)S(1)}, bf16[80,320]{1,0:T(8,128)(2,1)S(1)}, u32[]{:S(2)}, u32[]{:S(2)}) collective-permute-start(bf16[80,320]{1,0:T(8,128)(2,1)S(1)} %get-tuple-element.21), channel_id=1, source_target_pairs={{0,24},{4,28},{8,16},{12,20},{16,8},{20,12},{24,0},{28,4},{1,25},{... | collective-permute-start | bytes 153608 | tf_op jit(solution)/shard_map/ppermute | solution.py:22
  15.0 5.6 %collective-permute-start.8 = (bf16[80,320]{1,0:T(8,128)(2,1)S(1)}, bf16[80,320]{1,0:T(8,128)(2,1)S(1)}, u32[]{:S(2)}, u32[]{:S(2)}) collective-permute-start(bf16[80,320]{1,0:T(8,128)(2,1)S(1)} %get-tuple-element.23), channel_id=1, source_target_pairs={{0,8},{4,12},{8,0},{12,4},{16,24},{20,28},{24,16},{28,20},{1,9},{5... | collective-permute-start | bytes 153608 | tf_op jit(solution)/shard_map/ppermute | solution.py:22
  16.5 4.6 %collective-permute-start.9 = (bf16[80,320]{1,0:T(8,128)(2,1)S(1)}, bf16[80,320]{1,0:T(8,128)(2,1)S(1)}, u32[]{:S(2)}, u32[]{:S(2)}) collective-permute-start(bf16[80,320]{1,0:T(8,128)(2,1)S(1)} %get-tuple-element.22), channel_id=1, source_target_pairs={{0,16},{4,20},{8,24},{12,28},{16,0},{20,4},{24,8},{28,12},{1,17},{... | collective-permute-start | bytes 153608 | tf_op jit(solution)/shard_map/ppermute | solution.py:22
  16.9 5.6 %collective-permute-start.11 = (bf16[80,320]{1,0:T(8,128)(2,1)S(1)}, bf16[80,320]{1,0:T(8,128)(2,1)S(1)}, u32[]{:S(2)}, u32[]{:S(2)}) collective-permute-start(bf16[80,320]{1,0:T(8,128)(2,1)S(1)} %get-tuple-element.26), channel_id=1, source_target_pairs={{0,8},{4,12},{8,0},{12,4},{16,24},{20,28},{24,16},{28,20},{1,9},{5... | collective-permute-start | bytes 153608 | tf_op jit(solution)/shard_map/ppermute | solution.py:22
  18.1 4.8 %collective-permute-start.12 = (bf16[80,320]{1,0:T(8,128)(2,1)S(1)}, bf16[80,320]{1,0:T(8,128)(2,1)S(1)}, u32[]{:S(2)}, u32[]{:S(2)}) collective-permute-start(bf16[80,320]{1,0:T(8,128)(2,1)S(1)} %get-tuple-element.25), channel_id=1, source_target_pairs={{0,16},{4,20},{8,24},{12,28},{16,0},{20,4},{24,8},{28,12},{1,17},{... | collective-permute-start | bytes 153608 | tf_op jit(solution)/shard_map/ppermute | solution.py:22
  19.1 5.1 %collective-permute-start.13 = (bf16[80,320]{1,0:T(8,128)(2,1)S(1)}, bf16[80,320]{1,0:T(8,128)(2,1)S(1)}, u32[]{:S(2)}, u32[]{:S(2)}) collective-permute-start(bf16[80,320]{1,0:T(8,128)(2,1)S(1)} %get-tuple-element.24), channel_id=1, source_target_pairs={{0,24},{4,28},{8,16},{12,20},{16,8},{20,12},{24,0},{28,4},{1,25},{... | collective-permute-start | bytes 153608 | tf_op jit(solution)/shard_map/ppermute | solution.py:22
  21.8 3.3 %collective-permute-start.14 = (bf16[320,320]{1,0:T(8,128)(2,1)S(1)}, bf16[320,320]{1,0:T(8,128)(2,1)S(1)}, u32[]{:S(2)}, u32[]{:S(2)}) collective-permute-start(bf16[320,320]{1,0:T(8,128)(2,1)S(1)} %bitcast.86), channel_id=1, source_target_pairs={{0,1},{4,5},{8,9},{12,13},{16,17},{20,21},{24,25},{28,29}} | collective-permute-start | bytes 614408 | tf_op jit(solution)/shard_map/ppermute | solution.py:166
  25.8 11.6 %collective-permute-start.15 = (bf16[320,320]{1,0:T(8,128)(2,1)S(1)}, bf16[320,320]{1,0:T(8,128)(2,1)S(1)}, u32[]{:S(2)}, u32[]{:S(2)}) collective-permute-start(bf16[320,320]{1,0:T(8,128)(2,1)S(1)} %add_convert_fusion.3), channel_id=1, source_target_pairs={{1,2},{0,1},{5,6},{4,5},{9,10},{8,9},{13,14},{12,13},{17,18},{16,1... | collective-permute-start | bytes 614408 | tf_op jit(solution)/shard_map/ppermute | solution.py:166
  38.1 8.1 %collective-permute-start.16 = (bf16[320,320]{1,0:T(8,128)(2,1)S(1)}, bf16[320,320]{1,0:T(8,128)(2,1)S(1)}, u32[]{:S(2)}, u32[]{:S(2)}) collective-permute-start(bf16[320,320]{1,0:T(8,128)(2,1)S(1)} %add_convert_fusion.2), channel_id=1, source_target_pairs={{2,3},{1,2},{6,7},{5,6},{10,11},{9,10},{14,15},{13,14},{18,19},{17... | collective-permute-start | bytes 614408 | tf_op jit(solution)/shard_map/ppermute | solution.py:166
  46.9 5.6 %collective-permute-start.17 = (bf16[320,320]{1,0:T(8,128)(2,1)S(1)}, bf16[320,320]{1,0:T(8,128)(2,1)S(1)}, u32[]{:S(2)}, u32[]{:S(2)}) collective-permute-start(bf16[320,320]{1,0:T(8,128)(2,1)S(1)} %add_convert_fusion.1), channel_id=1, source_target_pairs={{2,3},{6,7},{10,11},{14,15},{18,19},{22,23},{26,27},{30,31}} | collective-permute-start | bytes 614408 | tf_op jit(solution)/shard_map/ppermute | solution.py:166
  52.5 1.0 %copy-start.2 = (bf16[1,1,320,640]{3,2,1,0:T(8,128)(2,1)S(1)}, bf16[1,1,320,640]{3,2,1,0:T(8,128)(2,1)}, u32[]{:S(2)}) copy-start(bf16[1,1,320,640]{3,2,1,0:T(8,128)(2,1)} %param.5) | copy-start | bytes 1228804

commit v2 on v1

v2 whole, which is shorter than its diff:
```python
import functools

import jax
import jax.numpy as jnp
from jax import lax
from jax.experimental import pallas as pl
from jax.experimental.pallas import tpu as pltpu
from jax.sharding import PartitionSpec as P

ENERGY = "energy"
SLAB = "slab"
WHOLE = pl.BlockSpec(memory_space=pltpu.VMEM)
SCALAR = pl.BlockSpec(memory_space=pltpu.SMEM)


def in_vmem(*arrays):
    return [pltpu.with_memory_space_constraint(x, pltpu.VMEM) for x in arrays]


def swap_with(array, mask):
    devices = lax.axis_size(ENERGY)
    return lax.ppermute(array, ENERGY, [(i, i ^ mask) for i in range(devices)])


def swap_across(array, mask):
    devices, slabs = lax.axis_size(ENERGY), lax.axis_size(SLAB)
    pairs = [(e * slabs + s, (e ^ mask) * slabs + (s ^ 1)) for e in range(devices) for s in range(slabs)]
    return lax.ppermute(array, (ENERGY, SLAB), pairs)


def conv_kernel(chips, place_ref, inter_ref, *refs):
    pieces = refs[: 2 * chips]
    out_ref, a_ref, b_ref, w_ref, v_ref, sum_ref = refs[2 * chips :]
    chip, side = place_ref[0], place_ref[1]
    rows, width = inter_ref.shape[1:]
    half = width // 2
    left = lax.broadcasted_iota(jnp.int32, (rows, width), 1) < half

    def swapped(x):
        return jnp.concatenate([x[:, half:], x[:, :half]], axis=1)

    @pl.when(side == 0)
    def _():
        a_ref[0] = jnp.zeros((rows, width), jnp.float32)
        b_ref[0] = jnp.zeros((rows, width), jnp.float32)

    for other in range(2):
        for j in range(chips):
            x = pieces[other * chips + j][...].astype(jnp.float32)
            y = swapped(x)
            slot = 2 * (chip ^ j) + (side ^ other) + 1 - side
            a_ref[slot] = jnp.where(left, x, y)
            b_ref[slot] = jnp.where(left, y, x)
    for m in range(2 * chips):
        x = inter_ref[m].astype(jnp.float32)
        y = swapped(x)
        w_ref[m] = x
        v_ref[m] = jnp.where(left, -y, y)

    step = 8 if rows % 8 == 0 else rows
    lanes = 128 if width % 128 == 0 else width

    def tile(t, carry):
        here = pl.ds(pl.multiple_of(t * step, step), step)
        for c in range(0, width, lanes):
            at = pl.ds(c, lanes)
            for j in range(chips):
                total = None
                for m in range(2 * j + 2):
                    s = 2 * j + 1 - m
                    term = a_ref[s, here, at] * v_ref[m, here, at] - b_ref[s, here, at] * w_ref[m, here, at]
                    total = term if total is None else total + term
                sum_ref[chip ^ j, here, at] = total
        return carry

    lax.fori_loop(0, rows // step, tile, 0)
    out_ref[...] = sum_ref[...].astype(jnp.bfloat16)


def convolve(chips, place, inter, pieces):
    count, rows, width = inter.shape
    block = lambda n: pltpu.VMEM((n, rows, width), jnp.float32)
    return pl.pallas_call(
        functools.partial(conv_kernel, chips),
        out_shape=pltpu.VMEM((chips, rows, width), jnp.bfloat16),
        in_specs=[SCALAR] + [WHOLE] * (1 + 2 * chips),
        out_specs=WHOLE,
        scratch_shapes=[block(count + 1), block(count + 1), block(count), block(count), block(chips)],
        compiler_params=pltpu.CompilerParams(vmem_limit_bytes=24 << 20),
        cost_estimate=pl.CostEstimate(flops=count * count * rows * width * 4, bytes_accessed=0, transcendentals=0),
    )(place, *in_vmem(inter, *pieces))


def dot(a, b):
    return jnp.dot(a, b, preferred_element_type=jnp.float32)


def dot_t(a, b):
    return lax.dot_general(a, b, (((1,), (1,)), ((), ())), preferred_element_type=jnp.float32)


def moved(link, parts):
    size = link.shape[0]
    left = jnp.concatenate([dot(link, x).astype(jnp.bfloat16) for x in parts], axis=0)
    out = dot_t(left, link)
    return [out[i * size : (i + 1) * size] for i in range(len(parts))]


def first_kernel(chips, place_ref, link_ref, *refs):
    own, before = refs[:chips], refs[chips : 2 * chips]
    re_ref, im_ref, own_ref, before_ref = refs[2 * chips :]
    chip, odd = place_ref[0], place_ref[2]
    for j in range(chips):
        own_ref[chip ^ j] = own[j][...]
        before_ref[chip ^ j] = before[j][...]
    _, rows, width = own_ref.shape
    half = width // 2
    x = own_ref[...].reshape(chips * rows, width)

    @pl.when(odd == 0)
    def _():
        re_ref[...] = x[:, :half]
        im_ref[...] = x[:, half:]

    @pl.when(odd == 1)
    def _():
        y = before_ref[...].reshape(chips * rows, width)
        re, im = moved(link_ref[...], [y[:, :half], y[:, half:]])
        re_ref[...] = (x[:, :half].astype(jnp.float32) + re).astype(jnp.bfloat16)
        im_ref[...] = (x[:, half:].astype(jnp.float32) + im).astype(jnp.bfloat16)


def first_state(chips, place, link, own, before):
    rows, width = own[0].shape
    part = pltpu.VMEM((chips * rows, width // 2), jnp.bfloat16)
    block = pltpu.VMEM((chips, rows, width), jnp.bfloat16)
    return pl.pallas_call(
        functools.partial(first_kernel, chips),
        out_shape=[part, part],
        in_specs=[SCALAR] + [WHOLE] * (1 + 2 * chips),
        out_specs=[WHOLE, WHOLE],
        scratch_shapes=[block, block],
    )(place, *in_vmem(link, *own, *before))


def advance(place_ref, link_ref, link_before_ref, re_ref, im_ref, early_im_ref, early_re_ref, late_ref, x_ref):
    odd = place_ref[2]

    @pl.when(odd == 0)
    def _():
        x_ref[0] = late_ref[...]
        x_ref[1] = early_im_ref[...]

    @pl.when(odd == 1)
    def _():
        parts = moved(link_before_ref[...], [early_re_ref[...], late_ref[...]])
        x_ref[0] = parts[0].astype(jnp.bfloat16)
        x_ref[1] = parts[1].astype(jnp.bfloat16)

    re, im = moved(link_ref[...], [x_ref[0], x_ref[1]])
    return (
        (re_ref[...].astype(jnp.float32) + re).astype(jnp.bfloat16),
        (im_ref[...].astype(jnp.float32) + im).astype(jnp.bfloat16),
    )


def advance_kernel(*refs):
    *given, new_re_ref, new_im_ref, x_ref = refs
    new_re_ref[...], new_im_ref[...] = advance(*given, x_ref)


def last_kernel(*refs):
    *given, green_ref, out_ref, x_ref = refs
    re, im = advance(*given, x_ref)
    half = re.shape[1]
    green = green_ref[...]
    green_re, green_im = green[:, :half], green[:, half:]
    right = jnp.concatenate([jnp.concatenate([re, im], axis=1), jnp.concatenate([-im, re], axis=1)], axis=0)
    left = dot(green, right).astype(jnp.bfloat16)
    adjoint = jnp.concatenate([green, jnp.concatenate([-green_im, green_re], axis=1)], axis=0)
    out_ref[...] = dot_t(left, adjoint).astype(jnp.bfloat16)


def next_state(*given):
    part = pltpu.VMEM(given[3].shape, jnp.bfloat16)
    return pl.pallas_call(
        advance_kernel,
        out_shape=[part, part],
        in_specs=[SCALAR] + [WHOLE] * (len(given) - 1),
        out_specs=[WHOLE, WHOLE],
        scratch_shapes=[pltpu.VMEM((2,) + given[3].shape, jnp.bfloat16)],
    )(given[0], *in_vmem(*given[1:]))


def correction(*given):
    return pl.pallas_call(
        last_kernel,
        out_shape=jax.ShapeDtypeStruct(given[-1].shape, jnp.bfloat16),
        in_specs=[SCALAR] + [WHOLE] * (len(given) - 1),
        out_specs=WHOLE,
        scratch_shapes=[pltpu.VMEM((2,) + given[3].shape, jnp.bfloat16)],
    )(given[0], *in_vmem(*given[1:]))


def local(g_lesser, g_retarded, screened, coupling):
    devices = lax.axis_size(ENERGY)
    slabs = lax.axis_size(SLAB)
    chips = devices // 2
    me = lax.axis_index(ENERGY)
    slab = lax.axis_index(SLAB)
    chip, side, odd = me // 2, me % 2, slab % 2
    place = jnp.stack([chip, side, odd]).astype(jnp.int32)

    lesser = g_lesser[0, 0]
    size, width = lesser.shape
    rows = size // chips
    inter = screened[:, 0]
    inter_other = swap_with(inter, 1)
    first = jnp.where(side == 0, inter, inter_other)
    second = jnp.where(side == 0, inter_other, inter)
    inter_rows = jnp.concatenate([first, second], axis=1)

    mine = [lax.dynamic_slice(lesser, (rows * (chip ^ j), 0), (rows, width)) for j in range(chips)]
    pieces = [mine[0]] + [swap_with(mine[j], 2 * j) for j in range(1, chips)]
    pieces = pieces + [swap_with(x, 1) for x in pieces]
    sigma = convolve(chips, place, inter_rows, pieces)

    link = coupling[0]
    link_before = lax.ppermute(link, SLAB, [(s, s ^ 1) for s in range(slabs)])
    before = [swap_across(sigma[j], 2 * j) for j in range(chips)]
    own = [sigma[0]] + [swap_with(sigma[j], 2 * j) for j in range(1, chips)]
    re, im = first_state(chips, place, link, own, before)

    for s in range(1, slabs - 1, 2):
        early_im = lax.ppermute(im, SLAB, [(s, s + 1)])
        early_re = lax.ppermute(re, SLAB, [(s, s + 2)])
        late = lax.ppermute(jnp.where(odd == 1, re, early_im), SLAB, [(s, s + 1), (s + 1, s + 2)])
        given = (place, link, link_before, re, im, early_im, early_re, late)
        if s + 3 < slabs:
            re, im = next_state(*given)
    return correction(*given, g_retarded[0, 0])[None, None]


def solution(mesh):
    placed = (
        P(ENERGY, SLAB, None, None),
        P(ENERGY, SLAB, None, None),
        P(None, SLAB, ENERGY, None),
        P(SLAB, None, None),
    )
    return jax.shard_map(
        local,
        mesh=mesh,
        in_specs=placed,
        out_specs=P(ENERGY, SLAB, None, None),
        check_vma=False,
    )
```

time: 58.9 us -> 56.3 us (0.956)
  matrix products: 6.12 us -> 0 us
  starting transfers between devices: 16.5 us -> 21.4 us
  Pallas kernels: 3.44 us -> 6.16 us
  waiting for transfers between devices: 28.6 us -> 26.3 us
  other arithmetic: 1.27 us -> 0.26 us
    ppermute x4 -> x8, starting transfers between devices: 5.82 us -> 13.4 us  [the longest x4 8.26 us: swap_across(): return lax.ppermute(array, (ENERGY, SLAB), pairs)]
    dot_general x12 -> x0, matrix products: 6.12 us -> none  [the longest x4 2.84 us: moved(): lax.dot_general(left, link, (((1,), (1,)), ((), ())), preferred_element_t...]
    ppermute x4 -> x8, waiting for transfers between devices: 20.1 us -> 16.3 us  [the longest x1 7.47 us: local(): early_im = lax.ppermute(im, SLAB, [(s, s + 1)])]
    pallas_call x3, Pallas kernels: 3.44 us -> 6.16 us  [the longest x1 3.15 us: correction(): pl.pallas_call(last_kernel, out_shape=jax.ShapeDtypeStruct(given[-1].shap...]
    ppermute x14 -> x11, starting transfers between devices: 10.7 us -> 7.97 us  [swap_with(): return lax.ppermute(array, ENERGY, [(i, i ^ mask) for i in range(devices)])]
    ppermute x14 -> x11, waiting for transfers between devices: 8.54 us -> 9.99 us  [swap_with(): return lax.ppermute(array, ENERGY, [(i, i ^ mask) for i in range(devices)])]
    concatenate x1 -> x0, other arithmetic: 0.89 us -> none  [sandwich(): return jnp.concatenate([out_re, out_im], axis=-1).astype(jnp.bfloat16)]
  transfers between devices with their start and end apart: 18 -> 19, of which waited for: 12 -> 10; matrix products, arithmetic and copies ran while one was open for 3% -> 3% of each run, Pallas kernels for 2% -> 0%
where the time goes in v2:
time: 56.3 us; the launch traced here: 55.5 us
  waiting for transfers between devices  26.3 us (47%)
  starting transfers between devices  21.4 us (38%)
  Pallas kernels  6.16 us (11%)
  local copies, waits for them, and re-layouts  1.19 us (2%)
    ppermute x11, waiting for transfers between devices, swap_with(): return lax.ppermute(array, ENERGY, [(i, i ^ mask) for i in range(devices)])  9.99 us
    ppermute x4, starting transfers between devices, swap_across(): return lax.ppermute(array, (ENERGY, SLAB), pairs)  8.26 us
    ppermute x11, starting transfers between devices, swap_with(): return lax.ppermute(array, ENERGY, [(i, i ^ mask) for i in range(devices)])  7.97 us
    ppermute x1, waiting for transfers between devices, local(): early_im = lax.ppermute(im, SLAB, [(s, s + 1)])  7.47 us
    ppermute x1, waiting for transfers between devices, local(): lax.ppermute(jnp.where(odd == 1, re, early_im), SLAB, [(s, s + 1), (s + 1...  7.24 us
    pallas_call x1, Pallas kernels, correction(): pl.pallas_call(last_kernel, out_shape=jax.ShapeDtypeStruct(given[-1].shap...  3.15 us
    pallas_call x1, Pallas kernels, convolve(): pl.pallas_call(functools.partial(conv_kernel, chips), out_shape=pltpu.VME...  1.97 us
    ppermute x1, starting transfers between devices, local(): lax.ppermute(jnp.where(odd == 1, re, early_im), SLAB, [(s, s + 1), (s + 1...  1.92 us
  transfers between devices with their start and end apart: 19, of which 10 were waited for; matrix products, arithmetic and copies ran while one was open for 3% of the time, Pallas kernels for 0%

profile of v2, /device:TPU:16, one launch (start us, length us, event | category | flops | bytes accessed | tf_op | source)
XLA Modules:
  0.0 55.5 jit_solution(15176089464379697415)
XLA Ops:
  0.0 1.1 %dynamic-slice_bitcast_fusion = (bf16[80,640]{1,0:T(8,128)(2,1)S(1)}, bf16[80,640]{1,0:T(8,128)(2,1)S(1)}, bf16[80,640]{1,0:T(8,128)(2,1)S(1)}, bf16[80,640]{1,0:T(8,128)(2,1)S(1)}) fusion(bf16[1,1,320,640]{3,2,1,0:T(8,128)(2,1)} %param.4, s32[]{:T(128)S(6)} %select_n.56, s32[]{:T(128)S(6)} %select_n.54, s32[]{:T(128)S(6)} %select_n.53, s32[]{:T(128)S(6)} %select_n.55), kind=kLoop, calls=%fused_computation.8 | loop fusion | bytes 819216 | tf_op jit(solution)/shard_map/dynamic_slice | solution.py:223
  1.1 1.6 %collective-permute-start.2 = (bf16[80,640]{1,0:T(8,128)(2,1)S(1)}, bf16[80,640]{1,0:T(8,128)(2,1)S(1)}, u32[]{:S(2)}, u32[]{:S(2)}) collective-permute-start(bf16[80,640]{1,0:T(8,128)(2,1)S(1)} %get-tuple-element.16), channel_id=1, source_target_pairs={{0,8},{4,12},{8,0},{12,4},{16,24},{20,28},{24,16},{28,20},{1,9},{5... | collective-permute-start | bytes 307208 | tf_op jit(solution)/shard_map/ppermute | solution.py:22
  2.7 1.5 %collective-permute-start.3 = (bf16[80,640]{1,0:T(8,128)(2,1)S(1)}, bf16[80,640]{1,0:T(8,128)(2,1)S(1)}, u32[]{:S(2)}, u32[]{:S(2)}) collective-permute-start(bf16[80,640]{1,0:T(8,128)(2,1)S(1)} %get-tuple-element.18), channel_id=1, source_target_pairs={{0,16},{4,20},{8,24},{12,28},{16,0},{20,4},{24,8},{28,12},{1,17},{... | collective-permute-start | bytes 307208 | tf_op jit(solution)/shard_map/ppermute | solution.py:22
  4.8 1.7 %collective-permute-done.2.refs_1_ = bf16[80,640]{1,0:T(8,128)(2,1)S(1)} collective-permute-done((bf16[80,640]{1,0:T(8,128)(2,1)S(1)}, bf16[80,640]{1,0:T(8,128)(2,1)S(1)}, u32[]{:S(2)}, u32[]{:S(2)}) %collective-permute-start.2) | collective-permute-done | bytes 102432 | tf_op jit(solution)/shard_map/ppermute | solution.py:22
  6.5 2.4 %collective-permute-done.3.refs_2_ = bf16[80,640]{1,0:T(8,128)(2,1)S(1)} collective-permute-done((bf16[80,640]{1,0:T(8,128)(2,1)S(1)}, bf16[80,640]{1,0:T(8,128)(2,1)S(1)}, u32[]{:S(2)}, u32[]{:S(2)}) %collective-permute-start.3) | collective-permute-done | bytes 102432 | tf_op jit(solution)/shard_map/ppermute | solution.py:22
  8.9 1.0 %collective-permute-done.4.refs_3_ = bf16[80,640]{1,0:T(8,128)(2,1)S(1)} collective-permute-done((bf16[80,640]{1,0:T(8,128)(2,1)S(1)}, bf16[80,640]{1,0:T(8,128)(2,1)S(1)}, u32[]{:S(2)}, u32[]{:S(2)}) %collective-permute-start.4) | collective-permute-done | bytes 102432 | tf_op jit(solution)/shard_map/ppermute | solution.py:22
  10.2 1.0 %collective-permute-done.8.refs_7_ = bf16[80,640]{1,0:T(8,128)(2,1)S(1)} collective-permute-done((bf16[80,640]{1,0:T(8,128)(2,1)S(1)}, bf16[80,640]{1,0:T(8,128)(2,1)S(1)}, u32[]{:S(2)}, u32[]{:S(2)}) %collective-permute-start.8) | collective-permute-done | bytes 102432 | tf_op jit(solution)/shard_map/ppermute | solution.py:22
  11.2 2.0 %shard_map.46 = bf16[4,80,640]{2,1,0:T(8,128)(2,1)S(1)} custom-call(s32[3]{0:T(128)S(1)} %pad_add_fusion.place_ref.refs_0_, bf16[8,80,640]{2,1,0:T(8,128)(2,1)S(1)} %pad_maximum_fusion.inter_ref, bf16[80,640]{1,0:T(8,128)(2,1)S(1)} %get-tuple-element.17.refs_0_, bf16[80,640]{1,0:T(8,128)(2,1)S(1)} %collective-permute-done.2.refs_1_, ...), custom_call_target="tpu_custom_call" | custom-call | flops 13107200 | tf_op jit(solution)/shard_map/pallas_call | solution.py:83
  13.2 1.7 %collective-permute-start.10 = (bf16[80,640]{1,0:T(8,128)(2,1)S(1)}, bf16[80,640]{1,0:T(8,128)(2,1)S(1)}, u32[]{:S(2)}, u32[]{:S(2)}) collective-permute-start(bf16[80,640]{1,0:T(8,128)(2,1)S(1)} %get-tuple-element.12), channel_id=1, source_target_pairs={{0,16},{4,20},{8,24},{12,28},{16,0},{20,4},{24,8},{28,12},{1,17},{... | collective-permute-start | bytes 307208 | tf_op jit(solution)/shard_map/ppermute | solution.py:22
  14.9 1.0 %collective-permute-start.11 = (bf16[80,640]{1,0:T(8,128)(2,1)S(1)}, bf16[80,640]{1,0:T(8,128)(2,1)S(1)}, u32[]{:S(2)}, u32[]{:S(2)}) collective-permute-start(bf16[80,640]{1,0:T(8,128)(2,1)S(1)} %get-tuple-element.11), channel_id=1, source_target_pairs={{0,24},{4,28},{8,16},{12,20},{16,8},{20,12},{24,0},{28,4},{1,25},{... | collective-permute-start | bytes 307208 | tf_op jit(solution)/shard_map/ppermute | solution.py:22
  16.0 2.0 %collective-permute-start.14 = (bf16[80,640]{1,0:T(8,128)(2,1)S(1)}, bf16[80,640]{1,0:T(8,128)(2,1)S(1)}, u32[]{:S(2)}, u32[]{:S(2)}) collective-permute-start(bf16[80,640]{1,0:T(8,128)(2,1)S(1)} %get-tuple-element.12), channel_id=1, source_target_pairs={{0,17},{1,16},{2,19},{3,18},{4,21},{5,20},{6,23},{7,22},{8,25},{9,... | collective-permute-start | bytes 307208 | tf_op jit(solution)/shard_map/ppermute | solution.py:28
  18.4 2.5 %collective-permute-start.13 = (bf16[80,640]{1,0:T(8,128)(2,1)S(1)}, bf16[80,640]{1,0:T(8,128)(2,1)S(1)}, u32[]{:S(2)}, u32[]{:S(2)}) collective-permute-start(bf16[80,640]{1,0:T(8,128)(2,1)S(1)} %get-tuple-element.13), channel_id=1, source_target_pairs={{0,9},{1,8},{2,11},{3,10},{4,13},{5,12},{6,15},{7,14},{8,1},{9,0},... | collective-permute-start | bytes 307208 | tf_op jit(solution)/shard_map/ppermute | solution.py:28
  20.9 1.1 %collective-permute-done.10.refs_2_ = bf16[80,640]{1,0:T(8,128)(2,1)S(1)} collective-permute-done((bf16[80,640]{1,0:T(8,128)(2,1)S(1)}, bf16[80,640]{1,0:T(8,128)(2,1)S(1)}, u32[]{:S(2)}, u32[]{:S(2)}) %collective-permute-start.10) | collective-permute-done | bytes 102432 | tf_op jit(solution)/shard_map/ppermute | solution.py:22
  22.0 3.3 %collective-permute-start.15 = (bf16[80,640]{1,0:T(8,128)(2,1)S(1)}, bf16[80,640]{1,0:T(8,128)(2,1)S(1)}, u32[]{:S(2)}, u32[]{:S(2)}) collective-permute-start(bf16[80,640]{1,0:T(8,128)(2,1)S(1)} %get-tuple-element.11), channel_id=1, source_target_pairs={{0,25},{1,24},{2,27},{3,26},{4,29},{5,28},{6,31},{7,30},{8,17},{9,... | collective-permute-start | bytes 307208 | tf_op jit(solution)/shard_map/ppermute | solution.py:28
  25.3 1.6 %collective-permute-start.9 = (bf16[80,640]{1,0:T(8,128)(2,1)S(1)}, bf16[80,640]{1,0:T(8,128)(2,1)S(1)}, u32[]{:S(2)}, u32[]{:S(2)}) collective-permute-start(bf16[80,640]{1,0:T(8,128)(2,1)S(1)} %get-tuple-element.13), channel_id=1, source_target_pairs={{0,8},{4,12},{8,0},{12,4},{16,24},{20,28},{24,16},{28,20},{1,9},{5... | collective-permute-start | bytes 307208 | tf_op jit(solution)/shard_map/ppermute | solution.py:22
  26.9 1.6 %collective-permute-done.15.refs_7_ = bf16[80,640]{1,0:T(8,128)(2,1)S(1)} collective-permute-done((bf16[80,640]{1,0:T(8,128)(2,1)S(1)}, bf16[80,640]{1,0:T(8,128)(2,1)S(1)}, u32[]{:S(2)}, u32[]{:S(2)}) %collective-permute-start.15) | collective-permute-done | bytes 102432 | tf_op jit(solution)/shard_map/ppermute | solution.py:28
  28.6 2.7 %collective-permute-done.9.refs_1_ = bf16[80,640]{1,0:T(8,128)(2,1)S(1)} collective-permute-done((bf16[80,640]{1,0:T(8,128)(2,1)S(1)}, bf16[80,640]{1,0:T(8,128)(2,1)S(1)}, u32[]{:S(2)}, u32[]{:S(2)}) %collective-permute-start.9) | collective-permute-done | bytes 102432 | tf_op jit(solution)/shard_map/ppermute | solution.py:22
  31.3 1.0 %shard_map.47 = (bf16[320,320]{1,0:T(8,128)(2,1)S(1)}, bf16[320,320]{1,0:T(8,128)(2,1)S(1)}) custom-call(s32[3]{0:T(128)} %copy-done.2, bf16[320,320]{1,0:T(8,128)(2,1)S(1)} %bitcast.25, bf16[80,640]{1,0:T(8,128)(2,1)S(1)} %get-tuple-element.14.refs_0_, bf16[80,640]{1,0:T(8,128)(2,1)S(1)} %collective-permute-done.9.refs_1_, ...), custom_call_target="tpu_custom_call" | custom-call | tf_op jit(solution)/shard_map/pallas_call | solution.py:137
  32.4 1.3 %collective-permute-start.16 = (bf16[320,320]{1,0:T(8,128)(2,1)S(1)}, bf16[320,320]{1,0:T(8,128)(2,1)S(1)}, u32[]{:S(2)}, u32[]{:S(2)}) collective-permute-start(bf16[320,320]{1,0:T(8,128)(2,1)S(1)} %get-tuple-element.8.refs_4_), channel_id=1, source_target_pairs={{1,2},{5,6},{9,10},{13,14},{17,18},{21,22},{25,26},{29,30}} | collective-permute-start | bytes 614408 | tf_op jit(solution)/shard_map/ppermute | solution.py:235
  33.7 1.3 %collective-permute-start = (bf16[320,320]{1,0:T(8,128)(2,1)S(1)}, bf16[320,320]{1,0:T(8,128)(2,1)S(1)}, u32[]{:S(2)}, u32[]{:S(2)}) collective-permute-start(bf16[320,320]{1,0:T(8,128)(2,1)S(1)} %bitcast.26), channel_id=1, source_target_pairs={{0,1},{1,0},{2,3},{3,2},{4,5},{5,4},{6,7},{7,6},{8,9},{9,8},{10,11... | collective-permute-start | bytes 614408 | tf_op jit(solution)/shard_map/ppermute | solution.py:229
  35.6 7.5 %collective-permute-done.16.refs_5_ = bf16[320,320]{1,0:T(8,128)(2,1)S(1)} collective-permute-done((bf16[320,320]{1,0:T(8,128)(2,1)S(1)}, bf16[320,320]{1,0:T(8,128)(2,1)S(1)}, u32[]{:S(2)}, u32[]{:S(2)}) %collective-permute-start.16) | collective-permute-done | bytes 204832 | tf_op jit(solution)/shard_map/ppermute | solution.py:235
  43.2 1.9 %collective-permute-start.18 = (bf16[320,320]{1,0:T(8,128)(2,1)S(1)}, bf16[320,320]{1,0:T(8,128)(2,1)S(1)}, u32[]{:S(2)}, u32[]{:S(2)}) collective-permute-start(bf16[320,320]{1,0:T(8,128)(2,1)S(1)} %broadcast_select_fusion.2), channel_id=1, source_target_pairs={{1,2},{2,3},{5,6},{6,7},{9,10},{10,11},{13,14},{14,15},{17,18},{18... | collective-permute-start | bytes 614408 | tf_op jit(solution)/shard_map/ppermute | solution.py:237
  45.1 7.2 %collective-permute-done.18.refs_7_ = bf16[320,320]{1,0:T(8,128)(2,1)S(1)} collective-permute-done((bf16[320,320]{1,0:T(8,128)(2,1)S(1)}, bf16[320,320]{1,0:T(8,128)(2,1)S(1)}, u32[]{:S(2)}, u32[]{:S(2)}) %collective-permute-start.18) | collective-permute-done | bytes 204832 | tf_op jit(solution)/shard_map/ppermute | solution.py:237
  52.3 3.1 %shard_map.48 = bf16[320,640]{1,0:T(8,128)(2,1)} custom-call(s32[3]{0:T(128)} %copy-done.2, bf16[320,320]{1,0:T(8,128)(2,1)S(1)} %bitcast.27, bf16[320,320]{1,0:T(8,128)(2,1)S(1)} %collective-permute-done.refs_2_, bf16[320,320]{1,0:T(8,128)(2,1)S(1)} %get-tuple-element.7.refs_3_, bf16[320,320]{1,0:T(8,128)(2,1)S(1)} %get-tuple-element.8.refs_4_, ...), custom_call_target="tpu_custom_call" | custom-call | tf_op jit(solution)/shard_map/pallas_call | solution.py:196
  (31 shorter events, 2.1 us)
Async XLA Ops:
  0.0 9.9 %copy-start.3 = (bf16[8,1,40,640]{3,2,1,0:T(8,128)(2,1)S(1)}, bf16[8,1,40,640]{3,2,1,0:T(8,128)(2,1)}, u32[]{:S(2)}) copy-start(bf16[8,1,40,640]{3,2,1,0:T(8,128)(2,1)} %param.6) | copy-start | bytes 1228804
  0.0 9.9 %collective-permute-start.1 = (bf16[8,40,640]{2,1,0:T(8,128)(2,1)}, bf16[8,40,640]{2,1,0:T(8,128)(2,1)S(1)}, u32[]{:S(2)}, u32[]{:S(2)}) collective-permute-start(bf16[8,40,640]{2,1,0:T(8,128)(2,1)} %bitcast.29), channel_id=1, source_target_pairs={{0,4},{4,0},{8,12},{12,8},{16,20},{20,16},{24,28},{28,24},{1,5},{5... | collective-permute-start | bytes 1228808 | tf_op jit(solution)/shard_map/ppermute | solution.py:22
  1.1 5.3 %collective-permute-start.2 = (bf16[80,640]{1,0:T(8,128)(2,1)S(1)}, bf16[80,640]{1,0:T(8,128)(2,1)S(1)}, u32[]{:S(2)}, u32[]{:S(2)}) collective-permute-start(bf16[80,640]{1,0:T(8,128)(2,1)S(1)} %get-tuple-element.16), channel_id=1, source_target_pairs={{0,8},{4,12},{8,0},{12,4},{16,24},{20,28},{24,16},{28,20},{1,9},{5... | collective-permute-start | bytes 307208 | tf_op jit(solution)/shard_map/ppermute | solution.py:22
  2.7 6.2 %collective-permute-start.3 = (bf16[80,640]{1,0:T(8,128)(2,1)S(1)}, bf16[80,640]{1,0:T(8,128)(2,1)S(1)}, u32[]{:S(2)}, u32[]{:S(2)}) collective-permute-start(bf16[80,640]{1,0:T(8,128)(2,1)S(1)} %get-tuple-element.18), channel_id=1, source_target_pairs={{0,16},{4,20},{8,24},{12,28},{16,0},{20,4},{24,8},{28,12},{1,17},{... | collective-permute-start | bytes 307208 | tf_op jit(solution)/shard_map/ppermute | solution.py:22
  4.2 5.6 %collective-permute-start.4 = (bf16[80,640]{1,0:T(8,128)(2,1)S(1)}, bf16[80,640]{1,0:T(8,128)(2,1)S(1)}, u32[]{:S(2)}, u32[]{:S(2)}) collective-permute-start(bf16[80,640]{1,0:T(8,128)(2,1)S(1)} %get-tuple-element.15), channel_id=1, source_target_pairs={{0,24},{4,28},{8,16},{12,20},{16,8},{20,12},{24,0},{28,4},{1,25},{... | collective-permute-start | bytes 307208 | tf_op jit(solution)/shard_map/ppermute | solution.py:22
  4.7 5.3 %collective-permute-start.5 = (bf16[80,640]{1,0:T(8,128)(2,1)S(1)}, bf16[80,640]{1,0:T(8,128)(2,1)S(1)}, u32[]{:S(2)}, u32[]{:S(2)}) collective-permute-start(bf16[80,640]{1,0:T(8,128)(2,1)S(1)} %get-tuple-element.17.refs_0_), channel_id=1, source_target_pairs={{0,4},{4,0},{8,12},{12,8},{16,20},{20,16},{24,28},{28,24},{1,5},{5... | collective-permute-start | bytes 307208 | tf_op jit(solution)/shard_map/ppermute | solution.py:22
  4.8 6.4 %copy-start.2 = (s32[3]{0:T(128)}, s32[3]{0:T(128)S(1)}, u32[]{:S(2)}) copy-start(s32[3]{0:T(128)S(1)} %pad_add_fusion.place_ref.refs_0_) | copy-start | bytes 40
  6.4 3.6 %collective-permute-start.6 = (bf16[80,640]{1,0:T(8,128)(2,1)S(1)}, bf16[80,640]{1,0:T(8,128)(2,1)S(1)}, u32[]{:S(2)}, u32[]{:S(2)}) collective-permute-start(bf16[80,640]{1,0:T(8,128)(2,1)S(1)} %collective-permute-done.2.refs_1_), channel_id=1, source_target_pairs={{0,4},{4,0},{8,12},{12,8},{16,20},{20,16},{24,28},{28,24},{1,5},{5... | collective-permute-start | bytes 307208 | tf_op jit(solution)/shard_map/ppermute | solution.py:22
  8.9 1.3 %collective-permute-start.7 = (bf16[80,640]{1,0:T(8,128)(2,1)S(1)}, bf16[80,640]{1,0:T(8,128)(2,1)S(1)}, u32[]{:S(2)}, u32[]{:S(2)}) collective-permute-start(bf16[80,640]{1,0:T(8,128)(2,1)S(1)} %collective-permute-done.3.refs_2_), channel_id=1, source_target_pairs={{0,4},{4,0},{8,12},{12,8},{16,20},{20,16},{24,28},{28,24},{1,5},{5... | collective-permute-start | bytes 307208 | tf_op jit(solution)/shard_map/ppermute | solution.py:22
  9.9 1.3 %collective-permute-start.8 = (bf16[80,640]{1,0:T(8,128)(2,1)S(1)}, bf16[80,640]{1,0:T(8,128)(2,1)S(1)}, u32[]{:S(2)}, u32[]{:S(2)}) collective-permute-start(bf16[80,640]{1,0:T(8,128)(2,1)S(1)} %collective-permute-done.4.refs_3_), channel_id=1, source_target_pairs={{0,4},{4,0},{8,12},{12,8},{16,20},{20,16},{24,28},{28,24},{1,5},{5... | collective-permute-start | bytes 307208 | tf_op jit(solution)/shard_map/ppermute | solution.py:22
  13.1 18.2 %copy-start = (bf16[1,320,320]{2,1,0:T(8,128)(2,1)S(1)}, bf16[1,320,320]{2,1,0:T(8,128)(2,1)}, u32[]{:S(2)}) copy-start(bf16[1,320,320]{2,1,0:T(8,128)(2,1)} %param.7) | copy-start | bytes 614404
  13.2 8.8 %collective-permute-start.10 = (bf16[80,640]{1,0:T(8,128)(2,1)S(1)}, bf16[80,640]{1,0:T(8,128)(2,1)S(1)}, u32[]{:S(2)}, u32[]{:S(2)}) collective-permute-start(bf16[80,640]{1,0:T(8,128)(2,1)S(1)} %get-tuple-element.12), channel_id=1, source_target_pairs={{0,16},{4,20},{8,24},{12,28},{16,0},{20,4},{24,8},{28,12},{1,17},{... | collective-permute-start | bytes 307208 | tf_op jit(solution)/shard_map/ppermute | solution.py:22
  14.9 10.4 %collective-permute-start.11 = (bf16[80,640]{1,0:T(8,128)(2,1)S(1)}, bf16[80,640]{1,0:T(8,128)(2,1)S(1)}, u32[]{:S(2)}, u32[]{:S(2)}) collective-permute-start(bf16[80,640]{1,0:T(8,128)(2,1)S(1)} %get-tuple-element.11), channel_id=1, source_target_pairs={{0,24},{4,28},{8,16},{12,20},{16,8},{20,12},{24,0},{28,4},{1,25},{... | collective-permute-start | bytes 307208 | tf_op jit(solution)/shard_map/ppermute | solution.py:22
  16.0 11.0 %collective-permute-start.14 = (bf16[80,640]{1,0:T(8,128)(2,1)S(1)}, bf16[80,640]{1,0:T(8,128)(2,1)S(1)}, u32[]{:S(2)}, u32[]{:S(2)}) collective-permute-start(bf16[80,640]{1,0:T(8,128)(2,1)S(1)} %get-tuple-element.12), channel_id=1, source_target_pairs={{0,17},{1,16},{2,19},{3,18},{4,21},{5,20},{6,23},{7,22},{8,25},{9,... | collective-permute-start | bytes 307208 | tf_op jit(solution)/shard_map/ppermute | solution.py:28
  17.9 9.0 %collective-permute-start.12 = (bf16[80,640]{1,0:T(8,128)(2,1)S(1)}, bf16[80,640]{1,0:T(8,128)(2,1)S(1)}, u32[]{:S(2)}, u32[]{:S(2)}) collective-permute-start(bf16[80,640]{1,0:T(8,128)(2,1)S(1)} %get-tuple-element.14.refs_0_), channel_id=1, source_target_pairs={{0,1},{1,0},{2,3},{3,2},{4,5},{5,4},{6,7},{7,6},{8,9},{9,8},{10,11... | collective-permute-start | bytes 307208 | tf_op jit(solution)/shard_map/ppermute | solution.py:28
  18.4 8.5 %collective-permute-start.13 = (bf16[80,640]{1,0:T(8,128)(2,1)S(1)}, bf16[80,640]{1,0:T(8,128)(2,1)S(1)}, u32[]{:S(2)}, u32[]{:S(2)}) collective-permute-start(bf16[80,640]{1,0:T(8,128)(2,1)S(1)} %get-tuple-element.13), channel_id=1, source_target_pairs={{0,9},{1,8},{2,11},{3,10},{4,13},{5,12},{6,15},{7,14},{8,1},{9,0},... | collective-permute-start | bytes 307208 | tf_op jit(solution)/shard_map/ppermute | solution.py:28
  22.0 6.6 %collective-permute-start.15 = (bf16[80,640]{1,0:T(8,128)(2,1)S(1)}, bf16[80,640]{1,0:T(8,128)(2,1)S(1)}, u32[]{:S(2)}, u32[]{:S(2)}) collective-permute-start(bf16[80,640]{1,0:T(8,128)(2,1)S(1)} %get-tuple-element.11), channel_id=1, source_target_pairs={{0,25},{1,24},{2,27},{3,26},{4,29},{5,28},{6,31},{7,30},{8,17},{9,... | collective-permute-start | bytes 307208 | tf_op jit(solution)/shard_map/ppermute | solution.py:28
  25.3 6.0 %collective-permute-start.9 = (bf16[80,640]{1,0:T(8,128)(2,1)S(1)}, bf16[80,640]{1,0:T(8,128)(2,1)S(1)}, u32[]{:S(2)}, u32[]{:S(2)}) collective-permute-start(bf16[80,640]{1,0:T(8,128)(2,1)S(1)} %get-tuple-element.13), channel_id=1, source_target_pairs={{0,8},{4,12},{8,0},{12,4},{16,24},{20,28},{24,16},{28,20},{1,9},{5... | collective-permute-start | bytes 307208 | tf_op jit(solution)/shard_map/ppermute | solution.py:22
  31.3 21.0 %copy-start.1 = (bf16[1,1,320,640]{3,2,1,0:T(8,128)(2,1)S(1)}, bf16[1,1,320,640]{3,2,1,0:T(8,128)(2,1)}, u32[]{:S(2)}) copy-start(bf16[1,1,320,640]{3,2,1,0:T(8,128)(2,1)} %param.5) | copy-start | bytes 1228804
  32.4 10.8 %collective-permute-start.16 = (bf16[320,320]{1,0:T(8,128)(2,1)S(1)}, bf16[320,320]{1,0:T(8,128)(2,1)S(1)}, u32[]{:S(2)}, u32[]{:S(2)}) collective-permute-start(bf16[320,320]{1,0:T(8,128)(2,1)S(1)} %get-tuple-element.8.refs_4_), channel_id=1, source_target_pairs={{1,2},{5,6},{9,10},{13,14},{17,18},{21,22},{25,26},{29,30}} | collective-permute-start | bytes 614408 | tf_op jit(solution)/shard_map/ppermute | solution.py:235
  33.7 11.4 %collective-permute-start = (bf16[320,320]{1,0:T(8,128)(2,1)S(1)}, bf16[320,320]{1,0:T(8,128)(2,1)S(1)}, u32[]{:S(2)}, u32[]{:S(2)}) collective-permute-start(bf16[320,320]{1,0:T(8,128)(2,1)S(1)} %bitcast.26), channel_id=1, source_target_pairs={{0,1},{1,0},{2,3},{3,2},{4,5},{5,4},{6,7},{7,6},{8,9},{9,8},{10,11... | collective-permute-start | bytes 614408 | tf_op jit(solution)/shard_map/ppermute | solution.py:229
  35.0 10.1 %collective-permute-start.17 = (bf16[320,320]{1,0:T(8,128)(2,1)S(1)}, bf16[320,320]{1,0:T(8,128)(2,1)S(1)}, u32[]{:S(2)}, u32[]{:S(2)}) collective-permute-start(bf16[320,320]{1,0:T(8,128)(2,1)S(1)} %get-tuple-element.7.refs_3_), channel_id=1, source_target_pairs={{1,3},{5,7},{9,11},{13,15},{17,19},{21,23},{25,27},{29,31}} | collective-permute-start | bytes 614408 | tf_op jit(solution)/shard_map/ppermute | solution.py:236
  43.2 9.2 %collective-permute-start.18 = (bf16[320,320]{1,0:T(8,128)(2,1)S(1)}, bf16[320,320]{1,0:T(8,128)(2,1)S(1)}, u32[]{:S(2)}, u32[]{:S(2)}) collective-permute-start(bf16[320,320]{1,0:T(8,128)(2,1)S(1)} %broadcast_select_fusion.2), channel_id=1, source_target_pairs={{1,2},{2,3},{5,6},{6,7},{9,10},{10,11},{13,14},{14,15},{17,18},{18... | collective-permute-start | bytes 614408 | tf_op jit(solution)/shard_map/ppermute | solution.py:237

commit v3 on v1

v3 whole, which is shorter than its diff:
```python
import functools

import jax
import jax.numpy as jnp
from jax import lax
from jax.experimental import pallas as pl
from jax.experimental.pallas import tpu as pltpu
from jax.sharding import PartitionSpec as P

ENERGY = "energy"
SLAB = "slab"
WHOLE = pl.BlockSpec(memory_space=pltpu.VMEM)


def in_vmem(*arrays):
    return [pltpu.with_memory_space_constraint(x, pltpu.VMEM) for x in arrays]


def swap_with(array, mask):
    devices = lax.axis_size(ENERGY)
    return lax.ppermute(array, ENERGY, [(i, i ^ mask) for i in range(devices)])


def swap_slabs(array, slab_to):
    devices, slabs = lax.axis_size(ENERGY), lax.axis_size(SLAB)
    pairs = []
    for e in range(devices):
        for s in range(slabs):
            to = (e, slab_to[s]) if s in slab_to else (e ^ 1, s)
            pairs.append((e * slabs + s, to[0] * slabs + to[1]))
    return lax.ppermute(array, (ENERGY, SLAB), pairs)


def call(kernel, outs, given, scratch=()):
    outs = [pltpu.VMEM(shape, dtype) for shape, dtype in outs]
    return pl.pallas_call(
        kernel,
        out_shape=outs,
        in_specs=[WHOLE] * len(given),
        out_specs=[WHOLE] * len(outs),
        scratch_shapes=list(scratch),
        compiler_params=pltpu.CompilerParams(vmem_limit_bytes=10 << 20),
    )(*in_vmem(*given))


def conv_kernel(chips, inter_ref, *refs):
    pieces = refs[: 2 * chips]
    out_ref, a_ref, b_ref, w_ref, v_ref, sum_ref = refs[2 * chips :]
    me = lax.axis_index(ENERGY)
    chip, side = me // 2, me % 2
    rows, width = inter_ref.shape[1:]
    half = width // 2
    left = lax.broadcasted_iota(jnp.int32, (rows, width), 1) < half

    def swapped(x):
        return jnp.concatenate([x[:, half:], x[:, :half]], axis=1)

    @pl.when(side == 0)
    def _():
        a_ref[0] = jnp.zeros((rows, width), jnp.float32)
        b_ref[0] = jnp.zeros((rows, width), jnp.float32)

    for other in range(2):
        for j in range(chips):
            x = pieces[other * chips + j][...].astype(jnp.float32)
            y = swapped(x)
            slot = 2 * (chip ^ j) + (side ^ other) + 1 - side
            a_ref[slot] = jnp.where(left, x, y)
            b_ref[slot] = jnp.where(left, y, x)
    for m in range(2 * chips):
        x = inter_ref[m].astype(jnp.float32)
        y = swapped(x)
        w_ref[m] = x
        v_ref[m] = jnp.where(left, -y, y)

    step = 8 if rows % 8 == 0 else rows
    lanes = 128 if width % 128 == 0 else width

    def tile(t, carry):
        here = pl.ds(pl.multiple_of(t * step, step), step)
        for c in range(0, width, lanes):
            at = pl.ds(c, lanes)
            for j in range(chips):
                total = None
                for m in range(2 * j + 2):
                    s = 2 * j + 1 - m
                    term = a_ref[s, here, at] * v_ref[m, here, at] - b_ref[s, here, at] * w_ref[m, here, at]
                    total = term if total is None else total + term
                sum_ref[chip ^ j, here, at] = total
        return carry

    lax.fori_loop(0, rows // step, tile, 0)
    out_ref[...] = sum_ref[...].astype(jnp.bfloat16)


def convolve(chips, inter, pieces):
    count, rows, width = inter.shape
    block = lambda n: pltpu.VMEM((n, rows, width), jnp.float32)
    return pl.pallas_call(
        functools.partial(conv_kernel, chips),
        out_shape=pltpu.VMEM((chips, rows, width), jnp.bfloat16),
        in_specs=[WHOLE] * (1 + 2 * chips),
        out_specs=WHOLE,
        scratch_shapes=[block(count + 1), block(count + 1), block(count), block(count), block(chips)],
        compiler_params=pltpu.CompilerParams(vmem_limit_bytes=16 << 20),
        cost_estimate=pl.CostEstimate(flops=count * count * rows * width * 4, bytes_accessed=0, transcendentals=0),
    )(*in_vmem(inter, *pieces))


def dot(a, b):
    return jnp.dot(a, b, preferred_element_type=jnp.float32)


def packed(x):
    half = x.shape[0] // 2
    return jnp.concatenate([x[:half], x[half:]], axis=1)


def unpacked(x):
    size = x.shape[1] // 2
    return jnp.concatenate([x[:, :size], x[:, size:]], axis=0)


def moved(link_ref, turned_ref, x):
    return dot(dot(link_ref[...], x).astype(jnp.bfloat16), turned_ref[...])


def gather_kernel(*refs):
    chip = lax.axis_index(ENERGY) // 2
    first_ref, *others, re_ref, im_ref, all_ref = refs
    chips, rows, width = all_ref.shape
    half = width // 2
    for j, piece in enumerate([first_ref[0], *(ref[...] for ref in others)]):
        all_ref[chip ^ j] = piece
    whole = all_ref[...].reshape(chips * rows, width)
    re_ref[...] = packed(whole[:, :half])
    im_ref[...] = packed(whole[:, half:])


def gathered(own, pieces):
    chips, rows, width = own.shape
    part = ((chips * rows // 2, width), jnp.bfloat16)
    return call(gather_kernel, [part, part], [own, *pieces], [pltpu.VMEM(own.shape, own.dtype)])


def prepare_kernel(link_ref, before_ref, green_ref, turned_ref, step_ref, turned_step_ref, stack_ref, first_ref, second_ref):
    odd = lax.axis_index(SLAB) % 2
    turned_ref[...] = link_ref[...].T

    @pl.when(odd == 0)
    def _():
        step_ref[...] = link_ref[...]

    @pl.when(odd == 1)
    def _():
        step_ref[...] = dot(link_ref[...], before_ref[...]).astype(jnp.bfloat16)

    turned_step_ref[...] = step_ref[...].T
    size = green_ref.shape[0]
    re, im = green_ref[:, :size], green_ref[:, size:]
    stack_ref[:size] = re
    stack_ref[size:] = im
    first_ref[...] = jnp.concatenate([re, -im], axis=0).T
    second_ref[...] = jnp.concatenate([im, re], axis=0).T


def carry_in(turn, link_ref, turned_ref, state_ref, came, out_ref):
    @pl.when(turn)
    def _():
        state = unpacked(state_ref[...]).astype(jnp.float32)
        out_ref[...] = packed((state + moved(link_ref, turned_ref, unpacked(came))).astype(jnp.bfloat16))

    @pl.when(jnp.logical_not(turn))
    def _():
        out_ref[...] = state_ref[...]


def first_kernel(link_ref, turned_ref, own_ref, came_ref, out_ref):
    carry_in(lax.axis_index(SLAB) % 2 == 1, link_ref, turned_ref, own_ref, came_ref[...], out_ref)


def advance_kernel(pair, step_ref, turned_ref, state_ref, near_ref, far_ref, out_ref):
    slab = lax.axis_index(SLAB)
    came = jnp.where(slab % 2 == 0, near_ref[...], far_ref[...])
    carry_in(slab // 2 == pair, step_ref, turned_ref, state_ref, came, out_ref)


def early_kernel(pair, step_ref, turned_ref, stack_ref, re_ref, near_ref, far_ref, out_ref, x_ref):
    advance_kernel(pair, step_ref, turned_ref, re_ref, near_ref, far_ref, x_ref)
    out_ref[...] = dot(stack_ref[...], unpacked(x_ref[...]))


def late_kernel(pair, step_ref, turned_ref, stack_ref, first_ref, second_ref, im_ref, near_ref, far_ref, early_ref, out_ref, x_ref):
    advance_kernel(pair, step_ref, turned_ref, im_ref, near_ref, far_ref, x_ref)
    late = dot(stack_ref[...], unpacked(x_ref[...]))
    size = x_ref.shape[1] // 2
    left_re = (early_ref[:size] - late[size:]).astype(jnp.bfloat16)
    left_im = (late[:size] + early_ref[size:]).astype(jnp.bfloat16)
    out_ref[...] = (dot(left_re, first_ref[...]) + dot(left_im, second_ref[...])).astype(jnp.bfloat16)


def local(g_lesser, g_retarded, screened, coupling):
    devices = lax.axis_size(ENERGY)
    slabs = lax.axis_size(SLAB)
    chips = devices // 2
    me = lax.axis_index(ENERGY)
    chip, side = me // 2, me % 2

    lesser = g_lesser[0, 0]
    size, width = lesser.shape
    rows = size // chips
    inter = screened[:, 0]
    inter_other = swap_with(inter, 1)
    first = jnp.where(side == 0, inter, inter_other)
    second = jnp.where(side == 0, inter_other, inter)
    inter_rows = jnp.concatenate([first, second], axis=1)

    link = coupling[0]
    other_in_pair = {s: s ^ 1 for s in range(slabs)}
    link_before = swap_slabs(link, other_in_pair)
    square = (link.shape, jnp.bfloat16)
    tall, wide = ((2 * size, size), jnp.bfloat16), ((size, 2 * size), jnp.bfloat16)
    prepared = call(prepare_kernel, [square, square, square, tall, wide, wide], [link, link_before, g_retarded[0, 0]])

    mine = [lax.dynamic_slice(lesser, (rows * (chip ^ j), 0), (rows, width)) for j in range(chips)]
    pieces = [mine[0]] + [swap_with(mine[j], 2 * j) for j in range(1, chips)]
    pieces = pieces + [swap_with(x, 1) for x in pieces]
    inter_rows, prepared = lax.optimization_barrier((inter_rows, prepared))
    turned, step, turned_step, stack, adjoint_first, adjoint_second = prepared
    sigma = convolve(chips, inter_rows, pieces)

    own_re, own_im = gathered(sigma, [swap_with(sigma[j], 2 * j) for j in range(1, chips)])
    part = (own_re.shape, own_re.dtype)
    came_re = swap_slabs(own_re, other_in_pair)
    own_im, came_re = lax.optimization_barrier((own_im, came_re))
    came_im = swap_slabs(own_im, other_in_pair)
    (re,) = call(first_kernel, [part], [link, turned, own_re, came_re])
    (im,) = call(first_kernel, [part], [link, turned, own_im, came_im])

    for s in range(1, slabs - 1, 2):
        pair = (s + 1) // 2
        near_re = swap_slabs(re, {s: s + 1, s + 1: s})
        near_im = swap_slabs(im, {s: s + 1, s + 1: s})
        far_re = swap_slabs(near_re, {s + 1: s + 2, s + 2: s + 1})
        far_im = swap_slabs(near_im, {s + 1: s + 2, s + 2: s + 1})
        if s + 3 < slabs:
            advance = functools.partial(advance_kernel, pair)
            (re,) = call(advance, [part], [step, turned_step, re, near_re, far_re])
            (im,) = call(advance, [part], [step, turned_step, im, near_im, far_im])
    scratch = pltpu.VMEM(re.shape, jnp.bfloat16)
    (early,) = call(
        functools.partial(early_kernel, pair),
        [((2 * size, size), jnp.float32)],
        [step, turned_step, stack, re, near_re, far_re],
        [scratch],
    )
    given = [step, turned_step, stack, adjoint_first, adjoint_second, im, near_im, far_im, early]
    out = pl.pallas_call(
        functools.partial(late_kernel, pair),
        out_shape=jax.ShapeDtypeStruct((size, width), jnp.bfloat16),
        in_specs=[WHOLE] * len(given),
        out_specs=WHOLE,
        scratch_shapes=[scratch],
        compiler_params=pltpu.CompilerParams(vmem_limit_bytes=10 << 20),
    )(*in_vmem(*given))
    return out[None, None]


def solution(mesh):
    placed = (
        P(ENERGY, SLAB, None, None),
        P(ENERGY, SLAB, None, None),
        P(None, SLAB, ENERGY, None),
        P(SLAB, None, None),
    )
    return jax.shard_map(
        local,
        mesh=mesh,
        in_specs=placed,
        out_specs=P(ENERGY, SLAB, None, None),
        check_vma=False,
    )
```

time: 58.9 us -> 50.1 us (0.85); the launches traced: 57.7 us -> 49.8 us
  matrix products: 6.12 us -> 0 us
  starting transfers between devices: 16.5 us -> 12.4 us
  Pallas kernels: 3.44 us -> 6.42 us
  other arithmetic: 1.27 us -> 0.16 us
  waiting for transfers between devices: 28.6 us -> 29.6 us
    dot_general x12 -> x0, matrix products: 6.12 us -> none  [the longest x4 2.84 us: moved(): lax.dot_general(left, link, (((1,), (1,)), ((), ())), preferred_element_t...]
    ppermute x14 -> x11, starting transfers between devices: 10.7 us -> 7.69 us  [swap_with(): return lax.ppermute(array, ENERGY, [(i, i ^ mask) for i in range(devices)])]
    pallas_call x3 -> x7, Pallas kernels: 3.44 us -> 6.42 us  [the longest x5 2.5 us: call(): pl.pallas_call(kernel, out_shape=outs, in_specs=[WHOLE] * len(given), out...]
    ppermute x14 -> x11, waiting for transfers between devices: 8.54 us -> 9.83 us  [swap_with(): return lax.ppermute(array, ENERGY, [(i, i ^ mask) for i in range(devices)])]
    ppermute x4 -> x7, starting transfers between devices: 5.82 us -> 4.69 us  [swap_slabs(): return lax.ppermute(array, (ENERGY, SLAB), pairs)]
    concatenate x1 -> x0, other arithmetic: 0.89 us -> none  [sandwich(): return jnp.concatenate([out_re, out_im], axis=-1).astype(jnp.bfloat16)]
    ppermute x4 -> x7, waiting for transfers between devices: 20.1 us -> 19.7 us  [swap_slabs(): return lax.ppermute(array, (ENERGY, SLAB), pairs)]
  transfers between devices with their start and end apart: 18 -> 18, of which waited for: 12 -> 12; matrix products, arithmetic and copies ran while one was open for 3% -> 2% of each run, Pallas kernels for 2% -> 5%
where the time goes in v3:
time: 50.1 us; the launch traced here: 49.8 us
  waiting for transfers between devices  29.6 us (59%)
  starting transfers between devices  12.4 us (25%)
  Pallas kernels  6.42 us (13%)
  local copies, waits for them, and re-layouts  1.12 us (2%)
    ppermute x7, waiting for transfers between devices, swap_slabs(): return lax.ppermute(array, (ENERGY, SLAB), pairs)  19.7 us
    ppermute x11, waiting for transfers between devices, swap_with(): return lax.ppermute(array, ENERGY, [(i, i ^ mask) for i in range(devices)])  9.83 us
    ppermute x11, starting transfers between devices, swap_with(): return lax.ppermute(array, ENERGY, [(i, i ^ mask) for i in range(devices)])  7.69 us
    ppermute x7, starting transfers between devices, swap_slabs(): return lax.ppermute(array, (ENERGY, SLAB), pairs)  4.69 us
    pallas_call x5, Pallas kernels, call(): pl.pallas_call(kernel, out_shape=outs, in_specs=[WHOLE] * len(given), out...  2.5 us
    pallas_call x1, Pallas kernels, local(): pl.pallas_call(functools.partial(late_kernel, pair), out_shape=jax.ShapeD...  2.49 us
    pallas_call x1, Pallas kernels, convolve(): pl.pallas_call(functools.partial(conv_kernel, chips), out_shape=pltpu.VME...  1.44 us
    dynamic_slice x1, local copies, waits for them, and re-layouts, local(): lax.dynamic_slice(lesser, (rows * (chip ^ j), 0), (rows, width))  1.08 us
  transfers between devices with their start and end apart: 18, of which 12 were waited for; matrix products, arithmetic and copies ran while one was open for 2% of the time, Pallas kernels for 5%

profile of v3, /device:TPU:16, one launch (start us, length us, event | category | flops | bytes accessed | tf_op | source)
XLA Modules:
  0.0 49.8 jit_solution(17321923985911022199)
XLA Ops:
  0.1 1.6 %collective-permute-start.1 = (bf16[320,320]{1,0:T(8,128)(2,1)}, bf16[320,320]{1,0:T(8,128)(2,1)S(1)}, u32[]{:S(2)}, u32[]{:S(2)}) collective-permute-start(bf16[320,320]{1,0:T(8,128)(2,1)} %bitcast.20), channel_id=1, source_target_pairs={{0,1},{1,0},{2,3},{3,2},{4,5},{5,4},{6,7},{7,6},{8,9},{9,8},{10,11... | collective-permute-start | bytes 614408 | tf_op jit(solution)/shard_map/ppermute | solution.py:31
  1.7 1.1 %dynamic-slice_bitcast_fusion = (bf16[80,640]{1,0:T(8,128)(2,1)S(1)}, bf16[80,640]{1,0:T(8,128)(2,1)S(1)}, bf16[80,640]{1,0:T(8,128)(2,1)S(1)}, bf16[80,640]{1,0:T(8,128)(2,1)S(1)}) fusion(bf16[1,1,320,640]{3,2,1,0:T(8,128)(2,1)} %param.4, s32[]{:T(128)S(6)} %select_n.43, s32[]{:T(128)S(6)} %select_n.41, s32[]{:T(128)S(6)} %select_n.40, s32[]{:T(128)S(6)} %select_n.42), kind=kLoop, calls=%fused_computation.6 | loop fusion | bytes 819216 | tf_op jit(solution)/shard_map/dynamic_slice | solution.py:225
  2.8 1.6 %collective-permute-start.2 = (bf16[80,640]{1,0:T(8,128)(2,1)S(1)}, bf16[80,640]{1,0:T(8,128)(2,1)S(1)}, u32[]{:S(2)}, u32[]{:S(2)}) collective-permute-start(bf16[80,640]{1,0:T(8,128)(2,1)S(1)} %get-tuple-element.45), channel_id=1, source_target_pairs={{0,8},{4,12},{8,0},{12,4},{16,24},{20,28},{24,16},{28,20},{1,9},{5... | collective-permute-start | bytes 307208 | tf_op jit(solution)/shard_map/ppermute | solution.py:21
  4.4 1.5 %collective-permute-start.3 = (bf16[80,640]{1,0:T(8,128)(2,1)S(1)}, bf16[80,640]{1,0:T(8,128)(2,1)S(1)}, u32[]{:S(2)}, u32[]{:S(2)}) collective-permute-start(bf16[80,640]{1,0:T(8,128)(2,1)S(1)} %get-tuple-element.47), channel_id=1, source_target_pairs={{0,16},{4,20},{8,24},{12,28},{16,0},{20,4},{24,8},{28,12},{1,17},{... | collective-permute-start | bytes 307208 | tf_op jit(solution)/shard_map/ppermute | solution.py:21
  6.4 1.5 %collective-permute-done.2.refs_1_ = bf16[80,640]{1,0:T(8,128)(2,1)S(1)} collective-permute-done((bf16[80,640]{1,0:T(8,128)(2,1)S(1)}, bf16[80,640]{1,0:T(8,128)(2,1)S(1)}, u32[]{:S(2)}, u32[]{:S(2)}) %collective-permute-start.2) | collective-permute-done | bytes 102432 | tf_op jit(solution)/shard_map/ppermute | solution.py:21
  7.8 2.4 %collective-permute-done.3.refs_2_ = bf16[80,640]{1,0:T(8,128)(2,1)S(1)} collective-permute-done((bf16[80,640]{1,0:T(8,128)(2,1)S(1)}, bf16[80,640]{1,0:T(8,128)(2,1)S(1)}, u32[]{:S(2)}, u32[]{:S(2)}) %collective-permute-start.3) | collective-permute-done | bytes 102432 | tf_op jit(solution)/shard_map/ppermute | solution.py:21
  10.3 1.2 %collective-permute-done.4.refs_3_ = bf16[80,640]{1,0:T(8,128)(2,1)S(1)} collective-permute-done((bf16[80,640]{1,0:T(8,128)(2,1)S(1)}, bf16[80,640]{1,0:T(8,128)(2,1)S(1)}, u32[]{:S(2)}, u32[]{:S(2)}) %collective-permute-start.4) | collective-permute-done | bytes 102432 | tf_op jit(solution)/shard_map/ppermute | solution.py:21
  12.0 1.0 %shard_map.46 = (bf16[320,320]{1,0:T(8,128)(2,1)S(1)}, bf16[320,320]{1,0:T(8,128)(2,1)S(1)}, bf16[320,320]{1,0:T(8,128)(2,1)S(1)}, bf16[640,320]{1,0:T(8,128)(2,...) custom-call(bf16[320,320]{1,0:T(8,128)(2,1)S(1)} %bitcast.21, ...), custom_call_target="tpu_custom_call" | custom-call | tf_op jit(solution)/shard_map/pallas_call | solution.py:36
  13.2 1.4 %shard_map.47.refs_0_ = bf16[4,80,640]{2,1,0:T(8,128)(2,1)S(1)} custom-call(bf16[8,80,640]{2,1,0:T(8,128)(2,1)S(1)} %pad_maximum_fusion.inter_ref, bf16[80,640]{1,0:T(8,128)(2,1)S(1)} %get-tuple-element.46.refs_0_, bf16[80,640]{1,0:T(8,128)(2,1)S(1)} %collective-permute-done.2.refs_1_, bf16[80,640]{1,0:T(8,128)(2,1)S(1)} %collective-permute-done.3.refs_2_, ...), custom_call_target="tpu_custom_call" | custom-call | flops 13107200 | tf_op jit(solution)/shard_map/pallas_call | solution.py:99
  14.7 1.1 %collective-permute-start.9 = (bf16[80,640]{1,0:T(8,128)(2,1)S(1)}, bf16[80,640]{1,0:T(8,128)(2,1)S(1)}, u32[]{:S(2)}, u32[]{:S(2)}) collective-permute-start(bf16[80,640]{1,0:T(8,128)(2,1)S(1)} %get-tuple-element.43), channel_id=1, source_target_pairs={{0,8},{4,12},{8,0},{12,4},{16,24},{20,28},{24,16},{28,20},{1,9},{5... | collective-permute-start | bytes 307208 | tf_op jit(solution)/shard_map/ppermute | solution.py:21
  15.8 0.9 %collective-permute-start.10 = (bf16[80,640]{1,0:T(8,128)(2,1)S(1)}, bf16[80,640]{1,0:T(8,128)(2,1)S(1)}, u32[]{:S(2)}, u32[]{:S(2)}) collective-permute-start(bf16[80,640]{1,0:T(8,128)(2,1)S(1)} %get-tuple-element.42), channel_id=1, source_target_pairs={{0,16},{4,20},{8,24},{12,28},{16,0},{20,4},{24,8},{28,12},{1,17},{... | collective-permute-start | bytes 307208 | tf_op jit(solution)/shard_map/ppermute | solution.py:21
  16.7 1.6 %collective-permute-start.11 = (bf16[80,640]{1,0:T(8,128)(2,1)S(1)}, bf16[80,640]{1,0:T(8,128)(2,1)S(1)}, u32[]{:S(2)}, u32[]{:S(2)}) collective-permute-start(bf16[80,640]{1,0:T(8,128)(2,1)S(1)} %get-tuple-element.41), channel_id=1, source_target_pairs={{0,24},{4,28},{8,16},{12,20},{16,8},{20,12},{24,0},{28,4},{1,25},{... | collective-permute-start | bytes 307208 | tf_op jit(solution)/shard_map/ppermute | solution.py:21
  18.3 1.6 %collective-permute-done.9.refs_1_ = bf16[80,640]{1,0:T(8,128)(2,1)S(1)} collective-permute-done((bf16[80,640]{1,0:T(8,128)(2,1)S(1)}, bf16[80,640]{1,0:T(8,128)(2,1)S(1)}, u32[]{:S(2)}, u32[]{:S(2)}) %collective-permute-start.9) | collective-permute-done | bytes 102432 | tf_op jit(solution)/shard_map/ppermute | solution.py:21
  19.8 1.5 %collective-permute-done.10.refs_2_ = bf16[80,640]{1,0:T(8,128)(2,1)S(1)} collective-permute-done((bf16[80,640]{1,0:T(8,128)(2,1)S(1)}, bf16[80,640]{1,0:T(8,128)(2,1)S(1)}, u32[]{:S(2)}, u32[]{:S(2)}) %collective-permute-start.10) | collective-permute-done | bytes 102432 | tf_op jit(solution)/shard_map/ppermute | solution.py:21
  21.4 1.6 %collective-permute-done.11.refs_3_ = bf16[80,640]{1,0:T(8,128)(2,1)S(1)} collective-permute-done((bf16[80,640]{1,0:T(8,128)(2,1)S(1)}, bf16[80,640]{1,0:T(8,128)(2,1)S(1)}, u32[]{:S(2)}, u32[]{:S(2)}) %collective-permute-start.11) | collective-permute-done | bytes 102432 | tf_op jit(solution)/shard_map/ppermute | solution.py:21
  24.0 5.9 %collective-permute-done.12.came_ref = bf16[160,640]{1,0:T(8,128)(2,1)S(1)} collective-permute-done((bf16[160,640]{1,0:T(8,128)(2,1)S(1)}, bf16[160,640]{1,0:T(8,128)(2,1)S(1)}, u32[]{:S(2)}, u32[]{:S(2)}) %collective-permute-start.12) | collective-permute-done | bytes 204832 | tf_op jit(solution)/shard_map/ppermute | solution.py:31
  30.7 0.9 %collective-permute-start.16 = (bf16[160,640]{1,0:T(8,128)(2,1)S(1)}, bf16[160,640]{1,0:T(8,128)(2,1)S(1)}, u32[]{:S(2)}, u32[]{:S(2)}) collective-permute-start(bf16[160,640]{1,0:T(8,128)(2,1)S(1)} %shard_map.50.re_ref), channel_id=1, source_target_pairs={{0,4},{1,2},{2,1},{3,7},{4,0},{5,6},{6,5},{7,3},{8,12},{9,10},{10,... | collective-permute-start | bytes 614408 | tf_op jit(solution)/shard_map/ppermute | solution.py:31
  31.6 4.1 %collective-permute-done.13.came_ref = bf16[160,640]{1,0:T(8,128)(2,1)S(1)} collective-permute-done((bf16[160,640]{1,0:T(8,128)(2,1)S(1)}, bf16[160,640]{1,0:T(8,128)(2,1)S(1)}, u32[]{:S(2)}, u32[]{:S(2)}) %collective-permute-start.13) | collective-permute-done | bytes 204832 | tf_op jit(solution)/shard_map/ppermute | solution.py:31
  36.0 0.9 %collective-permute-done.16.near_ref = bf16[160,640]{1,0:T(8,128)(2,1)S(1)} collective-permute-done((bf16[160,640]{1,0:T(8,128)(2,1)S(1)}, bf16[160,640]{1,0:T(8,128)(2,1)S(1)}, u32[]{:S(2)}, u32[]{:S(2)}) %collective-permute-start.16) | collective-permute-done | bytes 204832 | tf_op jit(solution)/shard_map/ppermute | solution.py:31
  37.3 4.3 %collective-permute-done.14.near_ref = bf16[160,640]{1,0:T(8,128)(2,1)S(1)} collective-permute-done((bf16[160,640]{1,0:T(8,128)(2,1)S(1)}, bf16[160,640]{1,0:T(8,128)(2,1)S(1)}, u32[]{:S(2)}, u32[]{:S(2)}) %collective-permute-start.14) | collective-permute-done | bytes 204832 | tf_op jit(solution)/shard_map/ppermute | solution.py:31
  41.5 3.3 %collective-permute-done.17.far_ref = bf16[160,640]{1,0:T(8,128)(2,1)S(1)} collective-permute-done((bf16[160,640]{1,0:T(8,128)(2,1)S(1)}, bf16[160,640]{1,0:T(8,128)(2,1)S(1)}, u32[]{:S(2)}, u32[]{:S(2)}) %collective-permute-start.17) | collective-permute-done | bytes 204832 | tf_op jit(solution)/shard_map/ppermute | solution.py:31
  44.8 1.2 %shard_map.51.early_ref = f32[640,320]{1,0:T(8,128)S(1)} custom-call(bf16[320,320]{1,0:T(8,128)(2,1)S(1)} %get-tuple-element.28.step_ref, bf16[320,320]{1,0:T(8,128)(2,1)S(1)} %get-tuple-element.29.turned_ref, bf16[640,320]{1,0:T(8,128)(2,1)S(1)} %get-tuple-element.30.stack_ref, bf16[160,640]{1,0:T(8,128)(2,1)S(1)} %shard_map.50.re_ref, ...), custom_call_target="tpu_custom_call" | custom-call | tf_op jit(solution)/shard_map/pallas_call | solution.py:36
  46.0 1.3 %collective-permute-done.15.far_ref = bf16[160,640]{1,0:T(8,128)(2,1)S(1)} collective-permute-done((bf16[160,640]{1,0:T(8,128)(2,1)S(1)}, bf16[160,640]{1,0:T(8,128)(2,1)S(1)}, u32[]{:S(2)}, u32[]{:S(2)}) %collective-permute-start.15) | collective-permute-done | bytes 204832 | tf_op jit(solution)/shard_map/ppermute | solution.py:31
  47.3 2.5 %shard_map.52 = bf16[320,640]{1,0:T(8,128)(2,1)} custom-call(bf16[320,320]{1,0:T(8,128)(2,1)S(1)} %get-tuple-element.28.step_ref, bf16[320,320]{1,0:T(8,128)(2,1)S(1)} %get-tuple-element.29.turned_ref, bf16[640,320]{1,0:T(8,128)(2,1)S(1)} %get-tuple-element.30.stack_ref, bf16[320,640]{1,0:T(8,128)(2,1)S(1)} %get-tuple-element.31.first_ref, ...), custom_call_target="tpu_custom_call" | custom-call | tf_op jit(solution)/shard_map/pallas_call | solution.py:258
  (29 shorter events, 3.7 us)
Async XLA Ops:
  0.0 12.0 %copy-start = (bf16[1,320,320]{2,1,0:T(8,128)(2,1)S(1)}, bf16[1,320,320]{2,1,0:T(8,128)(2,1)}, u32[]{:S(2)}) copy-start(bf16[1,320,320]{2,1,0:T(8,128)(2,1)} %param.7) | copy-start | bytes 614404
  0.0 12.0 %copy-start.1 = (bf16[1,1,320,640]{3,2,1,0:T(8,128)(2,1)S(1)}, bf16[1,1,320,640]{3,2,1,0:T(8,128)(2,1)}, u32[]{:S(2)}) copy-start(bf16[1,1,320,640]{3,2,1,0:T(8,128)(2,1)} %param.5) | copy-start | bytes 1228804
  0.0 13.0 %copy-start.2 = (bf16[8,1,40,640]{3,2,1,0:T(8,128)(2,1)S(1)}, bf16[8,1,40,640]{3,2,1,0:T(8,128)(2,1)}, u32[]{:S(2)}) copy-start(bf16[8,1,40,640]{3,2,1,0:T(8,128)(2,1)} %param.6) | copy-start | bytes 1228804
  0.0 13.0 %collective-permute-start = (bf16[8,40,640]{2,1,0:T(8,128)(2,1)}, bf16[8,40,640]{2,1,0:T(8,128)(2,1)S(1)}, u32[]{:S(2)}, u32[]{:S(2)}) collective-permute-start(bf16[8,40,640]{2,1,0:T(8,128)(2,1)} %bitcast.25), channel_id=1, source_target_pairs={{0,4},{4,0},{8,12},{12,8},{16,20},{20,16},{24,28},{28,24},{1,5},{5... | collective-permute-start | bytes 1228808 | tf_op jit(solution)/shard_map/ppermute | solution.py:21
  0.1 11.4 %collective-permute-start.1 = (bf16[320,320]{1,0:T(8,128)(2,1)}, bf16[320,320]{1,0:T(8,128)(2,1)S(1)}, u32[]{:S(2)}, u32[]{:S(2)}) collective-permute-start(bf16[320,320]{1,0:T(8,128)(2,1)} %bitcast.20), channel_id=1, source_target_pairs={{0,1},{1,0},{2,3},{3,2},{4,5},{5,4},{6,7},{7,6},{8,9},{9,8},{10,11... | collective-permute-start | bytes 614408 | tf_op jit(solution)/shard_map/ppermute | solution.py:31
  2.8 5.0 %collective-permute-start.2 = (bf16[80,640]{1,0:T(8,128)(2,1)S(1)}, bf16[80,640]{1,0:T(8,128)(2,1)S(1)}, u32[]{:S(2)}, u32[]{:S(2)}) collective-permute-start(bf16[80,640]{1,0:T(8,128)(2,1)S(1)} %get-tuple-element.45), channel_id=1, source_target_pairs={{0,8},{4,12},{8,0},{12,4},{16,24},{20,28},{24,16},{28,20},{1,9},{5... | collective-permute-start | bytes 307208 | tf_op jit(solution)/shard_map/ppermute | solution.py:21
  4.4 5.9 %collective-permute-start.3 = (bf16[80,640]{1,0:T(8,128)(2,1)S(1)}, bf16[80,640]{1,0:T(8,128)(2,1)S(1)}, u32[]{:S(2)}, u32[]{:S(2)}) collective-permute-start(bf16[80,640]{1,0:T(8,128)(2,1)S(1)} %get-tuple-element.47), channel_id=1, source_target_pairs={{0,16},{4,20},{8,24},{12,28},{16,0},{20,4},{24,8},{28,12},{1,17},{... | collective-permute-start | bytes 307208 | tf_op jit(solution)/shard_map/ppermute | solution.py:21
  5.9 5.6 %collective-permute-start.4 = (bf16[80,640]{1,0:T(8,128)(2,1)S(1)}, bf16[80,640]{1,0:T(8,128)(2,1)S(1)}, u32[]{:S(2)}, u32[]{:S(2)}) collective-permute-start(bf16[80,640]{1,0:T(8,128)(2,1)S(1)} %get-tuple-element.44), channel_id=1, source_target_pairs={{0,24},{4,28},{8,16},{12,20},{16,8},{20,12},{24,0},{28,4},{1,25},{... | collective-permute-start | bytes 307208 | tf_op jit(solution)/shard_map/ppermute | solution.py:21
  7.8 5.4 %collective-permute-start.5 = (bf16[80,640]{1,0:T(8,128)(2,1)S(1)}, bf16[80,640]{1,0:T(8,128)(2,1)S(1)}, u32[]{:S(2)}, u32[]{:S(2)}) collective-permute-start(bf16[80,640]{1,0:T(8,128)(2,1)S(1)} %get-tuple-element.46.refs_0_), channel_id=1, source_target_pairs={{0,4},{4,0},{8,12},{12,8},{16,20},{20,16},{24,28},{28,24},{1,5},{5... | collective-permute-start | bytes 307208 | tf_op jit(solution)/shard_map/ppermute | solution.py:21
  10.3 2.9 %collective-permute-start.6 = (bf16[80,640]{1,0:T(8,128)(2,1)S(1)}, bf16[80,640]{1,0:T(8,128)(2,1)S(1)}, u32[]{:S(2)}, u32[]{:S(2)}) collective-permute-start(bf16[80,640]{1,0:T(8,128)(2,1)S(1)} %collective-permute-done.2.refs_1_), channel_id=1, source_target_pairs={{0,4},{4,0},{8,12},{12,8},{16,20},{20,16},{24,28},{28,24},{1,5},{5... | collective-permute-start | bytes 307208 | tf_op jit(solution)/shard_map/ppermute | solution.py:21
  11.4 1.8 %collective-permute-start.7 = (bf16[80,640]{1,0:T(8,128)(2,1)S(1)}, bf16[80,640]{1,0:T(8,128)(2,1)S(1)}, u32[]{:S(2)}, u32[]{:S(2)}) collective-permute-start(bf16[80,640]{1,0:T(8,128)(2,1)S(1)} %collective-permute-done.3.refs_2_), channel_id=1, source_target_pairs={{0,4},{4,0},{8,12},{12,8},{16,20},{20,16},{24,28},{28,24},{1,5},{5... | collective-permute-start | bytes 307208 | tf_op jit(solution)/shard_map/ppermute | solution.py:21
  11.5 1.8 %collective-permute-start.8 = (bf16[80,640]{1,0:T(8,128)(2,1)S(1)}, bf16[80,640]{1,0:T(8,128)(2,1)S(1)}, u32[]{:S(2)}, u32[]{:S(2)}) collective-permute-start(bf16[80,640]{1,0:T(8,128)(2,1)S(1)} %collective-permute-done.4.refs_3_), channel_id=1, source_target_pairs={{0,4},{4,0},{8,12},{12,8},{16,20},{20,16},{24,28},{28,24},{1,5},{5... | collective-permute-start | bytes 307208 | tf_op jit(solution)/shard_map/ppermute | solution.py:21
  14.7 5.1 %collective-permute-start.9 = (bf16[80,640]{1,0:T(8,128)(2,1)S(1)}, bf16[80,640]{1,0:T(8,128)(2,1)S(1)}, u32[]{:S(2)}, u32[]{:S(2)}) collective-permute-start(bf16[80,640]{1,0:T(8,128)(2,1)S(1)} %get-tuple-element.43), channel_id=1, source_target_pairs={{0,8},{4,12},{8,0},{12,4},{16,24},{20,28},{24,16},{28,20},{1,9},{5... | collective-permute-start | bytes 307208 | tf_op jit(solution)/shard_map/ppermute | solution.py:21
  15.8 5.6 %collective-permute-start.10 = (bf16[80,640]{1,0:T(8,128)(2,1)S(1)}, bf16[80,640]{1,0:T(8,128)(2,1)S(1)}, u32[]{:S(2)}, u32[]{:S(2)}) collective-permute-start(bf16[80,640]{1,0:T(8,128)(2,1)S(1)} %get-tuple-element.42), channel_id=1, source_target_pairs={{0,16},{4,20},{8,24},{12,28},{16,0},{20,4},{24,8},{28,12},{1,17},{... | collective-permute-start | bytes 307208 | tf_op jit(solution)/shard_map/ppermute | solution.py:21
  16.7 6.3 %collective-permute-start.11 = (bf16[80,640]{1,0:T(8,128)(2,1)S(1)}, bf16[80,640]{1,0:T(8,128)(2,1)S(1)}, u32[]{:S(2)}, u32[]{:S(2)}) collective-permute-start(bf16[80,640]{1,0:T(8,128)(2,1)S(1)} %get-tuple-element.41), channel_id=1, source_target_pairs={{0,24},{4,28},{8,16},{12,20},{16,8},{20,12},{24,0},{28,4},{1,25},{... | collective-permute-start | bytes 307208 | tf_op jit(solution)/shard_map/ppermute | solution.py:21
  23.2 6.7 %collective-permute-start.12 = (bf16[160,640]{1,0:T(8,128)(2,1)S(1)}, bf16[160,640]{1,0:T(8,128)(2,1)S(1)}, u32[]{:S(2)}, u32[]{:S(2)}) collective-permute-start(bf16[160,640]{1,0:T(8,128)(2,1)S(1)} %get-tuple-element.36.own_ref), channel_id=1, source_target_pairs={{0,1},{1,0},{2,3},{3,2},{4,5},{5,4},{6,7},{7,6},{8,9},{9,8},{10,11... | collective-permute-start | bytes 614408 | tf_op jit(solution)/shard_map/ppermute | solution.py:31
  29.9 5.8 %collective-permute-start.13 = (bf16[160,640]{1,0:T(8,128)(2,1)S(1)}, bf16[160,640]{1,0:T(8,128)(2,1)S(1)}, u32[]{:S(2)}, u32[]{:S(2)}) collective-permute-start(bf16[160,640]{1,0:T(8,128)(2,1)S(1)} %get-tuple-element.37.own_ref), channel_id=1, source_target_pairs={{0,1},{1,0},{2,3},{3,2},{4,5},{5,4},{6,7},{7,6},{8,9},{9,8},{10,11... | collective-permute-start | bytes 614408 | tf_op jit(solution)/shard_map/ppermute | solution.py:31
  30.7 6.3 %collective-permute-start.16 = (bf16[160,640]{1,0:T(8,128)(2,1)S(1)}, bf16[160,640]{1,0:T(8,128)(2,1)S(1)}, u32[]{:S(2)}, u32[]{:S(2)}) collective-permute-start(bf16[160,640]{1,0:T(8,128)(2,1)S(1)} %shard_map.50.re_ref), channel_id=1, source_target_pairs={{0,4},{1,2},{2,1},{3,7},{4,0},{5,6},{6,5},{7,3},{8,12},{9,10},{10,... | collective-permute-start | bytes 614408 | tf_op jit(solution)/shard_map/ppermute | solution.py:31
  35.7 5.8 %collective-permute-start.14 = (bf16[160,640]{1,0:T(8,128)(2,1)S(1)}, bf16[160,640]{1,0:T(8,128)(2,1)S(1)}, u32[]{:S(2)}, u32[]{:S(2)}) collective-permute-start(bf16[160,640]{1,0:T(8,128)(2,1)S(1)} %shard_map.49.im_ref), channel_id=1, source_target_pairs={{0,4},{1,2},{2,1},{3,7},{4,0},{5,6},{6,5},{7,3},{8,12},{9,10},{10,... | collective-permute-start | bytes 614408 | tf_op jit(solution)/shard_map/ppermute | solution.py:31
  37.0 7.8 %collective-permute-start.17 = (bf16[160,640]{1,0:T(8,128)(2,1)S(1)}, bf16[160,640]{1,0:T(8,128)(2,1)S(1)}, u32[]{:S(2)}, u32[]{:S(2)}) collective-permute-start(bf16[160,640]{1,0:T(8,128)(2,1)S(1)} %collective-permute-done.16.near_ref), channel_id=1, source_target_pairs={{0,4},{1,5},{2,3},{3,2},{4,0},{5,1},{6,7},{7,6},{8,12},{9,13},{10,... | collective-permute-start | bytes 614408 | tf_op jit(solution)/shard_map/ppermute | solution.py:31
  41.5 5.8 %collective-permute-start.15 = (bf16[160,640]{1,0:T(8,128)(2,1)S(1)}, bf16[160,640]{1,0:T(8,128)(2,1)S(1)}, u32[]{:S(2)}, u32[]{:S(2)}) collective-permute-start(bf16[160,640]{1,0:T(8,128)(2,1)S(1)} %collective-permute-done.14.near_ref), channel_id=1, source_target_pairs={{0,4},{1,5},{2,3},{3,2},{4,0},{5,1},{6,7},{7,6},{8,12},{9,13},{10,... | collective-permute-start | bytes 614408 | tf_op jit(solution)/shard_map/ppermute | solution.py:31

commit v4 on v3

--- a/solution.py
+++ b/solution.py
@@ -128,13 +128,13 @@
 def gather_kernel(*refs):
     chip = lax.axis_index(ENERGY) // 2
     first_ref, *others, re_ref, im_ref, all_ref = refs
+    all_ref[chip] = first_ref[0]
+    for j, ref in enumerate(others):
+        all_ref[chip ^ (j + 1)] = ref[...]
     chips, rows, width = all_ref.shape
-    half = width // 2
-    for j, piece in enumerate([first_ref[0], *(ref[...] for ref in others)]):
-        all_ref[chip ^ j] = piece
     whole = all_ref[...].reshape(chips * rows, width)
-    re_ref[...] = packed(whole[:, :half])
-    im_ref[...] = packed(whole[:, half:])
+    re_ref[...] = packed(whole[:, : width // 2])
+    im_ref[...] = packed(whole[:, width // 2 :])
 
 
 def gathered(own, pieces):
@@ -143,60 +143,131 @@
     return call(gather_kernel, [part, part], [own, *pieces], [pltpu.VMEM(own.shape, own.dtype)])
 
 
-def prepare_kernel(link_ref, before_ref, green_ref, turned_ref, step_ref, turned_step_ref, stack_ref, first_ref, second_ref):
-    odd = lax.axis_index(SLAB) % 2
+def adjoint(stack, sign):
+    size = stack.shape[1]
+    re, im = stack[:size], stack[size:]
+    return jnp.concatenate([re, -im] if sign > 0 else [im, re], axis=0).T
+
+
+def prepare_kernel(pair, link_ref, before_ref, green_ref, turned_ref, step_ref, turned_step_ref, *refs):
+    stack_ref, first_ref, second_ref, far_stack_ref, far_first_ref, far_second_ref, half_a_ref, half_b_ref = refs
+    slab = lax.axis_index(SLAB)
     turned_ref[...] = link_ref[...].T
 
-    @pl.when(odd == 0)
+    @pl.when(slab % 2 == 0)
     def _():
         step_ref[...] = link_ref[...]
 
-    @pl.when(odd == 1)
+    @pl.when(slab % 2 == 1)
     def _():
         step_ref[...] = dot(link_ref[...], before_ref[...]).astype(jnp.bfloat16)
 
     turned_step_ref[...] = step_ref[...].T
     size = green_ref.shape[0]
-    re, im = green_ref[:, :size], green_ref[:, size:]
-    stack_ref[:size] = re
-    stack_ref[size:] = im
-    first_ref[...] = jnp.concatenate([re, -im], axis=0).T
-    second_ref[...] = jnp.concatenate([im, re], axis=0).T
-
-
-def carry_in(turn, link_ref, turned_ref, state_ref, came, out_ref):
+    stack_ref[:size] = green_ref[:, :size]
+    stack_ref[size:] = green_ref[:, size:]
+    first_ref[...] = adjoint(stack_ref[...], 1)
+    second_ref[...] = adjoint(stack_ref[...], -1)
+
+    @pl.when(slab // 2 == pair)
+    def _():
+        far_stack_ref[...] = dot(stack_ref[...], step_ref[...]).astype(jnp.bfloat16)
+        far_first_ref[...] = adjoint(far_stack_ref[...], 1)
+        far_second_ref[...] = adjoint(far_stack_ref[...], -1)
+        quarter = size // 4
+        columns = [far_stack_ref[:, i * quarter : (i + 1) * quarter] for i in range(4)]
+        half_a_ref[...] = jnp.concatenate([columns[0], columns[2]], axis=1)
+        half_b_ref[...] = jnp.concatenate([columns[1], columns[3]], axis=1)
+
+
+def joined(refs):
+    return jnp.concatenate([ref[...] for ref in refs], axis=0)
+
+
+def carry_in(turn, link_ref, turned_ref, state, came, out_refs):
+    rows = out_refs[0].shape[0]
+
     @pl.when(turn)
     def _():
-        state = unpacked(state_ref[...]).astype(jnp.float32)
-        out_ref[...] = packed((state + moved(link_ref, turned_ref, unpacked(came))).astype(jnp.bfloat16))
+        out = (unpacked(state).astype(jnp.float32) + moved(link_ref, turned_ref, unpacked(came))).astype(jnp.bfloat16)
+        out = packed(out)
+        for i, ref in enumerate(out_refs):
+            ref[...] = out[i * rows : (i + 1) * rows]
 
     @pl.when(jnp.logical_not(turn))
     def _():
-        out_ref[...] = state_ref[...]
-
-
-def first_kernel(link_ref, turned_ref, own_ref, came_ref, out_ref):
-    carry_in(lax.axis_index(SLAB) % 2 == 1, link_ref, turned_ref, own_ref, came_ref[...], out_ref)
-
-
-def advance_kernel(pair, step_ref, turned_ref, state_ref, near_ref, far_ref, out_ref):
-    slab = lax.axis_index(SLAB)
-    came = jnp.where(slab % 2 == 0, near_ref[...], far_ref[...])
-    carry_in(slab // 2 == pair, step_ref, turned_ref, state_ref, came, out_ref)
-
-
-def early_kernel(pair, step_ref, turned_ref, stack_ref, re_ref, near_ref, far_ref, out_ref, x_ref):
-    advance_kernel(pair, step_ref, turned_ref, re_ref, near_ref, far_ref, x_ref)
-    out_ref[...] = dot(stack_ref[...], unpacked(x_ref[...]))
-
-
-def late_kernel(pair, step_ref, turned_ref, stack_ref, first_ref, second_ref, im_ref, near_ref, far_ref, early_ref, out_ref, x_ref):
-    advance_kernel(pair, step_ref, turned_ref, im_ref, near_ref, far_ref, x_ref)
-    late = dot(stack_ref[...], unpacked(x_ref[...]))
-    size = x_ref.shape[1] // 2
-    left_re = (early_ref[:size] - late[size:]).astype(jnp.bfloat16)
-    left_im = (late[:size] + early_ref[size:]).astype(jnp.bfloat16)
-    out_ref[...] = (dot(left_re, first_ref[...]) + dot(left_im, second_ref[...])).astype(jnp.bfloat16)
+        for i, ref in enumerate(out_refs):
+            ref[...] = state[i * rows : (i + 1) * rows]
+
+
+def first_kernel(link_ref, turned_ref, own_ref, came_ref, *out_refs):
+    carry_in(lax.axis_index(SLAB) % 2 == 1, link_ref, turned_ref, own_ref[...], came_ref[...], out_refs)
+
+
+def arrived(refs):
+    near, far = refs[: len(refs) // 2], refs[len(refs) // 2 :]
+    return jnp.where(lax.axis_index(SLAB) % 2 == 0, joined(near), joined(far))
+
+
+def advance_kernel(pair, link_ref, turned_ref, *refs):
+    parts = len(refs) // 4
+    state, came, outs = refs[:parts], refs[parts : 3 * parts], refs[3 * parts :]
+    carry_in(lax.axis_index(SLAB) // 2 == pair, link_ref, turned_ref, joined(state), arrived(came), outs)
+
+
+def base_kernel(stack_ref, first_ref, second_ref, re_ref, *refs):
+    *im_refs, out_ref = refs
+    re = dot(stack_ref[...], unpacked(re_ref[...]))
+    im = dot(stack_ref[...], unpacked(joined(im_refs)))
+    size = re.shape[1]
+    left_re = (re[:size] - im[size:]).astype(jnp.bfloat16)
+    left_im = (im[:size] + re[size:]).astype(jnp.bfloat16)
+    out_ref[...] = dot(left_re, first_ref[...]) + dot(left_im, second_ref[...])
+
+
+def early_kernel(pair, far_stack_ref, far_first_ref, far_second_ref, half_ref, base_ref, *refs):
+    *came, out_ref, left_ref = refs
+    turn = lax.axis_index(SLAB) // 2 == pair
+
+    @pl.when(turn)
+    def _():
+        left = dot(far_stack_ref[...], unpacked(arrived(came[::2]))).astype(jnp.bfloat16)
+        size = left.shape[1]
+        out_ref[...] = base_ref[...] + dot(left[:size], far_first_ref[...]) + dot(left[size:], far_second_ref[...])
+        left_ref[...] = dot(half_ref[...], unpacked(arrived(came[1::2])))
+
+    @pl.when(jnp.logical_not(turn))
+    def _():
+        out_ref[...] = base_ref[...]
+
+
+def late_kernel(pair, far_first_ref, far_second_ref, half_ref, early_ref, early_left_ref, *refs):
+    *came, out_ref, left_ref, result_ref, sems = refs
+    size, width = result_ref.shape
+    turn = lax.axis_index(SLAB) // 2 == pair
+    cut = width // 256 * 128 if width % 128 == 0 else width // 2
+
+    @pl.when(turn)
+    def _():
+        left_ref[...] = (early_left_ref[...] + dot(half_ref[...], unpacked(arrived(came)))).astype(jnp.bfloat16)
+
+    copies = []
+    for n, block in enumerate((slice(0, cut), slice(cut, width))):
+
+        @pl.when(turn)
+        def _():
+            late = dot(left_ref[:size], far_second_ref[:, block]) - dot(left_ref[size:], far_first_ref[:, block])
+            result_ref[:, block] = (early_ref[:, block] + late).astype(jnp.bfloat16)
+
+        @pl.when(jnp.logical_not(turn))
+        def _():
+            result_ref[:, block] = early_ref[:, block].astype(jnp.bfloat16)
+
+        copy = pltpu.make_async_copy(result_ref.at[:, block], out_ref.at[:, block], sems.at[n])
+        copy.start()
+        copies.append(copy)
+    for copy in copies:
+        copy.wait()
 
 
 def local(g_lesser, g_retarded, screened, coupling):
@@ -215,52 +286,63 @@
     second = jnp.where(side == 0, inter_other, inter)
     inter_rows = jnp.concatenate([first, second], axis=1)
 
+    mine = [lax.dynamic_slice(lesser, (rows * (chip ^ j), 0), (rows, width)) for j in range(chips)]
+    pieces = [mine[0]] + [swap_with(mine[j], 2 * j) for j in range(1, chips)]
+
     link = coupling[0]
     other_in_pair = {s: s ^ 1 for s in range(slabs)}
     link_before = swap_slabs(link, other_in_pair)
+
+    pieces = pieces + [swap_with(x, 1) for x in pieces]
+    sigma = convolve(chips, inter_rows, pieces)
+    sigma, link_before = lax.optimization_barrier((sigma, link_before))
+    own_re, own_im = gathered(sigma, [swap_with(sigma[j], 2 * j) for j in range(1, chips)])
+
+    own_re, own_im, link_before = lax.optimization_barrier((own_re, own_im, link_before))
     square = (link.shape, jnp.bfloat16)
     tall, wide = ((2 * size, size), jnp.bfloat16), ((size, 2 * size), jnp.bfloat16)
-    prepared = call(prepare_kernel, [square, square, square, tall, wide, wide], [link, link_before, g_retarded[0, 0]])
-
-    mine = [lax.dynamic_slice(lesser, (rows * (chip ^ j), 0), (rows, width)) for j in range(chips)]
-    pieces = [mine[0]] + [swap_with(mine[j], 2 * j) for j in range(1, chips)]
-    pieces = pieces + [swap_with(x, 1) for x in pieces]
-    inter_rows, prepared = lax.optimization_barrier((inter_rows, prepared))
-    turned, step, turned_step, stack, adjoint_first, adjoint_second = prepared
-    sigma = convolve(chips, inter_rows, pieces)
-
-    own_re, own_im = gathered(sigma, [swap_with(sigma[j], 2 * j) for j in range(1, chips)])
+    thin = ((2 * size, size // 2), jnp.bfloat16)
+    last_pair = slabs // 2 - 1
+    prepared = call(
+        functools.partial(prepare_kernel, last_pair),
+        [square, square, square, tall, wide, wide, tall, wide, wide, thin, thin],
+        [link, link_before, g_retarded[0, 0]],
+    )
+    turned, step, turned_step, *base, far_stack, far_first, far_second, half_a, half_b = prepared
+    came_re = swap_slabs(own_re, other_in_pair)
+    came_im = swap_slabs(own_im, other_in_pair)
     part = (own_re.shape, own_re.dtype)
-    came_re = swap_slabs(own_re, other_in_pair)
-    own_im, came_re = lax.optimization_barrier((own_im, came_re))
-    came_im = swap_slabs(own_im, other_in_pair)
-    (re,) = call(first_kernel, [part], [link, turned, own_re, came_re])
-    (im,) = call(first_kernel, [part], [link, turned, own_im, came_im])
+    halves = [((size // 4, width), own_im.dtype)] * 2
+    total = [((size, width), jnp.float32)]
+    re = call(first_kernel, [part], [link, turned, own_re, came_re])
+    im = call(first_kernel, halves, [link, turned, own_im, came_im])
 
     for s in range(1, slabs - 1, 2):
         pair = (s + 1) // 2
-        near_re = swap_slabs(re, {s: s + 1, s + 1: s})
-        near_im = swap_slabs(im, {s: s + 1, s + 1: s})
-        far_re = swap_slabs(near_re, {s + 1: s + 2, s + 2: s + 1})
-        far_im = swap_slabs(near_im, {s + 1: s + 2, s + 2: s + 1})
-        if s + 3 < slabs:
+        near, far = {s: s + 1, s + 1: s}, {s + 1: s + 2, s + 2: s + 1}
+        near_re = [swap_slabs(x, near) for x in re]
+        near_im = [swap_slabs(x, near) for x in im]
+        far_re = [swap_slabs(x, far) for x in near_re]
+        far_im = [swap_slabs(x, far) for x in near_im]
+        if pair < last_pair:
             advance = functools.partial(advance_kernel, pair)
-            (re,) = call(advance, [part], [step, turned_step, re, near_re, far_re])
-            (im,) = call(advance, [part], [step, turned_step, im, near_im, far_im])
-    scratch = pltpu.VMEM(re.shape, jnp.bfloat16)
-    (early,) = call(
-        functools.partial(early_kernel, pair),
-        [((2 * size, size), jnp.float32)],
-        [step, turned_step, stack, re, near_re, far_re],
-        [scratch],
-    )
-    given = [step, turned_step, stack, adjoint_first, adjoint_second, im, near_im, far_im, early]
+            re = call(advance, [part], [step, turned_step, *re, *near_re, *far_re])
+            im = call(advance, halves, [step, turned_step, *im, *near_im, *far_im])
+    (out,) = call(base_kernel, total, [*base, *re, *im])
+    early = [far_stack, far_first, far_second, half_a, out, near_re[0], near_im[0], far_re[0], far_im[0]]
+    left = ((2 * size, size), jnp.float32)
+    out, left = call(functools.partial(early_kernel, last_pair), [*total, left], early)
+    given = [far_first, far_second, half_b, out, left, near_im[1], far_im[1]]
     out = pl.pallas_call(
-        functools.partial(late_kernel, pair),
+        functools.partial(late_kernel, last_pair),
         out_shape=jax.ShapeDtypeStruct((size, width), jnp.bfloat16),
         in_specs=[WHOLE] * len(given),
-        out_specs=WHOLE,
-        scratch_shapes=[scratch],
+        out_specs=pl.BlockSpec(memory_space=pl.ANY),
+        scratch_shapes=[
+            pltpu.VMEM((2 * size, size), jnp.bfloat16),
+            pltpu.VMEM((size, width), jnp.bfloat16),
+            pltpu.SemaphoreType.DMA((2,)),
+        ],
         compiler_params=pltpu.CompilerParams(vmem_limit_bytes=10 << 20),
     )(*in_vmem(*given))
     return out[None, None]

time: 50.1 us -> 47.8 us (0.954)
  waiting for transfers between devices: 29.6 us -> 21.9 us
  starting transfers between devices: 12.4 us -> 15.7 us
  Pallas kernels: 6.42 us -> 8.6 us
    ppermute x7 -> x9, waiting for transfers between devices: 19.7 us -> 12.5 us  [swap_slabs(): return lax.ppermute(array, (ENERGY, SLAB), pairs)]
    ppermute x7 -> x9, starting transfers between devices: 4.69 us -> 8.07 us  [swap_slabs(): return lax.ppermute(array, (ENERGY, SLAB), pairs)]
    pallas_call x5 -> x6, Pallas kernels: 2.5 us -> 5.37 us  [call(): pl.pallas_call(kernel, out_shape=outs, in_specs=[WHOLE] * len(given), out...]
    pallas_call x1, Pallas kernels: 2.49 us -> 1.81 us  [local(): pl.pallas_call(functools.partial(late_kernel, last_pair), out_shape=jax.S...]
  transfers between devices with their start and end apart: 18 -> 20, of which waited for: 12 -> 14; matrix products, arithmetic and copies ran while one was open for 2% -> 3% of each run, Pallas kernels for 5% -> 14%
where the time goes in v4:
time: 47.8 us; the launch traced here: 47.7 us
  waiting for transfers between devices  21.9 us (46%)
  starting transfers between devices  15.7 us (33%)
  Pallas kernels  8.6 us (18%)
  local copies, waits for them, and re-layouts  1.18 us (2%)
    ppermute x9, waiting for transfers between devices, swap_slabs(): return lax.ppermute(array, (ENERGY, SLAB), pairs)  12.5 us
    ppermute x11, waiting for transfers between devices, swap_with(): return lax.ppermute(array, ENERGY, [(i, i ^ mask) for i in range(devices)])  9.42 us
    ppermute x9, starting transfers between devices, swap_slabs(): return lax.ppermute(array, (ENERGY, SLAB), pairs)  8.07 us
    ppermute x11, starting transfers between devices, swap_with(): return lax.ppermute(array, ENERGY, [(i, i ^ mask) for i in range(devices)])  7.62 us
    pallas_call x6, Pallas kernels, call(): pl.pallas_call(kernel, out_shape=outs, in_specs=[WHOLE] * len(given), out...  5.37 us
    pallas_call x1, Pallas kernels, local(): pl.pallas_call(functools.partial(late_kernel, last_pair), out_shape=jax.S...  1.81 us
    pallas_call x1, Pallas kernels, convolve(): pl.pallas_call(functools.partial(conv_kernel, chips), out_shape=pltpu.VME...  1.42 us
    dynamic_slice x1, local copies, waits for them, and re-layouts, local(): lax.dynamic_slice(lesser, (rows * (chip ^ j), 0), (rows, width))  1.13 us
  transfers between devices with their start and end apart: 20, of which 14 were waited for; matrix products, arithmetic and copies ran while one was open for 3% of the time, Pallas kernels for 14%

profile of v4, /device:TPU:16, one launch (start us, length us, event | category | flops | bytes accessed | tf_op | source)
XLA Modules:
  0.0 47.7 jit_solution(16613268021022853077)
XLA Ops:
  0.0 1.1 %dynamic-slice_bitcast_fusion = (bf16[80,640]{1,0:T(8,128)(2,1)S(1)}, bf16[80,640]{1,0:T(8,128)(2,1)S(1)}, bf16[80,640]{1,0:T(8,128)(2,1)S(1)}, bf16[80,640]{1,0:T(8,128)(2,1)S(1)}) fusion(bf16[1,1,320,640]{3,2,1,0:T(8,128)(2,1)} %param.4, s32[]{:T(128)S(6)} %select_n.43, s32[]{:T(128)S(6)} %select_n.41, s32[]{:T(128)S(6)} %select_n.40, s32[]{:T(128)S(6)} %select_n.42), kind=kLoop, calls=%fused_computation.6 | loop fusion | bytes 819216 | tf_op jit(solution)/shard_map/dynamic_slice | solution.py:289
  1.1 1.6 %collective-permute-start.1 = (bf16[80,640]{1,0:T(8,128)(2,1)S(1)}, bf16[80,640]{1,0:T(8,128)(2,1)S(1)}, u32[]{:S(2)}, u32[]{:S(2)}) collective-permute-start(bf16[80,640]{1,0:T(8,128)(2,1)S(1)} %get-tuple-element.51), channel_id=1, source_target_pairs={{0,8},{4,12},{8,0},{12,4},{16,24},{20,28},{24,16},{28,20},{1,9},{5... | collective-permute-start | bytes 307208 | tf_op jit(solution)/shard_map/ppermute | solution.py:21
  2.7 1.5 %collective-permute-start.2 = (bf16[80,640]{1,0:T(8,128)(2,1)S(1)}, bf16[80,640]{1,0:T(8,128)(2,1)S(1)}, u32[]{:S(2)}, u32[]{:S(2)}) collective-permute-start(bf16[80,640]{1,0:T(8,128)(2,1)S(1)} %get-tuple-element.53), channel_id=1, source_target_pairs={{0,16},{4,20},{8,24},{12,28},{16,0},{20,4},{24,8},{28,12},{1,17},{... | collective-permute-start | bytes 307208 | tf_op jit(solution)/shard_map/ppermute | solution.py:21
  4.7 1.7 %collective-permute-done.1.refs_1_ = bf16[80,640]{1,0:T(8,128)(2,1)S(1)} collective-permute-done((bf16[80,640]{1,0:T(8,128)(2,1)S(1)}, bf16[80,640]{1,0:T(8,128)(2,1)S(1)}, u32[]{:S(2)}, u32[]{:S(2)}) %collective-permute-start.1) | collective-permute-done | bytes 102432 | tf_op jit(solution)/shard_map/ppermute | solution.py:21
  6.4 1.6 %collective-permute-start.8 = (bf16[320,320]{1,0:T(8,128)(2,1)}, bf16[320,320]{1,0:T(8,128)(2,1)S(1)}, u32[]{:S(2)}, u32[]{:S(2)}) collective-permute-start(bf16[320,320]{1,0:T(8,128)(2,1)} %bitcast.20), channel_id=1, source_target_pairs={{0,1},{1,0},{2,3},{3,2},{4,5},{5,4},{6,7},{7,6},{8,9},{9,8},{10,11... | collective-permute-start | bytes 614408 | tf_op jit(solution)/shard_map/ppermute | solution.py:31
  11.3 1.4 %shard_map.46.refs_0_ = bf16[4,80,640]{2,1,0:T(8,128)(2,1)S(1)} custom-call(bf16[8,80,640]{2,1,0:T(8,128)(2,1)S(1)} %pad_maximum_fusion.inter_ref, bf16[80,640]{1,0:T(8,128)(2,1)S(1)} %get-tuple-element.52.refs_0_, bf16[80,640]{1,0:T(8,128)(2,1)S(1)} %collective-permute-done.1.refs_1_, bf16[80,640]{1,0:T(8,128)(2,1)S(1)} %collective-permute-done.2.refs_2_, ...), custom_call_target="tpu_custom_call" | custom-call | flops 13107200 | tf_op jit(solution)/shard_map/pallas_call | solution.py:99
  12.8 1.4 %collective-permute-done.8.before_ref = bf16[320,320]{1,0:T(8,128)(2,1)S(1)} collective-permute-done((bf16[320,320]{1,0:T(8,128)(2,1)}, bf16[320,320]{1,0:T(8,128)(2,1)S(1)}, u32[]{:S(2)}, u32[]{:S(2)}) %collective-permute-start.8) | collective-permute-done | bytes 204832 | tf_op jit(solution)/shard_map/ppermute | solution.py:31
  14.2 1.6 %collective-permute-start.9 = (bf16[80,640]{1,0:T(8,128)(2,1)S(1)}, bf16[80,640]{1,0:T(8,128)(2,1)S(1)}, u32[]{:S(2)}, u32[]{:S(2)}) collective-permute-start(bf16[80,640]{1,0:T(8,128)(2,1)S(1)} %get-tuple-element.49), channel_id=1, source_target_pairs={{0,8},{4,12},{8,0},{12,4},{16,24},{20,28},{24,16},{28,20},{1,9},{5... | collective-permute-start | bytes 307208 | tf_op jit(solution)/shard_map/ppermute | solution.py:21
  15.8 1.5 %collective-permute-start.10 = (bf16[80,640]{1,0:T(8,128)(2,1)S(1)}, bf16[80,640]{1,0:T(8,128)(2,1)S(1)}, u32[]{:S(2)}, u32[]{:S(2)}) collective-permute-start(bf16[80,640]{1,0:T(8,128)(2,1)S(1)} %get-tuple-element.48), channel_id=1, source_target_pairs={{0,16},{4,20},{8,24},{12,28},{16,0},{20,4},{24,8},{28,12},{1,17},{... | collective-permute-start | bytes 307208 | tf_op jit(solution)/shard_map/ppermute | solution.py:21
  17.8 2.2 %collective-permute-done.9.refs_1_ = bf16[80,640]{1,0:T(8,128)(2,1)S(1)} collective-permute-done((bf16[80,640]{1,0:T(8,128)(2,1)S(1)}, bf16[80,640]{1,0:T(8,128)(2,1)S(1)}, u32[]{:S(2)}, u32[]{:S(2)}) %collective-permute-start.9) | collective-permute-done | bytes 102432 | tf_op jit(solution)/shard_map/ppermute | solution.py:21
  19.9 1.0 %collective-permute-done.10.refs_2_ = bf16[80,640]{1,0:T(8,128)(2,1)S(1)} collective-permute-done((bf16[80,640]{1,0:T(8,128)(2,1)S(1)}, bf16[80,640]{1,0:T(8,128)(2,1)S(1)}, u32[]{:S(2)}, u32[]{:S(2)}) %collective-permute-start.10) | collective-permute-done | bytes 102432 | tf_op jit(solution)/shard_map/ppermute | solution.py:21
  21.0 1.9 %collective-permute-done.11.refs_3_ = bf16[80,640]{1,0:T(8,128)(2,1)S(1)} collective-permute-done((bf16[80,640]{1,0:T(8,128)(2,1)S(1)}, bf16[80,640]{1,0:T(8,128)(2,1)S(1)}, u32[]{:S(2)}, u32[]{:S(2)}) %collective-permute-start.11) | collective-permute-done | bytes 102432 | tf_op jit(solution)/shard_map/ppermute | solution.py:21
  23.0 1.6 %collective-permute-start.12 = (bf16[160,640]{1,0:T(8,128)(2,1)S(1)}, bf16[160,640]{1,0:T(8,128)(2,1)S(1)}, u32[]{:S(2)}, u32[]{:S(2)}) collective-permute-start(bf16[160,640]{1,0:T(8,128)(2,1)S(1)} %get-tuple-element.39.own_ref), channel_id=1, source_target_pairs={{0,1},{1,0},{2,3},{3,2},{4,5},{5,4},{6,7},{7,6},{8,9},{9,8},{10,11... | collective-permute-start | bytes 614408 | tf_op jit(solution)/shard_map/ppermute | solution.py:31
  25.1 2.5 %shard_map.48 = (bf16[320,320]{1,0:T(8,128)(2,1)S(1)}, bf16[320,320]{1,0:T(8,128)(2,1)}, bf16[320,320]{1,0:T(8,128)(2,1)}, bf16[640,320]{1,0:T(8,128)(2,1)S(1)},...) custom-call(bf16[320,320]{1,0:T(8,128)(2,1)S(1)} %bitcast.21, ...), custom_call_target="tpu_custom_call" | custom-call | tf_op jit(solution)/shard_map/pallas_call | solution.py:36
  27.6 2.1 %collective-permute-done.12.came_ref = bf16[160,640]{1,0:T(8,128)(2,1)S(1)} collective-permute-done((bf16[160,640]{1,0:T(8,128)(2,1)S(1)}, bf16[160,640]{1,0:T(8,128)(2,1)S(1)}, u32[]{:S(2)}, u32[]{:S(2)}) %collective-permute-start.12) | collective-permute-done | bytes 204832 | tf_op jit(solution)/shard_map/ppermute | solution.py:31
  29.7 1.2 %collective-permute-start.14 = (bf16[160,640]{1,0:T(8,128)(2,1)S(1)}, bf16[160,640]{1,0:T(8,128)(2,1)S(1)}, u32[]{:S(2)}, u32[]{:S(2)}) collective-permute-start(bf16[160,640]{1,0:T(8,128)(2,1)S(1)} %shard_map.49.re_ref), channel_id=1, source_target_pairs={{0,4},{1,2},{2,1},{3,7},{4,0},{5,6},{6,5},{7,3},{8,12},{9,10},{10,... | collective-permute-start | bytes 614408 | tf_op jit(solution)/shard_map/ppermute | solution.py:31
  31.9 1.2 %collective-permute-start.15 = (bf16[80,640]{1,0:T(8,128)(2,1)S(1)}, bf16[80,640]{1,0:T(8,128)(2,1)S(1)}, u32[]{:S(2)}, u32[]{:S(2)}) collective-permute-start(bf16[80,640]{1,0:T(8,128)(2,1)S(1)} %get-tuple-element.41.refs_0_), channel_id=1, source_target_pairs={{0,4},{1,2},{2,1},{3,7},{4,0},{5,6},{6,5},{7,3},{8,12},{9,10},{10,... | collective-permute-start | bytes 307208 | tf_op jit(solution)/shard_map/ppermute | solution.py:31
  33.1 2.4 %collective-permute-done.14.refs_0_ = bf16[160,640]{1,0:T(8,128)(2,1)S(1)} collective-permute-done((bf16[160,640]{1,0:T(8,128)(2,1)S(1)}, bf16[160,640]{1,0:T(8,128)(2,1)S(1)}, u32[]{:S(2)}, u32[]{:S(2)}) %collective-permute-start.14) | collective-permute-done | bytes 204832 | tf_op jit(solution)/shard_map/ppermute | solution.py:31
  35.6 1.1 %collective-permute-start.18 = (bf16[80,640]{1,0:T(8,128)(2,1)S(1)}, bf16[80,640]{1,0:T(8,128)(2,1)S(1)}, u32[]{:S(2)}, u32[]{:S(2)}) collective-permute-start(bf16[80,640]{1,0:T(8,128)(2,1)S(1)} %get-tuple-element.42.refs_1_), channel_id=1, source_target_pairs={{0,4},{1,2},{2,1},{3,7},{4,0},{5,6},{6,5},{7,3},{8,12},{9,10},{10,... | collective-permute-start | bytes 307208 | tf_op jit(solution)/shard_map/ppermute | solution.py:31
  37.6 2.6 %collective-permute-done.18.refs_0_ = bf16[80,640]{1,0:T(8,128)(2,1)S(1)} collective-permute-done((bf16[80,640]{1,0:T(8,128)(2,1)S(1)}, bf16[80,640]{1,0:T(8,128)(2,1)S(1)}, u32[]{:S(2)}, u32[]{:S(2)}) %collective-permute-start.18) | collective-permute-done | bytes 102432 | tf_op jit(solution)/shard_map/ppermute | solution.py:31
  40.3 1.4 %shard_map.51.base_ref = f32[320,640]{1,0:T(8,128)S(1)} custom-call(bf16[640,320]{1,0:T(8,128)(2,1)S(1)} %get-tuple-element.35.stack_ref, bf16[320,640]{1,0:T(8,128)(2,1)S(1)} %get-tuple-element.36.first_ref, bf16[320,640]{1,0:T(8,128)(2,1)S(1)} %get-tuple-element.37.second_ref, bf16[160,640]{1,0:T(8,128)(2,1)S(1)} %shard_map.49.re_ref, ...), custom_call_target="tpu_custom_call" | custom-call | tf_op jit(solution)/shard_map/pallas_call | solution.py:36
  41.7 3.0 %collective-permute-done.17.refs_3_ = bf16[80,640]{1,0:T(8,128)(2,1)S(1)} collective-permute-done((bf16[80,640]{1,0:T(8,128)(2,1)S(1)}, bf16[80,640]{1,0:T(8,128)(2,1)S(1)}, u32[]{:S(2)}, u32[]{:S(2)}) %collective-permute-start.17) | collective-permute-done | bytes 102432 | tf_op jit(solution)/shard_map/ppermute | solution.py:31
  44.6 1.2 %shard_map.52 = (f32[320,640]{1,0:T(8,128)S(1)}, f32[640,320]{1,0:T(8,128)S(1)}) custom-call(bf16[640,320]{1,0:T(8,128)(2,1)S(1)} %get-tuple-element.33.far_stack_ref, bf16[320,640]{1,0:T(8,128)(2,1)S(1)} %get-tuple-element.30.far_first_ref, bf16[320,640]{1,0:T(8,128)(2,1)S(1)} %get-tuple-element.31.far_second_ref, ...), custom_call_target="tpu_custom_call" | custom-call | tf_op jit(solution)/shard_map/pallas_call | solution.py:36
  45.8 1.8 %shard_map.53 = bf16[320,640]{1,0:T(8,128)(2,1)} custom-call(bf16[320,640]{1,0:T(8,128)(2,1)S(1)} %get-tuple-element.30.far_first_ref, bf16[320,640]{1,0:T(8,128)(2,1)S(1)} %get-tuple-element.31.far_second_ref, bf16[640,160]{1,0:T(8,128)(2,1)S(1)} %get-tuple-element.32.half_ref, f32[320,640]{1,0:T(8,128)S(1)} %get-tuple-element.43.early_ref, ...), custom_call_target="tpu_custom_call" | custom-call | tf_op jit(solution)/shard_map/pallas_call | solution.py:336
  (34 shorter events, 6.9 us)
Async XLA Ops:
  0.0 10.4 %copy-start.2 = (bf16[8,1,40,640]{3,2,1,0:T(8,128)(2,1)S(1)}, bf16[8,1,40,640]{3,2,1,0:T(8,128)(2,1)}, u32[]{:S(2)}) copy-start(bf16[8,1,40,640]{3,2,1,0:T(8,128)(2,1)} %param.6) | copy-start | bytes 1228804
  0.0 9.9 %collective-permute-start = (bf16[8,40,640]{2,1,0:T(8,128)(2,1)}, bf16[8,40,640]{2,1,0:T(8,128)(2,1)S(1)}, u32[]{:S(2)}, u32[]{:S(2)}) collective-permute-start(bf16[8,40,640]{2,1,0:T(8,128)(2,1)} %bitcast.25), channel_id=1, source_target_pairs={{0,4},{4,0},{8,12},{12,8},{16,20},{20,16},{24,28},{28,24},{1,5},{5... | collective-permute-start | bytes 1228808 | tf_op jit(solution)/shard_map/ppermute | solution.py:21
  1.1 5.3 %collective-permute-start.1 = (bf16[80,640]{1,0:T(8,128)(2,1)S(1)}, bf16[80,640]{1,0:T(8,128)(2,1)S(1)}, u32[]{:S(2)}, u32[]{:S(2)}) collective-permute-start(bf16[80,640]{1,0:T(8,128)(2,1)S(1)} %get-tuple-element.51), channel_id=1, source_target_pairs={{0,8},{4,12},{8,0},{12,4},{16,24},{20,28},{24,16},{28,20},{1,9},{5... | collective-permute-start | bytes 307208 | tf_op jit(solution)/shard_map/ppermute | solution.py:21
  2.7 6.2 %collective-permute-start.2 = (bf16[80,640]{1,0:T(8,128)(2,1)S(1)}, bf16[80,640]{1,0:T(8,128)(2,1)S(1)}, u32[]{:S(2)}, u32[]{:S(2)}) collective-permute-start(bf16[80,640]{1,0:T(8,128)(2,1)S(1)} %get-tuple-element.53), channel_id=1, source_target_pairs={{0,16},{4,20},{8,24},{12,28},{16,0},{20,4},{24,8},{28,12},{1,17},{... | collective-permute-start | bytes 307208 | tf_op jit(solution)/shard_map/ppermute | solution.py:21
  4.2 5.6 %collective-permute-start.3 = (bf16[80,640]{1,0:T(8,128)(2,1)S(1)}, bf16[80,640]{1,0:T(8,128)(2,1)S(1)}, u32[]{:S(2)}, u32[]{:S(2)}) collective-permute-start(bf16[80,640]{1,0:T(8,128)(2,1)S(1)} %get-tuple-element.50), channel_id=1, source_target_pairs={{0,24},{4,28},{8,16},{12,20},{16,8},{20,12},{24,0},{28,4},{1,25},{... | collective-permute-start | bytes 307208 | tf_op jit(solution)/shard_map/ppermute | solution.py:21
  4.7 5.8 %collective-permute-start.4 = (bf16[80,640]{1,0:T(8,128)(2,1)S(1)}, bf16[80,640]{1,0:T(8,128)(2,1)S(1)}, u32[]{:S(2)}, u32[]{:S(2)}) collective-permute-start(bf16[80,640]{1,0:T(8,128)(2,1)S(1)} %get-tuple-element.52.refs_0_), channel_id=1, source_target_pairs={{0,4},{4,0},{8,12},{12,8},{16,20},{20,16},{24,28},{28,24},{1,5},{5... | collective-permute-start | bytes 307208 | tf_op jit(solution)/shard_map/ppermute | solution.py:21
  6.4 7.7 %collective-permute-start.8 = (bf16[320,320]{1,0:T(8,128)(2,1)}, bf16[320,320]{1,0:T(8,128)(2,1)S(1)}, u32[]{:S(2)}, u32[]{:S(2)}) collective-permute-start(bf16[320,320]{1,0:T(8,128)(2,1)} %bitcast.20), channel_id=1, source_target_pairs={{0,1},{1,0},{2,3},{3,2},{4,5},{5,4},{6,7},{7,6},{8,9},{9,8},{10,11... | collective-permute-start | bytes 614408 | tf_op jit(solution)/shard_map/ppermute | solution.py:31
  8.9 1.7 %collective-permute-start.5 = (bf16[80,640]{1,0:T(8,128)(2,1)S(1)}, bf16[80,640]{1,0:T(8,128)(2,1)S(1)}, u32[]{:S(2)}, u32[]{:S(2)}) collective-permute-start(bf16[80,640]{1,0:T(8,128)(2,1)S(1)} %collective-permute-done.1.refs_1_), channel_id=1, source_target_pairs={{0,4},{4,0},{8,12},{12,8},{16,20},{20,16},{24,28},{28,24},{1,5},{5... | collective-permute-start | bytes 307208 | tf_op jit(solution)/shard_map/ppermute | solution.py:21
  9.9 1.3 %collective-permute-start.6 = (bf16[80,640]{1,0:T(8,128)(2,1)S(1)}, bf16[80,640]{1,0:T(8,128)(2,1)S(1)}, u32[]{:S(2)}, u32[]{:S(2)}) collective-permute-start(bf16[80,640]{1,0:T(8,128)(2,1)S(1)} %collective-permute-done.2.refs_2_), channel_id=1, source_target_pairs={{0,4},{4,0},{8,12},{12,8},{16,20},{20,16},{24,28},{28,24},{1,5},{5... | collective-permute-start | bytes 307208 | tf_op jit(solution)/shard_map/ppermute | solution.py:21
  9.9 1.5 %collective-permute-start.7 = (bf16[80,640]{1,0:T(8,128)(2,1)S(1)}, bf16[80,640]{1,0:T(8,128)(2,1)S(1)}, u32[]{:S(2)}, u32[]{:S(2)}) collective-permute-start(bf16[80,640]{1,0:T(8,128)(2,1)S(1)} %collective-permute-done.3.refs_3_), channel_id=1, source_target_pairs={{0,4},{4,0},{8,12},{12,8},{16,20},{20,16},{24,28},{28,24},{1,5},{5... | collective-permute-start | bytes 307208 | tf_op jit(solution)/shard_map/ppermute | solution.py:21
  12.7 12.4 %copy-start = (bf16[1,320,320]{2,1,0:T(8,128)(2,1)S(1)}, bf16[1,320,320]{2,1,0:T(8,128)(2,1)}, u32[]{:S(2)}) copy-start(bf16[1,320,320]{2,1,0:T(8,128)(2,1)} %param.7) | copy-start | bytes 614404
  12.8 12.4 %copy-start.1 = (bf16[1,1,320,640]{3,2,1,0:T(8,128)(2,1)S(1)}, bf16[1,1,320,640]{3,2,1,0:T(8,128)(2,1)}, u32[]{:S(2)}) copy-start(bf16[1,1,320,640]{3,2,1,0:T(8,128)(2,1)} %param.5) | copy-start | bytes 1228804
  14.2 5.7 %collective-permute-start.9 = (bf16[80,640]{1,0:T(8,128)(2,1)S(1)}, bf16[80,640]{1,0:T(8,128)(2,1)S(1)}, u32[]{:S(2)}, u32[]{:S(2)}) collective-permute-start(bf16[80,640]{1,0:T(8,128)(2,1)S(1)} %get-tuple-element.49), channel_id=1, source_target_pairs={{0,8},{4,12},{8,0},{12,4},{16,24},{20,28},{24,16},{28,20},{1,9},{5... | collective-permute-start | bytes 307208 | tf_op jit(solution)/shard_map/ppermute | solution.py:21
  15.8 5.2 %collective-permute-start.10 = (bf16[80,640]{1,0:T(8,128)(2,1)S(1)}, bf16[80,640]{1,0:T(8,128)(2,1)S(1)}, u32[]{:S(2)}, u32[]{:S(2)}) collective-permute-start(bf16[80,640]{1,0:T(8,128)(2,1)S(1)} %get-tuple-element.48), channel_id=1, source_target_pairs={{0,16},{4,20},{8,24},{12,28},{16,0},{20,4},{24,8},{28,12},{1,17},{... | collective-permute-start | bytes 307208 | tf_op jit(solution)/shard_map/ppermute | solution.py:21
  17.3 5.6 %collective-permute-start.11 = (bf16[80,640]{1,0:T(8,128)(2,1)S(1)}, bf16[80,640]{1,0:T(8,128)(2,1)S(1)}, u32[]{:S(2)}, u32[]{:S(2)}) collective-permute-start(bf16[80,640]{1,0:T(8,128)(2,1)S(1)} %get-tuple-element.47), channel_id=1, source_target_pairs={{0,24},{4,28},{8,16},{12,20},{16,8},{20,12},{24,0},{28,4},{1,25},{... | collective-permute-start | bytes 307208 | tf_op jit(solution)/shard_map/ppermute | solution.py:21
  23.0 6.7 %collective-permute-start.12 = (bf16[160,640]{1,0:T(8,128)(2,1)S(1)}, bf16[160,640]{1,0:T(8,128)(2,1)S(1)}, u32[]{:S(2)}, u32[]{:S(2)}) collective-permute-start(bf16[160,640]{1,0:T(8,128)(2,1)S(1)} %get-tuple-element.39.own_ref), channel_id=1, source_target_pairs={{0,1},{1,0},{2,3},{3,2},{4,5},{5,4},{6,7},{7,6},{8,9},{9,8},{10,11... | collective-permute-start | bytes 614408 | tf_op jit(solution)/shard_map/ppermute | solution.py:31
  24.7 7.2 %collective-permute-start.13 = (bf16[160,640]{1,0:T(8,128)(2,1)S(1)}, bf16[160,640]{1,0:T(8,128)(2,1)S(1)}, u32[]{:S(2)}, u32[]{:S(2)}) collective-permute-start(bf16[160,640]{1,0:T(8,128)(2,1)S(1)} %get-tuple-element.40.own_ref), channel_id=1, source_target_pairs={{0,1},{1,0},{2,3},{3,2},{4,5},{5,4},{6,7},{7,6},{8,9},{9,8},{10,11... | collective-permute-start | bytes 614408 | tf_op jit(solution)/shard_map/ppermute | solution.py:31
  29.7 5.8 %collective-permute-start.14 = (bf16[160,640]{1,0:T(8,128)(2,1)S(1)}, bf16[160,640]{1,0:T(8,128)(2,1)S(1)}, u32[]{:S(2)}, u32[]{:S(2)}) collective-permute-start(bf16[160,640]{1,0:T(8,128)(2,1)S(1)} %shard_map.49.re_ref), channel_id=1, source_target_pairs={{0,4},{1,2},{2,1},{3,7},{4,0},{5,6},{6,5},{7,3},{8,12},{9,10},{10,... | collective-permute-start | bytes 614408 | tf_op jit(solution)/shard_map/ppermute | solution.py:31
  31.9 4.8 %collective-permute-start.15 = (bf16[80,640]{1,0:T(8,128)(2,1)S(1)}, bf16[80,640]{1,0:T(8,128)(2,1)S(1)}, u32[]{:S(2)}, u32[]{:S(2)}) collective-permute-start(bf16[80,640]{1,0:T(8,128)(2,1)S(1)} %get-tuple-element.41.refs_0_), channel_id=1, source_target_pairs={{0,4},{1,2},{2,1},{3,7},{4,0},{5,6},{6,5},{7,3},{8,12},{9,10},{10,... | collective-permute-start | bytes 307208 | tf_op jit(solution)/shard_map/ppermute | solution.py:31
  35.6 9.1 %collective-permute-start.16 = (bf16[160,640]{1,0:T(8,128)(2,1)S(1)}, bf16[160,640]{1,0:T(8,128)(2,1)S(1)}, u32[]{:S(2)}, u32[]{:S(2)}) collective-permute-start(bf16[160,640]{1,0:T(8,128)(2,1)S(1)} %collective-permute-done.14.refs_0_), channel_id=1, source_target_pairs={{0,4},{1,5},{2,3},{3,2},{4,0},{5,1},{6,7},{7,6},{8,12},{9,13},{10,... | collective-permute-start | bytes 614408 | tf_op jit(solution)/shard_map/ppermute | solution.py:31
  35.6 4.7 %collective-permute-start.18 = (bf16[80,640]{1,0:T(8,128)(2,1)S(1)}, bf16[80,640]{1,0:T(8,128)(2,1)S(1)}, u32[]{:S(2)}, u32[]{:S(2)}) collective-permute-start(bf16[80,640]{1,0:T(8,128)(2,1)S(1)} %get-tuple-element.42.refs_1_), channel_id=1, source_target_pairs={{0,4},{1,2},{2,1},{3,7},{4,0},{5,6},{6,5},{7,3},{8,12},{9,10},{10,... | collective-permute-start | bytes 307208 | tf_op jit(solution)/shard_map/ppermute | solution.py:31
  36.7 7.9 %collective-permute-start.17 = (bf16[80,640]{1,0:T(8,128)(2,1)S(1)}, bf16[80,640]{1,0:T(8,128)(2,1)S(1)}, u32[]{:S(2)}, u32[]{:S(2)}) collective-permute-start(bf16[80,640]{1,0:T(8,128)(2,1)S(1)} %collective-permute-done.15.refs_1_), channel_id=1, source_target_pairs={{0,4},{1,5},{2,3},{3,2},{4,0},{5,1},{6,7},{7,6},{8,12},{9,13},{10,... | collective-permute-start | bytes 307208 | tf_op jit(solution)/shard_map/ppermute | solution.py:31
  40.3 5.6 %collective-permute-start.19 = (bf16[80,640]{1,0:T(8,128)(2,1)S(1)}, bf16[80,640]{1,0:T(8,128)(2,1)S(1)}, u32[]{:S(2)}, u32[]{:S(2)}) collective-permute-start(bf16[80,640]{1,0:T(8,128)(2,1)S(1)} %collective-permute-done.18.refs_0_), channel_id=1, source_target_pairs={{0,4},{1,5},{2,3},{3,2},{4,0},{5,1},{6,7},{7,6},{8,12},{9,13},{10,... | collective-permute-start | bytes 307208 | tf_op jit(solution)/shard_map/ppermute | solution.py:31

commit v5 on v4

--- a/solution.py
+++ b/solution.py
@@ -26,7 +26,7 @@
     pairs = []
     for e in range(devices):
         for s in range(slabs):
-            to = (e, slab_to[s]) if s in slab_to else (e ^ 1, s)
+            to = (e, slab_to[s]) if s in slab_to else (e ^ (2 if s % 2 else 4), s)
             pairs.append((e * slabs + s, to[0] * slabs + to[1]))
     return lax.ppermute(array, (ENERGY, SLAB), pairs)
 
@@ -215,30 +215,37 @@
     carry_in(lax.axis_index(SLAB) // 2 == pair, link_ref, turned_ref, joined(state), arrived(came), outs)
 
 
-def base_kernel(stack_ref, first_ref, second_ref, re_ref, *refs):
-    *im_refs, out_ref = refs
-    re = dot(stack_ref[...], unpacked(re_ref[...]))
-    im = dot(stack_ref[...], unpacked(joined(im_refs)))
+def base_kernel(stack_ref, first_ref, second_ref, *refs):
+    *state, out_ref = refs
+    re = dot(stack_ref[...], unpacked(joined(state[:2])))
+    im = dot(stack_ref[...], unpacked(joined(state[2:])))
     size = re.shape[1]
     left_re = (re[:size] - im[size:]).astype(jnp.bfloat16)
     left_im = (im[:size] + re[size:]).astype(jnp.bfloat16)
     out_ref[...] = dot(left_re, first_ref[...]) + dot(left_im, second_ref[...])
 
 
-def early_kernel(pair, far_stack_ref, far_first_ref, far_second_ref, half_ref, base_ref, *refs):
-    *came, out_ref, left_ref = refs
+def early_kernel(pair, far_stack_ref, far_first_ref, far_second_ref, base_ref, *refs):
+    *came, out_ref = refs
     turn = lax.axis_index(SLAB) // 2 == pair
 
     @pl.when(turn)
     def _():
-        left = dot(far_stack_ref[...], unpacked(arrived(came[::2]))).astype(jnp.bfloat16)
+        left = dot(far_stack_ref[...], unpacked(arrived(came))).astype(jnp.bfloat16)
         size = left.shape[1]
         out_ref[...] = base_ref[...] + dot(left[:size], far_first_ref[...]) + dot(left[size:], far_second_ref[...])
-        left_ref[...] = dot(half_ref[...], unpacked(arrived(came[1::2])))
 
     @pl.when(jnp.logical_not(turn))
     def _():
         out_ref[...] = base_ref[...]
+
+
+def half_kernel(pair, half_ref, *refs):
+    *came, left_ref = refs
+
+    @pl.when(lax.axis_index(SLAB) // 2 == pair)
+    def _():
+        left_ref[...] = dot(half_ref[...], unpacked(arrived(came)))
 
 
 def late_kernel(pair, far_first_ref, far_second_ref, half_ref, early_ref, early_left_ref, *refs):
@@ -311,27 +318,28 @@
     turned, step, turned_step, *base, far_stack, far_first, far_second, half_a, half_b = prepared
     came_re = swap_slabs(own_re, other_in_pair)
     came_im = swap_slabs(own_im, other_in_pair)
-    part = (own_re.shape, own_re.dtype)
     halves = [((size // 4, width), own_im.dtype)] * 2
     total = [((size, width), jnp.float32)]
-    re = call(first_kernel, [part], [link, turned, own_re, came_re])
+    re = call(first_kernel, halves, [link, turned, own_re, came_re])
     im = call(first_kernel, halves, [link, turned, own_im, came_im])
 
     for s in range(1, slabs - 1, 2):
         pair = (s + 1) // 2
-        near, far = {s: s + 1, s + 1: s}, {s + 1: s + 2, s + 2: s + 1}
+        near, far = {s: s + 1, s + 1: s}, other_in_pair
         near_re = [swap_slabs(x, near) for x in re]
         near_im = [swap_slabs(x, near) for x in im]
         far_re = [swap_slabs(x, far) for x in near_re]
         far_im = [swap_slabs(x, far) for x in near_im]
         if pair < last_pair:
             advance = functools.partial(advance_kernel, pair)
-            re = call(advance, [part], [step, turned_step, *re, *near_re, *far_re])
+            re = call(advance, halves, [step, turned_step, *re, *near_re, *far_re])
             im = call(advance, halves, [step, turned_step, *im, *near_im, *far_im])
     (out,) = call(base_kernel, total, [*base, *re, *im])
-    early = [far_stack, far_first, far_second, half_a, out, near_re[0], near_im[0], far_re[0], far_im[0]]
-    left = ((2 * size, size), jnp.float32)
-    out, left = call(functools.partial(early_kernel, last_pair), [*total, left], early)
+    early = [far_stack, far_first, far_second, out, *near_re, *far_re]
+    (out,) = call(functools.partial(early_kernel, last_pair), total, early)
+    far_im[0], out = lax.optimization_barrier((far_im[0], out))
+    left = [((2 * size, size), jnp.float32)]
+    (left,) = call(functools.partial(half_kernel, last_pair), left, [half_a, near_im[0], far_im[0]])
     given = [far_first, far_second, half_b, out, left, near_im[1], far_im[1]]
     out = pl.pallas_call(
         functools.partial(late_kernel, last_pair),

time: 47.8 us -> 45.7 us (0.956)
  waiting for transfers between devices: 21.9 us -> 13.1 us
  starting transfers between devices: 15.7 us -> 21.7 us
    ppermute x9 -> x11, waiting for transfers between devices: 12.5 us -> 4.6 us  [swap_slabs(): return lax.ppermute(array, (ENERGY, SLAB), pairs)]
    ppermute x9 -> x11, starting transfers between devices: 8.07 us -> 14.1 us  [swap_slabs(): return lax.ppermute(array, (ENERGY, SLAB), pairs)]
    ppermute x11, waiting for transfers between devices: 9.42 us -> 8.46 us  [swap_with(): return lax.ppermute(array, ENERGY, [(i, i ^ mask) for i in range(devices)])]
    pallas_call x6 -> x7, Pallas kernels: 5.37 us -> 5.63 us  [call(): pl.pallas_call(kernel, out_shape=outs, in_specs=[WHOLE] * len(given), out...]
  transfers between devices with their start and end apart: 20 -> 22, of which waited for: 14 -> 13; matrix products, arithmetic and copies ran while one was open for 3% -> 3% of each run, Pallas kernels for 14% -> 15%
where the time goes in v5:
time: 45.7 us; the launch traced here: 45.1 us
  starting transfers between devices  21.7 us (47%)
  waiting for transfers between devices  13.1 us (29%)
  Pallas kernels  8.84 us (19%)
  local copies, waits for them, and re-layouts  1.18 us (3%)
    ppermute x11, starting transfers between devices, swap_slabs(): return lax.ppermute(array, (ENERGY, SLAB), pairs)  14.1 us
    ppermute x11, waiting for transfers between devices, swap_with(): return lax.ppermute(array, ENERGY, [(i, i ^ mask) for i in range(devices)])  8.46 us
    ppermute x11, starting transfers between devices, swap_with(): return lax.ppermute(array, ENERGY, [(i, i ^ mask) for i in range(devices)])  7.63 us
    pallas_call x7, Pallas kernels, call(): pl.pallas_call(kernel, out_shape=outs, in_specs=[WHOLE] * len(given), out...  5.63 us
    ppermute x11, waiting for transfers between devices, swap_slabs(): return lax.ppermute(array, (ENERGY, SLAB), pairs)  4.6 us
    pallas_call x1, Pallas kernels, local(): pl.pallas_call(functools.partial(late_kernel, last_pair), out_shape=jax.S...  1.79 us
    pallas_call x1, Pallas kernels, convolve(): pl.pallas_call(functools.partial(conv_kernel, chips), out_shape=pltpu.VME...  1.42 us
    dynamic_slice x1, local copies, waits for them, and re-layouts, local(): lax.dynamic_slice(lesser, (rows * (chip ^ j), 0), (rows, width))  1.13 us
  transfers between devices with their start and end apart: 22, of which 13 were waited for; matrix products, arithmetic and copies ran while one was open for 3% of the time, Pallas kernels for 15%

profile of v5, /device:TPU:16, one launch (start us, length us, event | category | flops | bytes accessed | tf_op | source)
XLA Modules:
  0.0 45.1 jit_solution(9221992696089378651)
XLA Ops:
  0.0 1.1 %dynamic-slice_bitcast_fusion = (bf16[80,640]{1,0:T(8,128)(2,1)S(1)}, bf16[80,640]{1,0:T(8,128)(2,1)S(1)}, bf16[80,640]{1,0:T(8,128)(2,1)S(1)}, bf16[80,640]{1,0:T(8,128)(2,1)S(1)}) fusion(bf16[1,1,320,640]{3,2,1,0:T(8,128)(2,1)} %param.4, s32[]{:T(128)S(6)} %select_n.43, s32[]{:T(128)S(6)} %select_n.41, s32[]{:T(128)S(6)} %select_n.40, s32[]{:T(128)S(6)} %select_n.42), kind=kLoop, calls=%fused_computation.6 | loop fusion | bytes 819216 | tf_op jit(solution)/shard_map/dynamic_slice | solution.py:296
  1.1 1.6 %collective-permute-start.1 = (bf16[80,640]{1,0:T(8,128)(2,1)S(1)}, bf16[80,640]{1,0:T(8,128)(2,1)S(1)}, u32[]{:S(2)}, u32[]{:S(2)}) collective-permute-start(bf16[80,640]{1,0:T(8,128)(2,1)S(1)} %get-tuple-element.55), channel_id=1, source_target_pairs={{0,8},{4,12},{8,0},{12,4},{16,24},{20,28},{24,16},{28,20},{1,9},{5... | collective-permute-start | bytes 307208 | tf_op jit(solution)/shard_map/ppermute | solution.py:21
  2.7 1.5 %collective-permute-start.2 = (bf16[80,640]{1,0:T(8,128)(2,1)S(1)}, bf16[80,640]{1,0:T(8,128)(2,1)S(1)}, u32[]{:S(2)}, u32[]{:S(2)}) collective-permute-start(bf16[80,640]{1,0:T(8,128)(2,1)S(1)} %get-tuple-element.57), channel_id=1, source_target_pairs={{0,16},{4,20},{8,24},{12,28},{16,0},{20,4},{24,8},{28,12},{1,17},{... | collective-permute-start | bytes 307208 | tf_op jit(solution)/shard_map/ppermute | solution.py:21
  4.7 1.7 %collective-permute-done.1.refs_1_ = bf16[80,640]{1,0:T(8,128)(2,1)S(1)} collective-permute-done((bf16[80,640]{1,0:T(8,128)(2,1)S(1)}, bf16[80,640]{1,0:T(8,128)(2,1)S(1)}, u32[]{:S(2)}, u32[]{:S(2)}) %collective-permute-start.1) | collective-permute-done | bytes 102432 | tf_op jit(solution)/shard_map/ppermute | solution.py:21
  6.4 1.6 %collective-permute-start.8 = (bf16[320,320]{1,0:T(8,128)(2,1)}, bf16[320,320]{1,0:T(8,128)(2,1)S(1)}, u32[]{:S(2)}, u32[]{:S(2)}) collective-permute-start(bf16[320,320]{1,0:T(8,128)(2,1)} %bitcast.20), channel_id=1, source_target_pairs={{0,1},{1,0},{2,3},{3,2},{4,5},{5,4},{6,7},{7,6},{8,9},{9,8},{10,11... | collective-permute-start | bytes 614408 | tf_op jit(solution)/shard_map/ppermute | solution.py:31
  8.9 1.0 %collective-permute-done.3.refs_3_ = bf16[80,640]{1,0:T(8,128)(2,1)S(1)} collective-permute-done((bf16[80,640]{1,0:T(8,128)(2,1)S(1)}, bf16[80,640]{1,0:T(8,128)(2,1)S(1)}, u32[]{:S(2)}, u32[]{:S(2)}) %collective-permute-start.3) | collective-permute-done | bytes 102432 | tf_op jit(solution)/shard_map/ppermute | solution.py:21
  11.3 1.4 %shard_map.46.refs_0_ = bf16[4,80,640]{2,1,0:T(8,128)(2,1)S(1)} custom-call(bf16[8,80,640]{2,1,0:T(8,128)(2,1)S(1)} %pad_maximum_fusion.inter_ref, bf16[80,640]{1,0:T(8,128)(2,1)S(1)} %get-tuple-element.56.refs_0_, bf16[80,640]{1,0:T(8,128)(2,1)S(1)} %collective-permute-done.1.refs_1_, bf16[80,640]{1,0:T(8,128)(2,1)S(1)} %collective-permute-done.2.refs_2_, ...), custom_call_target="tpu_custom_call" | custom-call | flops 13107200 | tf_op jit(solution)/shard_map/pallas_call | solution.py:99
  12.8 1.4 %collective-permute-done.8.before_ref = bf16[320,320]{1,0:T(8,128)(2,1)S(1)} collective-permute-done((bf16[320,320]{1,0:T(8,128)(2,1)}, bf16[320,320]{1,0:T(8,128)(2,1)S(1)}, u32[]{:S(2)}, u32[]{:S(2)}) %collective-permute-start.8) | collective-permute-done | bytes 204832 | tf_op jit(solution)/shard_map/ppermute | solution.py:31
  14.2 1.6 %collective-permute-start.10 = (bf16[80,640]{1,0:T(8,128)(2,1)S(1)}, bf16[80,640]{1,0:T(8,128)(2,1)S(1)}, u32[]{:S(2)}, u32[]{:S(2)}) collective-permute-start(bf16[80,640]{1,0:T(8,128)(2,1)S(1)} %get-tuple-element.52), channel_id=1, source_target_pairs={{0,16},{4,20},{8,24},{12,28},{16,0},{20,4},{24,8},{28,12},{1,17},{... | collective-permute-start | bytes 307208 | tf_op jit(solution)/shard_map/ppermute | solution.py:21
  15.8 1.4 %collective-permute-start.11 = (bf16[80,640]{1,0:T(8,128)(2,1)S(1)}, bf16[80,640]{1,0:T(8,128)(2,1)S(1)}, u32[]{:S(2)}, u32[]{:S(2)}) collective-permute-start(bf16[80,640]{1,0:T(8,128)(2,1)S(1)} %get-tuple-element.51), channel_id=1, source_target_pairs={{0,24},{4,28},{8,16},{12,20},{16,8},{20,12},{24,0},{28,4},{1,25},{... | collective-permute-start | bytes 307208 | tf_op jit(solution)/shard_map/ppermute | solution.py:21
  17.8 2.3 %collective-permute-done.10.refs_2_ = bf16[80,640]{1,0:T(8,128)(2,1)S(1)} collective-permute-done((bf16[80,640]{1,0:T(8,128)(2,1)S(1)}, bf16[80,640]{1,0:T(8,128)(2,1)S(1)}, u32[]{:S(2)}, u32[]{:S(2)}) %collective-permute-start.10) | collective-permute-done | bytes 102432 | tf_op jit(solution)/shard_map/ppermute | solution.py:21
  20.0 1.4 %collective-permute-done.11.refs_3_ = bf16[80,640]{1,0:T(8,128)(2,1)S(1)} collective-permute-done((bf16[80,640]{1,0:T(8,128)(2,1)S(1)}, bf16[80,640]{1,0:T(8,128)(2,1)S(1)}, u32[]{:S(2)}, u32[]{:S(2)}) %collective-permute-start.11) | collective-permute-done | bytes 102432 | tf_op jit(solution)/shard_map/ppermute | solution.py:21
  22.1 1.6 %collective-permute-start.15 = (bf16[160,640]{1,0:T(8,128)(2,1)S(1)}, bf16[160,640]{1,0:T(8,128)(2,1)S(1)}, u32[]{:S(2)}, u32[]{:S(2)}) collective-permute-start(bf16[160,640]{1,0:T(8,128)(2,1)S(1)} %get-tuple-element.42.own_ref), channel_id=1, source_target_pairs={{0,1},{1,0},{2,3},{3,2},{4,5},{5,4},{6,7},{7,6},{8,9},{9,8},{10,11... | collective-permute-start | bytes 614408 | tf_op jit(solution)/shard_map/ppermute | solution.py:31
  24.2 2.5 %shard_map.48 = (bf16[320,320]{1,0:T(8,128)(2,1)S(1)}, bf16[320,320]{1,0:T(8,128)(2,1)}, bf16[320,320]{1,0:T(8,128)(2,1)}, bf16[640,320]{1,0:T(8,128)(2,1)S(1)},...) custom-call(bf16[320,320]{1,0:T(8,128)(2,1)S(1)} %bitcast.21, ...), custom_call_target="tpu_custom_call" | custom-call | tf_op jit(solution)/shard_map/pallas_call | solution.py:36
  26.7 2.1 %collective-permute-done.15.came_ref = bf16[160,640]{1,0:T(8,128)(2,1)S(1)} collective-permute-done((bf16[160,640]{1,0:T(8,128)(2,1)S(1)}, bf16[160,640]{1,0:T(8,128)(2,1)S(1)}, u32[]{:S(2)}, u32[]{:S(2)}) %collective-permute-start.15) | collective-permute-done | bytes 204832 | tf_op jit(solution)/shard_map/ppermute | solution.py:31
  28.8 1.2 %collective-permute-start.16 = (bf16[80,640]{1,0:T(8,128)(2,1)S(1)}, bf16[80,640]{1,0:T(8,128)(2,1)S(1)}, u32[]{:S(2)}, u32[]{:S(2)}) collective-permute-start(bf16[80,640]{1,0:T(8,128)(2,1)S(1)} %get-tuple-element.43.refs_0_), channel_id=1, source_target_pairs={{0,16},{1,2},{2,1},{3,11},{4,20},{5,6},{6,5},{7,15},{8,24},{9,10},... | collective-permute-start | bytes 307208 | tf_op jit(solution)/shard_map/ppermute | solution.py:31
  31.0 1.8 %collective-permute-start.13 = (bf16[80,640]{1,0:T(8,128)(2,1)S(1)}, bf16[80,640]{1,0:T(8,128)(2,1)S(1)}, u32[]{:S(2)}, u32[]{:S(2)}) collective-permute-start(bf16[80,640]{1,0:T(8,128)(2,1)S(1)} %get-tuple-element.37.refs_2_), channel_id=1, source_target_pairs={{0,16},{1,2},{2,1},{3,11},{4,20},{5,6},{6,5},{7,15},{8,24},{9,10},... | collective-permute-start | bytes 307208 | tf_op jit(solution)/shard_map/ppermute | solution.py:31
  33.6 2.4 %collective-permute-start.18 = (bf16[80,640]{1,0:T(8,128)(2,1)S(1)}, bf16[80,640]{1,0:T(8,128)(2,1)S(1)}, u32[]{:S(2)}, u32[]{:S(2)}) collective-permute-start(bf16[80,640]{1,0:T(8,128)(2,1)S(1)} %collective-permute-done.16.refs_0_), channel_id=1, source_target_pairs={{0,1},{1,0},{2,3},{3,2},{4,5},{5,4},{6,7},{7,6},{8,9},{9,8},{10,11... | collective-permute-start | bytes 307208 | tf_op jit(solution)/shard_map/ppermute | solution.py:31
  36.0 1.0 %collective-permute-start.19 = (bf16[80,640]{1,0:T(8,128)(2,1)S(1)}, bf16[80,640]{1,0:T(8,128)(2,1)S(1)}, u32[]{:S(2)}, u32[]{:S(2)}) collective-permute-start(bf16[80,640]{1,0:T(8,128)(2,1)S(1)} %collective-permute-done.17.refs_1_), channel_id=1, source_target_pairs={{0,1},{1,0},{2,3},{3,2},{4,5},{5,4},{6,7},{7,6},{8,9},{9,8},{10,11... | collective-permute-start | bytes 307208 | tf_op jit(solution)/shard_map/ppermute | solution.py:31
  37.0 1.6 %collective-permute-start.14 = (bf16[80,640]{1,0:T(8,128)(2,1)S(1)}, bf16[80,640]{1,0:T(8,128)(2,1)S(1)}, u32[]{:S(2)}, u32[]{:S(2)}) collective-permute-start(bf16[80,640]{1,0:T(8,128)(2,1)S(1)} %collective-permute-done.13.refs_0_), channel_id=1, source_target_pairs={{0,1},{1,0},{2,3},{3,2},{4,5},{5,4},{6,7},{7,6},{8,9},{9,8},{10,11... | collective-permute-start | bytes 307208 | tf_op jit(solution)/shard_map/ppermute | solution.py:31
  38.6 1.2 %collective-permute-start.21 = (bf16[80,640]{1,0:T(8,128)(2,1)S(1)}, bf16[80,640]{1,0:T(8,128)(2,1)S(1)}, u32[]{:S(2)}, u32[]{:S(2)}) collective-permute-start(bf16[80,640]{1,0:T(8,128)(2,1)S(1)} %collective-permute-done.20.refs_0_), channel_id=1, source_target_pairs={{0,1},{1,0},{2,3},{3,2},{4,5},{5,4},{6,7},{7,6},{8,9},{9,8},{10,11... | collective-permute-start | bytes 307208 | tf_op jit(solution)/shard_map/ppermute | solution.py:31
  39.8 1.4 %shard_map.51.base_ref = f32[320,640]{1,0:T(8,128)S(1)} custom-call(bf16[640,320]{1,0:T(8,128)(2,1)S(1)} %get-tuple-element.39.stack_ref, bf16[320,640]{1,0:T(8,128)(2,1)S(1)} %get-tuple-element.40.first_ref, bf16[320,640]{1,0:T(8,128)(2,1)S(1)} %get-tuple-element.41.second_ref, bf16[80,640]{1,0:T(8,128)(2,1)S(1)} %get-tuple-element.43.refs_0_, ...), custom_call_target="tpu_custom_call" | custom-call | tf_op jit(solution)/shard_map/pallas_call | solution.py:36
  41.2 1.1 %shard_map.52.early_ref = f32[320,640]{1,0:T(8,128)S(1)} custom-call(bf16[640,320]{1,0:T(8,128)(2,1)S(1)} %get-tuple-element.38.far_stack_ref, bf16[320,640]{1,0:T(8,128)(2,1)S(1)} %get-tuple-element.32.far_first_ref, bf16[320,640]{1,0:T(8,128)(2,1)S(1)} %get-tuple-element.33.far_second_ref, f32[320,640]{1,0:T(8,128)S(1)} %shard_map.51.base_ref, ...), custom_call_target="tpu_custom_call" | custom-call | tf_op jit(solution)/shard_map/pallas_call | solution.py:36
  43.3 1.8 %shard_map.54 = bf16[320,640]{1,0:T(8,128)(2,1)} custom-call(bf16[320,640]{1,0:T(8,128)(2,1)S(1)} %get-tuple-element.32.far_first_ref, bf16[320,640]{1,0:T(8,128)(2,1)S(1)} %get-tuple-element.33.far_second_ref, bf16[640,160]{1,0:T(8,128)(2,1)S(1)} %get-tuple-element.34.half_ref, f32[320,640]{1,0:T(8,128)S(1)} %shard_map.52.early_ref, ...), custom_call_target="tpu_custom_call" | custom-call | tf_op jit(solution)/shard_map/pallas_call | solution.py:344
  (39 shorter events, 7.2 us)
Async XLA Ops:
  0.0 9.9 %collective-permute-start = (bf16[8,40,640]{2,1,0:T(8,128)(2,1)}, bf16[8,40,640]{2,1,0:T(8,128)(2,1)S(1)}, u32[]{:S(2)}, u32[]{:S(2)}) collective-permute-start(bf16[8,40,640]{2,1,0:T(8,128)(2,1)} %bitcast.25), channel_id=1, source_target_pairs={{0,4},{4,0},{8,12},{12,8},{16,20},{20,16},{24,28},{28,24},{1,5},{5... | collective-permute-start | bytes 1228808 | tf_op jit(solution)/shard_map/ppermute | solution.py:21
  1.1 5.3 %collective-permute-start.1 = (bf16[80,640]{1,0:T(8,128)(2,1)S(1)}, bf16[80,640]{1,0:T(8,128)(2,1)S(1)}, u32[]{:S(2)}, u32[]{:S(2)}) collective-permute-start(bf16[80,640]{1,0:T(8,128)(2,1)S(1)} %get-tuple-element.55), channel_id=1, source_target_pairs={{0,8},{4,12},{8,0},{12,4},{16,24},{20,28},{24,16},{28,20},{1,9},{5... | collective-permute-start | bytes 307208 | tf_op jit(solution)/shard_map/ppermute | solution.py:21
  2.7 6.2 %collective-permute-start.2 = (bf16[80,640]{1,0:T(8,128)(2,1)S(1)}, bf16[80,640]{1,0:T(8,128)(2,1)S(1)}, u32[]{:S(2)}, u32[]{:S(2)}) collective-permute-start(bf16[80,640]{1,0:T(8,128)(2,1)S(1)} %get-tuple-element.57), channel_id=1, source_target_pairs={{0,16},{4,20},{8,24},{12,28},{16,0},{20,4},{24,8},{28,12},{1,17},{... | collective-permute-start | bytes 307208 | tf_op jit(solution)/shard_map/ppermute | solution.py:21
  4.2 5.6 %collective-permute-start.3 = (bf16[80,640]{1,0:T(8,128)(2,1)S(1)}, bf16[80,640]{1,0:T(8,128)(2,1)S(1)}, u32[]{:S(2)}, u32[]{:S(2)}) collective-permute-start(bf16[80,640]{1,0:T(8,128)(2,1)S(1)} %get-tuple-element.54), channel_id=1, source_target_pairs={{0,24},{4,28},{8,16},{12,20},{16,8},{20,12},{24,0},{28,4},{1,25},{... | collective-permute-start | bytes 307208 | tf_op jit(solution)/shard_map/ppermute | solution.py:21
  4.7 5.8 %collective-permute-start.4 = (bf16[80,640]{1,0:T(8,128)(2,1)S(1)}, bf16[80,640]{1,0:T(8,128)(2,1)S(1)}, u32[]{:S(2)}, u32[]{:S(2)}) collective-permute-start(bf16[80,640]{1,0:T(8,128)(2,1)S(1)} %get-tuple-element.56.refs_0_), channel_id=1, source_target_pairs={{0,4},{4,0},{8,12},{12,8},{16,20},{20,16},{24,28},{28,24},{1,5},{5... | collective-permute-start | bytes 307208 | tf_op jit(solution)/shard_map/ppermute | solution.py:21
  6.4 7.7 %collective-permute-start.8 = (bf16[320,320]{1,0:T(8,128)(2,1)}, bf16[320,320]{1,0:T(8,128)(2,1)S(1)}, u32[]{:S(2)}, u32[]{:S(2)}) collective-permute-start(bf16[320,320]{1,0:T(8,128)(2,1)} %bitcast.20), channel_id=1, source_target_pairs={{0,1},{1,0},{2,3},{3,2},{4,5},{5,4},{6,7},{7,6},{8,9},{9,8},{10,11... | collective-permute-start | bytes 614408 | tf_op jit(solution)/shard_map/ppermute | solution.py:31
  8.9 1.7 %collective-permute-start.5 = (bf16[80,640]{1,0:T(8,128)(2,1)S(1)}, bf16[80,640]{1,0:T(8,128)(2,1)S(1)}, u32[]{:S(2)}, u32[]{:S(2)}) collective-permute-start(bf16[80,640]{1,0:T(8,128)(2,1)S(1)} %collective-permute-done.1.refs_1_), channel_id=1, source_target_pairs={{0,4},{4,0},{8,12},{12,8},{16,20},{20,16},{24,28},{28,24},{1,5},{5... | collective-permute-start | bytes 307208 | tf_op jit(solution)/shard_map/ppermute | solution.py:21
  9.9 1.3 %collective-permute-start.6 = (bf16[80,640]{1,0:T(8,128)(2,1)S(1)}, bf16[80,640]{1,0:T(8,128)(2,1)S(1)}, u32[]{:S(2)}, u32[]{:S(2)}) collective-permute-start(bf16[80,640]{1,0:T(8,128)(2,1)S(1)} %collective-permute-done.2.refs_2_), channel_id=1, source_target_pairs={{0,4},{4,0},{8,12},{12,8},{16,20},{20,16},{24,28},{28,24},{1,5},{5... | collective-permute-start | bytes 307208 | tf_op jit(solution)/shard_map/ppermute | solution.py:21
  9.9 1.5 %collective-permute-start.7 = (bf16[80,640]{1,0:T(8,128)(2,1)S(1)}, bf16[80,640]{1,0:T(8,128)(2,1)S(1)}, u32[]{:S(2)}, u32[]{:S(2)}) collective-permute-start(bf16[80,640]{1,0:T(8,128)(2,1)S(1)} %collective-permute-done.3.refs_3_), channel_id=1, source_target_pairs={{0,4},{4,0},{8,12},{12,8},{16,20},{20,16},{24,28},{28,24},{1,5},{5... | collective-permute-start | bytes 307208 | tf_op jit(solution)/shard_map/ppermute | solution.py:21
  12.7 11.4 %copy-start = (bf16[1,320,320]{2,1,0:T(8,128)(2,1)S(1)}, bf16[1,320,320]{2,1,0:T(8,128)(2,1)}, u32[]{:S(2)}) copy-start(bf16[1,320,320]{2,1,0:T(8,128)(2,1)} %param.7) | copy-start | bytes 614404
  12.8 11.4 %copy-start.1 = (bf16[1,1,320,640]{3,2,1,0:T(8,128)(2,1)S(1)}, bf16[1,1,320,640]{3,2,1,0:T(8,128)(2,1)}, u32[]{:S(2)}) copy-start(bf16[1,1,320,640]{3,2,1,0:T(8,128)(2,1)} %param.5) | copy-start | bytes 1228804
  14.2 5.8 %collective-permute-start.10 = (bf16[80,640]{1,0:T(8,128)(2,1)S(1)}, bf16[80,640]{1,0:T(8,128)(2,1)S(1)}, u32[]{:S(2)}, u32[]{:S(2)}) collective-permute-start(bf16[80,640]{1,0:T(8,128)(2,1)S(1)} %get-tuple-element.52), channel_id=1, source_target_pairs={{0,16},{4,20},{8,24},{12,28},{16,0},{20,4},{24,8},{28,12},{1,17},{... | collective-permute-start | bytes 307208 | tf_op jit(solution)/shard_map/ppermute | solution.py:21
  15.8 5.6 %collective-permute-start.11 = (bf16[80,640]{1,0:T(8,128)(2,1)S(1)}, bf16[80,640]{1,0:T(8,128)(2,1)S(1)}, u32[]{:S(2)}, u32[]{:S(2)}) collective-permute-start(bf16[80,640]{1,0:T(8,128)(2,1)S(1)} %get-tuple-element.51), channel_id=1, source_target_pairs={{0,24},{4,28},{8,16},{12,20},{16,8},{20,12},{24,0},{28,4},{1,25},{... | collective-permute-start | bytes 307208 | tf_op jit(solution)/shard_map/ppermute | solution.py:21
  17.2 4.7 %collective-permute-start.9 = (bf16[80,640]{1,0:T(8,128)(2,1)S(1)}, bf16[80,640]{1,0:T(8,128)(2,1)S(1)}, u32[]{:S(2)}, u32[]{:S(2)}) collective-permute-start(bf16[80,640]{1,0:T(8,128)(2,1)S(1)} %get-tuple-element.53), channel_id=1, source_target_pairs={{0,8},{4,12},{8,0},{12,4},{16,24},{20,28},{24,16},{28,20},{1,9},{5... | collective-permute-start | bytes 307208 | tf_op jit(solution)/shard_map/ppermute | solution.py:21
  22.1 6.7 %collective-permute-start.15 = (bf16[160,640]{1,0:T(8,128)(2,1)S(1)}, bf16[160,640]{1,0:T(8,128)(2,1)S(1)}, u32[]{:S(2)}, u32[]{:S(2)}) collective-permute-start(bf16[160,640]{1,0:T(8,128)(2,1)S(1)} %get-tuple-element.42.own_ref), channel_id=1, source_target_pairs={{0,1},{1,0},{2,3},{3,2},{4,5},{5,4},{6,7},{7,6},{8,9},{9,8},{10,11... | collective-permute-start | bytes 614408 | tf_op jit(solution)/shard_map/ppermute | solution.py:31
  23.7 7.3 %collective-permute-start.12 = (bf16[160,640]{1,0:T(8,128)(2,1)S(1)}, bf16[160,640]{1,0:T(8,128)(2,1)S(1)}, u32[]{:S(2)}, u32[]{:S(2)}) collective-permute-start(bf16[160,640]{1,0:T(8,128)(2,1)S(1)} %get-tuple-element.36.own_ref), channel_id=1, source_target_pairs={{0,1},{1,0},{2,3},{3,2},{4,5},{5,4},{6,7},{7,6},{8,9},{9,8},{10,11... | collective-permute-start | bytes 614408 | tf_op jit(solution)/shard_map/ppermute | solution.py:31
  28.8 4.7 %collective-permute-start.16 = (bf16[80,640]{1,0:T(8,128)(2,1)S(1)}, bf16[80,640]{1,0:T(8,128)(2,1)S(1)}, u32[]{:S(2)}, u32[]{:S(2)}) collective-permute-start(bf16[80,640]{1,0:T(8,128)(2,1)S(1)} %get-tuple-element.43.refs_0_), channel_id=1, source_target_pairs={{0,16},{1,2},{2,1},{3,11},{4,20},{5,6},{6,5},{7,15},{8,24},{9,10},... | collective-permute-start | bytes 307208 | tf_op jit(solution)/shard_map/ppermute | solution.py:31
  30.0 6.0 %collective-permute-start.17 = (bf16[80,640]{1,0:T(8,128)(2,1)S(1)}, bf16[80,640]{1,0:T(8,128)(2,1)S(1)}, u32[]{:S(2)}, u32[]{:S(2)}) collective-permute-start(bf16[80,640]{1,0:T(8,128)(2,1)S(1)} %get-tuple-element.44.refs_1_), channel_id=1, source_target_pairs={{0,16},{1,2},{2,1},{3,11},{4,20},{5,6},{6,5},{7,15},{8,24},{9,10},... | collective-permute-start | bytes 307208 | tf_op jit(solution)/shard_map/ppermute | solution.py:31
  31.0 6.0 %collective-permute-start.13 = (bf16[80,640]{1,0:T(8,128)(2,1)S(1)}, bf16[80,640]{1,0:T(8,128)(2,1)S(1)}, u32[]{:S(2)}, u32[]{:S(2)}) collective-permute-start(bf16[80,640]{1,0:T(8,128)(2,1)S(1)} %get-tuple-element.37.refs_2_), channel_id=1, source_target_pairs={{0,16},{1,2},{2,1},{3,11},{4,20},{5,6},{6,5},{7,15},{8,24},{9,10},... | collective-permute-start | bytes 307208 | tf_op jit(solution)/shard_map/ppermute | solution.py:31
  32.8 5.8 %collective-permute-start.20 = (bf16[80,640]{1,0:T(8,128)(2,1)S(1)}, bf16[80,640]{1,0:T(8,128)(2,1)S(1)}, u32[]{:S(2)}, u32[]{:S(2)}) collective-permute-start(bf16[80,640]{1,0:T(8,128)(2,1)S(1)} %get-tuple-element.45.refs_3_), channel_id=1, source_target_pairs={{0,16},{1,2},{2,1},{3,11},{4,20},{5,6},{6,5},{7,15},{8,24},{9,10},... | collective-permute-start | bytes 307208 | tf_op jit(solution)/shard_map/ppermute | solution.py:31
  33.6 7.7 %collective-permute-start.18 = (bf16[80,640]{1,0:T(8,128)(2,1)S(1)}, bf16[80,640]{1,0:T(8,128)(2,1)S(1)}, u32[]{:S(2)}, u32[]{:S(2)}) collective-permute-start(bf16[80,640]{1,0:T(8,128)(2,1)S(1)} %collective-permute-done.16.refs_0_), channel_id=1, source_target_pairs={{0,1},{1,0},{2,3},{3,2},{4,5},{5,4},{6,7},{7,6},{8,9},{9,8},{10,11... | collective-permute-start | bytes 307208 | tf_op jit(solution)/shard_map/ppermute | solution.py:31
  36.0 5.2 %collective-permute-start.19 = (bf16[80,640]{1,0:T(8,128)(2,1)S(1)}, bf16[80,640]{1,0:T(8,128)(2,1)S(1)}, u32[]{:S(2)}, u32[]{:S(2)}) collective-permute-start(bf16[80,640]{1,0:T(8,128)(2,1)S(1)} %collective-permute-done.17.refs_1_), channel_id=1, source_target_pairs={{0,1},{1,0},{2,3},{3,2},{4,5},{5,4},{6,7},{7,6},{8,9},{9,8},{10,11... | collective-permute-start | bytes 307208 | tf_op jit(solution)/shard_map/ppermute | solution.py:31
  37.0 5.3 %collective-permute-start.14 = (bf16[80,640]{1,0:T(8,128)(2,1)S(1)}, bf16[80,640]{1,0:T(8,128)(2,1)S(1)}, u32[]{:S(2)}, u32[]{:S(2)}) collective-permute-start(bf16[80,640]{1,0:T(8,128)(2,1)S(1)} %collective-permute-done.13.refs_0_), channel_id=1, source_target_pairs={{0,1},{1,0},{2,3},{3,2},{4,5},{5,4},{6,7},{7,6},{8,9},{9,8},{10,11... | collective-permute-start | bytes 307208 | tf_op jit(solution)/shard_map/ppermute | solution.py:31
  38.6 4.7 %collective-permute-start.21 = (bf16[80,640]{1,0:T(8,128)(2,1)S(1)}, bf16[80,640]{1,0:T(8,128)(2,1)S(1)}, u32[]{:S(2)}, u32[]{:S(2)}) collective-permute-start(bf16[80,640]{1,0:T(8,128)(2,1)S(1)} %collective-permute-done.20.refs_0_), channel_id=1, source_target_pairs={{0,1},{1,0},{2,3},{3,2},{4,5},{5,4},{6,7},{7,6},{8,9},{9,8},{10,11... | collective-permute-start | bytes 307208 | tf_op jit(solution)/shard_map/ppermute | solution.py:31
  (1 other events, 10.4 us)

commit v6 on v4

--- a/solution.py
+++ b/solution.py
@@ -21,12 +21,12 @@
     return lax.ppermute(array, ENERGY, [(i, i ^ mask) for i in range(devices)])
 
 
-def swap_slabs(array, slab_to):
+def swap_slabs(array, slab_to, idle=1):
     devices, slabs = lax.axis_size(ENERGY), lax.axis_size(SLAB)
     pairs = []
     for e in range(devices):
         for s in range(slabs):
-            to = (e, slab_to[s]) if s in slab_to else (e ^ 1, s)
+            to = (e, slab_to[s]) if s in slab_to else (e ^ idle, s)
             pairs.append((e * slabs + s, to[0] * slabs + to[1]))
     return lax.ppermute(array, (ENERGY, SLAB), pairs)
 
@@ -200,8 +200,10 @@
             ref[...] = state[i * rows : (i + 1) * rows]
 
 
-def first_kernel(link_ref, turned_ref, own_ref, came_ref, *out_refs):
-    carry_in(lax.axis_index(SLAB) % 2 == 1, link_ref, turned_ref, own_ref[...], came_ref[...], out_refs)
+def first_kernel(last_pair, link_ref, turned_ref, own_ref, came_ref, *out_refs):
+    slab = lax.axis_index(SLAB)
+    turn = jnp.logical_and(slab % 2 == 1, slab // 2 < last_pair)
+    carry_in(turn, link_ref, turned_ref, own_ref[...], came_ref[...], out_refs)
 
 
 def arrived(refs):
@@ -215,53 +217,59 @@
     carry_in(lax.axis_index(SLAB) // 2 == pair, link_ref, turned_ref, joined(state), arrived(came), outs)
 
 
-def base_kernel(stack_ref, first_ref, second_ref, re_ref, *refs):
-    *im_refs, out_ref = refs
-    re = dot(stack_ref[...], unpacked(re_ref[...]))
-    im = dot(stack_ref[...], unpacked(joined(im_refs)))
+def base_kernel(last_pair, link_ref, turned_ref, stack_ref, first_ref, second_ref, *refs):
+    *state, came_re_ref, came_im_ref, out_ref, re_ref, im_ref = refs
+    slab = lax.axis_index(SLAB)
+    turn = jnp.logical_and(slab % 2 == 1, slab // 2 == last_pair)
+    for parts, came_ref, ref in ((state[:2], came_re_ref, re_ref), (state[2:], came_im_ref, im_ref)):
+        own = unpacked(joined(parts))
+
+        @pl.when(turn)
+        def _():
+            ref[...] = (own.astype(jnp.float32) + moved(link_ref, turned_ref, unpacked(came_ref[...]))).astype(jnp.bfloat16)
+
+        @pl.when(jnp.logical_not(turn))
+        def _():
+            ref[...] = own
+
+    re, im = dot(stack_ref[...], re_ref[...]), dot(stack_ref[...], im_ref[...])
     size = re.shape[1]
     left_re = (re[:size] - im[size:]).astype(jnp.bfloat16)
     left_im = (im[:size] + re[size:]).astype(jnp.bfloat16)
     out_ref[...] = dot(left_re, first_ref[...]) + dot(left_im, second_ref[...])
 
 
-def early_kernel(pair, far_stack_ref, far_first_ref, far_second_ref, half_ref, base_ref, *refs):
-    *came, out_ref, left_ref = refs
-    turn = lax.axis_index(SLAB) // 2 == pair
-
-    @pl.when(turn)
-    def _():
-        left = dot(far_stack_ref[...], unpacked(arrived(came[::2]))).astype(jnp.bfloat16)
-        size = left.shape[1]
-        out_ref[...] = base_ref[...] + dot(left[:size], far_first_ref[...]) + dot(left[size:], far_second_ref[...])
-        left_ref[...] = dot(half_ref[...], unpacked(arrived(came[1::2])))
-
-    @pl.when(jnp.logical_not(turn))
-    def _():
-        out_ref[...] = base_ref[...]
-
-
-def late_kernel(pair, far_first_ref, far_second_ref, half_ref, early_ref, early_left_ref, *refs):
-    *came, out_ref, left_ref, result_ref, sems = refs
+def left_kernel(pair, matrix_ref, *refs):
+    *came, out_ref = refs
+
+    @pl.when(lax.axis_index(SLAB) // 2 == pair)
+    def _():
+        out_ref[...] = dot(matrix_ref[...], unpacked(arrived(came)))
+
+
+def late_kernel(pair, far_first_ref, far_second_ref, half_ref, base_ref, re_ref, im_ref, *refs):
+    *came, out_ref, left_re_ref, left_im_ref, result_ref, sems = refs
     size, width = result_ref.shape
     turn = lax.axis_index(SLAB) // 2 == pair
     cut = width // 256 * 128 if width % 128 == 0 else width // 2
 
     @pl.when(turn)
     def _():
-        left_ref[...] = (early_left_ref[...] + dot(half_ref[...], unpacked(arrived(came)))).astype(jnp.bfloat16)
+        im = im_ref[...] + dot(half_ref[...], unpacked(arrived(came)))
+        left_re_ref[...] = (re_ref[:size] - im[size:]).astype(jnp.bfloat16)
+        left_im_ref[...] = (im[:size] + re_ref[size:]).astype(jnp.bfloat16)
 
     copies = []
     for n, block in enumerate((slice(0, cut), slice(cut, width))):
 
         @pl.when(turn)
         def _():
-            late = dot(left_ref[:size], far_second_ref[:, block]) - dot(left_ref[size:], far_first_ref[:, block])
-            result_ref[:, block] = (early_ref[:, block] + late).astype(jnp.bfloat16)
+            late = dot(left_re_ref[...], far_first_ref[:, block]) + dot(left_im_ref[...], far_second_ref[:, block])
+            result_ref[:, block] = (base_ref[:, block] + late).astype(jnp.bfloat16)
 
         @pl.when(jnp.logical_not(turn))
         def _():
-            result_ref[:, block] = early_ref[:, block].astype(jnp.bfloat16)
+            result_ref[:, block] = base_ref[:, block].astype(jnp.bfloat16)
 
         copy = pltpu.make_async_copy(result_ref.at[:, block], out_ref.at[:, block], sems.at[n])
         copy.start()
@@ -311,35 +319,45 @@
     turned, step, turned_step, *base, far_stack, far_first, far_second, half_a, half_b = prepared
     came_re = swap_slabs(own_re, other_in_pair)
     came_im = swap_slabs(own_im, other_in_pair)
-    part = (own_re.shape, own_re.dtype)
+    part = ((size // 2, width), own_im.dtype)
     halves = [((size // 4, width), own_im.dtype)] * 2
     total = [((size, width), jnp.float32)]
-    re = call(first_kernel, [part], [link, turned, own_re, came_re])
-    im = call(first_kernel, halves, [link, turned, own_im, came_im])
+    first = functools.partial(first_kernel, last_pair)
+    re = call(first, halves, [link, turned, own_re, came_re])
+    im = call(first, halves, [link, turned, own_im, came_im])
 
     for s in range(1, slabs - 1, 2):
         pair = (s + 1) // 2
         near, far = {s: s + 1, s + 1: s}, {s + 1: s + 2, s + 2: s + 1}
-        near_re = [swap_slabs(x, near) for x in re]
-        near_im = [swap_slabs(x, near) for x in im]
+        near_re = [swap_slabs(x, near, 2) for x in re]
+        near_im = [swap_slabs(x, near, 2) for x in im]
+        if pair == last_pair:
+            near_im[1], came_re, came_im = lax.optimization_barrier((near_im[1], came_re, came_im))
         far_re = [swap_slabs(x, far) for x in near_re]
         far_im = [swap_slabs(x, far) for x in near_im]
         if pair < last_pair:
             advance = functools.partial(advance_kernel, pair)
-            re = call(advance, [part], [step, turned_step, *re, *near_re, *far_re])
+            re = call(advance, halves, [step, turned_step, *re, *near_re, *far_re])
             im = call(advance, halves, [step, turned_step, *im, *near_im, *far_im])
-    (out,) = call(base_kernel, total, [*base, *re, *im])
-    early = [far_stack, far_first, far_second, half_a, out, near_re[0], near_im[0], far_re[0], far_im[0]]
-    left = ((2 * size, size), jnp.float32)
-    out, left = call(functools.partial(early_kernel, last_pair), [*total, left], early)
-    given = [far_first, far_second, half_b, out, left, near_im[1], far_im[1]]
+    total = [((size, width), jnp.float32)]
+    given = [link, turned, *base, *re, *im, came_re, came_im]
+    scratch = [pltpu.VMEM(link.shape, link.dtype)] * 2
+    (out,) = call(functools.partial(base_kernel, last_pair), total, given, scratch)
+    left = functools.partial(left_kernel, last_pair)
+    products = [((2 * size, size), jnp.float32)]
+    far_re[0], out = lax.optimization_barrier((far_re[0], out))
+    (left_re,) = call(left, products, [far_stack, *near_re, *far_re])
+    far_im[0], left_re = lax.optimization_barrier((far_im[0], left_re))
+    (left_im,) = call(left, products, [half_a, near_im[0], far_im[0]])
+    given = [far_first, far_second, half_b, out, left_re, left_im, near_im[1], far_im[1]]
     out = pl.pallas_call(
         functools.partial(late_kernel, last_pair),
         out_shape=jax.ShapeDtypeStruct((size, width), jnp.bfloat16),
         in_specs=[WHOLE] * len(given),
         out_specs=pl.BlockSpec(memory_space=pl.ANY),
         scratch_shapes=[
-            pltpu.VMEM((2 * size, size), jnp.bfloat16),
+            pltpu.VMEM((size, size), jnp.bfloat16),
+            pltpu.VMEM((size, size), jnp.bfloat16),
             pltpu.VMEM((size, width), jnp.bfloat16),
             pltpu.SemaphoreType.DMA((2,)),
         ],

time: 47.8 us -> 44.4 us (0.929)
  waiting for transfers between devices: 21.9 us -> 13.7 us
  starting transfers between devices: 15.7 us -> 20.3 us
    ppermute x9 -> x11, waiting for transfers between devices: 12.5 us -> 5.19 us  [swap_slabs(): return lax.ppermute(array, (ENERGY, SLAB), pairs)]
    ppermute x9 -> x11, starting transfers between devices: 8.07 us -> 12.7 us  [swap_slabs(): return lax.ppermute(array, (ENERGY, SLAB), pairs)]
    ppermute x11, waiting for transfers between devices: 9.42 us -> 8.46 us  [swap_with(): return lax.ppermute(array, ENERGY, [(i, i ^ mask) for i in range(devices)])]
    pallas_call x6 -> x7, Pallas kernels: 5.37 us -> 5.29 us  [call(): pl.pallas_call(kernel, out_shape=outs, in_specs=[WHOLE] * len(given), out...]
  transfers between devices with their start and end apart: 20 -> 22, of which waited for: 14 -> 15; matrix products, arithmetic and copies ran while one was open for 3% -> 3% of each run, Pallas kernels for 14% -> 15%
where the time goes in v6:
time: 44.4 us; the launch traced here: 44.1 us
  starting transfers between devices  20.3 us (46%)
  waiting for transfers between devices  13.7 us (31%)
  Pallas kernels  8.67 us (20%)
  local copies, waits for them, and re-layouts  1.18 us (3%)
    ppermute x11, starting transfers between devices, swap_slabs(): return lax.ppermute(array, (ENERGY, SLAB), pairs)  12.7 us
    ppermute x11, waiting for transfers between devices, swap_with(): return lax.ppermute(array, ENERGY, [(i, i ^ mask) for i in range(devices)])  8.46 us
    ppermute x11, starting transfers between devices, swap_with(): return lax.ppermute(array, ENERGY, [(i, i ^ mask) for i in range(devices)])  7.63 us
    pallas_call x7, Pallas kernels, call(): pl.pallas_call(kernel, out_shape=outs, in_specs=[WHOLE] * len(given), out...  5.29 us
    ppermute x11, waiting for transfers between devices, swap_slabs(): return lax.ppermute(array, (ENERGY, SLAB), pairs)  5.19 us
    pallas_call x1, Pallas kernels, local(): pl.pallas_call(functools.partial(late_kernel, last_pair), out_shape=jax.S...  1.96 us
    pallas_call x1, Pallas kernels, convolve(): pl.pallas_call(functools.partial(conv_kernel, chips), out_shape=pltpu.VME...  1.42 us
    dynamic_slice x1, local copies, waits for them, and re-layouts, local(): lax.dynamic_slice(lesser, (rows * (chip ^ j), 0), (rows, width))  1.13 us
  transfers between devices with their start and end apart: 22, of which 15 were waited for; matrix products, arithmetic and copies ran while one was open for 3% of the time, Pallas kernels for 15%

profile of v6, /device:TPU:16, one launch (start us, length us, event | category | flops | bytes accessed | tf_op | source)
XLA Modules:
  0.0 44.1 jit_solution(3256509979996278350)
XLA Ops:
  0.0 1.1 %dynamic-slice_bitcast_fusion = (bf16[80,640]{1,0:T(8,128)(2,1)S(1)}, bf16[80,640]{1,0:T(8,128)(2,1)S(1)}, bf16[80,640]{1,0:T(8,128)(2,1)S(1)}, bf16[80,640]{1,0:T(8,128)(2,1)S(1)}) fusion(bf16[1,1,320,640]{3,2,1,0:T(8,128)(2,1)} %param.4, s32[]{:T(128)S(6)} %select_n.43, s32[]{:T(128)S(6)} %select_n.41, s32[]{:T(128)S(6)} %select_n.40, s32[]{:T(128)S(6)} %select_n.42), kind=kLoop, calls=%fused_computation.6 | loop fusion | bytes 819216 | tf_op jit(solution)/shard_map/dynamic_slice | solution.py:297
  1.1 1.6 %collective-permute-start.1 = (bf16[80,640]{1,0:T(8,128)(2,1)S(1)}, bf16[80,640]{1,0:T(8,128)(2,1)S(1)}, u32[]{:S(2)}, u32[]{:S(2)}) collective-permute-start(bf16[80,640]{1,0:T(8,128)(2,1)S(1)} %get-tuple-element.65), channel_id=1, source_target_pairs={{0,8},{4,12},{8,0},{12,4},{16,24},{20,28},{24,16},{28,20},{1,9},{5... | collective-permute-start | bytes 307208 | tf_op jit(solution)/shard_map/ppermute | solution.py:21
  2.7 1.5 %collective-permute-start.2 = (bf16[80,640]{1,0:T(8,128)(2,1)S(1)}, bf16[80,640]{1,0:T(8,128)(2,1)S(1)}, u32[]{:S(2)}, u32[]{:S(2)}) collective-permute-start(bf16[80,640]{1,0:T(8,128)(2,1)S(1)} %get-tuple-element.67), channel_id=1, source_target_pairs={{0,16},{4,20},{8,24},{12,28},{16,0},{20,4},{24,8},{28,12},{1,17},{... | collective-permute-start | bytes 307208 | tf_op jit(solution)/shard_map/ppermute | solution.py:21
  4.7 1.7 %collective-permute-done.1.refs_1_ = bf16[80,640]{1,0:T(8,128)(2,1)S(1)} collective-permute-done((bf16[80,640]{1,0:T(8,128)(2,1)S(1)}, bf16[80,640]{1,0:T(8,128)(2,1)S(1)}, u32[]{:S(2)}, u32[]{:S(2)}) %collective-permute-start.1) | collective-permute-done | bytes 102432 | tf_op jit(solution)/shard_map/ppermute | solution.py:21
  6.4 1.6 %collective-permute-start.8 = (bf16[320,320]{1,0:T(8,128)(2,1)}, bf16[320,320]{1,0:T(8,128)(2,1)S(1)}, u32[]{:S(2)}, u32[]{:S(2)}) collective-permute-start(bf16[320,320]{1,0:T(8,128)(2,1)} %bitcast.20), channel_id=1, source_target_pairs={{0,1},{1,0},{2,3},{3,2},{4,5},{5,4},{6,7},{7,6},{8,9},{9,8},{10,11... | collective-permute-start | bytes 614408 | tf_op jit(solution)/shard_map/ppermute | solution.py:31
  8.9 1.0 %collective-permute-done.3.refs_3_ = bf16[80,640]{1,0:T(8,128)(2,1)S(1)} collective-permute-done((bf16[80,640]{1,0:T(8,128)(2,1)S(1)}, bf16[80,640]{1,0:T(8,128)(2,1)S(1)}, u32[]{:S(2)}, u32[]{:S(2)}) %collective-permute-start.3) | collective-permute-done | bytes 102432 | tf_op jit(solution)/shard_map/ppermute | solution.py:21
  11.3 1.4 %shard_map.46.refs_0_ = bf16[4,80,640]{2,1,0:T(8,128)(2,1)S(1)} custom-call(bf16[8,80,640]{2,1,0:T(8,128)(2,1)S(1)} %pad_maximum_fusion.inter_ref, bf16[80,640]{1,0:T(8,128)(2,1)S(1)} %get-tuple-element.66.refs_0_, bf16[80,640]{1,0:T(8,128)(2,1)S(1)} %collective-permute-done.1.refs_1_, bf16[80,640]{1,0:T(8,128)(2,1)S(1)} %collective-permute-done.2.refs_2_, ...), custom_call_target="tpu_custom_call" | custom-call | flops 13107200 | tf_op jit(solution)/shard_map/pallas_call | solution.py:99
  12.8 1.4 %collective-permute-done.8.before_ref = bf16[320,320]{1,0:T(8,128)(2,1)S(1)} collective-permute-done((bf16[320,320]{1,0:T(8,128)(2,1)}, bf16[320,320]{1,0:T(8,128)(2,1)S(1)}, u32[]{:S(2)}, u32[]{:S(2)}) %collective-permute-start.8) | collective-permute-done | bytes 204832 | tf_op jit(solution)/shard_map/ppermute | solution.py:31
  14.2 1.6 %collective-permute-start.10 = (bf16[80,640]{1,0:T(8,128)(2,1)S(1)}, bf16[80,640]{1,0:T(8,128)(2,1)S(1)}, u32[]{:S(2)}, u32[]{:S(2)}) collective-permute-start(bf16[80,640]{1,0:T(8,128)(2,1)S(1)} %get-tuple-element.62), channel_id=1, source_target_pairs={{0,16},{4,20},{8,24},{12,28},{16,0},{20,4},{24,8},{28,12},{1,17},{... | collective-permute-start | bytes 307208 | tf_op jit(solution)/shard_map/ppermute | solution.py:21
  15.8 1.4 %collective-permute-start.11 = (bf16[80,640]{1,0:T(8,128)(2,1)S(1)}, bf16[80,640]{1,0:T(8,128)(2,1)S(1)}, u32[]{:S(2)}, u32[]{:S(2)}) collective-permute-start(bf16[80,640]{1,0:T(8,128)(2,1)S(1)} %get-tuple-element.61), channel_id=1, source_target_pairs={{0,24},{4,28},{8,16},{12,20},{16,8},{20,12},{24,0},{28,4},{1,25},{... | collective-permute-start | bytes 307208 | tf_op jit(solution)/shard_map/ppermute | solution.py:21
  17.8 2.3 %collective-permute-done.10.refs_2_ = bf16[80,640]{1,0:T(8,128)(2,1)S(1)} collective-permute-done((bf16[80,640]{1,0:T(8,128)(2,1)S(1)}, bf16[80,640]{1,0:T(8,128)(2,1)S(1)}, u32[]{:S(2)}, u32[]{:S(2)}) %collective-permute-start.10) | collective-permute-done | bytes 102432 | tf_op jit(solution)/shard_map/ppermute | solution.py:21
  20.0 1.4 %collective-permute-done.11.refs_3_ = bf16[80,640]{1,0:T(8,128)(2,1)S(1)} collective-permute-done((bf16[80,640]{1,0:T(8,128)(2,1)S(1)}, bf16[80,640]{1,0:T(8,128)(2,1)S(1)}, u32[]{:S(2)}, u32[]{:S(2)}) %collective-permute-start.11) | collective-permute-done | bytes 102432 | tf_op jit(solution)/shard_map/ppermute | solution.py:21
  22.1 1.6 %collective-permute-start.12 = (bf16[160,640]{1,0:T(8,128)(2,1)S(1)}, bf16[160,640]{1,0:T(8,128)(2,1)S(1)}, u32[]{:S(2)}, u32[]{:S(2)}) collective-permute-start(bf16[160,640]{1,0:T(8,128)(2,1)S(1)} %get-tuple-element.41.own_ref), channel_id=1, source_target_pairs={{0,1},{1,0},{2,3},{3,2},{4,5},{5,4},{6,7},{7,6},{8,9},{9,8},{10,11... | collective-permute-start | bytes 614408 | tf_op jit(solution)/shard_map/ppermute | solution.py:31
  24.2 2.5 %shard_map.48 = (bf16[320,320]{1,0:T(8,128)(2,1)S(1)}, bf16[320,320]{1,0:T(8,128)(2,1)}, bf16[320,320]{1,0:T(8,128)(2,1)}, bf16[640,320]{1,0:T(8,128)(2,1)S(1)},...) custom-call(bf16[320,320]{1,0:T(8,128)(2,1)S(1)} %bitcast.21, ...), custom_call_target="tpu_custom_call" | custom-call | tf_op jit(solution)/shard_map/pallas_call | solution.py:36
  26.7 2.1 %collective-permute-done.12.came_ref.refs_4_ = bf16[160,640]{1,0:T(8,128)(2,1)S(1)} collective-permute-done((bf16[160,640]{1,0:T(8,128)(2,1)S(1)}, bf16[160,640]{1,0:T(8,128)(2,1)S(1)}, u32[]{:S(2)}, u32[]{:S(2)}) %collective-permute-start.12) | collective-permute-done | bytes 204832 | tf_op jit(solution)/shard_map/ppermute | solution.py:31
  28.8 1.2 %collective-permute-start.13 = (bf16[80,640]{1,0:T(8,128)(2,1)S(1)}, bf16[80,640]{1,0:T(8,128)(2,1)S(1)}, u32[]{:S(2)}, u32[]{:S(2)}) collective-permute-start(bf16[80,640]{1,0:T(8,128)(2,1)S(1)} %get-tuple-element.42.refs_0_), channel_id=1, source_target_pairs={{0,8},{1,2},{2,1},{3,11},{4,12},{5,6},{6,5},{7,15},{8,0},{9,10},{1... | collective-permute-start | bytes 307208 | tf_op jit(solution)/shard_map/ppermute | solution.py:31
  30.0 0.9 %collective-permute-start.19 = (bf16[80,640]{1,0:T(8,128)(2,1)S(1)}, bf16[80,640]{1,0:T(8,128)(2,1)S(1)}, u32[]{:S(2)}, u32[]{:S(2)}) collective-permute-start(bf16[80,640]{1,0:T(8,128)(2,1)S(1)} %get-tuple-element.46.refs_1_), channel_id=1, source_target_pairs={{0,8},{1,2},{2,1},{3,11},{4,12},{5,6},{6,5},{7,15},{8,0},{9,10},{1... | collective-permute-start | bytes 307208 | tf_op jit(solution)/shard_map/ppermute | solution.py:31
  31.0 1.8 %collective-permute-start.17 = (bf16[80,640]{1,0:T(8,128)(2,1)S(1)}, bf16[80,640]{1,0:T(8,128)(2,1)S(1)}, u32[]{:S(2)}, u32[]{:S(2)}) collective-permute-start(bf16[80,640]{1,0:T(8,128)(2,1)S(1)} %get-tuple-element.48.refs_2_), channel_id=1, source_target_pairs={{0,8},{1,2},{2,1},{3,11},{4,12},{5,6},{6,5},{7,15},{8,0},{9,10},{1... | collective-permute-start | bytes 307208 | tf_op jit(solution)/shard_map/ppermute | solution.py:31
  33.6 1.6 %collective-permute-start.14 = (bf16[80,640]{1,0:T(8,128)(2,1)S(1)}, bf16[80,640]{1,0:T(8,128)(2,1)S(1)}, u32[]{:S(2)}, u32[]{:S(2)}) collective-permute-start(bf16[80,640]{1,0:T(8,128)(2,1)S(1)} %collective-permute-done.13.refs_0_), channel_id=1, source_target_pairs={{0,4},{1,5},{2,3},{3,2},{4,0},{5,1},{6,7},{7,6},{8,12},{9,13},{10,... | collective-permute-start | bytes 307208 | tf_op jit(solution)/shard_map/ppermute | solution.py:31
  35.1 1.2 %collective-permute-start.20 = (bf16[80,640]{1,0:T(8,128)(2,1)S(1)}, bf16[80,640]{1,0:T(8,128)(2,1)S(1)}, u32[]{:S(2)}, u32[]{:S(2)}) collective-permute-start(bf16[80,640]{1,0:T(8,128)(2,1)S(1)} %collective-permute-done.19.refs_1_), channel_id=1, source_target_pairs={{0,4},{1,5},{2,3},{3,2},{4,0},{5,1},{6,7},{7,6},{8,12},{9,13},{10,... | collective-permute-start | bytes 307208 | tf_op jit(solution)/shard_map/ppermute | solution.py:31
  36.3 1.1 %collective-permute-start.18 = (bf16[80,640]{1,0:T(8,128)(2,1)S(1)}, bf16[80,640]{1,0:T(8,128)(2,1)S(1)}, u32[]{:S(2)}, u32[]{:S(2)}) collective-permute-start(bf16[80,640]{1,0:T(8,128)(2,1)S(1)} %collective-permute-done.17.refs_0_), channel_id=1, source_target_pairs={{0,4},{1,5},{2,3},{3,2},{4,0},{5,1},{6,7},{7,6},{8,12},{9,13},{10,... | collective-permute-start | bytes 307208 | tf_op jit(solution)/shard_map/ppermute | solution.py:31
  37.5 1.0 %collective-permute-start.21 = (bf16[80,640]{1,0:T(8,128)(2,1)S(1)}, bf16[80,640]{1,0:T(8,128)(2,1)S(1)}, u32[]{:S(2)}, u32[]{:S(2)}) collective-permute-start(bf16[80,640]{1,0:T(8,128)(2,1)S(1)} %collective-permute-done.16.refs_0_), channel_id=1, source_target_pairs={{0,4},{1,5},{2,3},{3,2},{4,0},{5,1},{6,7},{7,6},{8,12},{9,13},{10,... | collective-permute-start | bytes 307208 | tf_op jit(solution)/shard_map/ppermute | solution.py:31
  38.5 1.6 %shard_map.51.base_ref = f32[320,640]{1,0:T(8,128)S(1)} custom-call(bf16[320,320]{1,0:T(8,128)(2,1)S(1)} %bitcast.24, bf16[320,320]{1,0:T(8,128)(2,1)S(1)} %get-tuple-element.40.turned_ref, bf16[640,320]{1,0:T(8,128)(2,1)S(1)} %get-tuple-element.43.stack_ref, bf16[320,640]{1,0:T(8,128)(2,1)S(1)} %get-tuple-element.44.first_ref, ...), custom_call_target="tpu_custom_call" | custom-call | tf_op jit(solution)/shard_map/pallas_call | solution.py:36
  42.2 2.0 %shard_map.54 = bf16[320,640]{1,0:T(8,128)(2,1)} custom-call(bf16[320,640]{1,0:T(8,128)(2,1)S(1)} %get-tuple-element.37.far_first_ref, bf16[320,640]{1,0:T(8,128)(2,1)S(1)} %get-tuple-element.38.far_second_ref, bf16[640,160]{1,0:T(8,128)(2,1)S(1)} %get-tuple-element.39.half_ref, f32[320,640]{1,0:T(8,128)S(1)} %shard_map.51.base_ref, ...), custom_call_target="tpu_custom_call" | custom-call | tf_op jit(solution)/shard_map/pallas_call | solution.py:353
  (39 shorter events, 7.4 us)
Async XLA Ops:
  0.0 9.9 %collective-permute-start = (bf16[8,40,640]{2,1,0:T(8,128)(2,1)}, bf16[8,40,640]{2,1,0:T(8,128)(2,1)S(1)}, u32[]{:S(2)}, u32[]{:S(2)}) collective-permute-start(bf16[8,40,640]{2,1,0:T(8,128)(2,1)} %bitcast.26), channel_id=1, source_target_pairs={{0,4},{4,0},{8,12},{12,8},{16,20},{20,16},{24,28},{28,24},{1,5},{5... | collective-permute-start | bytes 1228808 | tf_op jit(solution)/shard_map/ppermute | solution.py:21
  1.1 5.3 %collective-permute-start.1 = (bf16[80,640]{1,0:T(8,128)(2,1)S(1)}, bf16[80,640]{1,0:T(8,128)(2,1)S(1)}, u32[]{:S(2)}, u32[]{:S(2)}) collective-permute-start(bf16[80,640]{1,0:T(8,128)(2,1)S(1)} %get-tuple-element.65), channel_id=1, source_target_pairs={{0,8},{4,12},{8,0},{12,4},{16,24},{20,28},{24,16},{28,20},{1,9},{5... | collective-permute-start | bytes 307208 | tf_op jit(solution)/shard_map/ppermute | solution.py:21
  2.7 6.2 %collective-permute-start.2 = (bf16[80,640]{1,0:T(8,128)(2,1)S(1)}, bf16[80,640]{1,0:T(8,128)(2,1)S(1)}, u32[]{:S(2)}, u32[]{:S(2)}) collective-permute-start(bf16[80,640]{1,0:T(8,128)(2,1)S(1)} %get-tuple-element.67), channel_id=1, source_target_pairs={{0,16},{4,20},{8,24},{12,28},{16,0},{20,4},{24,8},{28,12},{1,17},{... | collective-permute-start | bytes 307208 | tf_op jit(solution)/shard_map/ppermute | solution.py:21
  4.2 5.6 %collective-permute-start.3 = (bf16[80,640]{1,0:T(8,128)(2,1)S(1)}, bf16[80,640]{1,0:T(8,128)(2,1)S(1)}, u32[]{:S(2)}, u32[]{:S(2)}) collective-permute-start(bf16[80,640]{1,0:T(8,128)(2,1)S(1)} %get-tuple-element.64), channel_id=1, source_target_pairs={{0,24},{4,28},{8,16},{12,20},{16,8},{20,12},{24,0},{28,4},{1,25},{... | collective-permute-start | bytes 307208 | tf_op jit(solution)/shard_map/ppermute | solution.py:21
  4.7 5.8 %collective-permute-start.4 = (bf16[80,640]{1,0:T(8,128)(2,1)S(1)}, bf16[80,640]{1,0:T(8,128)(2,1)S(1)}, u32[]{:S(2)}, u32[]{:S(2)}) collective-permute-start(bf16[80,640]{1,0:T(8,128)(2,1)S(1)} %get-tuple-element.66.refs_0_), channel_id=1, source_target_pairs={{0,4},{4,0},{8,12},{12,8},{16,20},{20,16},{24,28},{28,24},{1,5},{5... | collective-permute-start | bytes 307208 | tf_op jit(solution)/shard_map/ppermute | solution.py:21
  6.4 7.7 %collective-permute-start.8 = (bf16[320,320]{1,0:T(8,128)(2,1)}, bf16[320,320]{1,0:T(8,128)(2,1)S(1)}, u32[]{:S(2)}, u32[]{:S(2)}) collective-permute-start(bf16[320,320]{1,0:T(8,128)(2,1)} %bitcast.20), channel_id=1, source_target_pairs={{0,1},{1,0},{2,3},{3,2},{4,5},{5,4},{6,7},{7,6},{8,9},{9,8},{10,11... | collective-permute-start | bytes 614408 | tf_op jit(solution)/shard_map/ppermute | solution.py:31
  8.9 1.7 %collective-permute-start.5 = (bf16[80,640]{1,0:T(8,128)(2,1)S(1)}, bf16[80,640]{1,0:T(8,128)(2,1)S(1)}, u32[]{:S(2)}, u32[]{:S(2)}) collective-permute-start(bf16[80,640]{1,0:T(8,128)(2,1)S(1)} %collective-permute-done.1.refs_1_), channel_id=1, source_target_pairs={{0,4},{4,0},{8,12},{12,8},{16,20},{20,16},{24,28},{28,24},{1,5},{5... | collective-permute-start | bytes 307208 | tf_op jit(solution)/shard_map/ppermute | solution.py:21
  9.9 1.3 %collective-permute-start.6 = (bf16[80,640]{1,0:T(8,128)(2,1)S(1)}, bf16[80,640]{1,0:T(8,128)(2,1)S(1)}, u32[]{:S(2)}, u32[]{:S(2)}) collective-permute-start(bf16[80,640]{1,0:T(8,128)(2,1)S(1)} %collective-permute-done.2.refs_2_), channel_id=1, source_target_pairs={{0,4},{4,0},{8,12},{12,8},{16,20},{20,16},{24,28},{28,24},{1,5},{5... | collective-permute-start | bytes 307208 | tf_op jit(solution)/shard_map/ppermute | solution.py:21
  9.9 1.5 %collective-permute-start.7 = (bf16[80,640]{1,0:T(8,128)(2,1)S(1)}, bf16[80,640]{1,0:T(8,128)(2,1)S(1)}, u32[]{:S(2)}, u32[]{:S(2)}) collective-permute-start(bf16[80,640]{1,0:T(8,128)(2,1)S(1)} %collective-permute-done.3.refs_3_), channel_id=1, source_target_pairs={{0,4},{4,0},{8,12},{12,8},{16,20},{20,16},{24,28},{28,24},{1,5},{5... | collective-permute-start | bytes 307208 | tf_op jit(solution)/shard_map/ppermute | solution.py:21
  12.7 11.4 %copy-start = (bf16[1,320,320]{2,1,0:T(8,128)(2,1)S(1)}, bf16[1,320,320]{2,1,0:T(8,128)(2,1)}, u32[]{:S(2)}) copy-start(bf16[1,320,320]{2,1,0:T(8,128)(2,1)} %param.7) | copy-start | bytes 614404
  12.8 11.4 %copy-start.1 = (bf16[1,1,320,640]{3,2,1,0:T(8,128)(2,1)S(1)}, bf16[1,1,320,640]{3,2,1,0:T(8,128)(2,1)}, u32[]{:S(2)}) copy-start(bf16[1,1,320,640]{3,2,1,0:T(8,128)(2,1)} %param.5) | copy-start | bytes 1228804
  14.2 5.8 %collective-permute-start.10 = (bf16[80,640]{1,0:T(8,128)(2,1)S(1)}, bf16[80,640]{1,0:T(8,128)(2,1)S(1)}, u32[]{:S(2)}, u32[]{:S(2)}) collective-permute-start(bf16[80,640]{1,0:T(8,128)(2,1)S(1)} %get-tuple-element.62), channel_id=1, source_target_pairs={{0,16},{4,20},{8,24},{12,28},{16,0},{20,4},{24,8},{28,12},{1,17},{... | collective-permute-start | bytes 307208 | tf_op jit(solution)/shard_map/ppermute | solution.py:21
  15.8 5.6 %collective-permute-start.11 = (bf16[80,640]{1,0:T(8,128)(2,1)S(1)}, bf16[80,640]{1,0:T(8,128)(2,1)S(1)}, u32[]{:S(2)}, u32[]{:S(2)}) collective-permute-start(bf16[80,640]{1,0:T(8,128)(2,1)S(1)} %get-tuple-element.61), channel_id=1, source_target_pairs={{0,24},{4,28},{8,16},{12,20},{16,8},{20,12},{24,0},{28,4},{1,25},{... | collective-permute-start | bytes 307208 | tf_op jit(solution)/shard_map/ppermute | solution.py:21
  17.2 4.7 %collective-permute-start.9 = (bf16[80,640]{1,0:T(8,128)(2,1)S(1)}, bf16[80,640]{1,0:T(8,128)(2,1)S(1)}, u32[]{:S(2)}, u32[]{:S(2)}) collective-permute-start(bf16[80,640]{1,0:T(8,128)(2,1)S(1)} %get-tuple-element.63), channel_id=1, source_target_pairs={{0,8},{4,12},{8,0},{12,4},{16,24},{20,28},{24,16},{28,20},{1,9},{5... | collective-permute-start | bytes 307208 | tf_op jit(solution)/shard_map/ppermute | solution.py:21
  22.1 6.7 %collective-permute-start.12 = (bf16[160,640]{1,0:T(8,128)(2,1)S(1)}, bf16[160,640]{1,0:T(8,128)(2,1)S(1)}, u32[]{:S(2)}, u32[]{:S(2)}) collective-permute-start(bf16[160,640]{1,0:T(8,128)(2,1)S(1)} %get-tuple-element.41.own_ref), channel_id=1, source_target_pairs={{0,1},{1,0},{2,3},{3,2},{4,5},{5,4},{6,7},{7,6},{8,9},{9,8},{10,11... | collective-permute-start | bytes 614408 | tf_op jit(solution)/shard_map/ppermute | solution.py:31
  23.7 7.3 %collective-permute-start.15 = (bf16[160,640]{1,0:T(8,128)(2,1)S(1)}, bf16[160,640]{1,0:T(8,128)(2,1)S(1)}, u32[]{:S(2)}, u32[]{:S(2)}) collective-permute-start(bf16[160,640]{1,0:T(8,128)(2,1)S(1)} %get-tuple-element.47.own_ref), channel_id=1, source_target_pairs={{0,1},{1,0},{2,3},{3,2},{4,5},{5,4},{6,7},{7,6},{8,9},{9,8},{10,11... | collective-permute-start | bytes 614408 | tf_op jit(solution)/shard_map/ppermute | solution.py:31
  28.8 4.7 %collective-permute-start.13 = (bf16[80,640]{1,0:T(8,128)(2,1)S(1)}, bf16[80,640]{1,0:T(8,128)(2,1)S(1)}, u32[]{:S(2)}, u32[]{:S(2)}) collective-permute-start(bf16[80,640]{1,0:T(8,128)(2,1)S(1)} %get-tuple-element.42.refs_0_), channel_id=1, source_target_pairs={{0,8},{1,2},{2,1},{3,11},{4,12},{5,6},{6,5},{7,15},{8,0},{9,10},{1... | collective-permute-start | bytes 307208 | tf_op jit(solution)/shard_map/ppermute | solution.py:31
  30.0 5.1 %collective-permute-start.19 = (bf16[80,640]{1,0:T(8,128)(2,1)S(1)}, bf16[80,640]{1,0:T(8,128)(2,1)S(1)}, u32[]{:S(2)}, u32[]{:S(2)}) collective-permute-start(bf16[80,640]{1,0:T(8,128)(2,1)S(1)} %get-tuple-element.46.refs_1_), channel_id=1, source_target_pairs={{0,8},{1,2},{2,1},{3,11},{4,12},{5,6},{6,5},{7,15},{8,0},{9,10},{1... | collective-permute-start | bytes 307208 | tf_op jit(solution)/shard_map/ppermute | solution.py:31
  31.0 5.3 %collective-permute-start.17 = (bf16[80,640]{1,0:T(8,128)(2,1)S(1)}, bf16[80,640]{1,0:T(8,128)(2,1)S(1)}, u32[]{:S(2)}, u32[]{:S(2)}) collective-permute-start(bf16[80,640]{1,0:T(8,128)(2,1)S(1)} %get-tuple-element.48.refs_2_), channel_id=1, source_target_pairs={{0,8},{1,2},{2,1},{3,11},{4,12},{5,6},{6,5},{7,15},{8,0},{9,10},{1... | collective-permute-start | bytes 307208 | tf_op jit(solution)/shard_map/ppermute | solution.py:31
  32.8 4.7 %collective-permute-start.16 = (bf16[80,640]{1,0:T(8,128)(2,1)S(1)}, bf16[80,640]{1,0:T(8,128)(2,1)S(1)}, u32[]{:S(2)}, u32[]{:S(2)}) collective-permute-start(bf16[80,640]{1,0:T(8,128)(2,1)S(1)} %get-tuple-element.49.refs_3_), channel_id=1, source_target_pairs={{0,8},{1,2},{2,1},{3,11},{4,12},{5,6},{6,5},{7,15},{8,0},{9,10},{1... | collective-permute-start | bytes 307208 | tf_op jit(solution)/shard_map/ppermute | solution.py:31
  33.6 6.5 %collective-permute-start.14 = (bf16[80,640]{1,0:T(8,128)(2,1)S(1)}, bf16[80,640]{1,0:T(8,128)(2,1)S(1)}, u32[]{:S(2)}, u32[]{:S(2)}) collective-permute-start(bf16[80,640]{1,0:T(8,128)(2,1)S(1)} %collective-permute-done.13.refs_0_), channel_id=1, source_target_pairs={{0,4},{1,5},{2,3},{3,2},{4,0},{5,1},{6,7},{7,6},{8,12},{9,13},{10,... | collective-permute-start | bytes 307208 | tf_op jit(solution)/shard_map/ppermute | solution.py:31
  35.1 5.0 %collective-permute-start.20 = (bf16[80,640]{1,0:T(8,128)(2,1)S(1)}, bf16[80,640]{1,0:T(8,128)(2,1)S(1)}, u32[]{:S(2)}, u32[]{:S(2)}) collective-permute-start(bf16[80,640]{1,0:T(8,128)(2,1)S(1)} %collective-permute-done.19.refs_1_), channel_id=1, source_target_pairs={{0,4},{1,5},{2,3},{3,2},{4,0},{5,1},{6,7},{7,6},{8,12},{9,13},{10,... | collective-permute-start | bytes 307208 | tf_op jit(solution)/shard_map/ppermute | solution.py:31
  36.3 4.7 %collective-permute-start.18 = (bf16[80,640]{1,0:T(8,128)(2,1)S(1)}, bf16[80,640]{1,0:T(8,128)(2,1)S(1)}, u32[]{:S(2)}, u32[]{:S(2)}) collective-permute-start(bf16[80,640]{1,0:T(8,128)(2,1)S(1)} %collective-permute-done.17.refs_0_), channel_id=1, source_target_pairs={{0,4},{1,5},{2,3},{3,2},{4,0},{5,1},{6,7},{7,6},{8,12},{9,13},{10,... | collective-permute-start | bytes 307208 | tf_op jit(solution)/shard_map/ppermute | solution.py:31
  37.5 4.7 %collective-permute-start.21 = (bf16[80,640]{1,0:T(8,128)(2,1)S(1)}, bf16[80,640]{1,0:T(8,128)(2,1)S(1)}, u32[]{:S(2)}, u32[]{:S(2)}) collective-permute-start(bf16[80,640]{1,0:T(8,128)(2,1)S(1)} %collective-permute-done.16.refs_0_), channel_id=1, source_target_pairs={{0,4},{1,5},{2,3},{3,2},{4,0},{5,1},{6,7},{7,6},{8,12},{9,13},{10,... | collective-permute-start | bytes 307208 | tf_op jit(solution)/shard_map/ppermute | solution.py:31
  (1 other events, 10.4 us)

commit v7 on v6

--- a/solution.py
+++ b/solution.py
@@ -251,7 +251,7 @@
     *came, out_ref, left_re_ref, left_im_ref, result_ref, sems = refs
     size, width = result_ref.shape
     turn = lax.axis_index(SLAB) // 2 == pair
-    cut = width // 256 * 128 if width % 128 == 0 else width // 2
+    cut = width // 256 * 256 if width > 256 else width // 2
 
     @pl.when(turn)
     def _():

time: 44.4 us -> 44.1 us (level)
  no operation moved by 1% of the time
where the time goes in v7:
time: 44.1 us; the launch traced here: 43.8 us
  starting transfers between devices  20.3 us (46%)
  waiting for transfers between devices  13.7 us (31%)
  Pallas kernels  8.37 us (19%)
  local copies, waits for them, and re-layouts  1.18 us (3%)
    ppermute x11, starting transfers between devices, swap_slabs(): return lax.ppermute(array, (ENERGY, SLAB), pairs)  12.7 us
    ppermute x11, waiting for transfers between devices, swap_with(): return lax.ppermute(array, ENERGY, [(i, i ^ mask) for i in range(devices)])  8.46 us
    ppermute x11, starting transfers between devices, swap_with(): return lax.ppermute(array, ENERGY, [(i, i ^ mask) for i in range(devices)])  7.63 us
    pallas_call x7, Pallas kernels, call(): pl.pallas_call(kernel, out_shape=outs, in_specs=[WHOLE] * len(given), out...  5.29 us
    ppermute x11, waiting for transfers between devices, swap_slabs(): return lax.ppermute(array, (ENERGY, SLAB), pairs)  5.19 us
    pallas_call x1, Pallas kernels, local(): pl.pallas_call(functools.partial(late_kernel, last_pair), out_shape=jax.S...  1.66 us
    pallas_call x1, Pallas kernels, convolve(): pl.pallas_call(functools.partial(conv_kernel, chips), out_shape=pltpu.VME...  1.42 us
    dynamic_slice x1, local copies, waits for them, and re-layouts, local(): lax.dynamic_slice(lesser, (rows * (chip ^ j), 0), (rows, width))  1.13 us
  transfers between devices with their start and end apart: 22, of which 15 were waited for; matrix products, arithmetic and copies ran while one was open for 3% of the time, Pallas kernels for 15%

profile of v7, /device:TPU:16, one launch (start us, length us, event | category | flops | bytes accessed | tf_op | source)
XLA Modules:
  0.0 43.8 jit_solution(4465823923988461645)
XLA Ops:
  0.0 1.1 %dynamic-slice_bitcast_fusion = (bf16[80,640]{1,0:T(8,128)(2,1)S(1)}, bf16[80,640]{1,0:T(8,128)(2,1)S(1)}, bf16[80,640]{1,0:T(8,128)(2,1)S(1)}, bf16[80,640]{1,0:T(8,128)(2,1)S(1)}) fusion(bf16[1,1,320,640]{3,2,1,0:T(8,128)(2,1)} %param.4, s32[]{:T(128)S(6)} %select_n.43, s32[]{:T(128)S(6)} %select_n.41, s32[]{:T(128)S(6)} %select_n.40, s32[]{:T(128)S(6)} %select_n.42), kind=kLoop, calls=%fused_computation.6 | loop fusion | bytes 819216 | tf_op jit(solution)/shard_map/dynamic_slice | solution.py:297
  1.1 1.6 %collective-permute-start.1 = (bf16[80,640]{1,0:T(8,128)(2,1)S(1)}, bf16[80,640]{1,0:T(8,128)(2,1)S(1)}, u32[]{:S(2)}, u32[]{:S(2)}) collective-permute-start(bf16[80,640]{1,0:T(8,128)(2,1)S(1)} %get-tuple-element.65), channel_id=1, source_target_pairs={{0,8},{4,12},{8,0},{12,4},{16,24},{20,28},{24,16},{28,20},{1,9},{5... | collective-permute-start | bytes 307208 | tf_op jit(solution)/shard_map/ppermute | solution.py:21
  2.7 1.5 %collective-permute-start.2 = (bf16[80,640]{1,0:T(8,128)(2,1)S(1)}, bf16[80,640]{1,0:T(8,128)(2,1)S(1)}, u32[]{:S(2)}, u32[]{:S(2)}) collective-permute-start(bf16[80,640]{1,0:T(8,128)(2,1)S(1)} %get-tuple-element.67), channel_id=1, source_target_pairs={{0,16},{4,20},{8,24},{12,28},{16,0},{20,4},{24,8},{28,12},{1,17},{... | collective-permute-start | bytes 307208 | tf_op jit(solution)/shard_map/ppermute | solution.py:21
  4.7 1.7 %collective-permute-done.1.refs_1_ = bf16[80,640]{1,0:T(8,128)(2,1)S(1)} collective-permute-done((bf16[80,640]{1,0:T(8,128)(2,1)S(1)}, bf16[80,640]{1,0:T(8,128)(2,1)S(1)}, u32[]{:S(2)}, u32[]{:S(2)}) %collective-permute-start.1) | collective-permute-done | bytes 102432 | tf_op jit(solution)/shard_map/ppermute | solution.py:21
  6.4 1.6 %collective-permute-start.8 = (bf16[320,320]{1,0:T(8,128)(2,1)}, bf16[320,320]{1,0:T(8,128)(2,1)S(1)}, u32[]{:S(2)}, u32[]{:S(2)}) collective-permute-start(bf16[320,320]{1,0:T(8,128)(2,1)} %bitcast.20), channel_id=1, source_target_pairs={{0,1},{1,0},{2,3},{3,2},{4,5},{5,4},{6,7},{7,6},{8,9},{9,8},{10,11... | collective-permute-start | bytes 614408 | tf_op jit(solution)/shard_map/ppermute | solution.py:31
  8.9 1.0 %collective-permute-done.3.refs_3_ = bf16[80,640]{1,0:T(8,128)(2,1)S(1)} collective-permute-done((bf16[80,640]{1,0:T(8,128)(2,1)S(1)}, bf16[80,640]{1,0:T(8,128)(2,1)S(1)}, u32[]{:S(2)}, u32[]{:S(2)}) %collective-permute-start.3) | collective-permute-done | bytes 102432 | tf_op jit(solution)/shard_map/ppermute | solution.py:21
  11.3 1.4 %shard_map.46.refs_0_ = bf16[4,80,640]{2,1,0:T(8,128)(2,1)S(1)} custom-call(bf16[8,80,640]{2,1,0:T(8,128)(2,1)S(1)} %pad_maximum_fusion.inter_ref, bf16[80,640]{1,0:T(8,128)(2,1)S(1)} %get-tuple-element.66.refs_0_, bf16[80,640]{1,0:T(8,128)(2,1)S(1)} %collective-permute-done.1.refs_1_, bf16[80,640]{1,0:T(8,128)(2,1)S(1)} %collective-permute-done.2.refs_2_, ...), custom_call_target="tpu_custom_call" | custom-call | flops 13107200 | tf_op jit(solution)/shard_map/pallas_call | solution.py:99
  12.8 1.4 %collective-permute-done.8.before_ref = bf16[320,320]{1,0:T(8,128)(2,1)S(1)} collective-permute-done((bf16[320,320]{1,0:T(8,128)(2,1)}, bf16[320,320]{1,0:T(8,128)(2,1)S(1)}, u32[]{:S(2)}, u32[]{:S(2)}) %collective-permute-start.8) | collective-permute-done | bytes 204832 | tf_op jit(solution)/shard_map/ppermute | solution.py:31
  14.2 1.6 %collective-permute-start.10 = (bf16[80,640]{1,0:T(8,128)(2,1)S(1)}, bf16[80,640]{1,0:T(8,128)(2,1)S(1)}, u32[]{:S(2)}, u32[]{:S(2)}) collective-permute-start(bf16[80,640]{1,0:T(8,128)(2,1)S(1)} %get-tuple-element.62), channel_id=1, source_target_pairs={{0,16},{4,20},{8,24},{12,28},{16,0},{20,4},{24,8},{28,12},{1,17},{... | collective-permute-start | bytes 307208 | tf_op jit(solution)/shard_map/ppermute | solution.py:21
  15.8 1.4 %collective-permute-start.11 = (bf16[80,640]{1,0:T(8,128)(2,1)S(1)}, bf16[80,640]{1,0:T(8,128)(2,1)S(1)}, u32[]{:S(2)}, u32[]{:S(2)}) collective-permute-start(bf16[80,640]{1,0:T(8,128)(2,1)S(1)} %get-tuple-element.61), channel_id=1, source_target_pairs={{0,24},{4,28},{8,16},{12,20},{16,8},{20,12},{24,0},{28,4},{1,25},{... | collective-permute-start | bytes 307208 | tf_op jit(solution)/shard_map/ppermute | solution.py:21
  17.8 2.3 %collective-permute-done.10.refs_2_ = bf16[80,640]{1,0:T(8,128)(2,1)S(1)} collective-permute-done((bf16[80,640]{1,0:T(8,128)(2,1)S(1)}, bf16[80,640]{1,0:T(8,128)(2,1)S(1)}, u32[]{:S(2)}, u32[]{:S(2)}) %collective-permute-start.10) | collective-permute-done | bytes 102432 | tf_op jit(solution)/shard_map/ppermute | solution.py:21
  20.0 1.4 %collective-permute-done.11.refs_3_ = bf16[80,640]{1,0:T(8,128)(2,1)S(1)} collective-permute-done((bf16[80,640]{1,0:T(8,128)(2,1)S(1)}, bf16[80,640]{1,0:T(8,128)(2,1)S(1)}, u32[]{:S(2)}, u32[]{:S(2)}) %collective-permute-start.11) | collective-permute-done | bytes 102432 | tf_op jit(solution)/shard_map/ppermute | solution.py:21
  22.1 1.6 %collective-permute-start.12 = (bf16[160,640]{1,0:T(8,128)(2,1)S(1)}, bf16[160,640]{1,0:T(8,128)(2,1)S(1)}, u32[]{:S(2)}, u32[]{:S(2)}) collective-permute-start(bf16[160,640]{1,0:T(8,128)(2,1)S(1)} %get-tuple-element.41.own_ref), channel_id=1, source_target_pairs={{0,1},{1,0},{2,3},{3,2},{4,5},{5,4},{6,7},{7,6},{8,9},{9,8},{10,11... | collective-permute-start | bytes 614408 | tf_op jit(solution)/shard_map/ppermute | solution.py:31
  24.2 2.5 %shard_map.48 = (bf16[320,320]{1,0:T(8,128)(2,1)S(1)}, bf16[320,320]{1,0:T(8,128)(2,1)}, bf16[320,320]{1,0:T(8,128)(2,1)}, bf16[640,320]{1,0:T(8,128)(2,1)S(1)},...) custom-call(bf16[320,320]{1,0:T(8,128)(2,1)S(1)} %bitcast.21, ...), custom_call_target="tpu_custom_call" | custom-call | tf_op jit(solution)/shard_map/pallas_call | solution.py:36
  26.7 2.1 %collective-permute-done.12.came_ref.refs_4_ = bf16[160,640]{1,0:T(8,128)(2,1)S(1)} collective-permute-done((bf16[160,640]{1,0:T(8,128)(2,1)S(1)}, bf16[160,640]{1,0:T(8,128)(2,1)S(1)}, u32[]{:S(2)}, u32[]{:S(2)}) %collective-permute-start.12) | collective-permute-done | bytes 204832 | tf_op jit(solution)/shard_map/ppermute | solution.py:31
  28.8 1.2 %collective-permute-start.13 = (bf16[80,640]{1,0:T(8,128)(2,1)S(1)}, bf16[80,640]{1,0:T(8,128)(2,1)S(1)}, u32[]{:S(2)}, u32[]{:S(2)}) collective-permute-start(bf16[80,640]{1,0:T(8,128)(2,1)S(1)} %get-tuple-element.42.refs_0_), channel_id=1, source_target_pairs={{0,8},{1,2},{2,1},{3,11},{4,12},{5,6},{6,5},{7,15},{8,0},{9,10},{1... | collective-permute-start | bytes 307208 | tf_op jit(solution)/shard_map/ppermute | solution.py:31
  30.0 0.9 %collective-permute-start.19 = (bf16[80,640]{1,0:T(8,128)(2,1)S(1)}, bf16[80,640]{1,0:T(8,128)(2,1)S(1)}, u32[]{:S(2)}, u32[]{:S(2)}) collective-permute-start(bf16[80,640]{1,0:T(8,128)(2,1)S(1)} %get-tuple-element.46.refs_1_), channel_id=1, source_target_pairs={{0,8},{1,2},{2,1},{3,11},{4,12},{5,6},{6,5},{7,15},{8,0},{9,10},{1... | collective-permute-start | bytes 307208 | tf_op jit(solution)/shard_map/ppermute | solution.py:31
  31.0 1.8 %collective-permute-start.17 = (bf16[80,640]{1,0:T(8,128)(2,1)S(1)}, bf16[80,640]{1,0:T(8,128)(2,1)S(1)}, u32[]{:S(2)}, u32[]{:S(2)}) collective-permute-start(bf16[80,640]{1,0:T(8,128)(2,1)S(1)} %get-tuple-element.48.refs_2_), channel_id=1, source_target_pairs={{0,8},{1,2},{2,1},{3,11},{4,12},{5,6},{6,5},{7,15},{8,0},{9,10},{1... | collective-permute-start | bytes 307208 | tf_op jit(solution)/shard_map/ppermute | solution.py:31
  33.6 1.6 %collective-permute-start.14 = (bf16[80,640]{1,0:T(8,128)(2,1)S(1)}, bf16[80,640]{1,0:T(8,128)(2,1)S(1)}, u32[]{:S(2)}, u32[]{:S(2)}) collective-permute-start(bf16[80,640]{1,0:T(8,128)(2,1)S(1)} %collective-permute-done.13.refs_0_), channel_id=1, source_target_pairs={{0,4},{1,5},{2,3},{3,2},{4,0},{5,1},{6,7},{7,6},{8,12},{9,13},{10,... | collective-permute-start | bytes 307208 | tf_op jit(solution)/shard_map/ppermute | solution.py:31
  35.1 1.2 %collective-permute-start.20 = (bf16[80,640]{1,0:T(8,128)(2,1)S(1)}, bf16[80,640]{1,0:T(8,128)(2,1)S(1)}, u32[]{:S(2)}, u32[]{:S(2)}) collective-permute-start(bf16[80,640]{1,0:T(8,128)(2,1)S(1)} %collective-permute-done.19.refs_1_), channel_id=1, source_target_pairs={{0,4},{1,5},{2,3},{3,2},{4,0},{5,1},{6,7},{7,6},{8,12},{9,13},{10,... | collective-permute-start | bytes 307208 | tf_op jit(solution)/shard_map/ppermute | solution.py:31
  36.3 1.1 %collective-permute-start.18 = (bf16[80,640]{1,0:T(8,128)(2,1)S(1)}, bf16[80,640]{1,0:T(8,128)(2,1)S(1)}, u32[]{:S(2)}, u32[]{:S(2)}) collective-permute-start(bf16[80,640]{1,0:T(8,128)(2,1)S(1)} %collective-permute-done.17.refs_0_), channel_id=1, source_target_pairs={{0,4},{1,5},{2,3},{3,2},{4,0},{5,1},{6,7},{7,6},{8,12},{9,13},{10,... | collective-permute-start | bytes 307208 | tf_op jit(solution)/shard_map/ppermute | solution.py:31
  37.5 1.0 %collective-permute-start.21 = (bf16[80,640]{1,0:T(8,128)(2,1)S(1)}, bf16[80,640]{1,0:T(8,128)(2,1)S(1)}, u32[]{:S(2)}, u32[]{:S(2)}) collective-permute-start(bf16[80,640]{1,0:T(8,128)(2,1)S(1)} %collective-permute-done.16.refs_0_), channel_id=1, source_target_pairs={{0,4},{1,5},{2,3},{3,2},{4,0},{5,1},{6,7},{7,6},{8,12},{9,13},{10,... | collective-permute-start | bytes 307208 | tf_op jit(solution)/shard_map/ppermute | solution.py:31
  38.5 1.6 %shard_map.51.base_ref = f32[320,640]{1,0:T(8,128)S(1)} custom-call(bf16[320,320]{1,0:T(8,128)(2,1)S(1)} %bitcast.24, bf16[320,320]{1,0:T(8,128)(2,1)S(1)} %get-tuple-element.40.turned_ref, bf16[640,320]{1,0:T(8,128)(2,1)S(1)} %get-tuple-element.43.stack_ref, bf16[320,640]{1,0:T(8,128)(2,1)S(1)} %get-tuple-element.44.first_ref, ...), custom_call_target="tpu_custom_call" | custom-call | tf_op jit(solution)/shard_map/pallas_call | solution.py:36
  42.2 1.7 %shard_map.54 = bf16[320,640]{1,0:T(8,128)(2,1)} custom-call(bf16[320,640]{1,0:T(8,128)(2,1)S(1)} %get-tuple-element.37.far_first_ref, bf16[320,640]{1,0:T(8,128)(2,1)S(1)} %get-tuple-element.38.far_second_ref, bf16[640,160]{1,0:T(8,128)(2,1)S(1)} %get-tuple-element.39.half_ref, f32[320,640]{1,0:T(8,128)S(1)} %shard_map.51.base_ref, ...), custom_call_target="tpu_custom_call" | custom-call | tf_op jit(solution)/shard_map/pallas_call | solution.py:353
  (39 shorter events, 7.4 us)
Async XLA Ops:
  0.0 9.9 %collective-permute-start = (bf16[8,40,640]{2,1,0:T(8,128)(2,1)}, bf16[8,40,640]{2,1,0:T(8,128)(2,1)S(1)}, u32[]{:S(2)}, u32[]{:S(2)}) collective-permute-start(bf16[8,40,640]{2,1,0:T(8,128)(2,1)} %bitcast.26), channel_id=1, source_target_pairs={{0,4},{4,0},{8,12},{12,8},{16,20},{20,16},{24,28},{28,24},{1,5},{5... | collective-permute-start | bytes 1228808 | tf_op jit(solution)/shard_map/ppermute | solution.py:21
  1.1 5.3 %collective-permute-start.1 = (bf16[80,640]{1,0:T(8,128)(2,1)S(1)}, bf16[80,640]{1,0:T(8,128)(2,1)S(1)}, u32[]{:S(2)}, u32[]{:S(2)}) collective-permute-start(bf16[80,640]{1,0:T(8,128)(2,1)S(1)} %get-tuple-element.65), channel_id=1, source_target_pairs={{0,8},{4,12},{8,0},{12,4},{16,24},{20,28},{24,16},{28,20},{1,9},{5... | collective-permute-start | bytes 307208 | tf_op jit(solution)/shard_map/ppermute | solution.py:21
  2.7 6.2 %collective-permute-start.2 = (bf16[80,640]{1,0:T(8,128)(2,1)S(1)}, bf16[80,640]{1,0:T(8,128)(2,1)S(1)}, u32[]{:S(2)}, u32[]{:S(2)}) collective-permute-start(bf16[80,640]{1,0:T(8,128)(2,1)S(1)} %get-tuple-element.67), channel_id=1, source_target_pairs={{0,16},{4,20},{8,24},{12,28},{16,0},{20,4},{24,8},{28,12},{1,17},{... | collective-permute-start | bytes 307208 | tf_op jit(solution)/shard_map/ppermute | solution.py:21
  4.2 5.6 %collective-permute-start.3 = (bf16[80,640]{1,0:T(8,128)(2,1)S(1)}, bf16[80,640]{1,0:T(8,128)(2,1)S(1)}, u32[]{:S(2)}, u32[]{:S(2)}) collective-permute-start(bf16[80,640]{1,0:T(8,128)(2,1)S(1)} %get-tuple-element.64), channel_id=1, source_target_pairs={{0,24},{4,28},{8,16},{12,20},{16,8},{20,12},{24,0},{28,4},{1,25},{... | collective-permute-start | bytes 307208 | tf_op jit(solution)/shard_map/ppermute | solution.py:21
  4.7 5.8 %collective-permute-start.4 = (bf16[80,640]{1,0:T(8,128)(2,1)S(1)}, bf16[80,640]{1,0:T(8,128)(2,1)S(1)}, u32[]{:S(2)}, u32[]{:S(2)}) collective-permute-start(bf16[80,640]{1,0:T(8,128)(2,1)S(1)} %get-tuple-element.66.refs_0_), channel_id=1, source_target_pairs={{0,4},{4,0},{8,12},{12,8},{16,20},{20,16},{24,28},{28,24},{1,5},{5... | collective-permute-start | bytes 307208 | tf_op jit(solution)/shard_map/ppermute | solution.py:21
  6.4 7.7 %collective-permute-start.8 = (bf16[320,320]{1,0:T(8,128)(2,1)}, bf16[320,320]{1,0:T(8,128)(2,1)S(1)}, u32[]{:S(2)}, u32[]{:S(2)}) collective-permute-start(bf16[320,320]{1,0:T(8,128)(2,1)} %bitcast.20), channel_id=1, source_target_pairs={{0,1},{1,0},{2,3},{3,2},{4,5},{5,4},{6,7},{7,6},{8,9},{9,8},{10,11... | collective-permute-start | bytes 614408 | tf_op jit(solution)/shard_map/ppermute | solution.py:31
  8.9 1.7 %collective-permute-start.5 = (bf16[80,640]{1,0:T(8,128)(2,1)S(1)}, bf16[80,640]{1,0:T(8,128)(2,1)S(1)}, u32[]{:S(2)}, u32[]{:S(2)}) collective-permute-start(bf16[80,640]{1,0:T(8,128)(2,1)S(1)} %collective-permute-done.1.refs_1_), channel_id=1, source_target_pairs={{0,4},{4,0},{8,12},{12,8},{16,20},{20,16},{24,28},{28,24},{1,5},{5... | collective-permute-start | bytes 307208 | tf_op jit(solution)/shard_map/ppermute | solution.py:21
  9.9 1.3 %collective-permute-start.6 = (bf16[80,640]{1,0:T(8,128)(2,1)S(1)}, bf16[80,640]{1,0:T(8,128)(2,1)S(1)}, u32[]{:S(2)}, u32[]{:S(2)}) collective-permute-start(bf16[80,640]{1,0:T(8,128)(2,1)S(1)} %collective-permute-done.2.refs_2_), channel_id=1, source_target_pairs={{0,4},{4,0},{8,12},{12,8},{16,20},{20,16},{24,28},{28,24},{1,5},{5... | collective-permute-start | bytes 307208 | tf_op jit(solution)/shard_map/ppermute | solution.py:21
  9.9 1.5 %collective-permute-start.7 = (bf16[80,640]{1,0:T(8,128)(2,1)S(1)}, bf16[80,640]{1,0:T(8,128)(2,1)S(1)}, u32[]{:S(2)}, u32[]{:S(2)}) collective-permute-start(bf16[80,640]{1,0:T(8,128)(2,1)S(1)} %collective-permute-done.3.refs_3_), channel_id=1, source_target_pairs={{0,4},{4,0},{8,12},{12,8},{16,20},{20,16},{24,28},{28,24},{1,5},{5... | collective-permute-start | bytes 307208 | tf_op jit(solution)/shard_map/ppermute | solution.py:21
  12.7 11.4 %copy-start = (bf16[1,320,320]{2,1,0:T(8,128)(2,1)S(1)}, bf16[1,320,320]{2,1,0:T(8,128)(2,1)}, u32[]{:S(2)}) copy-start(bf16[1,320,320]{2,1,0:T(8,128)(2,1)} %param.7) | copy-start | bytes 614404
  12.8 11.4 %copy-start.1 = (bf16[1,1,320,640]{3,2,1,0:T(8,128)(2,1)S(1)}, bf16[1,1,320,640]{3,2,1,0:T(8,128)(2,1)}, u32[]{:S(2)}) copy-start(bf16[1,1,320,640]{3,2,1,0:T(8,128)(2,1)} %param.5) | copy-start | bytes 1228804
  14.2 5.8 %collective-permute-start.10 = (bf16[80,640]{1,0:T(8,128)(2,1)S(1)}, bf16[80,640]{1,0:T(8,128)(2,1)S(1)}, u32[]{:S(2)}, u32[]{:S(2)}) collective-permute-start(bf16[80,640]{1,0:T(8,128)(2,1)S(1)} %get-tuple-element.62), channel_id=1, source_target_pairs={{0,16},{4,20},{8,24},{12,28},{16,0},{20,4},{24,8},{28,12},{1,17},{... | collective-permute-start | bytes 307208 | tf_op jit(solution)/shard_map/ppermute | solution.py:21
  15.8 5.6 %collective-permute-start.11 = (bf16[80,640]{1,0:T(8,128)(2,1)S(1)}, bf16[80,640]{1,0:T(8,128)(2,1)S(1)}, u32[]{:S(2)}, u32[]{:S(2)}) collective-permute-start(bf16[80,640]{1,0:T(8,128)(2,1)S(1)} %get-tuple-element.61), channel_id=1, source_target_pairs={{0,24},{4,28},{8,16},{12,20},{16,8},{20,12},{24,0},{28,4},{1,25},{... | collective-permute-start | bytes 307208 | tf_op jit(solution)/shard_map/ppermute | solution.py:21
  17.2 4.7 %collective-permute-start.9 = (bf16[80,640]{1,0:T(8,128)(2,1)S(1)}, bf16[80,640]{1,0:T(8,128)(2,1)S(1)}, u32[]{:S(2)}, u32[]{:S(2)}) collective-permute-start(bf16[80,640]{1,0:T(8,128)(2,1)S(1)} %get-tuple-element.63), channel_id=1, source_target_pairs={{0,8},{4,12},{8,0},{12,4},{16,24},{20,28},{24,16},{28,20},{1,9},{5... | collective-permute-start | bytes 307208 | tf_op jit(solution)/shard_map/ppermute | solution.py:21
  22.1 6.7 %collective-permute-start.12 = (bf16[160,640]{1,0:T(8,128)(2,1)S(1)}, bf16[160,640]{1,0:T(8,128)(2,1)S(1)}, u32[]{:S(2)}, u32[]{:S(2)}) collective-permute-start(bf16[160,640]{1,0:T(8,128)(2,1)S(1)} %get-tuple-element.41.own_ref), channel_id=1, source_target_pairs={{0,1},{1,0},{2,3},{3,2},{4,5},{5,4},{6,7},{7,6},{8,9},{9,8},{10,11... | collective-permute-start | bytes 614408 | tf_op jit(solution)/shard_map/ppermute | solution.py:31
  23.7 7.3 %collective-permute-start.15 = (bf16[160,640]{1,0:T(8,128)(2,1)S(1)}, bf16[160,640]{1,0:T(8,128)(2,1)S(1)}, u32[]{:S(2)}, u32[]{:S(2)}) collective-permute-start(bf16[160,640]{1,0:T(8,128)(2,1)S(1)} %get-tuple-element.47.own_ref), channel_id=1, source_target_pairs={{0,1},{1,0},{2,3},{3,2},{4,5},{5,4},{6,7},{7,6},{8,9},{9,8},{10,11... | collective-permute-start | bytes 614408 | tf_op jit(solution)/shard_map/ppermute | solution.py:31
  28.8 4.7 %collective-permute-start.13 = (bf16[80,640]{1,0:T(8,128)(2,1)S(1)}, bf16[80,640]{1,0:T(8,128)(2,1)S(1)}, u32[]{:S(2)}, u32[]{:S(2)}) collective-permute-start(bf16[80,640]{1,0:T(8,128)(2,1)S(1)} %get-tuple-element.42.refs_0_), channel_id=1, source_target_pairs={{0,8},{1,2},{2,1},{3,11},{4,12},{5,6},{6,5},{7,15},{8,0},{9,10},{1... | collective-permute-start | bytes 307208 | tf_op jit(solution)/shard_map/ppermute | solution.py:31
  30.0 5.1 %collective-permute-start.19 = (bf16[80,640]{1,0:T(8,128)(2,1)S(1)}, bf16[80,640]{1,0:T(8,128)(2,1)S(1)}, u32[]{:S(2)}, u32[]{:S(2)}) collective-permute-start(bf16[80,640]{1,0:T(8,128)(2,1)S(1)} %get-tuple-element.46.refs_1_), channel_id=1, source_target_pairs={{0,8},{1,2},{2,1},{3,11},{4,12},{5,6},{6,5},{7,15},{8,0},{9,10},{1... | collective-permute-start | bytes 307208 | tf_op jit(solution)/shard_map/ppermute | solution.py:31
  31.0 5.3 %collective-permute-start.17 = (bf16[80,640]{1,0:T(8,128)(2,1)S(1)}, bf16[80,640]{1,0:T(8,128)(2,1)S(1)}, u32[]{:S(2)}, u32[]{:S(2)}) collective-permute-start(bf16[80,640]{1,0:T(8,128)(2,1)S(1)} %get-tuple-element.48.refs_2_), channel_id=1, source_target_pairs={{0,8},{1,2},{2,1},{3,11},{4,12},{5,6},{6,5},{7,15},{8,0},{9,10},{1... | collective-permute-start | bytes 307208 | tf_op jit(solution)/shard_map/ppermute | solution.py:31
  32.8 4.7 %collective-permute-start.16 = (bf16[80,640]{1,0:T(8,128)(2,1)S(1)}, bf16[80,640]{1,0:T(8,128)(2,1)S(1)}, u32[]{:S(2)}, u32[]{:S(2)}) collective-permute-start(bf16[80,640]{1,0:T(8,128)(2,1)S(1)} %get-tuple-element.49.refs_3_), channel_id=1, source_target_pairs={{0,8},{1,2},{2,1},{3,11},{4,12},{5,6},{6,5},{7,15},{8,0},{9,10},{1... | collective-permute-start | bytes 307208 | tf_op jit(solution)/shard_map/ppermute | solution.py:31
  33.6 6.5 %collective-permute-start.14 = (bf16[80,640]{1,0:T(8,128)(2,1)S(1)}, bf16[80,640]{1,0:T(8,128)(2,1)S(1)}, u32[]{:S(2)}, u32[]{:S(2)}) collective-permute-start(bf16[80,640]{1,0:T(8,128)(2,1)S(1)} %collective-permute-done.13.refs_0_), channel_id=1, source_target_pairs={{0,4},{1,5},{2,3},{3,2},{4,0},{5,1},{6,7},{7,6},{8,12},{9,13},{10,... | collective-permute-start | bytes 307208 | tf_op jit(solution)/shard_map/ppermute | solution.py:31
  35.1 5.0 %collective-permute-start.20 = (bf16[80,640]{1,0:T(8,128)(2,1)S(1)}, bf16[80,640]{1,0:T(8,128)(2,1)S(1)}, u32[]{:S(2)}, u32[]{:S(2)}) collective-permute-start(bf16[80,640]{1,0:T(8,128)(2,1)S(1)} %collective-permute-done.19.refs_1_), channel_id=1, source_target_pairs={{0,4},{1,5},{2,3},{3,2},{4,0},{5,1},{6,7},{7,6},{8,12},{9,13},{10,... | collective-permute-start | bytes 307208 | tf_op jit(solution)/shard_map/ppermute | solution.py:31
  36.3 4.7 %collective-permute-start.18 = (bf16[80,640]{1,0:T(8,128)(2,1)S(1)}, bf16[80,640]{1,0:T(8,128)(2,1)S(1)}, u32[]{:S(2)}, u32[]{:S(2)}) collective-permute-start(bf16[80,640]{1,0:T(8,128)(2,1)S(1)} %collective-permute-done.17.refs_0_), channel_id=1, source_target_pairs={{0,4},{1,5},{2,3},{3,2},{4,0},{5,1},{6,7},{7,6},{8,12},{9,13},{10,... | collective-permute-start | bytes 307208 | tf_op jit(solution)/shard_map/ppermute | solution.py:31
  37.5 4.7 %collective-permute-start.21 = (bf16[80,640]{1,0:T(8,128)(2,1)S(1)}, bf16[80,640]{1,0:T(8,128)(2,1)S(1)}, u32[]{:S(2)}, u32[]{:S(2)}) collective-permute-start(bf16[80,640]{1,0:T(8,128)(2,1)S(1)} %collective-permute-done.16.refs_0_), channel_id=1, source_target_pairs={{0,4},{1,5},{2,3},{3,2},{4,0},{5,1},{6,7},{7,6},{8,12},{9,13},{10,... | collective-permute-start | bytes 307208 | tf_op jit(solution)/shard_map/ppermute | solution.py:31
  (1 other events, 10.4 us)

commit v8 on v7

--- a/solution.py
+++ b/solution.py
@@ -43,12 +43,24 @@
     )(*in_vmem(*given))
 
 
-def conv_kernel(chips, inter_ref, *refs):
+def spread_kernel(inter_ref, other_ref, w_ref, v_ref):
+    side = lax.axis_index(ENERGY) % 2
+    count, rows, width = inter_ref.shape
+    left = lax.broadcasted_iota(jnp.int32, (2 * rows, width), 1) < width // 2
+    for m in range(count):
+        own, other = inter_ref[m].astype(jnp.float32), other_ref[m].astype(jnp.float32)
+        x = jnp.concatenate([jnp.where(side == 0, own, other), jnp.where(side == 0, other, own)], axis=0)
+        y = jnp.concatenate([x[:, width // 2 :], x[:, : width // 2]], axis=1)
+        w_ref[m] = x
+        v_ref[m] = jnp.where(left, -y, y)
+
+
+def conv_kernel(chips, w_ref, v_ref, *refs):
     pieces = refs[: 2 * chips]
-    out_ref, a_ref, b_ref, w_ref, v_ref, sum_ref = refs[2 * chips :]
+    out_ref, a_ref, b_ref, sum_ref = refs[2 * chips :]
     me = lax.axis_index(ENERGY)
     chip, side = me // 2, me % 2
-    rows, width = inter_ref.shape[1:]
+    rows, width = w_ref.shape[1:]
     half = width // 2
     left = lax.broadcasted_iota(jnp.int32, (rows, width), 1) < half
 
@@ -67,12 +79,6 @@
             slot = 2 * (chip ^ j) + (side ^ other) + 1 - side
             a_ref[slot] = jnp.where(left, x, y)
             b_ref[slot] = jnp.where(left, y, x)
-    for m in range(2 * chips):
-        x = inter_ref[m].astype(jnp.float32)
-        y = swapped(x)
-        w_ref[m] = x
-        v_ref[m] = jnp.where(left, -y, y)
-
     step = 8 if rows % 8 == 0 else rows
     lanes = 128 if width % 128 == 0 else width
 
@@ -94,17 +100,17 @@
 
 
 def convolve(chips, inter, pieces):
-    count, rows, width = inter.shape
+    count, rows, width = inter[0].shape
     block = lambda n: pltpu.VMEM((n, rows, width), jnp.float32)
     return pl.pallas_call(
         functools.partial(conv_kernel, chips),
         out_shape=pltpu.VMEM((chips, rows, width), jnp.bfloat16),
-        in_specs=[WHOLE] * (1 + 2 * chips),
+        in_specs=[WHOLE] * (2 + 2 * chips),
         out_specs=WHOLE,
-        scratch_shapes=[block(count + 1), block(count + 1), block(count), block(count), block(chips)],
+        scratch_shapes=[block(count + 1), block(count + 1), block(chips)],
         compiler_params=pltpu.CompilerParams(vmem_limit_bytes=16 << 20),
         cost_estimate=pl.CostEstimate(flops=count * count * rows * width * 4, bytes_accessed=0, transcendentals=0),
-    )(*in_vmem(inter, *pieces))
+    )(*in_vmem(*inter, *pieces))
 
 
 def dot(a, b):
@@ -290,19 +296,18 @@
     rows = size // chips
     inter = screened[:, 0]
     inter_other = swap_with(inter, 1)
-    first = jnp.where(side == 0, inter, inter_other)
-    second = jnp.where(side == 0, inter_other, inter)
-    inter_rows = jnp.concatenate([first, second], axis=1)
+    spread = call(spread_kernel, [((devices, rows, width), jnp.float32)] * 2, [inter, inter_other])
 
     mine = [lax.dynamic_slice(lesser, (rows * (chip ^ j), 0), (rows, width)) for j in range(chips)]
     pieces = [mine[0]] + [swap_with(mine[j], 2 * j) for j in range(1, chips)]
 
     link = coupling[0]
     other_in_pair = {s: s ^ 1 for s in range(slabs)}
+    link, spread = lax.optimization_barrier((link, spread))
     link_before = swap_slabs(link, other_in_pair)
 
     pieces = pieces + [swap_with(x, 1) for x in pieces]
-    sigma = convolve(chips, inter_rows, pieces)
+    sigma = convolve(chips, spread, pieces)
     sigma, link_before = lax.optimization_barrier((sigma, link_before))
     own_re, own_im = gathered(sigma, [swap_with(sigma[j], 2 * j) for j in range(1, chips)])
 

time: 44.1 us -> 43.9 us (level)
  waiting for transfers between devices: 13.7 us -> 12.3 us
  local copies, waits for them, and re-layouts: 1.18 us -> 2.16 us
    ppermute x11, waiting for transfers between devices: 8.46 us -> 7 us  [swap_with(): return lax.ppermute(array, ENERGY, [(i, i ^ mask) for i in range(devices)])]
    unnamed x6, local copies, waits for them, and re-layouts: 0.02 us -> 1.01 us
    pallas_call x7 -> x8, Pallas kernels: 5.29 us -> 5.71 us  [call(): pl.pallas_call(kernel, out_shape=outs, in_specs=[WHOLE] * len(given), out...]
  transfers between devices with their start and end apart: 22 -> 22, of which waited for: 15 -> 14; matrix products, arithmetic and copies ran while one was open for 3% -> 3% of each run, Pallas kernels for 15% -> 15%
where the time goes in v8:
time: 43.9 us; the launch traced here: 43.4 us
  starting transfers between devices  20.3 us (46%)
  waiting for transfers between devices  12.3 us (28%)
  Pallas kernels  8.54 us (19%)
  local copies, waits for them, and re-layouts  2.16 us (5%)
    ppermute x11, starting transfers between devices, swap_slabs(): return lax.ppermute(array, (ENERGY, SLAB), pairs)  12.7 us
    ppermute x11, starting transfers between devices, swap_with(): return lax.ppermute(array, ENERGY, [(i, i ^ mask) for i in range(devices)])  7.62 us
    ppermute x11, waiting for transfers between devices, swap_with(): return lax.ppermute(array, ENERGY, [(i, i ^ mask) for i in range(devices)])  7 us
    pallas_call x8, Pallas kernels, call(): pl.pallas_call(kernel, out_shape=outs, in_specs=[WHOLE] * len(given), out...  5.71 us
    ppermute x11, waiting for transfers between devices, swap_slabs(): return lax.ppermute(array, (ENERGY, SLAB), pairs)  5.25 us
    pallas_call x1, Pallas kernels, local(): pl.pallas_call(functools.partial(late_kernel, last_pair), out_shape=jax.S...  1.69 us
    pallas_call x1, Pallas kernels, convolve(): pl.pallas_call(functools.partial(conv_kernel, chips), out_shape=pltpu.VME...  1.15 us
    dynamic_slice x1, local copies, waits for them, and re-layouts, local(): lax.dynamic_slice(lesser, (rows * (chip ^ j), 0), (rows, width))  1.13 us
  transfers between devices with their start and end apart: 22, of which 14 were waited for; matrix products, arithmetic and copies ran while one was open for 3% of the time, Pallas kernels for 15%

profile of v8, /device:TPU:16, one launch (start us, length us, event | category | flops | bytes accessed | tf_op | source)
XLA Modules:
  0.0 43.4 jit_solution(15852735257709401536)
XLA Ops:
  0.0 1.1 %dynamic-slice_bitcast_fusion = (bf16[80,640]{1,0:T(8,128)(2,1)S(1)}, bf16[80,640]{1,0:T(8,128)(2,1)S(1)}, bf16[80,640]{1,0:T(8,128)(2,1)S(1)}, bf16[80,640]{1,0:T(8,128)(2,1)S(1)}) fusion(bf16[1,1,320,640]{3,2,1,0:T(8,128)(2,1)} %param.4, s32[]{:T(128)S(6)} %select_n.21, s32[]{:T(128)S(6)} %select_n.19, s32[]{:T(128)S(6)} %select_n.18, s32[]{:T(128)S(6)} %select_n.20), kind=kLoop, calls=%fused_computation.3 | loop fusion | bytes 819216 | tf_op jit(solution)/shard_map/dynamic_slice | solution.py:301
  1.1 1.6 %collective-permute-start.1 = (bf16[80,640]{1,0:T(8,128)(2,1)S(1)}, bf16[80,640]{1,0:T(8,128)(2,1)S(1)}, u32[]{:S(2)}, u32[]{:S(2)}) collective-permute-start(bf16[80,640]{1,0:T(8,128)(2,1)S(1)} %get-tuple-element.73), channel_id=1, source_target_pairs={{0,8},{4,12},{8,0},{12,4},{16,24},{20,28},{24,16},{28,20},{1,9},{5... | collective-permute-start | bytes 307208 | tf_op jit(solution)/shard_map/ppermute | solution.py:21
  2.7 1.5 %collective-permute-start.2 = (bf16[80,640]{1,0:T(8,128)(2,1)S(1)}, bf16[80,640]{1,0:T(8,128)(2,1)S(1)}, u32[]{:S(2)}, u32[]{:S(2)}) collective-permute-start(bf16[80,640]{1,0:T(8,128)(2,1)S(1)} %get-tuple-element.75), channel_id=1, source_target_pairs={{0,16},{4,20},{8,24},{12,28},{16,0},{20,4},{24,8},{28,12},{1,17},{... | collective-permute-start | bytes 307208 | tf_op jit(solution)/shard_map/ppermute | solution.py:21
  4.7 1.0 %copy-done.2 = bf16[8,1,40,640]{3,2,1,0:T(8,128)(2,1)S(1)} copy-done((bf16[8,1,40,640]{3,2,1,0:T(8,128)(2,1)S(1)}, bf16[8,1,40,640]{3,2,1,0:T(8,128)(2,1)}, u32[]{:S(2)}) %copy-start.2) | copy-done | bytes 409624
  6.1 1.6 %collective-permute-start.8 = (bf16[320,320]{1,0:T(8,128)(2,1)S(1)}, bf16[320,320]{1,0:T(8,128)(2,1)S(1)}, u32[]{:S(2)}, u32[]{:S(2)}) collective-permute-start(bf16[320,320]{1,0:T(8,128)(2,1)S(1)} %bitcast.18), channel_id=1, source_target_pairs={{0,1},{1,0},{2,3},{3,2},{4,5},{5,4},{6,7},{7,6},{8,9},{9,8},{10,11... | collective-permute-start | bytes 614408 | tf_op jit(solution)/shard_map/ppermute | solution.py:31
  8.9 1.0 %collective-permute-done.3.refs_3_ = bf16[80,640]{1,0:T(8,128)(2,1)S(1)} collective-permute-done((bf16[80,640]{1,0:T(8,128)(2,1)S(1)}, bf16[80,640]{1,0:T(8,128)(2,1)S(1)}, u32[]{:S(2)}, u32[]{:S(2)}) %collective-permute-start.3) | collective-permute-done | bytes 102432 | tf_op jit(solution)/shard_map/ppermute | solution.py:21
  10.2 1.0 %collective-permute-done.7.refs_7_ = bf16[80,640]{1,0:T(8,128)(2,1)S(1)} collective-permute-done((bf16[80,640]{1,0:T(8,128)(2,1)S(1)}, bf16[80,640]{1,0:T(8,128)(2,1)S(1)}, u32[]{:S(2)}, u32[]{:S(2)}) %collective-permute-start.7) | collective-permute-done | bytes 102432 | tf_op jit(solution)/shard_map/ppermute | solution.py:21
  11.2 1.1 %shard_map.47.refs_0_ = bf16[4,80,640]{2,1,0:T(8,128)(2,1)S(1)} custom-call(f32[8,80,640]{2,1,0:T(8,128)S(1)} %get-tuple-element.40.w_ref, f32[8,80,640]{2,1,0:T(8,128)S(1)} %get-tuple-element.41.v_ref, bf16[80,640]{1,0:T(8,128)(2,1)S(1)} %get-tuple-element.74.refs_0_, bf16[80,640]{1,0:T(8,128)(2,1)S(1)} %collective-permute-done.1.refs_1_, ...), custom_call_target="tpu_custom_call" | custom-call | flops 13107200 | tf_op jit(solution)/shard_map/pallas_call | solution.py:105
  12.3 1.4 %collective-permute-done.8.before_ref = bf16[320,320]{1,0:T(8,128)(2,1)S(1)} collective-permute-done((bf16[320,320]{1,0:T(8,128)(2,1)S(1)}, bf16[320,320]{1,0:T(8,128)(2,1)S(1)}, u32[]{:S(2)}, u32[]{:S(2)}) %collective-permute-start.8) | collective-permute-done | bytes 204832 | tf_op jit(solution)/shard_map/ppermute | solution.py:31
  13.7 1.6 %collective-permute-start.10 = (bf16[80,640]{1,0:T(8,128)(2,1)S(1)}, bf16[80,640]{1,0:T(8,128)(2,1)S(1)}, u32[]{:S(2)}, u32[]{:S(2)}) collective-permute-start(bf16[80,640]{1,0:T(8,128)(2,1)S(1)} %get-tuple-element.70), channel_id=1, source_target_pairs={{0,16},{4,20},{8,24},{12,28},{16,0},{20,4},{24,8},{28,12},{1,17},{... | collective-permute-start | bytes 307208 | tf_op jit(solution)/shard_map/ppermute | solution.py:21
  15.3 1.4 %collective-permute-start.11 = (bf16[80,640]{1,0:T(8,128)(2,1)S(1)}, bf16[80,640]{1,0:T(8,128)(2,1)S(1)}, u32[]{:S(2)}, u32[]{:S(2)}) collective-permute-start(bf16[80,640]{1,0:T(8,128)(2,1)S(1)} %get-tuple-element.69), channel_id=1, source_target_pairs={{0,24},{4,28},{8,16},{12,20},{16,8},{20,12},{24,0},{28,4},{1,25},{... | collective-permute-start | bytes 307208 | tf_op jit(solution)/shard_map/ppermute | solution.py:21
  17.2 2.3 %collective-permute-done.10.refs_2_ = bf16[80,640]{1,0:T(8,128)(2,1)S(1)} collective-permute-done((bf16[80,640]{1,0:T(8,128)(2,1)S(1)}, bf16[80,640]{1,0:T(8,128)(2,1)S(1)}, u32[]{:S(2)}, u32[]{:S(2)}) %collective-permute-start.10) | collective-permute-done | bytes 102432 | tf_op jit(solution)/shard_map/ppermute | solution.py:21
  19.5 1.5 %collective-permute-done.11.refs_3_ = bf16[80,640]{1,0:T(8,128)(2,1)S(1)} collective-permute-done((bf16[80,640]{1,0:T(8,128)(2,1)S(1)}, bf16[80,640]{1,0:T(8,128)(2,1)S(1)}, u32[]{:S(2)}, u32[]{:S(2)}) %collective-permute-start.11) | collective-permute-done | bytes 102432 | tf_op jit(solution)/shard_map/ppermute | solution.py:21
  21.6 1.6 %collective-permute-start.12 = (bf16[160,640]{1,0:T(8,128)(2,1)S(1)}, bf16[160,640]{1,0:T(8,128)(2,1)S(1)}, u32[]{:S(2)}, u32[]{:S(2)}) collective-permute-start(bf16[160,640]{1,0:T(8,128)(2,1)S(1)} %get-tuple-element.51.own_ref), channel_id=1, source_target_pairs={{0,1},{1,0},{2,3},{3,2},{4,5},{5,4},{6,7},{7,6},{8,9},{9,8},{10,11... | collective-permute-start | bytes 614408 | tf_op jit(solution)/shard_map/ppermute | solution.py:31
  23.7 2.5 %shard_map.49 = (bf16[320,320]{1,0:T(8,128)(2,1)S(1)}, bf16[320,320]{1,0:T(8,128)(2,1)}, bf16[320,320]{1,0:T(8,128)(2,1)}, bf16[640,320]{1,0:T(8,128)(2,1)S(1)},...) custom-call(bf16[320,320]{1,0:T(8,128)(2,1)S(1)} %bitcast.19, ...), custom_call_target="tpu_custom_call" | custom-call | tf_op jit(solution)/shard_map/pallas_call | solution.py:36
  26.2 2.2 %collective-permute-done.12.came_ref.refs_4_ = bf16[160,640]{1,0:T(8,128)(2,1)S(1)} collective-permute-done((bf16[160,640]{1,0:T(8,128)(2,1)S(1)}, bf16[160,640]{1,0:T(8,128)(2,1)S(1)}, u32[]{:S(2)}, u32[]{:S(2)}) %collective-permute-start.12) | collective-permute-done | bytes 204832 | tf_op jit(solution)/shard_map/ppermute | solution.py:31
  28.4 1.2 %collective-permute-start.13 = (bf16[80,640]{1,0:T(8,128)(2,1)S(1)}, bf16[80,640]{1,0:T(8,128)(2,1)S(1)}, u32[]{:S(2)}, u32[]{:S(2)}) collective-permute-start(bf16[80,640]{1,0:T(8,128)(2,1)S(1)} %get-tuple-element.52.refs_0_), channel_id=1, source_target_pairs={{0,8},{1,2},{2,1},{3,11},{4,12},{5,6},{6,5},{7,15},{8,0},{9,10},{1... | collective-permute-start | bytes 307208 | tf_op jit(solution)/shard_map/ppermute | solution.py:31
  30.6 1.8 %collective-permute-start.17 = (bf16[80,640]{1,0:T(8,128)(2,1)S(1)}, bf16[80,640]{1,0:T(8,128)(2,1)S(1)}, u32[]{:S(2)}, u32[]{:S(2)}) collective-permute-start(bf16[80,640]{1,0:T(8,128)(2,1)S(1)} %get-tuple-element.58.refs_2_), channel_id=1, source_target_pairs={{0,8},{1,2},{2,1},{3,11},{4,12},{5,6},{6,5},{7,15},{8,0},{9,10},{1... | collective-permute-start | bytes 307208 | tf_op jit(solution)/shard_map/ppermute | solution.py:31
  33.1 1.6 %collective-permute-start.14 = (bf16[80,640]{1,0:T(8,128)(2,1)S(1)}, bf16[80,640]{1,0:T(8,128)(2,1)S(1)}, u32[]{:S(2)}, u32[]{:S(2)}) collective-permute-start(bf16[80,640]{1,0:T(8,128)(2,1)S(1)} %collective-permute-done.13.refs_0_), channel_id=1, source_target_pairs={{0,4},{1,5},{2,3},{3,2},{4,0},{5,1},{6,7},{7,6},{8,12},{9,13},{10,... | collective-permute-start | bytes 307208 | tf_op jit(solution)/shard_map/ppermute | solution.py:31
  34.7 1.1 %collective-permute-start.20 = (bf16[80,640]{1,0:T(8,128)(2,1)S(1)}, bf16[80,640]{1,0:T(8,128)(2,1)S(1)}, u32[]{:S(2)}, u32[]{:S(2)}) collective-permute-start(bf16[80,640]{1,0:T(8,128)(2,1)S(1)} %collective-permute-done.19.refs_1_), channel_id=1, source_target_pairs={{0,4},{1,5},{2,3},{3,2},{4,0},{5,1},{6,7},{7,6},{8,12},{9,13},{10,... | collective-permute-start | bytes 307208 | tf_op jit(solution)/shard_map/ppermute | solution.py:31
  35.8 1.1 %collective-permute-start.18 = (bf16[80,640]{1,0:T(8,128)(2,1)S(1)}, bf16[80,640]{1,0:T(8,128)(2,1)S(1)}, u32[]{:S(2)}, u32[]{:S(2)}) collective-permute-start(bf16[80,640]{1,0:T(8,128)(2,1)S(1)} %collective-permute-done.17.refs_0_), channel_id=1, source_target_pairs={{0,4},{1,5},{2,3},{3,2},{4,0},{5,1},{6,7},{7,6},{8,12},{9,13},{10,... | collective-permute-start | bytes 307208 | tf_op jit(solution)/shard_map/ppermute | solution.py:31
  37.0 1.0 %collective-permute-start.21 = (bf16[80,640]{1,0:T(8,128)(2,1)S(1)}, bf16[80,640]{1,0:T(8,128)(2,1)S(1)}, u32[]{:S(2)}, u32[]{:S(2)}) collective-permute-start(bf16[80,640]{1,0:T(8,128)(2,1)S(1)} %collective-permute-done.16.refs_0_), channel_id=1, source_target_pairs={{0,4},{1,5},{2,3},{3,2},{4,0},{5,1},{6,7},{7,6},{8,12},{9,13},{10,... | collective-permute-start | bytes 307208 | tf_op jit(solution)/shard_map/ppermute | solution.py:31
  38.0 1.6 %shard_map.52.base_ref = f32[320,640]{1,0:T(8,128)S(1)} custom-call(bf16[320,320]{1,0:T(8,128)(2,1)S(1)} %bitcast.22, bf16[320,320]{1,0:T(8,128)(2,1)S(1)} %get-tuple-element.50.turned_ref, bf16[640,320]{1,0:T(8,128)(2,1)S(1)} %get-tuple-element.53.stack_ref, bf16[320,640]{1,0:T(8,128)(2,1)S(1)} %get-tuple-element.54.first_ref, ...), custom_call_target="tpu_custom_call" | custom-call | tf_op jit(solution)/shard_map/pallas_call | solution.py:36
  41.7 1.7 %shard_map.55 = bf16[320,640]{1,0:T(8,128)(2,1)} custom-call(bf16[320,640]{1,0:T(8,128)(2,1)S(1)} %get-tuple-element.47.far_first_ref, bf16[320,640]{1,0:T(8,128)(2,1)S(1)} %get-tuple-element.48.far_second_ref, bf16[640,160]{1,0:T(8,128)(2,1)S(1)} %get-tuple-element.49.half_ref, f32[320,640]{1,0:T(8,128)S(1)} %shard_map.52.base_ref, ...), custom_call_target="tpu_custom_call" | custom-call | tf_op jit(solution)/shard_map/pallas_call | solution.py:358
  (38 shorter events, 7.9 us)
Async XLA Ops:
  0.0 6.1 %copy-start = (bf16[1,320,320]{2,1,0:T(8,128)(2,1)S(1)}, bf16[1,320,320]{2,1,0:T(8,128)(2,1)}, u32[]{:S(2)}) copy-start(bf16[1,320,320]{2,1,0:T(8,128)(2,1)} %param.7) | copy-start | bytes 614404
  0.0 4.7 %collective-permute-start = (bf16[8,40,640]{2,1,0:T(8,128)(2,1)}, bf16[8,40,640]{2,1,0:T(8,128)(2,1)S(1)}, u32[]{:S(2)}, u32[]{:S(2)}) collective-permute-start(bf16[8,40,640]{2,1,0:T(8,128)(2,1)} %bitcast.24), channel_id=1, source_target_pairs={{0,4},{4,0},{8,12},{12,8},{16,20},{20,16},{24,28},{28,24},{1,5},{5... | collective-permute-start | bytes 1228808 | tf_op jit(solution)/shard_map/ppermute | solution.py:21
  1.1 6.6 %collective-permute-start.1 = (bf16[80,640]{1,0:T(8,128)(2,1)S(1)}, bf16[80,640]{1,0:T(8,128)(2,1)S(1)}, u32[]{:S(2)}, u32[]{:S(2)}) collective-permute-start(bf16[80,640]{1,0:T(8,128)(2,1)S(1)} %get-tuple-element.73), channel_id=1, source_target_pairs={{0,8},{4,12},{8,0},{12,4},{16,24},{20,28},{24,16},{28,20},{1,9},{5... | collective-permute-start | bytes 307208 | tf_op jit(solution)/shard_map/ppermute | solution.py:21
  2.7 6.2 %collective-permute-start.2 = (bf16[80,640]{1,0:T(8,128)(2,1)S(1)}, bf16[80,640]{1,0:T(8,128)(2,1)S(1)}, u32[]{:S(2)}, u32[]{:S(2)}) collective-permute-start(bf16[80,640]{1,0:T(8,128)(2,1)S(1)} %get-tuple-element.75), channel_id=1, source_target_pairs={{0,16},{4,20},{8,24},{12,28},{16,0},{20,4},{24,8},{28,12},{1,17},{... | collective-permute-start | bytes 307208 | tf_op jit(solution)/shard_map/ppermute | solution.py:21
  4.2 5.6 %collective-permute-start.3 = (bf16[80,640]{1,0:T(8,128)(2,1)S(1)}, bf16[80,640]{1,0:T(8,128)(2,1)S(1)}, u32[]{:S(2)}, u32[]{:S(2)}) collective-permute-start(bf16[80,640]{1,0:T(8,128)(2,1)S(1)} %get-tuple-element.72), channel_id=1, source_target_pairs={{0,24},{4,28},{8,16},{12,20},{16,8},{20,12},{24,0},{28,4},{1,25},{... | collective-permute-start | bytes 307208 | tf_op jit(solution)/shard_map/ppermute | solution.py:21
  6.1 7.5 %collective-permute-start.8 = (bf16[320,320]{1,0:T(8,128)(2,1)S(1)}, bf16[320,320]{1,0:T(8,128)(2,1)S(1)}, u32[]{:S(2)}, u32[]{:S(2)}) collective-permute-start(bf16[320,320]{1,0:T(8,128)(2,1)S(1)} %bitcast.18), channel_id=1, source_target_pairs={{0,1},{1,0},{2,3},{3,2},{4,5},{5,4},{6,7},{7,6},{8,9},{9,8},{10,11... | collective-permute-start | bytes 614408 | tf_op jit(solution)/shard_map/ppermute | solution.py:31
  7.8 15.9 %copy-start.1 = (bf16[1,1,320,640]{3,2,1,0:T(8,128)(2,1)S(1)}, bf16[1,1,320,640]{3,2,1,0:T(8,128)(2,1)}, u32[]{:S(2)}) copy-start(bf16[1,1,320,640]{3,2,1,0:T(8,128)(2,1)} %param.5) | copy-start | bytes 1228804
  7.8 2.1 %collective-permute-start.4 = (bf16[80,640]{1,0:T(8,128)(2,1)S(1)}, bf16[80,640]{1,0:T(8,128)(2,1)S(1)}, u32[]{:S(2)}, u32[]{:S(2)}) collective-permute-start(bf16[80,640]{1,0:T(8,128)(2,1)S(1)} %get-tuple-element.74.refs_0_), channel_id=1, source_target_pairs={{0,4},{4,0},{8,12},{12,8},{16,20},{20,16},{24,28},{28,24},{1,5},{5... | collective-permute-start | bytes 307208 | tf_op jit(solution)/shard_map/ppermute | solution.py:21
  7.8 2.1 %collective-permute-start.5 = (bf16[80,640]{1,0:T(8,128)(2,1)S(1)}, bf16[80,640]{1,0:T(8,128)(2,1)S(1)}, u32[]{:S(2)}, u32[]{:S(2)}) collective-permute-start(bf16[80,640]{1,0:T(8,128)(2,1)S(1)} %collective-permute-done.1.refs_1_), channel_id=1, source_target_pairs={{0,4},{4,0},{8,12},{12,8},{16,20},{20,16},{24,28},{28,24},{1,5},{5... | collective-permute-start | bytes 307208 | tf_op jit(solution)/shard_map/ppermute | solution.py:21
  8.9 1.3 %collective-permute-start.6 = (bf16[80,640]{1,0:T(8,128)(2,1)S(1)}, bf16[80,640]{1,0:T(8,128)(2,1)S(1)}, u32[]{:S(2)}, u32[]{:S(2)}) collective-permute-start(bf16[80,640]{1,0:T(8,128)(2,1)S(1)} %collective-permute-done.2.refs_2_), channel_id=1, source_target_pairs={{0,4},{4,0},{8,12},{12,8},{16,20},{20,16},{24,28},{28,24},{1,5},{5... | collective-permute-start | bytes 307208 | tf_op jit(solution)/shard_map/ppermute | solution.py:21
  9.9 1.3 %collective-permute-start.7 = (bf16[80,640]{1,0:T(8,128)(2,1)S(1)}, bf16[80,640]{1,0:T(8,128)(2,1)S(1)}, u32[]{:S(2)}, u32[]{:S(2)}) collective-permute-start(bf16[80,640]{1,0:T(8,128)(2,1)S(1)} %collective-permute-done.3.refs_3_), channel_id=1, source_target_pairs={{0,4},{4,0},{8,12},{12,8},{16,20},{20,16},{24,28},{28,24},{1,5},{5... | collective-permute-start | bytes 307208 | tf_op jit(solution)/shard_map/ppermute | solution.py:21
  13.7 5.8 %collective-permute-start.10 = (bf16[80,640]{1,0:T(8,128)(2,1)S(1)}, bf16[80,640]{1,0:T(8,128)(2,1)S(1)}, u32[]{:S(2)}, u32[]{:S(2)}) collective-permute-start(bf16[80,640]{1,0:T(8,128)(2,1)S(1)} %get-tuple-element.70), channel_id=1, source_target_pairs={{0,16},{4,20},{8,24},{12,28},{16,0},{20,4},{24,8},{28,12},{1,17},{... | collective-permute-start | bytes 307208 | tf_op jit(solution)/shard_map/ppermute | solution.py:21
  15.3 5.7 %collective-permute-start.11 = (bf16[80,640]{1,0:T(8,128)(2,1)S(1)}, bf16[80,640]{1,0:T(8,128)(2,1)S(1)}, u32[]{:S(2)}, u32[]{:S(2)}) collective-permute-start(bf16[80,640]{1,0:T(8,128)(2,1)S(1)} %get-tuple-element.69), channel_id=1, source_target_pairs={{0,24},{4,28},{8,16},{12,20},{16,8},{20,12},{24,0},{28,4},{1,25},{... | collective-permute-start | bytes 307208 | tf_op jit(solution)/shard_map/ppermute | solution.py:21
  16.7 4.7 %collective-permute-start.9 = (bf16[80,640]{1,0:T(8,128)(2,1)S(1)}, bf16[80,640]{1,0:T(8,128)(2,1)S(1)}, u32[]{:S(2)}, u32[]{:S(2)}) collective-permute-start(bf16[80,640]{1,0:T(8,128)(2,1)S(1)} %get-tuple-element.71), channel_id=1, source_target_pairs={{0,8},{4,12},{8,0},{12,4},{16,24},{20,28},{24,16},{28,20},{1,9},{5... | collective-permute-start | bytes 307208 | tf_op jit(solution)/shard_map/ppermute | solution.py:21
  21.6 6.8 %collective-permute-start.12 = (bf16[160,640]{1,0:T(8,128)(2,1)S(1)}, bf16[160,640]{1,0:T(8,128)(2,1)S(1)}, u32[]{:S(2)}, u32[]{:S(2)}) collective-permute-start(bf16[160,640]{1,0:T(8,128)(2,1)S(1)} %get-tuple-element.51.own_ref), channel_id=1, source_target_pairs={{0,1},{1,0},{2,3},{3,2},{4,5},{5,4},{6,7},{7,6},{8,9},{9,8},{10,11... | collective-permute-start | bytes 614408 | tf_op jit(solution)/shard_map/ppermute | solution.py:31
  23.2 7.3 %collective-permute-start.15 = (bf16[160,640]{1,0:T(8,128)(2,1)S(1)}, bf16[160,640]{1,0:T(8,128)(2,1)S(1)}, u32[]{:S(2)}, u32[]{:S(2)}) collective-permute-start(bf16[160,640]{1,0:T(8,128)(2,1)S(1)} %get-tuple-element.57.own_ref), channel_id=1, source_target_pairs={{0,1},{1,0},{2,3},{3,2},{4,5},{5,4},{6,7},{7,6},{8,9},{9,8},{10,11... | collective-permute-start | bytes 614408 | tf_op jit(solution)/shard_map/ppermute | solution.py:31
  28.4 4.7 %collective-permute-start.13 = (bf16[80,640]{1,0:T(8,128)(2,1)S(1)}, bf16[80,640]{1,0:T(8,128)(2,1)S(1)}, u32[]{:S(2)}, u32[]{:S(2)}) collective-permute-start(bf16[80,640]{1,0:T(8,128)(2,1)S(1)} %get-tuple-element.52.refs_0_), channel_id=1, source_target_pairs={{0,8},{1,2},{2,1},{3,11},{4,12},{5,6},{6,5},{7,15},{8,0},{9,10},{1... | collective-permute-start | bytes 307208 | tf_op jit(solution)/shard_map/ppermute | solution.py:31
  29.6 5.1 %collective-permute-start.19 = (bf16[80,640]{1,0:T(8,128)(2,1)S(1)}, bf16[80,640]{1,0:T(8,128)(2,1)S(1)}, u32[]{:S(2)}, u32[]{:S(2)}) collective-permute-start(bf16[80,640]{1,0:T(8,128)(2,1)S(1)} %get-tuple-element.56.refs_1_), channel_id=1, source_target_pairs={{0,8},{1,2},{2,1},{3,11},{4,12},{5,6},{6,5},{7,15},{8,0},{9,10},{1... | collective-permute-start | bytes 307208 | tf_op jit(solution)/shard_map/ppermute | solution.py:31
  30.6 5.3 %collective-permute-start.17 = (bf16[80,640]{1,0:T(8,128)(2,1)S(1)}, bf16[80,640]{1,0:T(8,128)(2,1)S(1)}, u32[]{:S(2)}, u32[]{:S(2)}) collective-permute-start(bf16[80,640]{1,0:T(8,128)(2,1)S(1)} %get-tuple-element.58.refs_2_), channel_id=1, source_target_pairs={{0,8},{1,2},{2,1},{3,11},{4,12},{5,6},{6,5},{7,15},{8,0},{9,10},{1... | collective-permute-start | bytes 307208 | tf_op jit(solution)/shard_map/ppermute | solution.py:31
  32.4 4.7 %collective-permute-start.16 = (bf16[80,640]{1,0:T(8,128)(2,1)S(1)}, bf16[80,640]{1,0:T(8,128)(2,1)S(1)}, u32[]{:S(2)}, u32[]{:S(2)}) collective-permute-start(bf16[80,640]{1,0:T(8,128)(2,1)S(1)} %get-tuple-element.59.refs_3_), channel_id=1, source_target_pairs={{0,8},{1,2},{2,1},{3,11},{4,12},{5,6},{6,5},{7,15},{8,0},{9,10},{1... | collective-permute-start | bytes 307208 | tf_op jit(solution)/shard_map/ppermute | solution.py:31
  33.1 6.5 %collective-permute-start.14 = (bf16[80,640]{1,0:T(8,128)(2,1)S(1)}, bf16[80,640]{1,0:T(8,128)(2,1)S(1)}, u32[]{:S(2)}, u32[]{:S(2)}) collective-permute-start(bf16[80,640]{1,0:T(8,128)(2,1)S(1)} %collective-permute-done.13.refs_0_), channel_id=1, source_target_pairs={{0,4},{1,5},{2,3},{3,2},{4,0},{5,1},{6,7},{7,6},{8,12},{9,13},{10,... | collective-permute-start | bytes 307208 | tf_op jit(solution)/shard_map/ppermute | solution.py:31
  34.7 4.9 %collective-permute-start.20 = (bf16[80,640]{1,0:T(8,128)(2,1)S(1)}, bf16[80,640]{1,0:T(8,128)(2,1)S(1)}, u32[]{:S(2)}, u32[]{:S(2)}) collective-permute-start(bf16[80,640]{1,0:T(8,128)(2,1)S(1)} %collective-permute-done.19.refs_1_), channel_id=1, source_target_pairs={{0,4},{1,5},{2,3},{3,2},{4,0},{5,1},{6,7},{7,6},{8,12},{9,13},{10,... | collective-permute-start | bytes 307208 | tf_op jit(solution)/shard_map/ppermute | solution.py:31
  35.8 4.7 %collective-permute-start.18 = (bf16[80,640]{1,0:T(8,128)(2,1)S(1)}, bf16[80,640]{1,0:T(8,128)(2,1)S(1)}, u32[]{:S(2)}, u32[]{:S(2)}) collective-permute-start(bf16[80,640]{1,0:T(8,128)(2,1)S(1)} %collective-permute-done.17.refs_0_), channel_id=1, source_target_pairs={{0,4},{1,5},{2,3},{3,2},{4,0},{5,1},{6,7},{7,6},{8,12},{9,13},{10,... | collective-permute-start | bytes 307208 | tf_op jit(solution)/shard_map/ppermute | solution.py:31
  37.0 4.7 %collective-permute-start.21 = (bf16[80,640]{1,0:T(8,128)(2,1)S(1)}, bf16[80,640]{1,0:T(8,128)(2,1)S(1)}, u32[]{:S(2)}, u32[]{:S(2)}) collective-permute-start(bf16[80,640]{1,0:T(8,128)(2,1)S(1)} %collective-permute-done.16.refs_0_), channel_id=1, source_target_pairs={{0,4},{1,5},{2,3},{3,2},{4,0},{5,1},{6,7},{7,6},{8,12},{9,13},{10,... | collective-permute-start | bytes 307208 | tf_op jit(solution)/shard_map/ppermute | solution.py:31
  (1 other events, 1.0 us)

commit v9 on v8

--- a/solution.py
+++ b/solution.py
@@ -14,6 +14,10 @@
 
 def in_vmem(*arrays):
     return [pltpu.with_memory_space_constraint(x, pltpu.VMEM) for x in arrays]
+
+
+def in_order(chips):
+    return [0] + sorted(range(1, chips), key=lambda j: (j & (j - 1) != 0, -j))
 
 
 def swap_with(array, mask):
@@ -133,20 +137,19 @@
 
 def gather_kernel(*refs):
     chip = lax.axis_index(ENERGY) // 2
-    first_ref, *others, re_ref, im_ref, all_ref = refs
-    all_ref[chip] = first_ref[0]
-    for j, ref in enumerate(others):
-        all_ref[chip ^ (j + 1)] = ref[...]
+    *pieces, re_ref, im_ref, all_ref = refs
+    for j, ref in zip(in_order(len(pieces)), pieces):
+        all_ref[chip ^ j] = ref[...]
     chips, rows, width = all_ref.shape
     whole = all_ref[...].reshape(chips * rows, width)
     re_ref[...] = packed(whole[:, : width // 2])
     im_ref[...] = packed(whole[:, width // 2 :])
 
 
-def gathered(own, pieces):
-    chips, rows, width = own.shape
+def gathered(pieces):
+    chips, (rows, width) = len(pieces), pieces[0].shape
     part = ((chips * rows // 2, width), jnp.bfloat16)
-    return call(gather_kernel, [part, part], [own, *pieces], [pltpu.VMEM(own.shape, own.dtype)])
+    return call(gather_kernel, [part, part], pieces, [pltpu.VMEM((chips, rows, width), jnp.bfloat16)])
 
 
 def adjoint(stack, sign):
@@ -206,10 +209,33 @@
             ref[...] = state[i * rows : (i + 1) * rows]
 
 
-def first_kernel(last_pair, link_ref, turned_ref, own_ref, came_ref, *out_refs):
+def assembled(pieces, lanes, rows_ref):
+    chip = lax.axis_index(ENERGY) // 2
+    for j, ref in zip(in_order(len(pieces)), pieces):
+        rows_ref[chip ^ j] = ref[:, lanes]
+    chips, rows, size = rows_ref.shape
+    return rows_ref[...].reshape(chips * rows, size)
+
+
+def first_kernel(last_pair, part, link_ref, turned_ref, own_ref, *refs):
+    *pieces, out_a_ref, out_b_ref, rows_ref = refs
+    size = link_ref.shape[0]
     slab = lax.axis_index(SLAB)
     turn = jnp.logical_and(slab % 2 == 1, slab // 2 < last_pair)
-    carry_in(turn, link_ref, turned_ref, own_ref[...], came_ref[...], out_refs)
+    half = out_a_ref.shape[0]
+
+    @pl.when(turn)
+    def _():
+        came = assembled(pieces, slice(part * size, (part + 1) * size), rows_ref)
+        own = unpacked(own_ref[...]).astype(jnp.float32)
+        out = packed((own + moved(link_ref, turned_ref, came)).astype(jnp.bfloat16))
+        out_a_ref[...] = out[:half]
+        out_b_ref[...] = out[half:]
+
+    @pl.when(jnp.logical_not(turn))
+    def _():
+        out_a_ref[...] = own_ref[:half]
+        out_b_ref[...] = own_ref[half:]
 
 
 def arrived(refs):
@@ -224,15 +250,18 @@
 
 
 def base_kernel(last_pair, link_ref, turned_ref, stack_ref, first_ref, second_ref, *refs):
-    *state, came_re_ref, came_im_ref, out_ref, re_ref, im_ref = refs
+    *given, out_ref, re_ref, im_ref, rows_ref = refs
+    state, pieces = given[:4], given[4:]
+    size = link_ref.shape[0]
     slab = lax.axis_index(SLAB)
     turn = jnp.logical_and(slab % 2 == 1, slab // 2 == last_pair)
-    for parts, came_ref, ref in ((state[:2], came_re_ref, re_ref), (state[2:], came_im_ref, im_ref)):
+    for parts, part, ref in ((state[:2], 0, re_ref), (state[2:], 1, im_ref)):
         own = unpacked(joined(parts))
 
         @pl.when(turn)
         def _():
-            ref[...] = (own.astype(jnp.float32) + moved(link_ref, turned_ref, unpacked(came_ref[...]))).astype(jnp.bfloat16)
+            came = assembled(pieces, slice(part * size, (part + 1) * size), rows_ref)
+            ref[...] = (own.astype(jnp.float32) + moved(link_ref, turned_ref, came)).astype(jnp.bfloat16)
 
         @pl.when(jnp.logical_not(turn))
         def _():
@@ -309,7 +338,9 @@
     pieces = pieces + [swap_with(x, 1) for x in pieces]
     sigma = convolve(chips, spread, pieces)
     sigma, link_before = lax.optimization_barrier((sigma, link_before))
-    own_re, own_im = gathered(sigma, [swap_with(sigma[j], 2 * j) for j in range(1, chips)])
+    own = [sigma[0]] + [swap_with(sigma[j], 2 * j) for j in in_order(chips)[1:]]
+    came = [swap_slabs(x, other_in_pair) for x in own]
+    own_re, own_im = gathered(own)
 
     own_re, own_im, link_before = lax.optimization_barrier((own_re, own_im, link_before))
     square = (link.shape, jnp.bfloat16)
@@ -322,14 +353,11 @@
         [link, link_before, g_retarded[0, 0]],
     )
     turned, step, turned_step, *base, far_stack, far_first, far_second, half_a, half_b = prepared
-    came_re = swap_slabs(own_re, other_in_pair)
-    came_im = swap_slabs(own_im, other_in_pair)
-    part = ((size // 2, width), own_im.dtype)
     halves = [((size // 4, width), own_im.dtype)] * 2
     total = [((size, width), jnp.float32)]
-    first = functools.partial(first_kernel, last_pair)
-    re = call(first, halves, [link, turned, own_re, came_re])
-    im = call(first, halves, [link, turned, own_im, came_im])
+    block = pltpu.VMEM((chips, rows, size), jnp.bfloat16)
+    re = call(functools.partial(first_kernel, last_pair, 0), halves, [link, turned, own_re, *came], [block])
+    im = call(functools.partial(first_kernel, last_pair, 1), halves, [link, turned, own_im, *came], [block])
 
     for s in range(1, slabs - 1, 2):
         pair = (s + 1) // 2
@@ -337,7 +365,7 @@
         near_re = [swap_slabs(x, near, 2) for x in re]
         near_im = [swap_slabs(x, near, 2) for x in im]
         if pair == last_pair:
-            near_im[1], came_re, came_im = lax.optimization_barrier((near_im[1], came_re, came_im))
+            near_im[1], came = lax.optimization_barrier((near_im[1], came))
         far_re = [swap_slabs(x, far) for x in near_re]
         far_im = [swap_slabs(x, far) for x in near_im]
         if pair < last_pair:
@@ -345,8 +373,8 @@
             re = call(advance, halves, [step, turned_step, *re, *near_re, *far_re])
             im = call(advance, halves, [step, turned_step, *im, *near_im, *far_im])
     total = [((size, width), jnp.float32)]
-    given = [link, turned, *base, *re, *im, came_re, came_im]
-    scratch = [pltpu.VMEM(link.shape, link.dtype)] * 2
+    given = [link, turned, *base, *re, *im, *came]
+    scratch = [pltpu.VMEM(link.shape, link.dtype)] * 2 + [block]
     (out,) = call(functools.partial(base_kernel, last_pair), total, given, scratch)
     left = functools.partial(left_kernel, last_pair)
     products = [((2 * size, size), jnp.float32)]

time: 43.9 us -> 43.6 us (level)
  starting transfers between devices: 20.3 us -> 24.5 us
  waiting for transfers between devices: 12.3 us -> 8.12 us
    ppermute x11 -> x13, starting transfers between devices: 12.7 us -> 16.9 us  [swap_slabs(): return lax.ppermute(array, (ENERGY, SLAB), pairs)]
    ppermute x11, waiting for transfers between devices: 7 us -> 3.55 us  [swap_with(): return lax.ppermute(array, ENERGY, [(i, i ^ mask) for i in range(devices)])]
    ppermute x11 -> x13, waiting for transfers between devices: 5.25 us -> 4.57 us  [swap_slabs(): return lax.ppermute(array, (ENERGY, SLAB), pairs)]
  transfers between devices with their start and end apart: 22 -> 24, of which waited for: 14 -> 10; matrix products, arithmetic and copies ran while one was open for 3% -> 3% of each run, Pallas kernels for 15% -> 16%
where the time goes in v9:
time: 43.6 us; the launch traced here: 43.4 us
  starting transfers between devices  24.5 us (56%)
  Pallas kernels  8.49 us (19%)
  waiting for transfers between devices  8.12 us (19%)
  local copies, waits for them, and re-layouts  2.17 us (5%)
    ppermute x13, starting transfers between devices, swap_slabs(): return lax.ppermute(array, (ENERGY, SLAB), pairs)  16.9 us
    ppermute x11, starting transfers between devices, swap_with(): return lax.ppermute(array, ENERGY, [(i, i ^ mask) for i in range(devices)])  7.62 us
    pallas_call x8, Pallas kernels, call(): pl.pallas_call(kernel, out_shape=outs, in_specs=[WHOLE] * len(given), out...  5.65 us
    ppermute x13, waiting for transfers between devices, swap_slabs(): return lax.ppermute(array, (ENERGY, SLAB), pairs)  4.57 us
    ppermute x11, waiting for transfers between devices, swap_with(): return lax.ppermute(array, ENERGY, [(i, i ^ mask) for i in range(devices)])  3.55 us
    pallas_call x1, Pallas kernels, local(): pl.pallas_call(functools.partial(late_kernel, last_pair), out_shape=jax.S...  1.7 us
    pallas_call x1, Pallas kernels, convolve(): pl.pallas_call(functools.partial(conv_kernel, chips), out_shape=pltpu.VME...  1.15 us
    dynamic_slice x1, local copies, waits for them, and re-layouts, local(): lax.dynamic_slice(lesser, (rows * (chip ^ j), 0), (rows, width))  1.13 us
  transfers between devices with their start and end apart: 24, of which 10 were waited for; matrix products, arithmetic and copies ran while one was open for 3% of the time, Pallas kernels for 16%

profile of v9, /device:TPU:16, one launch (start us, length us, event | category | flops | bytes accessed | tf_op | source)
XLA Modules:
  0.0 43.4 jit_solution(13649572922983302961)
XLA Ops:
  0.0 1.1 %dynamic-slice_bitcast_fusion = (bf16[80,640]{1,0:T(8,128)(2,1)S(1)}, bf16[80,640]{1,0:T(8,128)(2,1)S(1)}, bf16[80,640]{1,0:T(8,128)(2,1)S(1)}, bf16[80,640]{1,0:T(8,128)(2,1)S(1)}) fusion(bf16[1,1,320,640]{3,2,1,0:T(8,128)(2,1)} %param.4, s32[]{:T(128)S(6)} %select_n.21, s32[]{:T(128)S(6)} %select_n.19, s32[]{:T(128)S(6)} %select_n.18, s32[]{:T(128)S(6)} %select_n.20), kind=kLoop, calls=%fused_computation.4 | loop fusion | bytes 819216 | tf_op jit(solution)/shard_map/dynamic_slice | solution.py:330
  1.1 1.6 %collective-permute-start.1 = (bf16[80,640]{1,0:T(8,128)(2,1)S(1)}, bf16[80,640]{1,0:T(8,128)(2,1)S(1)}, u32[]{:S(2)}, u32[]{:S(2)}) collective-permute-start(bf16[80,640]{1,0:T(8,128)(2,1)S(1)} %get-tuple-element.78), channel_id=1, source_target_pairs={{0,8},{4,12},{8,0},{12,4},{16,24},{20,28},{24,16},{28,20},{1,9},{5... | collective-permute-start | bytes 307208 | tf_op jit(solution)/shard_map/ppermute | solution.py:25
  2.7 1.5 %collective-permute-start.2 = (bf16[80,640]{1,0:T(8,128)(2,1)S(1)}, bf16[80,640]{1,0:T(8,128)(2,1)S(1)}, u32[]{:S(2)}, u32[]{:S(2)}) collective-permute-start(bf16[80,640]{1,0:T(8,128)(2,1)S(1)} %get-tuple-element.80), channel_id=1, source_target_pairs={{0,16},{4,20},{8,24},{12,28},{16,0},{20,4},{24,8},{28,12},{1,17},{... | collective-permute-start | bytes 307208 | tf_op jit(solution)/shard_map/ppermute | solution.py:25
  4.7 1.0 %copy-done.2 = bf16[8,1,40,640]{3,2,1,0:T(8,128)(2,1)S(1)} copy-done((bf16[8,1,40,640]{3,2,1,0:T(8,128)(2,1)S(1)}, bf16[8,1,40,640]{3,2,1,0:T(8,128)(2,1)}, u32[]{:S(2)}) %copy-start.2) | copy-done | bytes 409624
  6.1 1.6 %collective-permute-start.8 = (bf16[320,320]{1,0:T(8,128)(2,1)S(1)}, bf16[320,320]{1,0:T(8,128)(2,1)S(1)}, u32[]{:S(2)}, u32[]{:S(2)}) collective-permute-start(bf16[320,320]{1,0:T(8,128)(2,1)S(1)} %bitcast.20), channel_id=1, source_target_pairs={{0,1},{1,0},{2,3},{3,2},{4,5},{5,4},{6,7},{7,6},{8,9},{9,8},{10,11... | collective-permute-start | bytes 614408 | tf_op jit(solution)/shard_map/ppermute | solution.py:35
  10.2 1.0 %collective-permute-done.7.refs_7_ = bf16[80,640]{1,0:T(8,128)(2,1)S(1)} collective-permute-done((bf16[80,640]{1,0:T(8,128)(2,1)S(1)}, bf16[80,640]{1,0:T(8,128)(2,1)S(1)}, u32[]{:S(2)}, u32[]{:S(2)}) %collective-permute-start.7) | collective-permute-done | bytes 102432 | tf_op jit(solution)/shard_map/ppermute | solution.py:25
  11.2 1.1 %shard_map.47 = bf16[4,80,640]{2,1,0:T(8,128)(2,1)S(1)} custom-call(f32[8,80,640]{2,1,0:T(8,128)S(1)} %get-tuple-element.42.w_ref, f32[8,80,640]{2,1,0:T(8,128)S(1)} %get-tuple-element.43.v_ref, bf16[80,640]{1,0:T(8,128)(2,1)S(1)} %get-tuple-element.79.refs_0_, bf16[80,640]{1,0:T(8,128)(2,1)S(1)} %collective-permute-done.1.refs_1_, ...), custom_call_target="tpu_custom_call" | custom-call | flops 13107200 | tf_op jit(solution)/shard_map/pallas_call | solution.py:109
  12.3 1.4 %collective-permute-done.8.before_ref = bf16[320,320]{1,0:T(8,128)(2,1)S(1)} collective-permute-done((bf16[320,320]{1,0:T(8,128)(2,1)S(1)}, bf16[320,320]{1,0:T(8,128)(2,1)S(1)}, u32[]{:S(2)}, u32[]{:S(2)}) %collective-permute-start.8) | collective-permute-done | bytes 204832 | tf_op jit(solution)/shard_map/ppermute | solution.py:35
  13.7 1.6 %collective-permute-start.9 = (bf16[80,640]{1,0:T(8,128)(2,1)S(1)}, bf16[80,640]{1,0:T(8,128)(2,1)S(1)}, u32[]{:S(2)}, u32[]{:S(2)}) collective-permute-start(bf16[80,640]{1,0:T(8,128)(2,1)S(1)} %get-tuple-element.75), channel_id=1, source_target_pairs={{0,16},{4,20},{8,24},{12,28},{16,0},{20,4},{24,8},{28,12},{1,17},{... | collective-permute-start | bytes 307208 | tf_op jit(solution)/shard_map/ppermute | solution.py:25
  15.3 1.5 %collective-permute-start.10 = (bf16[80,640]{1,0:T(8,128)(2,1)S(1)}, bf16[80,640]{1,0:T(8,128)(2,1)S(1)}, u32[]{:S(2)}, u32[]{:S(2)}) collective-permute-start(bf16[80,640]{1,0:T(8,128)(2,1)S(1)} %get-tuple-element.74), channel_id=1, source_target_pairs={{0,8},{4,12},{8,0},{12,4},{16,24},{20,28},{24,16},{28,20},{1,9},{5... | collective-permute-start | bytes 307208 | tf_op jit(solution)/shard_map/ppermute | solution.py:25
  17.3 1.6 %collective-permute-start.12 = (bf16[80,640]{1,0:T(8,128)(2,1)S(1)}, bf16[80,640]{1,0:T(8,128)(2,1)S(1)}, u32[]{:S(2)}, u32[]{:S(2)}) collective-permute-start(bf16[80,640]{1,0:T(8,128)(2,1)S(1)} %get-tuple-element.76.refs_0_), channel_id=1, source_target_pairs={{0,1},{1,0},{2,3},{3,2},{4,5},{5,4},{6,7},{7,6},{8,9},{9,8},{10,11... | collective-permute-start | bytes 307208 | tf_op jit(solution)/shard_map/ppermute | solution.py:35
  18.8 1.3 %collective-permute-start.13 = (bf16[80,640]{1,0:T(8,128)(2,1)S(1)}, bf16[80,640]{1,0:T(8,128)(2,1)S(1)}, u32[]{:S(2)}, u32[]{:S(2)}) collective-permute-start(bf16[80,640]{1,0:T(8,128)(2,1)S(1)} %collective-permute-done.9.refs_1_), channel_id=1, source_target_pairs={{0,1},{1,0},{2,3},{3,2},{4,5},{5,4},{6,7},{7,6},{8,9},{9,8},{10,11... | collective-permute-start | bytes 307208 | tf_op jit(solution)/shard_map/ppermute | solution.py:35
  20.2 1.5 %collective-permute-start.14 = (bf16[80,640]{1,0:T(8,128)(2,1)S(1)}, bf16[80,640]{1,0:T(8,128)(2,1)S(1)}, u32[]{:S(2)}, u32[]{:S(2)}) collective-permute-start(bf16[80,640]{1,0:T(8,128)(2,1)S(1)} %collective-permute-done.10.refs_2_), channel_id=1, source_target_pairs={{0,1},{1,0},{2,3},{3,2},{4,5},{5,4},{6,7},{7,6},{8,9},{9,8},{10,11... | collective-permute-start | bytes 307208 | tf_op jit(solution)/shard_map/ppermute | solution.py:35
  22.3 1.6 %collective-permute-start.15 = (bf16[80,640]{1,0:T(8,128)(2,1)S(1)}, bf16[80,640]{1,0:T(8,128)(2,1)S(1)}, u32[]{:S(2)}, u32[]{:S(2)}) collective-permute-start(bf16[80,640]{1,0:T(8,128)(2,1)S(1)} %collective-permute-done.11.refs_3_), channel_id=1, source_target_pairs={{0,1},{1,0},{2,3},{3,2},{4,5},{5,4},{6,7},{7,6},{8,9},{9,8},{10,11... | collective-permute-start | bytes 307208 | tf_op jit(solution)/shard_map/ppermute | solution.py:35
  24.1 2.5 %shard_map.49 = (bf16[320,320]{1,0:T(8,128)(2,1)S(1)}, bf16[320,320]{1,0:T(8,128)(2,1)}, bf16[320,320]{1,0:T(8,128)(2,1)}, bf16[640,320]{1,0:T(8,128)(2,1)S(1)},...) custom-call(bf16[320,320]{1,0:T(8,128)(2,1)S(1)} %bitcast.21, ...), custom_call_target="tpu_custom_call" | custom-call | tf_op jit(solution)/shard_map/pallas_call | solution.py:40
  27.2 1.2 %collective-permute-start.16 = (bf16[80,640]{1,0:T(8,128)(2,1)S(1)}, bf16[80,640]{1,0:T(8,128)(2,1)S(1)}, u32[]{:S(2)}, u32[]{:S(2)}) collective-permute-start(bf16[80,640]{1,0:T(8,128)(2,1)S(1)} %get-tuple-element.54.refs_0_), channel_id=1, source_target_pairs={{0,8},{1,2},{2,1},{3,11},{4,12},{5,6},{6,5},{7,15},{8,0},{9,10},{1... | collective-permute-start | bytes 307208 | tf_op jit(solution)/shard_map/ppermute | solution.py:35
  29.3 1.9 %collective-permute-start.19 = (bf16[80,640]{1,0:T(8,128)(2,1)S(1)}, bf16[80,640]{1,0:T(8,128)(2,1)S(1)}, u32[]{:S(2)}, u32[]{:S(2)}) collective-permute-start(bf16[80,640]{1,0:T(8,128)(2,1)S(1)} %get-tuple-element.60.refs_2_), channel_id=1, source_target_pairs={{0,8},{1,2},{2,1},{3,11},{4,12},{5,6},{6,5},{7,15},{8,0},{9,10},{1... | collective-permute-start | bytes 307208 | tf_op jit(solution)/shard_map/ppermute | solution.py:35
  31.4 1.7 %collective-permute-done.16.refs_0_ = bf16[80,640]{1,0:T(8,128)(2,1)S(1)} collective-permute-done((bf16[80,640]{1,0:T(8,128)(2,1)S(1)}, bf16[80,640]{1,0:T(8,128)(2,1)S(1)}, u32[]{:S(2)}, u32[]{:S(2)}) %collective-permute-start.16) | collective-permute-done | bytes 102432 | tf_op jit(solution)/shard_map/ppermute | solution.py:35
  33.1 1.6 %collective-permute-start.17 = (bf16[80,640]{1,0:T(8,128)(2,1)S(1)}, bf16[80,640]{1,0:T(8,128)(2,1)S(1)}, u32[]{:S(2)}, u32[]{:S(2)}) collective-permute-start(bf16[80,640]{1,0:T(8,128)(2,1)S(1)} %collective-permute-done.16.refs_0_), channel_id=1, source_target_pairs={{0,4},{1,5},{2,3},{3,2},{4,0},{5,1},{6,7},{7,6},{8,12},{9,13},{10,... | collective-permute-start | bytes 307208 | tf_op jit(solution)/shard_map/ppermute | solution.py:35
  34.6 1.3 %collective-permute-start.22 = (bf16[80,640]{1,0:T(8,128)(2,1)S(1)}, bf16[80,640]{1,0:T(8,128)(2,1)S(1)}, u32[]{:S(2)}, u32[]{:S(2)}) collective-permute-start(bf16[80,640]{1,0:T(8,128)(2,1)S(1)} %collective-permute-done.21.refs_1_), channel_id=1, source_target_pairs={{0,4},{1,5},{2,3},{3,2},{4,0},{5,1},{6,7},{7,6},{8,12},{9,13},{10,... | collective-permute-start | bytes 307208 | tf_op jit(solution)/shard_map/ppermute | solution.py:35
  36.0 1.1 %collective-permute-start.20 = (bf16[80,640]{1,0:T(8,128)(2,1)S(1)}, bf16[80,640]{1,0:T(8,128)(2,1)S(1)}, u32[]{:S(2)}, u32[]{:S(2)}) collective-permute-start(bf16[80,640]{1,0:T(8,128)(2,1)S(1)} %collective-permute-done.19.refs_0_), channel_id=1, source_target_pairs={{0,4},{1,5},{2,3},{3,2},{4,0},{5,1},{6,7},{7,6},{8,12},{9,13},{10,... | collective-permute-start | bytes 307208 | tf_op jit(solution)/shard_map/ppermute | solution.py:35
  37.1 1.1 %collective-permute-start.23 = (bf16[80,640]{1,0:T(8,128)(2,1)S(1)}, bf16[80,640]{1,0:T(8,128)(2,1)S(1)}, u32[]{:S(2)}, u32[]{:S(2)}) collective-permute-start(bf16[80,640]{1,0:T(8,128)(2,1)S(1)} %collective-permute-done.18.refs_0_), channel_id=1, source_target_pairs={{0,4},{1,5},{2,3},{3,2},{4,0},{5,1},{6,7},{7,6},{8,12},{9,13},{10,... | collective-permute-start | bytes 307208 | tf_op jit(solution)/shard_map/ppermute | solution.py:35
  38.2 1.6 %shard_map.52.base_ref = f32[320,640]{1,0:T(8,128)S(1)} custom-call(bf16[320,320]{1,0:T(8,128)(2,1)S(1)} %bitcast.24, bf16[320,320]{1,0:T(8,128)(2,1)S(1)} %get-tuple-element.52.turned_ref, bf16[640,320]{1,0:T(8,128)(2,1)S(1)} %get-tuple-element.55.stack_ref, bf16[320,640]{1,0:T(8,128)(2,1)S(1)} %get-tuple-element.56.first_ref, ...), custom_call_target="tpu_custom_call" | custom-call | tf_op jit(solution)/shard_map/pallas_call | solution.py:40
  41.7 1.7 %shard_map.55 = bf16[320,640]{1,0:T(8,128)(2,1)} custom-call(bf16[320,640]{1,0:T(8,128)(2,1)S(1)} %get-tuple-element.49.far_first_ref, bf16[320,640]{1,0:T(8,128)(2,1)S(1)} %get-tuple-element.50.far_second_ref, bf16[640,160]{1,0:T(8,128)(2,1)S(1)} %get-tuple-element.51.half_ref, f32[320,640]{1,0:T(8,128)S(1)} %shard_map.52.base_ref, ...), custom_call_target="tpu_custom_call" | custom-call | tf_op jit(solution)/shard_map/pallas_call | solution.py:386
  (42 shorter events, 8.2 us)
Async XLA Ops:
  0.0 4.7 %collective-permute-start = (bf16[8,40,640]{2,1,0:T(8,128)(2,1)}, bf16[8,40,640]{2,1,0:T(8,128)(2,1)S(1)}, u32[]{:S(2)}, u32[]{:S(2)}) collective-permute-start(bf16[8,40,640]{2,1,0:T(8,128)(2,1)} %bitcast.26), channel_id=1, source_target_pairs={{0,4},{4,0},{8,12},{12,8},{16,20},{20,16},{24,28},{28,24},{1,5},{5... | collective-permute-start | bytes 1228808 | tf_op jit(solution)/shard_map/ppermute | solution.py:25
  1.1 6.6 %collective-permute-start.1 = (bf16[80,640]{1,0:T(8,128)(2,1)S(1)}, bf16[80,640]{1,0:T(8,128)(2,1)S(1)}, u32[]{:S(2)}, u32[]{:S(2)}) collective-permute-start(bf16[80,640]{1,0:T(8,128)(2,1)S(1)} %get-tuple-element.78), channel_id=1, source_target_pairs={{0,8},{4,12},{8,0},{12,4},{16,24},{20,28},{24,16},{28,20},{1,9},{5... | collective-permute-start | bytes 307208 | tf_op jit(solution)/shard_map/ppermute | solution.py:25
  2.7 6.2 %collective-permute-start.2 = (bf16[80,640]{1,0:T(8,128)(2,1)S(1)}, bf16[80,640]{1,0:T(8,128)(2,1)S(1)}, u32[]{:S(2)}, u32[]{:S(2)}) collective-permute-start(bf16[80,640]{1,0:T(8,128)(2,1)S(1)} %get-tuple-element.80), channel_id=1, source_target_pairs={{0,16},{4,20},{8,24},{12,28},{16,0},{20,4},{24,8},{28,12},{1,17},{... | collective-permute-start | bytes 307208 | tf_op jit(solution)/shard_map/ppermute | solution.py:25
  4.2 5.6 %collective-permute-start.3 = (bf16[80,640]{1,0:T(8,128)(2,1)S(1)}, bf16[80,640]{1,0:T(8,128)(2,1)S(1)}, u32[]{:S(2)}, u32[]{:S(2)}) collective-permute-start(bf16[80,640]{1,0:T(8,128)(2,1)S(1)} %get-tuple-element.77), channel_id=1, source_target_pairs={{0,24},{4,28},{8,16},{12,20},{16,8},{20,12},{24,0},{28,4},{1,25},{... | collective-permute-start | bytes 307208 | tf_op jit(solution)/shard_map/ppermute | solution.py:25
  6.1 7.5 %collective-permute-start.8 = (bf16[320,320]{1,0:T(8,128)(2,1)S(1)}, bf16[320,320]{1,0:T(8,128)(2,1)S(1)}, u32[]{:S(2)}, u32[]{:S(2)}) collective-permute-start(bf16[320,320]{1,0:T(8,128)(2,1)S(1)} %bitcast.20), channel_id=1, source_target_pairs={{0,1},{1,0},{2,3},{3,2},{4,5},{5,4},{6,7},{7,6},{8,9},{9,8},{10,11... | collective-permute-start | bytes 614408 | tf_op jit(solution)/shard_map/ppermute | solution.py:35
  7.8 2.1 %collective-permute-start.4 = (bf16[80,640]{1,0:T(8,128)(2,1)S(1)}, bf16[80,640]{1,0:T(8,128)(2,1)S(1)}, u32[]{:S(2)}, u32[]{:S(2)}) collective-permute-start(bf16[80,640]{1,0:T(8,128)(2,1)S(1)} %get-tuple-element.79.refs_0_), channel_id=1, source_target_pairs={{0,4},{4,0},{8,12},{12,8},{16,20},{20,16},{24,28},{28,24},{1,5},{5... | collective-permute-start | bytes 307208 | tf_op jit(solution)/shard_map/ppermute | solution.py:25
  7.8 2.1 %collective-permute-start.5 = (bf16[80,640]{1,0:T(8,128)(2,1)S(1)}, bf16[80,640]{1,0:T(8,128)(2,1)S(1)}, u32[]{:S(2)}, u32[]{:S(2)}) collective-permute-start(bf16[80,640]{1,0:T(8,128)(2,1)S(1)} %collective-permute-done.1.refs_1_), channel_id=1, source_target_pairs={{0,4},{4,0},{8,12},{12,8},{16,20},{20,16},{24,28},{28,24},{1,5},{5... | collective-permute-start | bytes 307208 | tf_op jit(solution)/shard_map/ppermute | solution.py:25
  8.9 1.3 %collective-permute-start.6 = (bf16[80,640]{1,0:T(8,128)(2,1)S(1)}, bf16[80,640]{1,0:T(8,128)(2,1)S(1)}, u32[]{:S(2)}, u32[]{:S(2)}) collective-permute-start(bf16[80,640]{1,0:T(8,128)(2,1)S(1)} %collective-permute-done.2.refs_2_), channel_id=1, source_target_pairs={{0,4},{4,0},{8,12},{12,8},{16,20},{20,16},{24,28},{28,24},{1,5},{5... | collective-permute-start | bytes 307208 | tf_op jit(solution)/shard_map/ppermute | solution.py:25
  9.9 1.3 %collective-permute-start.7 = (bf16[80,640]{1,0:T(8,128)(2,1)S(1)}, bf16[80,640]{1,0:T(8,128)(2,1)S(1)}, u32[]{:S(2)}, u32[]{:S(2)}) collective-permute-start(bf16[80,640]{1,0:T(8,128)(2,1)S(1)} %collective-permute-done.3.refs_3_), channel_id=1, source_target_pairs={{0,4},{4,0},{8,12},{12,8},{16,20},{20,16},{24,28},{28,24},{1,5},{5... | collective-permute-start | bytes 307208 | tf_op jit(solution)/shard_map/ppermute | solution.py:25
  13.7 5.1 %collective-permute-start.9 = (bf16[80,640]{1,0:T(8,128)(2,1)S(1)}, bf16[80,640]{1,0:T(8,128)(2,1)S(1)}, u32[]{:S(2)}, u32[]{:S(2)}) collective-permute-start(bf16[80,640]{1,0:T(8,128)(2,1)S(1)} %get-tuple-element.75), channel_id=1, source_target_pairs={{0,16},{4,20},{8,24},{12,28},{16,0},{20,4},{24,8},{28,12},{1,17},{... | collective-permute-start | bytes 307208 | tf_op jit(solution)/shard_map/ppermute | solution.py:25
  15.3 4.9 %collective-permute-start.10 = (bf16[80,640]{1,0:T(8,128)(2,1)S(1)}, bf16[80,640]{1,0:T(8,128)(2,1)S(1)}, u32[]{:S(2)}, u32[]{:S(2)}) collective-permute-start(bf16[80,640]{1,0:T(8,128)(2,1)S(1)} %get-tuple-element.74), channel_id=1, source_target_pairs={{0,8},{4,12},{8,0},{12,4},{16,24},{20,28},{24,16},{28,20},{1,9},{5... | collective-permute-start | bytes 307208 | tf_op jit(solution)/shard_map/ppermute | solution.py:25
  16.8 5.6 %collective-permute-start.11 = (bf16[80,640]{1,0:T(8,128)(2,1)S(1)}, bf16[80,640]{1,0:T(8,128)(2,1)S(1)}, u32[]{:S(2)}, u32[]{:S(2)}) collective-permute-start(bf16[80,640]{1,0:T(8,128)(2,1)S(1)} %get-tuple-element.73), channel_id=1, source_target_pairs={{0,24},{4,28},{8,16},{12,20},{16,8},{20,12},{24,0},{28,4},{1,25},{... | collective-permute-start | bytes 307208 | tf_op jit(solution)/shard_map/ppermute | solution.py:25
  17.3 9.4 %collective-permute-start.12 = (bf16[80,640]{1,0:T(8,128)(2,1)S(1)}, bf16[80,640]{1,0:T(8,128)(2,1)S(1)}, u32[]{:S(2)}, u32[]{:S(2)}) collective-permute-start(bf16[80,640]{1,0:T(8,128)(2,1)S(1)} %get-tuple-element.76.refs_0_), channel_id=1, source_target_pairs={{0,1},{1,0},{2,3},{3,2},{4,5},{5,4},{6,7},{7,6},{8,9},{9,8},{10,11... | collective-permute-start | bytes 307208 | tf_op jit(solution)/shard_map/ppermute | solution.py:35
  18.8 7.8 %collective-permute-start.13 = (bf16[80,640]{1,0:T(8,128)(2,1)S(1)}, bf16[80,640]{1,0:T(8,128)(2,1)S(1)}, u32[]{:S(2)}, u32[]{:S(2)}) collective-permute-start(bf16[80,640]{1,0:T(8,128)(2,1)S(1)} %collective-permute-done.9.refs_1_), channel_id=1, source_target_pairs={{0,1},{1,0},{2,3},{3,2},{4,5},{5,4},{6,7},{7,6},{8,9},{9,8},{10,11... | collective-permute-start | bytes 307208 | tf_op jit(solution)/shard_map/ppermute | solution.py:35
  20.2 6.4 %collective-permute-start.14 = (bf16[80,640]{1,0:T(8,128)(2,1)S(1)}, bf16[80,640]{1,0:T(8,128)(2,1)S(1)}, u32[]{:S(2)}, u32[]{:S(2)}) collective-permute-start(bf16[80,640]{1,0:T(8,128)(2,1)S(1)} %collective-permute-done.10.refs_2_), channel_id=1, source_target_pairs={{0,1},{1,0},{2,3},{3,2},{4,5},{5,4},{6,7},{7,6},{8,9},{9,8},{10,11... | collective-permute-start | bytes 307208 | tf_op jit(solution)/shard_map/ppermute | solution.py:35
  22.3 4.8 %collective-permute-start.15 = (bf16[80,640]{1,0:T(8,128)(2,1)S(1)}, bf16[80,640]{1,0:T(8,128)(2,1)S(1)}, u32[]{:S(2)}, u32[]{:S(2)}) collective-permute-start(bf16[80,640]{1,0:T(8,128)(2,1)S(1)} %collective-permute-done.11.refs_3_), channel_id=1, source_target_pairs={{0,1},{1,0},{2,3},{3,2},{4,5},{5,4},{6,7},{7,6},{8,9},{9,8},{10,11... | collective-permute-start | bytes 307208 | tf_op jit(solution)/shard_map/ppermute | solution.py:35
  27.2 5.9 %collective-permute-start.16 = (bf16[80,640]{1,0:T(8,128)(2,1)S(1)}, bf16[80,640]{1,0:T(8,128)(2,1)S(1)}, u32[]{:S(2)}, u32[]{:S(2)}) collective-permute-start(bf16[80,640]{1,0:T(8,128)(2,1)S(1)} %get-tuple-element.54.refs_0_), channel_id=1, source_target_pairs={{0,8},{1,2},{2,1},{3,11},{4,12},{5,6},{6,5},{7,15},{8,0},{9,10},{1... | collective-permute-start | bytes 307208 | tf_op jit(solution)/shard_map/ppermute | solution.py:35
  28.4 6.3 %collective-permute-start.21 = (bf16[80,640]{1,0:T(8,128)(2,1)S(1)}, bf16[80,640]{1,0:T(8,128)(2,1)S(1)}, u32[]{:S(2)}, u32[]{:S(2)}) collective-permute-start(bf16[80,640]{1,0:T(8,128)(2,1)S(1)} %get-tuple-element.58.refs_1_), channel_id=1, source_target_pairs={{0,8},{1,2},{2,1},{3,11},{4,12},{5,6},{6,5},{7,15},{8,0},{9,10},{1... | collective-permute-start | bytes 307208 | tf_op jit(solution)/shard_map/ppermute | solution.py:35
  29.3 6.7 %collective-permute-start.19 = (bf16[80,640]{1,0:T(8,128)(2,1)S(1)}, bf16[80,640]{1,0:T(8,128)(2,1)S(1)}, u32[]{:S(2)}, u32[]{:S(2)}) collective-permute-start(bf16[80,640]{1,0:T(8,128)(2,1)S(1)} %get-tuple-element.60.refs_2_), channel_id=1, source_target_pairs={{0,8},{1,2},{2,1},{3,11},{4,12},{5,6},{6,5},{7,15},{8,0},{9,10},{1... | collective-permute-start | bytes 307208 | tf_op jit(solution)/shard_map/ppermute | solution.py:35
  31.2 5.8 %collective-permute-start.18 = (bf16[80,640]{1,0:T(8,128)(2,1)S(1)}, bf16[80,640]{1,0:T(8,128)(2,1)S(1)}, u32[]{:S(2)}, u32[]{:S(2)}) collective-permute-start(bf16[80,640]{1,0:T(8,128)(2,1)S(1)} %get-tuple-element.61.refs_3_), channel_id=1, source_target_pairs={{0,8},{1,2},{2,1},{3,11},{4,12},{5,6},{6,5},{7,15},{8,0},{9,10},{1... | collective-permute-start | bytes 307208 | tf_op jit(solution)/shard_map/ppermute | solution.py:35
  33.1 6.7 %collective-permute-start.17 = (bf16[80,640]{1,0:T(8,128)(2,1)S(1)}, bf16[80,640]{1,0:T(8,128)(2,1)S(1)}, u32[]{:S(2)}, u32[]{:S(2)}) collective-permute-start(bf16[80,640]{1,0:T(8,128)(2,1)S(1)} %collective-permute-done.16.refs_0_), channel_id=1, source_target_pairs={{0,4},{1,5},{2,3},{3,2},{4,0},{5,1},{6,7},{7,6},{8,12},{9,13},{10,... | collective-permute-start | bytes 307208 | tf_op jit(solution)/shard_map/ppermute | solution.py:35
  34.6 5.1 %collective-permute-start.22 = (bf16[80,640]{1,0:T(8,128)(2,1)S(1)}, bf16[80,640]{1,0:T(8,128)(2,1)S(1)}, u32[]{:S(2)}, u32[]{:S(2)}) collective-permute-start(bf16[80,640]{1,0:T(8,128)(2,1)S(1)} %collective-permute-done.21.refs_1_), channel_id=1, source_target_pairs={{0,4},{1,5},{2,3},{3,2},{4,0},{5,1},{6,7},{7,6},{8,12},{9,13},{10,... | collective-permute-start | bytes 307208 | tf_op jit(solution)/shard_map/ppermute | solution.py:35
  36.0 4.7 %collective-permute-start.20 = (bf16[80,640]{1,0:T(8,128)(2,1)S(1)}, bf16[80,640]{1,0:T(8,128)(2,1)S(1)}, u32[]{:S(2)}, u32[]{:S(2)}) collective-permute-start(bf16[80,640]{1,0:T(8,128)(2,1)S(1)} %collective-permute-done.19.refs_0_), channel_id=1, source_target_pairs={{0,4},{1,5},{2,3},{3,2},{4,0},{5,1},{6,7},{7,6},{8,12},{9,13},{10,... | collective-permute-start | bytes 307208 | tf_op jit(solution)/shard_map/ppermute | solution.py:35
  37.1 4.7 %collective-permute-start.23 = (bf16[80,640]{1,0:T(8,128)(2,1)S(1)}, bf16[80,640]{1,0:T(8,128)(2,1)S(1)}, u32[]{:S(2)}, u32[]{:S(2)}) collective-permute-start(bf16[80,640]{1,0:T(8,128)(2,1)S(1)} %collective-permute-done.18.refs_0_), channel_id=1, source_target_pairs={{0,4},{1,5},{2,3},{3,2},{4,0},{5,1},{6,7},{7,6},{8,12},{9,13},{10,... | collective-permute-start | bytes 307208 | tf_op jit(solution)/shard_map/ppermute | solution.py:35
  (3 other events, 23.5 us)

commit v10 on v9

--- a/solution.py
+++ b/solution.py
@@ -332,7 +332,7 @@
 
     link = coupling[0]
     other_in_pair = {s: s ^ 1 for s in range(slabs)}
-    link, spread = lax.optimization_barrier((link, spread))
+    pieces[1], link, spread = lax.optimization_barrier((pieces[1], link, spread))
     link_before = swap_slabs(link, other_in_pair)
 
     pieces = pieces + [swap_with(x, 1) for x in pieces]
@@ -363,7 +363,7 @@
         pair = (s + 1) // 2
         near, far = {s: s + 1, s + 1: s}, {s + 1: s + 2, s + 2: s + 1}
         near_re = [swap_slabs(x, near, 2) for x in re]
-        near_im = [swap_slabs(x, near, 2) for x in im]
+        near_im = [swap_slabs(x, near, 4) for x in im]
         if pair == last_pair:
             near_im[1], came = lax.optimization_barrier((near_im[1], came))
         far_re = [swap_slabs(x, far) for x in near_re]

time: 43.6 us -> 42.6 us (0.977)
  starting transfers between devices: 24.5 us -> 22.2 us
  waiting for transfers between devices: 8.12 us -> 9.47 us
    ppermute x13, starting transfers between devices: 16.9 us -> 14.6 us  [swap_slabs(): return lax.ppermute(array, (ENERGY, SLAB), pairs)]
    ppermute x11, waiting for transfers between devices: 3.55 us -> 4.58 us  [swap_with(): return lax.ppermute(array, ENERGY, [(i, i ^ mask) for i in range(devices)])]
  transfers between devices with their start and end apart: 24 -> 24, of which waited for: 10 -> 15; matrix products, arithmetic and copies ran while one was open for 3% -> 3% of each run, Pallas kernels for 16% -> 16%
where the time goes in v10:
time: 42.6 us; the launch traced here: 42.5 us
  starting transfers between devices  22.2 us (52%)
  waiting for transfers between devices  9.47 us (22%)
  Pallas kernels  8.49 us (20%)
  local copies, waits for them, and re-layouts  2.17 us (5%)
    ppermute x13, starting transfers between devices, swap_slabs(): return lax.ppermute(array, (ENERGY, SLAB), pairs)  14.6 us
    ppermute x11, starting transfers between devices, swap_with(): return lax.ppermute(array, ENERGY, [(i, i ^ mask) for i in range(devices)])  7.62 us
    pallas_call x8, Pallas kernels, call(): pl.pallas_call(kernel, out_shape=outs, in_specs=[WHOLE] * len(given), out...  5.65 us
    ppermute x13, waiting for transfers between devices, swap_slabs(): return lax.ppermute(array, (ENERGY, SLAB), pairs)  4.89 us
    ppermute x11, waiting for transfers between devices, swap_with(): return lax.ppermute(array, ENERGY, [(i, i ^ mask) for i in range(devices)])  4.58 us
    pallas_call x1, Pallas kernels, local(): pl.pallas_call(functools.partial(late_kernel, last_pair), out_shape=jax.S...  1.7 us
    pallas_call x1, Pallas kernels, convolve(): pl.pallas_call(functools.partial(conv_kernel, chips), out_shape=pltpu.VME...  1.15 us
    dynamic_slice x1, local copies, waits for them, and re-layouts, local(): lax.dynamic_slice(lesser, (rows * (chip ^ j), 0), (rows, width))  1.13 us
  transfers between devices with their start and end apart: 24, of which 15 were waited for; matrix products, arithmetic and copies ran while one was open for 3% of the time, Pallas kernels for 16%

profile of v10, /device:TPU:16, one launch (start us, length us, event | category | flops | bytes accessed | tf_op | source)
XLA Modules:
  0.0 42.5 jit_solution(10372876879854904409)
XLA Ops:
  0.0 1.1 %dynamic-slice_bitcast_fusion = (bf16[80,640]{1,0:T(8,128)(2,1)S(1)}, bf16[80,640]{1,0:T(8,128)(2,1)S(1)}, bf16[80,640]{1,0:T(8,128)(2,1)S(1)}, bf16[80,640]{1,0:T(8,128)(2,1)S(1)}) fusion(bf16[1,1,320,640]{3,2,1,0:T(8,128)(2,1)} %param.4, s32[]{:T(128)S(6)} %select_n.21, s32[]{:T(128)S(6)} %select_n.19, s32[]{:T(128)S(6)} %select_n.18, s32[]{:T(128)S(6)} %select_n.20), kind=kLoop, calls=%fused_computation.4 | loop fusion | bytes 819216 | tf_op jit(solution)/shard_map/dynamic_slice | solution.py:330
  1.1 1.6 %collective-permute-start = (bf16[80,640]{1,0:T(8,128)(2,1)S(1)}, bf16[80,640]{1,0:T(8,128)(2,1)S(1)}, u32[]{:S(2)}, u32[]{:S(2)}) collective-permute-start(bf16[80,640]{1,0:T(8,128)(2,1)S(1)} %get-tuple-element.81), channel_id=1, source_target_pairs={{0,8},{4,12},{8,0},{12,4},{16,24},{20,28},{24,16},{28,20},{1,9},{5... | collective-permute-start | bytes 307208 | tf_op jit(solution)/shard_map/ppermute | solution.py:25
  2.7 1.5 %collective-permute-start.2 = (bf16[80,640]{1,0:T(8,128)(2,1)S(1)}, bf16[80,640]{1,0:T(8,128)(2,1)S(1)}, u32[]{:S(2)}, u32[]{:S(2)}) collective-permute-start(bf16[80,640]{1,0:T(8,128)(2,1)S(1)} %get-tuple-element.82), channel_id=1, source_target_pairs={{0,16},{4,20},{8,24},{12,28},{16,0},{20,4},{24,8},{28,12},{1,17},{... | collective-permute-start | bytes 307208 | tf_op jit(solution)/shard_map/ppermute | solution.py:25
  4.7 1.0 %copy-done.2 = bf16[8,1,40,640]{3,2,1,0:T(8,128)(2,1)S(1)} copy-done((bf16[8,1,40,640]{3,2,1,0:T(8,128)(2,1)S(1)}, bf16[8,1,40,640]{3,2,1,0:T(8,128)(2,1)}, u32[]{:S(2)}) %copy-start.2) | copy-done | bytes 409624
  6.5 1.6 %collective-permute-start.8 = (bf16[320,320]{1,0:T(8,128)(2,1)S(1)}, bf16[320,320]{1,0:T(8,128)(2,1)S(1)}, u32[]{:S(2)}, u32[]{:S(2)}) collective-permute-start(bf16[320,320]{1,0:T(8,128)(2,1)S(1)} %bitcast.20), channel_id=1, source_target_pairs={{0,1},{1,0},{2,3},{3,2},{4,5},{5,4},{6,7},{7,6},{8,9},{9,8},{10,11... | collective-permute-start | bytes 614408 | tf_op jit(solution)/shard_map/ppermute | solution.py:35
  8.0 0.9 %collective-permute-done.2.refs_2_ = bf16[80,640]{1,0:T(8,128)(2,1)S(1)} collective-permute-done((bf16[80,640]{1,0:T(8,128)(2,1)S(1)}, bf16[80,640]{1,0:T(8,128)(2,1)S(1)}, u32[]{:S(2)}, u32[]{:S(2)}) %collective-permute-start.2) | collective-permute-done | bytes 102432 | tf_op jit(solution)/shard_map/ppermute | solution.py:25
  8.9 1.0 %collective-permute-done.3.refs_3_ = bf16[80,640]{1,0:T(8,128)(2,1)S(1)} collective-permute-done((bf16[80,640]{1,0:T(8,128)(2,1)S(1)}, bf16[80,640]{1,0:T(8,128)(2,1)S(1)}, u32[]{:S(2)}, u32[]{:S(2)}) %collective-permute-start.3) | collective-permute-done | bytes 102432 | tf_op jit(solution)/shard_map/ppermute | solution.py:25
  11.3 1.1 %shard_map.47 = bf16[4,80,640]{2,1,0:T(8,128)(2,1)S(1)} custom-call(f32[8,80,640]{2,1,0:T(8,128)S(1)} %get-tuple-element.43.w_ref, f32[8,80,640]{2,1,0:T(8,128)S(1)} %get-tuple-element.44.v_ref, bf16[80,640]{1,0:T(8,128)(2,1)S(1)} %get-tuple-element.80.refs_0_, bf16[80,640]{1,0:T(8,128)(2,1)S(1)} %collective-permute-done.refs_1_, ...), custom_call_target="tpu_custom_call" | custom-call | flops 13107200 | tf_op jit(solution)/shard_map/pallas_call | solution.py:109
  12.5 1.5 %collective-permute-done.8.before_ref = bf16[320,320]{1,0:T(8,128)(2,1)S(1)} collective-permute-done((bf16[320,320]{1,0:T(8,128)(2,1)S(1)}, bf16[320,320]{1,0:T(8,128)(2,1)S(1)}, u32[]{:S(2)}, u32[]{:S(2)}) %collective-permute-start.8) | collective-permute-done | bytes 204832 | tf_op jit(solution)/shard_map/ppermute | solution.py:35
  14.0 1.6 %collective-permute-start.9 = (bf16[80,640]{1,0:T(8,128)(2,1)S(1)}, bf16[80,640]{1,0:T(8,128)(2,1)S(1)}, u32[]{:S(2)}, u32[]{:S(2)}) collective-permute-start(bf16[80,640]{1,0:T(8,128)(2,1)S(1)} %get-tuple-element.77), channel_id=1, source_target_pairs={{0,16},{4,20},{8,24},{12,28},{16,0},{20,4},{24,8},{28,12},{1,17},{... | collective-permute-start | bytes 307208 | tf_op jit(solution)/shard_map/ppermute | solution.py:25
  15.6 1.5 %collective-permute-start.10 = (bf16[80,640]{1,0:T(8,128)(2,1)S(1)}, bf16[80,640]{1,0:T(8,128)(2,1)S(1)}, u32[]{:S(2)}, u32[]{:S(2)}) collective-permute-start(bf16[80,640]{1,0:T(8,128)(2,1)S(1)} %get-tuple-element.76), channel_id=1, source_target_pairs={{0,8},{4,12},{8,0},{12,4},{16,24},{20,28},{24,16},{28,20},{1,9},{5... | collective-permute-start | bytes 307208 | tf_op jit(solution)/shard_map/ppermute | solution.py:25
  17.6 1.6 %collective-permute-start.12 = (bf16[80,640]{1,0:T(8,128)(2,1)S(1)}, bf16[80,640]{1,0:T(8,128)(2,1)S(1)}, u32[]{:S(2)}, u32[]{:S(2)}) collective-permute-start(bf16[80,640]{1,0:T(8,128)(2,1)S(1)} %get-tuple-element.78.refs_0_), channel_id=1, source_target_pairs={{0,1},{1,0},{2,3},{3,2},{4,5},{5,4},{6,7},{7,6},{8,9},{9,8},{10,11... | collective-permute-start | bytes 307208 | tf_op jit(solution)/shard_map/ppermute | solution.py:35
  19.9 1.6 %collective-permute-start.13 = (bf16[80,640]{1,0:T(8,128)(2,1)S(1)}, bf16[80,640]{1,0:T(8,128)(2,1)S(1)}, u32[]{:S(2)}, u32[]{:S(2)}) collective-permute-start(bf16[80,640]{1,0:T(8,128)(2,1)S(1)} %collective-permute-done.9.refs_1_), channel_id=1, source_target_pairs={{0,1},{1,0},{2,3},{3,2},{4,5},{5,4},{6,7},{7,6},{8,9},{9,8},{10,11... | collective-permute-start | bytes 307208 | tf_op jit(solution)/shard_map/ppermute | solution.py:35
  22.7 1.6 %collective-permute-start.15 = (bf16[80,640]{1,0:T(8,128)(2,1)S(1)}, bf16[80,640]{1,0:T(8,128)(2,1)S(1)}, u32[]{:S(2)}, u32[]{:S(2)}) collective-permute-start(bf16[80,640]{1,0:T(8,128)(2,1)S(1)} %collective-permute-done.11.refs_3_), channel_id=1, source_target_pairs={{0,1},{1,0},{2,3},{3,2},{4,5},{5,4},{6,7},{7,6},{8,9},{9,8},{10,11... | collective-permute-start | bytes 307208 | tf_op jit(solution)/shard_map/ppermute | solution.py:35
  24.4 2.5 %shard_map.49 = (bf16[320,320]{1,0:T(8,128)(2,1)S(1)}, bf16[320,320]{1,0:T(8,128)(2,1)}, bf16[320,320]{1,0:T(8,128)(2,1)}, bf16[640,320]{1,0:T(8,128)(2,1)S(1)},...) custom-call(bf16[320,320]{1,0:T(8,128)(2,1)S(1)} %bitcast.21, ...), custom_call_target="tpu_custom_call" | custom-call | tf_op jit(solution)/shard_map/pallas_call | solution.py:40
  27.3 1.2 %collective-permute-start.16 = (bf16[80,640]{1,0:T(8,128)(2,1)S(1)}, bf16[80,640]{1,0:T(8,128)(2,1)S(1)}, u32[]{:S(2)}, u32[]{:S(2)}) collective-permute-start(bf16[80,640]{1,0:T(8,128)(2,1)S(1)} %get-tuple-element.56.refs_0_), channel_id=1, source_target_pairs={{0,8},{1,2},{2,1},{3,11},{4,12},{5,6},{6,5},{7,15},{8,0},{9,10},{1... | collective-permute-start | bytes 307208 | tf_op jit(solution)/shard_map/ppermute | solution.py:35
  28.5 0.9 %collective-permute-start.21 = (bf16[80,640]{1,0:T(8,128)(2,1)S(1)}, bf16[80,640]{1,0:T(8,128)(2,1)S(1)}, u32[]{:S(2)}, u32[]{:S(2)}) collective-permute-start(bf16[80,640]{1,0:T(8,128)(2,1)S(1)} %get-tuple-element.60.refs_1_), channel_id=1, source_target_pairs={{0,8},{1,2},{2,1},{3,11},{4,12},{5,6},{6,5},{7,15},{8,0},{9,10},{1... | collective-permute-start | bytes 307208 | tf_op jit(solution)/shard_map/ppermute | solution.py:35
  29.5 2.0 %collective-permute-start.19 = (bf16[80,640]{1,0:T(8,128)(2,1)S(1)}, bf16[80,640]{1,0:T(8,128)(2,1)S(1)}, u32[]{:S(2)}, u32[]{:S(2)}) collective-permute-start(bf16[80,640]{1,0:T(8,128)(2,1)S(1)} %get-tuple-element.62.refs_2_), channel_id=1, source_target_pairs={{0,16},{1,2},{2,1},{3,19},{4,20},{5,6},{6,5},{7,23},{8,24},{9,10},... | collective-permute-start | bytes 307208 | tf_op jit(solution)/shard_map/ppermute | solution.py:35
  31.6 1.3 %collective-permute-done.16.refs_0_ = bf16[80,640]{1,0:T(8,128)(2,1)S(1)} collective-permute-done((bf16[80,640]{1,0:T(8,128)(2,1)S(1)}, bf16[80,640]{1,0:T(8,128)(2,1)S(1)}, u32[]{:S(2)}, u32[]{:S(2)}) %collective-permute-start.16) | collective-permute-done | bytes 102432 | tf_op jit(solution)/shard_map/ppermute | solution.py:35
  33.9 0.9 %collective-permute-start.22 = (bf16[80,640]{1,0:T(8,128)(2,1)S(1)}, bf16[80,640]{1,0:T(8,128)(2,1)S(1)}, u32[]{:S(2)}, u32[]{:S(2)}) collective-permute-start(bf16[80,640]{1,0:T(8,128)(2,1)S(1)} %collective-permute-done.21.refs_1_), channel_id=1, source_target_pairs={{0,4},{1,5},{2,3},{3,2},{4,0},{5,1},{6,7},{7,6},{8,12},{9,13},{10,... | collective-permute-start | bytes 307208 | tf_op jit(solution)/shard_map/ppermute | solution.py:35
  35.0 0.9 %collective-permute-start.20 = (bf16[80,640]{1,0:T(8,128)(2,1)S(1)}, bf16[80,640]{1,0:T(8,128)(2,1)S(1)}, u32[]{:S(2)}, u32[]{:S(2)}) collective-permute-start(bf16[80,640]{1,0:T(8,128)(2,1)S(1)} %collective-permute-done.19.refs_0_), channel_id=1, source_target_pairs={{0,4},{1,5},{2,3},{3,2},{4,0},{5,1},{6,7},{7,6},{8,12},{9,13},{10,... | collective-permute-start | bytes 307208 | tf_op jit(solution)/shard_map/ppermute | solution.py:35
  36.1 1.0 %collective-permute-start.23 = (bf16[80,640]{1,0:T(8,128)(2,1)S(1)}, bf16[80,640]{1,0:T(8,128)(2,1)S(1)}, u32[]{:S(2)}, u32[]{:S(2)}) collective-permute-start(bf16[80,640]{1,0:T(8,128)(2,1)S(1)} %collective-permute-done.18.refs_0_), channel_id=1, source_target_pairs={{0,4},{1,5},{2,3},{3,2},{4,0},{5,1},{6,7},{7,6},{8,12},{9,13},{10,... | collective-permute-start | bytes 307208 | tf_op jit(solution)/shard_map/ppermute | solution.py:35
  37.1 1.6 %shard_map.52.base_ref = f32[320,640]{1,0:T(8,128)S(1)} custom-call(bf16[320,320]{1,0:T(8,128)(2,1)S(1)} %bitcast.24, bf16[320,320]{1,0:T(8,128)(2,1)S(1)} %get-tuple-element.54.turned_ref, bf16[640,320]{1,0:T(8,128)(2,1)S(1)} %get-tuple-element.57.stack_ref, bf16[320,640]{1,0:T(8,128)(2,1)S(1)} %get-tuple-element.58.first_ref, ...), custom_call_target="tpu_custom_call" | custom-call | tf_op jit(solution)/shard_map/pallas_call | solution.py:40
  40.8 1.7 %shard_map.55 = bf16[320,640]{1,0:T(8,128)(2,1)} custom-call(bf16[320,640]{1,0:T(8,128)(2,1)S(1)} %get-tuple-element.51.far_first_ref, bf16[320,640]{1,0:T(8,128)(2,1)S(1)} %get-tuple-element.52.far_second_ref, bf16[640,160]{1,0:T(8,128)(2,1)S(1)} %get-tuple-element.53.half_ref, f32[320,640]{1,0:T(8,128)S(1)} %shard_map.52.base_ref, ...), custom_call_target="tpu_custom_call" | custom-call | tf_op jit(solution)/shard_map/pallas_call | solution.py:386
  (42 shorter events, 9.4 us)
Async XLA Ops:
  0.0 4.7 %collective-permute-start.1 = (bf16[8,40,640]{2,1,0:T(8,128)(2,1)}, bf16[8,40,640]{2,1,0:T(8,128)(2,1)S(1)}, u32[]{:S(2)}, u32[]{:S(2)}) collective-permute-start(bf16[8,40,640]{2,1,0:T(8,128)(2,1)} %bitcast.26), channel_id=1, source_target_pairs={{0,4},{4,0},{8,12},{12,8},{16,20},{20,16},{24,28},{28,24},{1,5},{5... | collective-permute-start | bytes 1228808 | tf_op jit(solution)/shard_map/ppermute | solution.py:25
  1.1 5.3 %collective-permute-start = (bf16[80,640]{1,0:T(8,128)(2,1)S(1)}, bf16[80,640]{1,0:T(8,128)(2,1)S(1)}, u32[]{:S(2)}, u32[]{:S(2)}) collective-permute-start(bf16[80,640]{1,0:T(8,128)(2,1)S(1)} %get-tuple-element.81), channel_id=1, source_target_pairs={{0,8},{4,12},{8,0},{12,4},{16,24},{20,28},{24,16},{28,20},{1,9},{5... | collective-permute-start | bytes 307208 | tf_op jit(solution)/shard_map/ppermute | solution.py:25
  2.7 6.2 %collective-permute-start.2 = (bf16[80,640]{1,0:T(8,128)(2,1)S(1)}, bf16[80,640]{1,0:T(8,128)(2,1)S(1)}, u32[]{:S(2)}, u32[]{:S(2)}) collective-permute-start(bf16[80,640]{1,0:T(8,128)(2,1)S(1)} %get-tuple-element.82), channel_id=1, source_target_pairs={{0,16},{4,20},{8,24},{12,28},{16,0},{20,4},{24,8},{28,12},{1,17},{... | collective-permute-start | bytes 307208 | tf_op jit(solution)/shard_map/ppermute | solution.py:25
  4.2 5.6 %collective-permute-start.3 = (bf16[80,640]{1,0:T(8,128)(2,1)S(1)}, bf16[80,640]{1,0:T(8,128)(2,1)S(1)}, u32[]{:S(2)}, u32[]{:S(2)}) collective-permute-start(bf16[80,640]{1,0:T(8,128)(2,1)S(1)} %get-tuple-element.79), channel_id=1, source_target_pairs={{0,24},{4,28},{8,16},{12,20},{16,8},{20,12},{24,0},{28,4},{1,25},{... | collective-permute-start | bytes 307208 | tf_op jit(solution)/shard_map/ppermute | solution.py:25
  6.5 7.5 %collective-permute-start.8 = (bf16[320,320]{1,0:T(8,128)(2,1)S(1)}, bf16[320,320]{1,0:T(8,128)(2,1)S(1)}, u32[]{:S(2)}, u32[]{:S(2)}) collective-permute-start(bf16[320,320]{1,0:T(8,128)(2,1)S(1)} %bitcast.20), channel_id=1, source_target_pairs={{0,1},{1,0},{2,3},{3,2},{4,5},{5,4},{6,7},{7,6},{8,9},{9,8},{10,11... | collective-permute-start | bytes 614408 | tf_op jit(solution)/shard_map/ppermute | solution.py:35
  8.0 2.3 %collective-permute-start.4 = (bf16[80,640]{1,0:T(8,128)(2,1)S(1)}, bf16[80,640]{1,0:T(8,128)(2,1)S(1)}, u32[]{:S(2)}, u32[]{:S(2)}) collective-permute-start(bf16[80,640]{1,0:T(8,128)(2,1)S(1)} %get-tuple-element.80.refs_0_), channel_id=1, source_target_pairs={{0,4},{4,0},{8,12},{12,8},{16,20},{20,16},{24,28},{28,24},{1,5},{5... | collective-permute-start | bytes 307208 | tf_op jit(solution)/shard_map/ppermute | solution.py:25
  8.9 1.5 %collective-permute-start.6 = (bf16[80,640]{1,0:T(8,128)(2,1)S(1)}, bf16[80,640]{1,0:T(8,128)(2,1)S(1)}, u32[]{:S(2)}, u32[]{:S(2)}) collective-permute-start(bf16[80,640]{1,0:T(8,128)(2,1)S(1)} %collective-permute-done.2.refs_2_), channel_id=1, source_target_pairs={{0,4},{4,0},{8,12},{12,8},{16,20},{20,16},{24,28},{28,24},{1,5},{5... | collective-permute-start | bytes 307208 | tf_op jit(solution)/shard_map/ppermute | solution.py:25
  9.9 1.3 %collective-permute-start.7 = (bf16[80,640]{1,0:T(8,128)(2,1)S(1)}, bf16[80,640]{1,0:T(8,128)(2,1)S(1)}, u32[]{:S(2)}, u32[]{:S(2)}) collective-permute-start(bf16[80,640]{1,0:T(8,128)(2,1)S(1)} %collective-permute-done.3.refs_3_), channel_id=1, source_target_pairs={{0,4},{4,0},{8,12},{12,8},{16,20},{20,16},{24,28},{28,24},{1,5},{5... | collective-permute-start | bytes 307208 | tf_op jit(solution)/shard_map/ppermute | solution.py:25
  9.9 1.5 %collective-permute-start.5 = (bf16[80,640]{1,0:T(8,128)(2,1)S(1)}, bf16[80,640]{1,0:T(8,128)(2,1)S(1)}, u32[]{:S(2)}, u32[]{:S(2)}) collective-permute-start(bf16[80,640]{1,0:T(8,128)(2,1)S(1)} %collective-permute-done.refs_1_), channel_id=1, source_target_pairs={{0,4},{4,0},{8,12},{12,8},{16,20},{20,16},{24,28},{28,24},{1,5},{5... | collective-permute-start | bytes 307208 | tf_op jit(solution)/shard_map/ppermute | solution.py:25
  14.0 5.8 %collective-permute-start.9 = (bf16[80,640]{1,0:T(8,128)(2,1)S(1)}, bf16[80,640]{1,0:T(8,128)(2,1)S(1)}, u32[]{:S(2)}, u32[]{:S(2)}) collective-permute-start(bf16[80,640]{1,0:T(8,128)(2,1)S(1)} %get-tuple-element.77), channel_id=1, source_target_pairs={{0,16},{4,20},{8,24},{12,28},{16,0},{20,4},{24,8},{28,12},{1,17},{... | collective-permute-start | bytes 307208 | tf_op jit(solution)/shard_map/ppermute | solution.py:25
  15.6 5.8 %collective-permute-start.10 = (bf16[80,640]{1,0:T(8,128)(2,1)S(1)}, bf16[80,640]{1,0:T(8,128)(2,1)S(1)}, u32[]{:S(2)}, u32[]{:S(2)}) collective-permute-start(bf16[80,640]{1,0:T(8,128)(2,1)S(1)} %get-tuple-element.76), channel_id=1, source_target_pairs={{0,8},{4,12},{8,0},{12,4},{16,24},{20,28},{24,16},{28,20},{1,9},{5... | collective-permute-start | bytes 307208 | tf_op jit(solution)/shard_map/ppermute | solution.py:25
  17.1 5.6 %collective-permute-start.11 = (bf16[80,640]{1,0:T(8,128)(2,1)S(1)}, bf16[80,640]{1,0:T(8,128)(2,1)S(1)}, u32[]{:S(2)}, u32[]{:S(2)}) collective-permute-start(bf16[80,640]{1,0:T(8,128)(2,1)S(1)} %get-tuple-element.75), channel_id=1, source_target_pairs={{0,24},{4,28},{8,16},{12,20},{16,8},{20,12},{24,0},{28,4},{1,25},{... | collective-permute-start | bytes 307208 | tf_op jit(solution)/shard_map/ppermute | solution.py:25
  17.6 9.4 %collective-permute-start.12 = (bf16[80,640]{1,0:T(8,128)(2,1)S(1)}, bf16[80,640]{1,0:T(8,128)(2,1)S(1)}, u32[]{:S(2)}, u32[]{:S(2)}) collective-permute-start(bf16[80,640]{1,0:T(8,128)(2,1)S(1)} %get-tuple-element.78.refs_0_), channel_id=1, source_target_pairs={{0,1},{1,0},{2,3},{3,2},{4,5},{5,4},{6,7},{7,6},{8,9},{9,8},{10,11... | collective-permute-start | bytes 307208 | tf_op jit(solution)/shard_map/ppermute | solution.py:35
  19.9 7.1 %collective-permute-start.13 = (bf16[80,640]{1,0:T(8,128)(2,1)S(1)}, bf16[80,640]{1,0:T(8,128)(2,1)S(1)}, u32[]{:S(2)}, u32[]{:S(2)}) collective-permute-start(bf16[80,640]{1,0:T(8,128)(2,1)S(1)} %collective-permute-done.9.refs_1_), channel_id=1, source_target_pairs={{0,1},{1,0},{2,3},{3,2},{4,5},{5,4},{6,7},{7,6},{8,9},{9,8},{10,11... | collective-permute-start | bytes 307208 | tf_op jit(solution)/shard_map/ppermute | solution.py:35
  21.4 5.5 %collective-permute-start.14 = (bf16[80,640]{1,0:T(8,128)(2,1)S(1)}, bf16[80,640]{1,0:T(8,128)(2,1)S(1)}, u32[]{:S(2)}, u32[]{:S(2)}) collective-permute-start(bf16[80,640]{1,0:T(8,128)(2,1)S(1)} %collective-permute-done.10.refs_2_), channel_id=1, source_target_pairs={{0,1},{1,0},{2,3},{3,2},{4,5},{5,4},{6,7},{7,6},{8,9},{9,8},{10,11... | collective-permute-start | bytes 307208 | tf_op jit(solution)/shard_map/ppermute | solution.py:35
  22.7 4.7 %collective-permute-start.15 = (bf16[80,640]{1,0:T(8,128)(2,1)S(1)}, bf16[80,640]{1,0:T(8,128)(2,1)S(1)}, u32[]{:S(2)}, u32[]{:S(2)}) collective-permute-start(bf16[80,640]{1,0:T(8,128)(2,1)S(1)} %collective-permute-done.11.refs_3_), channel_id=1, source_target_pairs={{0,1},{1,0},{2,3},{3,2},{4,5},{5,4},{6,7},{7,6},{8,9},{9,8},{10,11... | collective-permute-start | bytes 307208 | tf_op jit(solution)/shard_map/ppermute | solution.py:35
  27.3 5.5 %collective-permute-start.16 = (bf16[80,640]{1,0:T(8,128)(2,1)S(1)}, bf16[80,640]{1,0:T(8,128)(2,1)S(1)}, u32[]{:S(2)}, u32[]{:S(2)}) collective-permute-start(bf16[80,640]{1,0:T(8,128)(2,1)S(1)} %get-tuple-element.56.refs_0_), channel_id=1, source_target_pairs={{0,8},{1,2},{2,1},{3,11},{4,12},{5,6},{6,5},{7,15},{8,0},{9,10},{1... | collective-permute-start | bytes 307208 | tf_op jit(solution)/shard_map/ppermute | solution.py:35
  28.5 5.4 %collective-permute-start.21 = (bf16[80,640]{1,0:T(8,128)(2,1)S(1)}, bf16[80,640]{1,0:T(8,128)(2,1)S(1)}, u32[]{:S(2)}, u32[]{:S(2)}) collective-permute-start(bf16[80,640]{1,0:T(8,128)(2,1)S(1)} %get-tuple-element.60.refs_1_), channel_id=1, source_target_pairs={{0,8},{1,2},{2,1},{3,11},{4,12},{5,6},{6,5},{7,15},{8,0},{9,10},{1... | collective-permute-start | bytes 307208 | tf_op jit(solution)/shard_map/ppermute | solution.py:35
  29.5 5.5 %collective-permute-start.19 = (bf16[80,640]{1,0:T(8,128)(2,1)S(1)}, bf16[80,640]{1,0:T(8,128)(2,1)S(1)}, u32[]{:S(2)}, u32[]{:S(2)}) collective-permute-start(bf16[80,640]{1,0:T(8,128)(2,1)S(1)} %get-tuple-element.62.refs_2_), channel_id=1, source_target_pairs={{0,16},{1,2},{2,1},{3,19},{4,20},{5,6},{6,5},{7,23},{8,24},{9,10},... | collective-permute-start | bytes 307208 | tf_op jit(solution)/shard_map/ppermute | solution.py:35
  31.4 4.7 %collective-permute-start.18 = (bf16[80,640]{1,0:T(8,128)(2,1)S(1)}, bf16[80,640]{1,0:T(8,128)(2,1)S(1)}, u32[]{:S(2)}, u32[]{:S(2)}) collective-permute-start(bf16[80,640]{1,0:T(8,128)(2,1)S(1)} %get-tuple-element.63.refs_3_), channel_id=1, source_target_pairs={{0,16},{1,2},{2,1},{3,19},{4,20},{5,6},{6,5},{7,23},{8,24},{9,10},... | collective-permute-start | bytes 307208 | tf_op jit(solution)/shard_map/ppermute | solution.py:35
  32.8 5.9 %collective-permute-start.17 = (bf16[80,640]{1,0:T(8,128)(2,1)S(1)}, bf16[80,640]{1,0:T(8,128)(2,1)S(1)}, u32[]{:S(2)}, u32[]{:S(2)}) collective-permute-start(bf16[80,640]{1,0:T(8,128)(2,1)S(1)} %collective-permute-done.16.refs_0_), channel_id=1, source_target_pairs={{0,4},{1,5},{2,3},{3,2},{4,0},{5,1},{6,7},{7,6},{8,12},{9,13},{10,... | collective-permute-start | bytes 307208 | tf_op jit(solution)/shard_map/ppermute | solution.py:35
  33.9 4.8 %collective-permute-start.22 = (bf16[80,640]{1,0:T(8,128)(2,1)S(1)}, bf16[80,640]{1,0:T(8,128)(2,1)S(1)}, u32[]{:S(2)}, u32[]{:S(2)}) collective-permute-start(bf16[80,640]{1,0:T(8,128)(2,1)S(1)} %collective-permute-done.21.refs_1_), channel_id=1, source_target_pairs={{0,4},{1,5},{2,3},{3,2},{4,0},{5,1},{6,7},{7,6},{8,12},{9,13},{10,... | collective-permute-start | bytes 307208 | tf_op jit(solution)/shard_map/ppermute | solution.py:35
  35.0 4.7 %collective-permute-start.20 = (bf16[80,640]{1,0:T(8,128)(2,1)S(1)}, bf16[80,640]{1,0:T(8,128)(2,1)S(1)}, u32[]{:S(2)}, u32[]{:S(2)}) collective-permute-start(bf16[80,640]{1,0:T(8,128)(2,1)S(1)} %collective-permute-done.19.refs_0_), channel_id=1, source_target_pairs={{0,4},{1,5},{2,3},{3,2},{4,0},{5,1},{6,7},{7,6},{8,12},{9,13},{10,... | collective-permute-start | bytes 307208 | tf_op jit(solution)/shard_map/ppermute | solution.py:35
  36.1 4.7 %collective-permute-start.23 = (bf16[80,640]{1,0:T(8,128)(2,1)S(1)}, bf16[80,640]{1,0:T(8,128)(2,1)S(1)}, u32[]{:S(2)}, u32[]{:S(2)}) collective-permute-start(bf16[80,640]{1,0:T(8,128)(2,1)S(1)} %collective-permute-done.18.refs_0_), channel_id=1, source_target_pairs={{0,4},{1,5},{2,3},{3,2},{4,0},{5,1},{6,7},{7,6},{8,12},{9,13},{10,... | collective-permute-start | bytes 307208 | tf_op jit(solution)/shard_map/ppermute | solution.py:35
  (3 other events, 23.9 us)

commit v11 on v10

--- a/solution.py
+++ b/solution.py
@@ -14,10 +14,6 @@
 
 def in_vmem(*arrays):
     return [pltpu.with_memory_space_constraint(x, pltpu.VMEM) for x in arrays]
-
-
-def in_order(chips):
-    return [0] + sorted(range(1, chips), key=lambda j: (j & (j - 1) != 0, -j))
 
 
 def swap_with(array, mask):
@@ -138,7 +134,7 @@
 def gather_kernel(*refs):
     chip = lax.axis_index(ENERGY) // 2
     *pieces, re_ref, im_ref, all_ref = refs
-    for j, ref in zip(in_order(len(pieces)), pieces):
+    for j, ref in enumerate(pieces):
         all_ref[chip ^ j] = ref[...]
     chips, rows, width = all_ref.shape
     whole = all_ref[...].reshape(chips * rows, width)
@@ -211,31 +207,34 @@
 
 def assembled(pieces, lanes, rows_ref):
     chip = lax.axis_index(ENERGY) // 2
-    for j, ref in zip(in_order(len(pieces)), pieces):
+    for j, ref in enumerate(pieces):
         rows_ref[chip ^ j] = ref[:, lanes]
     chips, rows, size = rows_ref.shape
     return rows_ref[...].reshape(chips * rows, size)
 
 
-def first_kernel(last_pair, part, link_ref, turned_ref, own_ref, *refs):
-    *pieces, out_a_ref, out_b_ref, rows_ref = refs
+def first_kernel(last_pair, link_ref, turned_ref, own_re_ref, own_im_ref, *refs):
+    *pieces, re_a_ref, re_b_ref, im_a_ref, im_b_ref, rows_ref = refs
+    parts = ((own_re_ref, re_a_ref, re_b_ref), (own_im_ref, im_a_ref, im_b_ref))
     size = link_ref.shape[0]
     slab = lax.axis_index(SLAB)
     turn = jnp.logical_and(slab % 2 == 1, slab // 2 < last_pair)
-    half = out_a_ref.shape[0]
+    half = re_a_ref.shape[0]
 
     @pl.when(turn)
     def _():
-        came = assembled(pieces, slice(part * size, (part + 1) * size), rows_ref)
-        own = unpacked(own_ref[...]).astype(jnp.float32)
-        out = packed((own + moved(link_ref, turned_ref, came)).astype(jnp.bfloat16))
-        out_a_ref[...] = out[:half]
-        out_b_ref[...] = out[half:]
+        for part, (own_ref, out_a_ref, out_b_ref) in enumerate(parts):
+            came = assembled(pieces, slice(part * size, (part + 1) * size), rows_ref)
+            own = unpacked(own_ref[...]).astype(jnp.float32)
+            out = packed((own + moved(link_ref, turned_ref, came)).astype(jnp.bfloat16))
+            out_a_ref[...] = out[:half]
+            out_b_ref[...] = out[half:]
 
     @pl.when(jnp.logical_not(turn))
     def _():
-        out_a_ref[...] = own_ref[:half]
-        out_b_ref[...] = own_ref[half:]
+        for own_ref, out_a_ref, out_b_ref in parts:
+            out_a_ref[...] = own_ref[:half]
+            out_b_ref[...] = own_ref[half:]
 
 
 def arrived(refs):
@@ -338,7 +337,7 @@
     pieces = pieces + [swap_with(x, 1) for x in pieces]
     sigma = convolve(chips, spread, pieces)
     sigma, link_before = lax.optimization_barrier((sigma, link_before))
-    own = [sigma[0]] + [swap_with(sigma[j], 2 * j) for j in in_order(chips)[1:]]
+    own = [sigma[0]] + [swap_with(sigma[j], 2 * j) for j in range(1, chips)]
     came = [swap_slabs(x, other_in_pair) for x in own]
     own_re, own_im = gathered(own)
 
@@ -356,8 +355,9 @@
     halves = [((size // 4, width), own_im.dtype)] * 2
     total = [((size, width), jnp.float32)]
     block = pltpu.VMEM((chips, rows, size), jnp.bfloat16)
-    re = call(functools.partial(first_kernel, last_pair, 0), halves, [link, turned, own_re, *came], [block])
-    im = call(functools.partial(first_kernel, last_pair, 1), halves, [link, turned, own_im, *came], [block])
+    given = [link, turned, own_re, own_im, *came]
+    states = call(functools.partial(first_kernel, last_pair), halves * 2, given, [block])
+    re, im = states[:2], states[2:]
 
     for s in range(1, slabs - 1, 2):
         pair = (s + 1) // 2

time: 42.6 us -> 42.7 us (level)
  waiting for transfers between devices: 9.47 us -> 8.53 us
  starting transfers between devices: 22.2 us -> 23 us
    ppermute x13, starting transfers between devices: 14.6 us -> 15.4 us  [swap_slabs(): return lax.ppermute(array, (ENERGY, SLAB), pairs)]
    ppermute x11, waiting for transfers between devices: 4.58 us -> 4.06 us  [swap_with(): return lax.ppermute(array, ENERGY, [(i, i ^ mask) for i in range(devices)])]
    pallas_call x8 -> x7, Pallas kernels: 5.65 us -> 5.67 us  [call(): pl.pallas_call(kernel, out_shape=outs, in_specs=[WHOLE] * len(given), out...]
where the time goes in v11:
time: 42.7 us; the launch traced here: 42.3 us
  starting transfers between devices  23 us (54%)
  waiting for transfers between devices  8.53 us (20%)
  Pallas kernels  8.51 us (20%)
  local copies, waits for them, and re-layouts  2.17 us (5%)
    ppermute x13, starting transfers between devices, swap_slabs(): return lax.ppermute(array, (ENERGY, SLAB), pairs)  15.4 us
    ppermute x11, starting transfers between devices, swap_with(): return lax.ppermute(array, ENERGY, [(i, i ^ mask) for i in range(devices)])  7.62 us
    pallas_call x7, Pallas kernels, call(): pl.pallas_call(kernel, out_shape=outs, in_specs=[WHOLE] * len(given), out...  5.67 us
    ppermute x13, waiting for transfers between devices, swap_slabs(): return lax.ppermute(array, (ENERGY, SLAB), pairs)  4.47 us
    ppermute x11, waiting for transfers between devices, swap_with(): return lax.ppermute(array, ENERGY, [(i, i ^ mask) for i in range(devices)])  4.06 us
    pallas_call x1, Pallas kernels, local(): pl.pallas_call(functools.partial(late_kernel, last_pair), out_shape=jax.S...  1.69 us
    pallas_call x1, Pallas kernels, convolve(): pl.pallas_call(functools.partial(conv_kernel, chips), out_shape=pltpu.VME...  1.15 us
    dynamic_slice x1, local copies, waits for them, and re-layouts, local(): lax.dynamic_slice(lesser, (rows * (chip ^ j), 0), (rows, width))  1.13 us
  transfers between devices with their start and end apart: 24, of which 15 were waited for; matrix products, arithmetic and copies ran while one was open for 3% of the time, Pallas kernels for 16%

profile of v11, /device:TPU:16, one launch (start us, length us, event | category | flops | bytes accessed | tf_op | source)
XLA Modules:
  0.0 42.3 jit_solution(16561665873434287505)
XLA Ops:
  0.0 1.1 %dynamic-slice_bitcast_fusion = (bf16[80,640]{1,0:T(8,128)(2,1)S(1)}, bf16[80,640]{1,0:T(8,128)(2,1)S(1)}, bf16[80,640]{1,0:T(8,128)(2,1)S(1)}, bf16[80,640]{1,0:T(8,128)(2,1)S(1)}) fusion(bf16[1,1,320,640]{3,2,1,0:T(8,128)(2,1)} %param.4, s32[]{:T(128)S(6)} %select_n.21, s32[]{:T(128)S(6)} %select_n.19, s32[]{:T(128)S(6)} %select_n.18, s32[]{:T(128)S(6)} %select_n.20), kind=kLoop, calls=%fused_computation.4 | loop fusion | bytes 819216 | tf_op jit(solution)/shard_map/dynamic_slice | solution.py:329
  1.1 1.6 %collective-permute-start = (bf16[80,640]{1,0:T(8,128)(2,1)S(1)}, bf16[80,640]{1,0:T(8,128)(2,1)S(1)}, u32[]{:S(2)}, u32[]{:S(2)}) collective-permute-start(bf16[80,640]{1,0:T(8,128)(2,1)S(1)} %get-tuple-element.81), channel_id=1, source_target_pairs={{0,8},{4,12},{8,0},{12,4},{16,24},{20,28},{24,16},{28,20},{1,9},{5... | collective-permute-start | bytes 307208 | tf_op jit(solution)/shard_map/ppermute | solution.py:21
  2.7 1.5 %collective-permute-start.2 = (bf16[80,640]{1,0:T(8,128)(2,1)S(1)}, bf16[80,640]{1,0:T(8,128)(2,1)S(1)}, u32[]{:S(2)}, u32[]{:S(2)}) collective-permute-start(bf16[80,640]{1,0:T(8,128)(2,1)S(1)} %get-tuple-element.82), channel_id=1, source_target_pairs={{0,16},{4,20},{8,24},{12,28},{16,0},{20,4},{24,8},{28,12},{1,17},{... | collective-permute-start | bytes 307208 | tf_op jit(solution)/shard_map/ppermute | solution.py:21
  4.7 1.0 %copy-done.2 = bf16[8,1,40,640]{3,2,1,0:T(8,128)(2,1)S(1)} copy-done((bf16[8,1,40,640]{3,2,1,0:T(8,128)(2,1)S(1)}, bf16[8,1,40,640]{3,2,1,0:T(8,128)(2,1)}, u32[]{:S(2)}) %copy-start.2) | copy-done | bytes 409624
  6.5 1.6 %collective-permute-start.8 = (bf16[320,320]{1,0:T(8,128)(2,1)S(1)}, bf16[320,320]{1,0:T(8,128)(2,1)S(1)}, u32[]{:S(2)}, u32[]{:S(2)}) collective-permute-start(bf16[320,320]{1,0:T(8,128)(2,1)S(1)} %bitcast.20), channel_id=1, source_target_pairs={{0,1},{1,0},{2,3},{3,2},{4,5},{5,4},{6,7},{7,6},{8,9},{9,8},{10,11... | collective-permute-start | bytes 614408 | tf_op jit(solution)/shard_map/ppermute | solution.py:31
  8.9 1.0 %collective-permute-done.3.refs_3_ = bf16[80,640]{1,0:T(8,128)(2,1)S(1)} collective-permute-done((bf16[80,640]{1,0:T(8,128)(2,1)S(1)}, bf16[80,640]{1,0:T(8,128)(2,1)S(1)}, u32[]{:S(2)}, u32[]{:S(2)}) %collective-permute-start.3) | collective-permute-done | bytes 102432 | tf_op jit(solution)/shard_map/ppermute | solution.py:21
  11.3 1.1 %shard_map.47 = bf16[4,80,640]{2,1,0:T(8,128)(2,1)S(1)} custom-call(f32[8,80,640]{2,1,0:T(8,128)S(1)} %get-tuple-element.43.w_ref, f32[8,80,640]{2,1,0:T(8,128)S(1)} %get-tuple-element.44.v_ref, bf16[80,640]{1,0:T(8,128)(2,1)S(1)} %get-tuple-element.80.refs_0_, bf16[80,640]{1,0:T(8,128)(2,1)S(1)} %collective-permute-done.refs_1_, ...), custom_call_target="tpu_custom_call" | custom-call | flops 13107200 | tf_op jit(solution)/shard_map/pallas_call | solution.py:105
  12.5 1.5 %collective-permute-done.8.before_ref = bf16[320,320]{1,0:T(8,128)(2,1)S(1)} collective-permute-done((bf16[320,320]{1,0:T(8,128)(2,1)S(1)}, bf16[320,320]{1,0:T(8,128)(2,1)S(1)}, u32[]{:S(2)}, u32[]{:S(2)}) %collective-permute-start.8) | collective-permute-done | bytes 204832 | tf_op jit(solution)/shard_map/ppermute | solution.py:31
  14.0 1.6 %collective-permute-start.9 = (bf16[80,640]{1,0:T(8,128)(2,1)S(1)}, bf16[80,640]{1,0:T(8,128)(2,1)S(1)}, u32[]{:S(2)}, u32[]{:S(2)}) collective-permute-start(bf16[80,640]{1,0:T(8,128)(2,1)S(1)} %get-tuple-element.77), channel_id=1, source_target_pairs={{0,8},{4,12},{8,0},{12,4},{16,24},{20,28},{24,16},{28,20},{1,9},{5... | collective-permute-start | bytes 307208 | tf_op jit(solution)/shard_map/ppermute | solution.py:21
  15.6 1.5 %collective-permute-start.10 = (bf16[80,640]{1,0:T(8,128)(2,1)S(1)}, bf16[80,640]{1,0:T(8,128)(2,1)S(1)}, u32[]{:S(2)}, u32[]{:S(2)}) collective-permute-start(bf16[80,640]{1,0:T(8,128)(2,1)S(1)} %get-tuple-element.76), channel_id=1, source_target_pairs={{0,16},{4,20},{8,24},{12,28},{16,0},{20,4},{24,8},{28,12},{1,17},{... | collective-permute-start | bytes 307208 | tf_op jit(solution)/shard_map/ppermute | solution.py:21
  17.6 1.6 %collective-permute-start.12 = (bf16[80,640]{1,0:T(8,128)(2,1)S(1)}, bf16[80,640]{1,0:T(8,128)(2,1)S(1)}, u32[]{:S(2)}, u32[]{:S(2)}) collective-permute-start(bf16[80,640]{1,0:T(8,128)(2,1)S(1)} %get-tuple-element.78.refs_0_), channel_id=1, source_target_pairs={{0,1},{1,0},{2,3},{3,2},{4,5},{5,4},{6,7},{7,6},{8,9},{9,8},{10,11... | collective-permute-start | bytes 307208 | tf_op jit(solution)/shard_map/ppermute | solution.py:31
  19.8 1.6 %collective-permute-start.13 = (bf16[80,640]{1,0:T(8,128)(2,1)S(1)}, bf16[80,640]{1,0:T(8,128)(2,1)S(1)}, u32[]{:S(2)}, u32[]{:S(2)}) collective-permute-start(bf16[80,640]{1,0:T(8,128)(2,1)S(1)} %collective-permute-done.9.refs_1_), channel_id=1, source_target_pairs={{0,1},{1,0},{2,3},{3,2},{4,5},{5,4},{6,7},{7,6},{8,9},{9,8},{10,11... | collective-permute-start | bytes 307208 | tf_op jit(solution)/shard_map/ppermute | solution.py:31
  21.4 1.0 %collective-permute-start.14 = (bf16[80,640]{1,0:T(8,128)(2,1)S(1)}, bf16[80,640]{1,0:T(8,128)(2,1)S(1)}, u32[]{:S(2)}, u32[]{:S(2)}) collective-permute-start(bf16[80,640]{1,0:T(8,128)(2,1)S(1)} %collective-permute-done.10.refs_2_), channel_id=1, source_target_pairs={{0,1},{1,0},{2,3},{3,2},{4,5},{5,4},{6,7},{7,6},{8,9},{9,8},{10,11... | collective-permute-start | bytes 307208 | tf_op jit(solution)/shard_map/ppermute | solution.py:31
  22.7 1.6 %collective-permute-start.15 = (bf16[80,640]{1,0:T(8,128)(2,1)S(1)}, bf16[80,640]{1,0:T(8,128)(2,1)S(1)}, u32[]{:S(2)}, u32[]{:S(2)}) collective-permute-start(bf16[80,640]{1,0:T(8,128)(2,1)S(1)} %collective-permute-done.11.refs_3_), channel_id=1, source_target_pairs={{0,1},{1,0},{2,3},{3,2},{4,5},{5,4},{6,7},{7,6},{8,9},{9,8},{10,11... | collective-permute-start | bytes 307208 | tf_op jit(solution)/shard_map/ppermute | solution.py:31
  24.4 2.5 %shard_map.49 = (bf16[320,320]{1,0:T(8,128)(2,1)S(1)}, bf16[320,320]{1,0:T(8,128)(2,1)}, bf16[320,320]{1,0:T(8,128)(2,1)}, bf16[640,320]{1,0:T(8,128)(2,1)S(1)},...) custom-call(bf16[320,320]{1,0:T(8,128)(2,1)S(1)} %bitcast.21, ...), custom_call_target="tpu_custom_call" | custom-call | tf_op jit(solution)/shard_map/pallas_call | solution.py:36
  27.4 1.5 %collective-permute-start.16 = (bf16[80,640]{1,0:T(8,128)(2,1)S(1)}, bf16[80,640]{1,0:T(8,128)(2,1)S(1)}, u32[]{:S(2)}, u32[]{:S(2)}) collective-permute-start(bf16[80,640]{1,0:T(8,128)(2,1)S(1)} %get-tuple-element.57.refs_0_), channel_id=1, source_target_pairs={{0,8},{1,2},{2,1},{3,11},{4,12},{5,6},{6,5},{7,15},{8,0},{9,10},{1... | collective-permute-start | bytes 307208 | tf_op jit(solution)/shard_map/ppermute | solution.py:31
  29.5 1.5 %collective-permute-start.19 = (bf16[80,640]{1,0:T(8,128)(2,1)S(1)}, bf16[80,640]{1,0:T(8,128)(2,1)S(1)}, u32[]{:S(2)}, u32[]{:S(2)}) collective-permute-start(bf16[80,640]{1,0:T(8,128)(2,1)S(1)} %get-tuple-element.62.refs_2_), channel_id=1, source_target_pairs={{0,16},{1,2},{2,1},{3,19},{4,20},{5,6},{6,5},{7,23},{8,24},{9,10},... | collective-permute-start | bytes 307208 | tf_op jit(solution)/shard_map/ppermute | solution.py:31
  31.5 1.2 %collective-permute-done.16.refs_0_ = bf16[80,640]{1,0:T(8,128)(2,1)S(1)} collective-permute-done((bf16[80,640]{1,0:T(8,128)(2,1)S(1)}, bf16[80,640]{1,0:T(8,128)(2,1)S(1)}, u32[]{:S(2)}, u32[]{:S(2)}) %collective-permute-start.16) | collective-permute-done | bytes 102432 | tf_op jit(solution)/shard_map/ppermute | solution.py:31
  32.7 1.0 %collective-permute-start.17 = (bf16[80,640]{1,0:T(8,128)(2,1)S(1)}, bf16[80,640]{1,0:T(8,128)(2,1)S(1)}, u32[]{:S(2)}, u32[]{:S(2)}) collective-permute-start(bf16[80,640]{1,0:T(8,128)(2,1)S(1)} %collective-permute-done.16.refs_0_), channel_id=1, source_target_pairs={{0,4},{1,5},{2,3},{3,2},{4,0},{5,1},{6,7},{7,6},{8,12},{9,13},{10,... | collective-permute-start | bytes 307208 | tf_op jit(solution)/shard_map/ppermute | solution.py:31
  33.8 1.0 %collective-permute-start.22 = (bf16[80,640]{1,0:T(8,128)(2,1)S(1)}, bf16[80,640]{1,0:T(8,128)(2,1)S(1)}, u32[]{:S(2)}, u32[]{:S(2)}) collective-permute-start(bf16[80,640]{1,0:T(8,128)(2,1)S(1)} %collective-permute-done.21.refs_1_), channel_id=1, source_target_pairs={{0,4},{1,5},{2,3},{3,2},{4,0},{5,1},{6,7},{7,6},{8,12},{9,13},{10,... | collective-permute-start | bytes 307208 | tf_op jit(solution)/shard_map/ppermute | solution.py:31
  34.9 0.9 %collective-permute-start.20 = (bf16[80,640]{1,0:T(8,128)(2,1)S(1)}, bf16[80,640]{1,0:T(8,128)(2,1)S(1)}, u32[]{:S(2)}, u32[]{:S(2)}) collective-permute-start(bf16[80,640]{1,0:T(8,128)(2,1)S(1)} %collective-permute-done.19.refs_0_), channel_id=1, source_target_pairs={{0,4},{1,5},{2,3},{3,2},{4,0},{5,1},{6,7},{7,6},{8,12},{9,13},{10,... | collective-permute-start | bytes 307208 | tf_op jit(solution)/shard_map/ppermute | solution.py:31
  36.0 1.0 %collective-permute-start.23 = (bf16[80,640]{1,0:T(8,128)(2,1)S(1)}, bf16[80,640]{1,0:T(8,128)(2,1)S(1)}, u32[]{:S(2)}, u32[]{:S(2)}) collective-permute-start(bf16[80,640]{1,0:T(8,128)(2,1)S(1)} %collective-permute-done.18.refs_0_), channel_id=1, source_target_pairs={{0,4},{1,5},{2,3},{3,2},{4,0},{5,1},{6,7},{7,6},{8,12},{9,13},{10,... | collective-permute-start | bytes 307208 | tf_op jit(solution)/shard_map/ppermute | solution.py:31
  37.0 1.6 %shard_map.51.base_ref = f32[320,640]{1,0:T(8,128)S(1)} custom-call(bf16[320,320]{1,0:T(8,128)(2,1)S(1)} %bitcast.23, bf16[320,320]{1,0:T(8,128)(2,1)S(1)} %get-tuple-element.54.turned_ref, bf16[640,320]{1,0:T(8,128)(2,1)S(1)} %get-tuple-element.58.stack_ref, bf16[320,640]{1,0:T(8,128)(2,1)S(1)} %get-tuple-element.59.first_ref, ...), custom_call_target="tpu_custom_call" | custom-call | tf_op jit(solution)/shard_map/pallas_call | solution.py:36
  40.6 1.7 %shard_map.54 = bf16[320,640]{1,0:T(8,128)(2,1)} custom-call(bf16[320,640]{1,0:T(8,128)(2,1)S(1)} %get-tuple-element.51.far_first_ref, bf16[320,640]{1,0:T(8,128)(2,1)S(1)} %get-tuple-element.52.far_second_ref, bf16[640,160]{1,0:T(8,128)(2,1)S(1)} %get-tuple-element.53.half_ref, f32[320,640]{1,0:T(8,128)S(1)} %shard_map.51.base_ref, ...), custom_call_target="tpu_custom_call" | custom-call | tf_op jit(solution)/shard_map/pallas_call | solution.py:386
  (41 shorter events, 9.1 us)
Async XLA Ops:
  0.0 4.7 %collective-permute-start.1 = (bf16[8,40,640]{2,1,0:T(8,128)(2,1)}, bf16[8,40,640]{2,1,0:T(8,128)(2,1)S(1)}, u32[]{:S(2)}, u32[]{:S(2)}) collective-permute-start(bf16[8,40,640]{2,1,0:T(8,128)(2,1)} %bitcast.25), channel_id=1, source_target_pairs={{0,4},{4,0},{8,12},{12,8},{16,20},{20,16},{24,28},{28,24},{1,5},{5... | collective-permute-start | bytes 1228808 | tf_op jit(solution)/shard_map/ppermute | solution.py:21
  1.1 5.3 %collective-permute-start = (bf16[80,640]{1,0:T(8,128)(2,1)S(1)}, bf16[80,640]{1,0:T(8,128)(2,1)S(1)}, u32[]{:S(2)}, u32[]{:S(2)}) collective-permute-start(bf16[80,640]{1,0:T(8,128)(2,1)S(1)} %get-tuple-element.81), channel_id=1, source_target_pairs={{0,8},{4,12},{8,0},{12,4},{16,24},{20,28},{24,16},{28,20},{1,9},{5... | collective-permute-start | bytes 307208 | tf_op jit(solution)/shard_map/ppermute | solution.py:21
  2.7 6.2 %collective-permute-start.2 = (bf16[80,640]{1,0:T(8,128)(2,1)S(1)}, bf16[80,640]{1,0:T(8,128)(2,1)S(1)}, u32[]{:S(2)}, u32[]{:S(2)}) collective-permute-start(bf16[80,640]{1,0:T(8,128)(2,1)S(1)} %get-tuple-element.82), channel_id=1, source_target_pairs={{0,16},{4,20},{8,24},{12,28},{16,0},{20,4},{24,8},{28,12},{1,17},{... | collective-permute-start | bytes 307208 | tf_op jit(solution)/shard_map/ppermute | solution.py:21
  4.2 5.6 %collective-permute-start.3 = (bf16[80,640]{1,0:T(8,128)(2,1)S(1)}, bf16[80,640]{1,0:T(8,128)(2,1)S(1)}, u32[]{:S(2)}, u32[]{:S(2)}) collective-permute-start(bf16[80,640]{1,0:T(8,128)(2,1)S(1)} %get-tuple-element.79), channel_id=1, source_target_pairs={{0,24},{4,28},{8,16},{12,20},{16,8},{20,12},{24,0},{28,4},{1,25},{... | collective-permute-start | bytes 307208 | tf_op jit(solution)/shard_map/ppermute | solution.py:21
  6.5 7.5 %collective-permute-start.8 = (bf16[320,320]{1,0:T(8,128)(2,1)S(1)}, bf16[320,320]{1,0:T(8,128)(2,1)S(1)}, u32[]{:S(2)}, u32[]{:S(2)}) collective-permute-start(bf16[320,320]{1,0:T(8,128)(2,1)S(1)} %bitcast.20), channel_id=1, source_target_pairs={{0,1},{1,0},{2,3},{3,2},{4,5},{5,4},{6,7},{7,6},{8,9},{9,8},{10,11... | collective-permute-start | bytes 614408 | tf_op jit(solution)/shard_map/ppermute | solution.py:31
  8.0 2.3 %collective-permute-start.4 = (bf16[80,640]{1,0:T(8,128)(2,1)S(1)}, bf16[80,640]{1,0:T(8,128)(2,1)S(1)}, u32[]{:S(2)}, u32[]{:S(2)}) collective-permute-start(bf16[80,640]{1,0:T(8,128)(2,1)S(1)} %get-tuple-element.80.refs_0_), channel_id=1, source_target_pairs={{0,4},{4,0},{8,12},{12,8},{16,20},{20,16},{24,28},{28,24},{1,5},{5... | collective-permute-start | bytes 307208 | tf_op jit(solution)/shard_map/ppermute | solution.py:21
  8.9 1.5 %collective-permute-start.6 = (bf16[80,640]{1,0:T(8,128)(2,1)S(1)}, bf16[80,640]{1,0:T(8,128)(2,1)S(1)}, u32[]{:S(2)}, u32[]{:S(2)}) collective-permute-start(bf16[80,640]{1,0:T(8,128)(2,1)S(1)} %collective-permute-done.2.refs_2_), channel_id=1, source_target_pairs={{0,4},{4,0},{8,12},{12,8},{16,20},{20,16},{24,28},{28,24},{1,5},{5... | collective-permute-start | bytes 307208 | tf_op jit(solution)/shard_map/ppermute | solution.py:21
  9.9 1.3 %collective-permute-start.7 = (bf16[80,640]{1,0:T(8,128)(2,1)S(1)}, bf16[80,640]{1,0:T(8,128)(2,1)S(1)}, u32[]{:S(2)}, u32[]{:S(2)}) collective-permute-start(bf16[80,640]{1,0:T(8,128)(2,1)S(1)} %collective-permute-done.3.refs_3_), channel_id=1, source_target_pairs={{0,4},{4,0},{8,12},{12,8},{16,20},{20,16},{24,28},{28,24},{1,5},{5... | collective-permute-start | bytes 307208 | tf_op jit(solution)/shard_map/ppermute | solution.py:21
  9.9 1.5 %collective-permute-start.5 = (bf16[80,640]{1,0:T(8,128)(2,1)S(1)}, bf16[80,640]{1,0:T(8,128)(2,1)S(1)}, u32[]{:S(2)}, u32[]{:S(2)}) collective-permute-start(bf16[80,640]{1,0:T(8,128)(2,1)S(1)} %collective-permute-done.refs_1_), channel_id=1, source_target_pairs={{0,4},{4,0},{8,12},{12,8},{16,20},{20,16},{24,28},{28,24},{1,5},{5... | collective-permute-start | bytes 307208 | tf_op jit(solution)/shard_map/ppermute | solution.py:21
  14.0 5.8 %collective-permute-start.9 = (bf16[80,640]{1,0:T(8,128)(2,1)S(1)}, bf16[80,640]{1,0:T(8,128)(2,1)S(1)}, u32[]{:S(2)}, u32[]{:S(2)}) collective-permute-start(bf16[80,640]{1,0:T(8,128)(2,1)S(1)} %get-tuple-element.77), channel_id=1, source_target_pairs={{0,8},{4,12},{8,0},{12,4},{16,24},{20,28},{24,16},{28,20},{1,9},{5... | collective-permute-start | bytes 307208 | tf_op jit(solution)/shard_map/ppermute | solution.py:21
  15.6 5.8 %collective-permute-start.10 = (bf16[80,640]{1,0:T(8,128)(2,1)S(1)}, bf16[80,640]{1,0:T(8,128)(2,1)S(1)}, u32[]{:S(2)}, u32[]{:S(2)}) collective-permute-start(bf16[80,640]{1,0:T(8,128)(2,1)S(1)} %get-tuple-element.76), channel_id=1, source_target_pairs={{0,16},{4,20},{8,24},{12,28},{16,0},{20,4},{24,8},{28,12},{1,17},{... | collective-permute-start | bytes 307208 | tf_op jit(solution)/shard_map/ppermute | solution.py:21
  17.1 5.6 %collective-permute-start.11 = (bf16[80,640]{1,0:T(8,128)(2,1)S(1)}, bf16[80,640]{1,0:T(8,128)(2,1)S(1)}, u32[]{:S(2)}, u32[]{:S(2)}) collective-permute-start(bf16[80,640]{1,0:T(8,128)(2,1)S(1)} %get-tuple-element.75), channel_id=1, source_target_pairs={{0,24},{4,28},{8,16},{12,20},{16,8},{20,12},{24,0},{28,4},{1,25},{... | collective-permute-start | bytes 307208 | tf_op jit(solution)/shard_map/ppermute | solution.py:21
  17.6 9.4 %collective-permute-start.12 = (bf16[80,640]{1,0:T(8,128)(2,1)S(1)}, bf16[80,640]{1,0:T(8,128)(2,1)S(1)}, u32[]{:S(2)}, u32[]{:S(2)}) collective-permute-start(bf16[80,640]{1,0:T(8,128)(2,1)S(1)} %get-tuple-element.78.refs_0_), channel_id=1, source_target_pairs={{0,1},{1,0},{2,3},{3,2},{4,5},{5,4},{6,7},{7,6},{8,9},{9,8},{10,11... | collective-permute-start | bytes 307208 | tf_op jit(solution)/shard_map/ppermute | solution.py:31
  19.8 7.1 %collective-permute-start.13 = (bf16[80,640]{1,0:T(8,128)(2,1)S(1)}, bf16[80,640]{1,0:T(8,128)(2,1)S(1)}, u32[]{:S(2)}, u32[]{:S(2)}) collective-permute-start(bf16[80,640]{1,0:T(8,128)(2,1)S(1)} %collective-permute-done.9.refs_1_), channel_id=1, source_target_pairs={{0,1},{1,0},{2,3},{3,2},{4,5},{5,4},{6,7},{7,6},{8,9},{9,8},{10,11... | collective-permute-start | bytes 307208 | tf_op jit(solution)/shard_map/ppermute | solution.py:31
  21.4 5.5 %collective-permute-start.14 = (bf16[80,640]{1,0:T(8,128)(2,1)S(1)}, bf16[80,640]{1,0:T(8,128)(2,1)S(1)}, u32[]{:S(2)}, u32[]{:S(2)}) collective-permute-start(bf16[80,640]{1,0:T(8,128)(2,1)S(1)} %collective-permute-done.10.refs_2_), channel_id=1, source_target_pairs={{0,1},{1,0},{2,3},{3,2},{4,5},{5,4},{6,7},{7,6},{8,9},{9,8},{10,11... | collective-permute-start | bytes 307208 | tf_op jit(solution)/shard_map/ppermute | solution.py:31
  22.7 4.7 %collective-permute-start.15 = (bf16[80,640]{1,0:T(8,128)(2,1)S(1)}, bf16[80,640]{1,0:T(8,128)(2,1)S(1)}, u32[]{:S(2)}, u32[]{:S(2)}) collective-permute-start(bf16[80,640]{1,0:T(8,128)(2,1)S(1)} %collective-permute-done.11.refs_3_), channel_id=1, source_target_pairs={{0,1},{1,0},{2,3},{3,2},{4,5},{5,4},{6,7},{7,6},{8,9},{9,8},{10,11... | collective-permute-start | bytes 307208 | tf_op jit(solution)/shard_map/ppermute | solution.py:31
  27.4 5.3 %collective-permute-start.16 = (bf16[80,640]{1,0:T(8,128)(2,1)S(1)}, bf16[80,640]{1,0:T(8,128)(2,1)S(1)}, u32[]{:S(2)}, u32[]{:S(2)}) collective-permute-start(bf16[80,640]{1,0:T(8,128)(2,1)S(1)} %get-tuple-element.57.refs_0_), channel_id=1, source_target_pairs={{0,8},{1,2},{2,1},{3,11},{4,12},{5,6},{6,5},{7,15},{8,0},{9,10},{1... | collective-permute-start | bytes 307208 | tf_op jit(solution)/shard_map/ppermute | solution.py:31
  28.9 4.9 %collective-permute-start.21 = (bf16[80,640]{1,0:T(8,128)(2,1)S(1)}, bf16[80,640]{1,0:T(8,128)(2,1)S(1)}, u32[]{:S(2)}, u32[]{:S(2)}) collective-permute-start(bf16[80,640]{1,0:T(8,128)(2,1)S(1)} %get-tuple-element.61.refs_1_), channel_id=1, source_target_pairs={{0,8},{1,2},{2,1},{3,11},{4,12},{5,6},{6,5},{7,15},{8,0},{9,10},{1... | collective-permute-start | bytes 307208 | tf_op jit(solution)/shard_map/ppermute | solution.py:31
  29.5 5.4 %collective-permute-start.19 = (bf16[80,640]{1,0:T(8,128)(2,1)S(1)}, bf16[80,640]{1,0:T(8,128)(2,1)S(1)}, u32[]{:S(2)}, u32[]{:S(2)}) collective-permute-start(bf16[80,640]{1,0:T(8,128)(2,1)S(1)} %get-tuple-element.62.refs_2_), channel_id=1, source_target_pairs={{0,16},{1,2},{2,1},{3,19},{4,20},{5,6},{6,5},{7,23},{8,24},{9,10},... | collective-permute-start | bytes 307208 | tf_op jit(solution)/shard_map/ppermute | solution.py:31
  30.9 5.0 %collective-permute-start.18 = (bf16[80,640]{1,0:T(8,128)(2,1)S(1)}, bf16[80,640]{1,0:T(8,128)(2,1)S(1)}, u32[]{:S(2)}, u32[]{:S(2)}) collective-permute-start(bf16[80,640]{1,0:T(8,128)(2,1)S(1)} %get-tuple-element.63.refs_3_), channel_id=1, source_target_pairs={{0,16},{1,2},{2,1},{3,19},{4,20},{5,6},{6,5},{7,23},{8,24},{9,10},... | collective-permute-start | bytes 307208 | tf_op jit(solution)/shard_map/ppermute | solution.py:31
  32.7 5.9 %collective-permute-start.17 = (bf16[80,640]{1,0:T(8,128)(2,1)S(1)}, bf16[80,640]{1,0:T(8,128)(2,1)S(1)}, u32[]{:S(2)}, u32[]{:S(2)}) collective-permute-start(bf16[80,640]{1,0:T(8,128)(2,1)S(1)} %collective-permute-done.16.refs_0_), channel_id=1, source_target_pairs={{0,4},{1,5},{2,3},{3,2},{4,0},{5,1},{6,7},{7,6},{8,12},{9,13},{10,... | collective-permute-start | bytes 307208 | tf_op jit(solution)/shard_map/ppermute | solution.py:31
  33.8 4.9 %collective-permute-start.22 = (bf16[80,640]{1,0:T(8,128)(2,1)S(1)}, bf16[80,640]{1,0:T(8,128)(2,1)S(1)}, u32[]{:S(2)}, u32[]{:S(2)}) collective-permute-start(bf16[80,640]{1,0:T(8,128)(2,1)S(1)} %collective-permute-done.21.refs_1_), channel_id=1, source_target_pairs={{0,4},{1,5},{2,3},{3,2},{4,0},{5,1},{6,7},{7,6},{8,12},{9,13},{10,... | collective-permute-start | bytes 307208 | tf_op jit(solution)/shard_map/ppermute | solution.py:31
  34.9 4.7 %collective-permute-start.20 = (bf16[80,640]{1,0:T(8,128)(2,1)S(1)}, bf16[80,640]{1,0:T(8,128)(2,1)S(1)}, u32[]{:S(2)}, u32[]{:S(2)}) collective-permute-start(bf16[80,640]{1,0:T(8,128)(2,1)S(1)} %collective-permute-done.19.refs_0_), channel_id=1, source_target_pairs={{0,4},{1,5},{2,3},{3,2},{4,0},{5,1},{6,7},{7,6},{8,12},{9,13},{10,... | collective-permute-start | bytes 307208 | tf_op jit(solution)/shard_map/ppermute | solution.py:31
  36.0 4.7 %collective-permute-start.23 = (bf16[80,640]{1,0:T(8,128)(2,1)S(1)}, bf16[80,640]{1,0:T(8,128)(2,1)S(1)}, u32[]{:S(2)}, u32[]{:S(2)}) collective-permute-start(bf16[80,640]{1,0:T(8,128)(2,1)S(1)} %collective-permute-done.18.refs_0_), channel_id=1, source_target_pairs={{0,4},{1,5},{2,3},{3,2},{4,0},{5,1},{6,7},{7,6},{8,12},{9,13},{10,... | collective-permute-start | bytes 307208 | tf_op jit(solution)/shard_map/ppermute | solution.py:31
  (3 other events, 23.9 us)
